TPU v7x, 32 devices: a whole 2x2x4 slice. The times are simulated.
32 devices in a mesh: row: 16 (over z, y, x), col: 2 (over core).
Axes of the slice: x: 2, y: 2, z: 4, core: 2. Of those that a mesh axis runs over, the one named last changes fastest.
Arguments:
- tokens: bfloat16 [8192, 768], P(('row', 'col')), may hold values from -6 to 6
- seg_ids: int32 [32, 256], P(('row', 'col')), may hold values from 0 to 15, never falling along the last dimension, each value on 1 to 128 neighbouring positions
- live_mask: int32 [32, 256], P(('row', 'col')), may hold values from 0 to 1, as said below
- ret_rows: int32 [8192, 16], P(('row', 'col')), may hold values from 0 to 65535, as said below
- enc_store: bfloat16 [65536, 768], P(('row', 'col')), may hold values from -6 to 6
- attn_in: bfloat16 [6, 768, 768], P(None, 'row', 'col'), may hold values from -0.21875 to 0.21875
- attn_out: bfloat16 [2, 768, 768], P(None, 'row', 'col'), may hold values from -0.625 to 0.625
- ff_in: bfloat16 [768, 3072], P('row', 'col'), may hold values from -0.21875 to 0.21875
- ff_out: bfloat16 [3072, 768], P('row', 'col'), may hold values from -0.109375 to 0.109375
- biases: bfloat16 [7, 768], P(None, 'row'), may hold values from -3 to 3
- ln_gain: bfloat16 [3, 768], P(None, 'row'), may hold values from 0.25 to 1.75
- ln_shift: bfloat16 [3, 768], P(None, 'row'), may hold values from -2 to 2
- ff_bias: bfloat16 [3072], P('row'), may hold values from -3 to 3
- cotangent: bfloat16 [8192, 768], P(('row', 'col')), may hold values from -6 to 6
Outputs:
- output: bfloat16 [8192, 768], P(('row', 'col'))
- grad_tokens: float32 [8192, 768], P(('row', 'col'))
- grad_store: float32 [65536, 768], P(('row', 'col'))
- grad_attn_in: float32 [6, 768, 768], P(None, 'row', 'col')
- grad_attn_out: float32 [2, 768, 768], P(None, 'row', 'col')
- grad_ff_in: float32 [768, 3072], P('row', 'col')
- grad_ff_out: float32 [3072, 768], P('row', 'col')
- grad_biases: float32 [7, 768], P(None, 'row')
- grad_ln_gain: float32 [3, 768], P(None, 'row')
- grad_ln_shift: float32 [3, 768], P(None, 'row')
- grad_ff_bias: float32 [3072], P('row')
Inputs may be any that keep to these rules, and one draw needn't show every extreme that they name: Shard k is the store rows k * 2048 to (k + 1) * 2048 - 1, and sequence p's rows of ret_rows are its tokens' rows. Of the 4096 entries of one sequence, at most 192 lie in any one shard; exactly 192 lie in each of the same half of the shards for every sequence. `live_mask`: the padding of a sequence, if any, is its last tokens, at most 32 of them.
All inputs are finite; a program needn't handle non-finite values.
Results may differ from a plain program's by a relative error of at most 0.025.
Values may be sent and summed in bfloat16 or wider, within the bound.
No kernel may reach another device: no remote copies, remote signals or barrier semaphores. Data moves between devices by JAX's collectives and lax.ppermute only.
A program may use at most 256 MiB of HBM per device.

v0:
```python
import jax
import jax.numpy as jnp
from jax import lax
from jax.sharding import PartitionSpec as P

H = 12
HD = 64


def norm_fwd(resid, gain, shift):
    row_mean = jnp.mean(resid, axis=-1, keepdims=True)
    centered = resid - row_mean
    inv_std = lax.rsqrt(jnp.mean(centered * centered, axis=-1, keepdims=True) + 1e-05)
    normed = centered * inv_std
    return (normed * gain + shift, normed, inv_std)


def norm_back(grad_in, normed, inv_std, gain):
    grad_gain = jnp.sum(grad_in * normed, axis=0)
    grad_shift = jnp.sum(grad_in, axis=0)
    scaled = grad_in * gain
    grad_resid = inv_std * (
        scaled
        - jnp.mean(scaled, axis=-1, keepdims=True)
        - normed * jnp.mean(scaled * normed, axis=-1, keepdims=True)
    )
    return (grad_resid, grad_gain, grad_shift)


def gelu_parts(pre_act):
    cdf_part = 0.5 * (1.0 + jax.scipy.special.erf(pre_act * 0.7071067811865476))
    density = jnp.exp(-0.5 * pre_act * pre_act) * 0.3989422804014327
    return (pre_act * cdf_part, cdf_part + pre_act * density)


def visible_mask(row_start, block_rows, seg_row, live_row):
    total = seg_row.shape[0]
    query_pos = row_start + jnp.arange(block_rows, dtype=jnp.int32)
    key_pos = jnp.arange(total, dtype=jnp.int32)
    return (
        (key_pos[None, :] <= query_pos[:, None])
        & (seg_row[:, None] == seg_row[None, :])
        & ((live_row[None, :] == 1) | (key_pos[None, :] == query_pos[:, None]))
    )


def self_scores(query_blk, key_rows, visible):
    scores = (
        jnp.einsum("qhd,khd->hqk", query_blk, key_rows, preferred_element_type=jnp.float32) * 0.125
    )
    return jnp.where(visible[None], scores, -1e30)


def plan_requests(ret_rows, shard_rows, peers, slots):
    flat = ret_rows.reshape(-1)
    owner = flat // shard_rows
    local_row = flat - owner * shard_rows
    order = jnp.argsort(owner, stable=True)
    sorted_owner = owner[order]
    first_pos = jnp.searchsorted(sorted_owner, sorted_owner, side="left")
    place_sorted = sorted_owner * slots + jnp.arange(flat.shape[0], dtype=jnp.int32) - first_pos
    place = jnp.zeros_like(flat).at[order].set(place_sorted)
    wanted = jnp.zeros((peers * slots,), jnp.int32).at[place].set(local_row)
    return (place, wanted)


def column_sum(array):
    return jnp.sum(array.astype(jnp.float32), axis=0)


def on_device(
    tokens,
    seg_ids,
    live_mask,
    ret_rows,
    enc_store,
    attn_in,
    attn_out,
    ff_in,
    ff_out,
    biases,
    ln_gain,
    ln_shift,
    ff_bias,
    cotangent,
):
    bf16 = jnp.bfloat16
    f32 = jnp.float32
    n_rows = lax.axis_size("row")
    n_cols = lax.axis_size("col")
    peers = n_rows * n_cols
    tok_count, model_dim = tokens.shape
    shard_rows = enc_store.shape[0]
    ret_count = ret_rows.shape[1]
    slots = 3 * ret_rows.size // (2 * peers)
    wide_in, wide_out, wide_ff1, wide_ff2 = (
        lax.all_gather(attn_in, "col", axis=2, tiled=True),
        lax.all_gather(attn_out, "col", axis=2, tiled=True),
        lax.all_gather(ff_in, "col", axis=1, tiled=True),
        lax.all_gather(ff_out, "col", axis=1, tiled=True),
    )
    w_in, w_out, w_ff1, w_ff2, bias_all, gain_all, shift_all, bias_ff = (
        lax.all_gather(wide_in, "row", axis=1, tiled=True),
        lax.all_gather(wide_out, "row", axis=1, tiled=True),
        lax.all_gather(wide_ff1, "row", axis=0, tiled=True),
        lax.all_gather(wide_ff2, "row", axis=0, tiled=True),
        lax.all_gather(biases, "row", axis=1, tiled=True),
        lax.all_gather(ln_gain, "row", axis=1, tiled=True),
        lax.all_gather(ln_shift, "row", axis=1, tiled=True),
        lax.all_gather(ff_bias, "row", axis=0, tiled=True),
    )
    bias_all = bias_all.astype(f32)
    gain_all = gain_all.astype(f32)
    shift_all = shift_all.astype(f32)
    bias_ff = bias_ff.astype(f32)
    place, wanted = plan_requests(ret_rows, shard_rows, peers, slots)
    asked = lax.all_to_all(
        lax.all_to_all(
            wanted.reshape(n_rows, n_cols, slots), "row", split_axis=0, concat_axis=0, tiled=True
        ),
        "col",
        split_axis=1,
        concat_axis=1,
        tiled=True,
    )
    answer = enc_store[asked]
    arrived = lax.all_to_all(
        lax.all_to_all(answer, "row", split_axis=0, concat_axis=0, tiled=True),
        "col",
        split_axis=1,
        concat_axis=1,
        tiled=True,
    )
    fetched = arrived.reshape(peers * slots, model_dim)[place].reshape(
        tok_count, ret_count, model_dim
    )
    tokens_wide = tokens.astype(f32)
    proj = jnp.einsum("td,kde->kte", tokens, w_in[:3], preferred_element_type=f32)
    queries = (proj[0] + bias_all[0]).astype(bf16).reshape(tok_count, H, HD)
    key_rows = proj[1].astype(bf16).reshape(tok_count, H, HD)
    values = (proj[2] + bias_all[1]).astype(bf16).reshape(tok_count, H, HD)
    seg_row = seg_ids[0]
    live_row = live_mask[0]
    block_rows = min(512, tok_count)
    row_start = 0
    visible = visible_mask(row_start, block_rows, seg_row, live_row)
    scores = self_scores(queries, key_rows, visible)
    row_max = jnp.max(scores, axis=-1, keepdims=True)
    expo = jnp.exp(scores - row_max)
    row_sum = jnp.sum(expo, axis=-1, keepdims=True)
    log_norms = [row_max + jnp.log(row_sum)]
    probs_low = (expo / row_sum).astype(bf16)
    pieces = jnp.einsum("hqk,khd->qhd", probs_low, values, preferred_element_type=f32)
    mixed_low = pieces.reshape(tok_count, model_dim).astype(bf16)
    branch = jnp.dot(mixed_low, w_out[0], preferred_element_type=f32) + bias_all[2]
    first, first_norm, first_scale = norm_fwd(tokens_wide + branch, gain_all[0], shift_all[0])
    first_low = first.astype(bf16)
    cross_q = (
        (jnp.dot(first_low, w_in[3], preferred_element_type=f32) + bias_all[3])
        .astype(bf16)
        .reshape(tok_count, H, HD)
    )
    key_heads = w_in[4].reshape(model_dim, H, HD)
    val_heads = w_in[5].reshape(model_dim, H, HD)
    query_keys = jnp.einsum("the,dhe->thd", cross_q, key_heads, preferred_element_type=f32).astype(
        bf16
    )
    cross_s = jnp.einsum("thd,trd->thr", query_keys, fetched, preferred_element_type=f32) * 0.125
    cross_p = jax.nn.softmax(cross_s, axis=-1)
    cross_pl = cross_p.astype(bf16)
    state_mix = jnp.einsum("thr,trd->thd", cross_pl, fetched, preferred_element_type=f32).astype(
        bf16
    )
    cross_heads = jnp.einsum(
        "thd,dhe->the", state_mix, val_heads, preferred_element_type=f32
    ) + bias_all[4].reshape(H, HD)
    cross_low = cross_heads.reshape(tok_count, model_dim).astype(bf16)
    branch_two = jnp.dot(cross_low, w_out[1], preferred_element_type=f32) + bias_all[5]
    second, second_norm, second_scale = norm_fwd(first + branch_two, gain_all[1], shift_all[1])
    second_low = second.astype(bf16)
    hidden_pre = jnp.dot(second_low, w_ff1, preferred_element_type=f32) + bias_ff
    hidden_act, hidden_slope = gelu_parts(hidden_pre)
    hidden_low = hidden_act.astype(bf16)
    branch_ffn = jnp.dot(hidden_low, w_ff2, preferred_element_type=f32) + bias_all[6]
    final, final_norm, final_scale = norm_fwd(second + branch_ffn, gain_all[2], shift_all[2])
    output = final.astype(bf16)
    back_in, back_out, back_ff1, back_ff2 = (
        lax.all_gather(attn_in, "col", axis=2, tiled=True),
        lax.all_gather(attn_out, "col", axis=2, tiled=True),
        lax.all_gather(ff_in, "col", axis=1, tiled=True),
        lax.all_gather(ff_out, "col", axis=1, tiled=True),
    )
    back_in, back_out, back_ff1, back_ff2, back_gain = (
        lax.all_gather(back_in, "row", axis=1, tiled=True),
        lax.all_gather(back_out, "row", axis=1, tiled=True),
        lax.all_gather(back_ff1, "row", axis=0, tiled=True),
        lax.all_gather(back_ff2, "row", axis=0, tiled=True),
        lax.all_gather(ln_gain, "row", axis=1, tiled=True),
    )
    back_gain = back_gain.astype(f32)
    grad_three, grad_g3, grad_s3 = norm_back(
        cotangent.astype(f32), final_norm, final_scale, back_gain[2]
    )
    grad_y = grad_three.astype(bf16)
    grad_w_ff2 = jnp.einsum("tf,td->fd", hidden_low, grad_y, preferred_element_type=f32)
    grad_hidden = jnp.einsum("td,fd->tf", grad_y, back_ff2, preferred_element_type=f32)
    grad_pre = (grad_hidden * hidden_slope).astype(bf16)
    grad_w_ff1 = jnp.einsum("td,tf->df", second_low, grad_pre, preferred_element_type=f32)
    grad_second = grad_three + jnp.einsum(
        "tf,df->td", grad_pre, back_ff1, preferred_element_type=f32
    )
    grad_two, grad_g2, grad_s2 = norm_back(grad_second, second_norm, second_scale, back_gain[1])
    grad_o2 = grad_two.astype(bf16)
    grad_w_o2 = jnp.einsum("td,te->de", cross_low, grad_o2, preferred_element_type=f32)
    grad_cmix = (
        jnp.einsum("te,de->td", grad_o2, back_out[1], preferred_element_type=f32)
        .astype(bf16)
        .reshape(tok_count, H, HD)
    )
    grad_w_v2 = jnp.einsum(
        "thd,the->dhe", state_mix, grad_cmix, preferred_element_type=f32
    ).reshape(model_dim, model_dim)
    grad_smix = jnp.einsum(
        "the,dhe->thd", grad_cmix, back_in[5].reshape(model_dim, H, HD), preferred_element_type=f32
    ).astype(bf16)
    grad_cp = jnp.einsum("thd,trd->thr", grad_smix, fetched, preferred_element_type=f32)
    grad_cs = (cross_p * (grad_cp - jnp.sum(cross_p * grad_cp, axis=-1, keepdims=True))).astype(
        bf16
    )
    grad_qk = (
        jnp.einsum("thr,trd->thd", grad_cs, fetched, preferred_element_type=f32) * 0.125
    ).astype(bf16)
    grad_w_k2 = jnp.einsum("thd,the->dhe", grad_qk, cross_q, preferred_element_type=f32).reshape(
        model_dim, model_dim
    )
    grad_cq = (
        jnp.einsum(
            "thd,dhe->the",
            grad_qk,
            back_in[4].reshape(model_dim, H, HD),
            preferred_element_type=f32,
        )
        .astype(bf16)
        .reshape(tok_count, model_dim)
    )
    both_weights = jnp.concatenate([cross_pl, grad_cs * jnp.asarray(0.125, bf16)], axis=1)
    both_rows = jnp.concatenate([grad_smix, query_keys], axis=1)
    grad_fetched = jnp.einsum(
        "thr,thd->trd", both_weights, both_rows, preferred_element_type=f32
    ).reshape(-1, model_dim)
    send_back = jnp.zeros((peers * slots, model_dim), f32).at[place].set(grad_fetched)
    returned = lax.all_to_all(
        lax.all_to_all(
            send_back.reshape(n_rows, n_cols, slots, model_dim).astype(jnp.bfloat16),
            "row",
            split_axis=0,
            concat_axis=0,
            tiled=True,
        ),
        "col",
        split_axis=1,
        concat_axis=1,
        tiled=True,
    ).astype(jnp.float32)
    grad_store = (
        jnp.zeros((shard_rows, model_dim), f32)
        .at[asked.reshape(-1)]
        .add(returned.reshape(-1, model_dim))
    )
    grad_w_q2 = jnp.einsum("td,te->de", first_low, grad_cq, preferred_element_type=f32)
    grad_first = grad_two + jnp.einsum("te,de->td", grad_cq, back_in[3], preferred_element_type=f32)
    grad_one, grad_g1, grad_s1 = norm_back(grad_first, first_norm, first_scale, back_gain[0])
    grad_o = grad_one.astype(bf16)
    grad_w_o = jnp.einsum("td,te->de", mixed_low, grad_o, preferred_element_type=f32)
    grad_mix = (
        jnp.einsum("te,de->td", grad_o, back_out[0], preferred_element_type=f32)
        .astype(bf16)
        .reshape(tok_count, H, HD)
    )
    grad_queries = []
    grad_keys = jnp.zeros((tok_count, H, HD), f32)
    grad_values = jnp.zeros((tok_count, H, HD), f32)
    for block_id, row_start in enumerate(range(0, tok_count, block_rows)):
        visible = visible_mask(row_start, block_rows, seg_row, live_row)
        probs = jnp.exp(self_scores(queries, key_rows, visible) - log_norms[block_id])
        grad_probs = jnp.einsum("qhd,khd->hqk", grad_mix, values, preferred_element_type=f32)
        grad_values = jnp.einsum(
            "hqk,qhd->khd", probs.astype(bf16), grad_mix, preferred_element_type=f32
        )
        grad_scores = (
            probs * (grad_probs - jnp.sum(probs * grad_probs, axis=-1, keepdims=True))
        ).astype(bf16)
        grad_queries.append(
            jnp.einsum("hqk,khd->qhd", grad_scores, key_rows, preferred_element_type=f32) * 0.125
        )
        grad_keys = (
            jnp.einsum("hqk,qhd->khd", grad_scores, queries, preferred_element_type=f32) * 0.125
        )
    grad_qkv = (
        jnp.stack([grad_queries[0], grad_keys, grad_values])
        .reshape(3, tok_count, model_dim)
        .astype(bf16)
    )
    grad_w_qkv = jnp.einsum("td,kte->kde", tokens, grad_qkv, preferred_element_type=f32)
    grad_tokens = grad_one + jnp.einsum(
        "kte,kde->td", grad_qkv, back_in[:3], preferred_element_type=f32
    )
    grad_in = jnp.concatenate(
        [grad_w_qkv, grad_w_q2[None], grad_w_k2[None], grad_w_v2[None]], axis=0
    )
    grad_out = jnp.stack([grad_w_o, grad_w_o2])
    grad_bias = jnp.stack(
        [
            column_sum(grad_qkv[0]),
            column_sum(grad_qkv[2]),
            column_sum(grad_o),
            column_sum(grad_cq),
            column_sum(grad_cmix.reshape(tok_count, model_dim)),
            column_sum(grad_o2),
            column_sum(grad_y),
        ]
    )
    grad_gain = jnp.stack([grad_g1, grad_g2, grad_g3])
    grad_shift = jnp.stack([grad_s1, grad_s2, grad_s3])
    grad_ffb = column_sum(grad_pre)
    part_in, part_out, part_ff1, part_ff2, part_bias, part_gain, part_shift, part_ffb = (
        lax.psum_scatter(
            grad_in.astype(jnp.bfloat16), "row", scatter_dimension=1, tiled=True
        ).astype(jnp.float32),
        lax.psum_scatter(
            grad_out.astype(jnp.bfloat16), "row", scatter_dimension=1, tiled=True
        ).astype(jnp.float32),
        lax.psum_scatter(
            grad_w_ff1.astype(jnp.bfloat16), "row", scatter_dimension=0, tiled=True
        ).astype(jnp.float32),
        lax.psum_scatter(
            grad_w_ff2.astype(jnp.bfloat16), "row", scatter_dimension=0, tiled=True
        ).astype(jnp.float32),
        lax.psum_scatter(
            grad_bias.astype(jnp.bfloat16), "row", scatter_dimension=1, tiled=True
        ).astype(jnp.float32),
        lax.psum_scatter(
            grad_gain.astype(jnp.bfloat16), "row", scatter_dimension=1, tiled=True
        ).astype(jnp.float32),
        lax.psum_scatter(
            grad_shift.astype(jnp.bfloat16), "row", scatter_dimension=1, tiled=True
        ).astype(jnp.float32),
        lax.psum_scatter(
            grad_ffb.astype(jnp.bfloat16), "row", scatter_dimension=0, tiled=True
        ).astype(jnp.float32),
    )
    sum_in, sum_out, sum_ff1, sum_ff2 = (
        lax.psum_scatter(
            part_in.astype(jnp.bfloat16), "col", scatter_dimension=2, tiled=True
        ).astype(jnp.float32),
        lax.psum_scatter(
            part_out.astype(jnp.bfloat16), "col", scatter_dimension=2, tiled=True
        ).astype(jnp.float32),
        lax.psum_scatter(
            part_ff1.astype(jnp.bfloat16), "col", scatter_dimension=1, tiled=True
        ).astype(jnp.float32),
        lax.psum_scatter(
            part_ff2.astype(jnp.bfloat16), "col", scatter_dimension=1, tiled=True
        ).astype(jnp.float32),
    )
    sum_bias, sum_gain, sum_shift, sum_ffb = lax.psum(
        (part_bias, part_gain, part_shift, part_ffb), "col"
    )
    return (
        output,
        grad_tokens,
        grad_store,
        sum_in,
        sum_out,
        sum_ff1,
        sum_ff2,
        sum_bias,
        sum_gain,
        sum_shift,
        sum_ffb,
    )


def solution(mesh):
    return jax.shard_map(
        on_device,
        mesh=mesh,
        in_specs=(
            P(("row", "col"), None),
            P(("row", "col"), None),
            P(("row", "col"), None),
            P(("row", "col"), None),
            P(("row", "col"), None),
            P(None, "row", "col"),
            P(None, "row", "col"),
            P("row", "col"),
            P("row", "col"),
            P(None, "row"),
            P(None, "row"),
            P(None, "row"),
            P("row"),
            P(("row", "col"), None),
        ),
        out_specs=(
            P(("row", "col"), None),
            P(("row", "col"), None),
            P(("row", "col"), None),
            P(None, "row", "col"),
            P(None, "row", "col"),
            P("row", "col"),
            P("row", "col"),
            P(None, "row"),
            P(None, "row"),
            P(None, "row"),
            P("row"),
        ),
        check_vma=False,
    )
```

profile of v0, /device:TPU:0, one launch (start us, length us, event | category | flops | bytes accessed | tf_op | source)
XLA Modules:
  0.0 2270.1 jit_solution(10387861676982001819)
XLA Ops:
  22.0 23.0 %gather_fusion.1 = s32[4096]{0:T(1024)S(1)} fusion(s32[4096]{0:T(1024)S(1)} %get-tuple-element.228, s32[4096]{0:T(1024)S(1)} %get-tuple-element.229), kind=kCustom, calls=%fused_computation.1 | custom fusion | bytes 49152 | tf_op jit(solution)/shard_map/gather | solution.py:59
  45.1 300.6 %while.25 = (s32[]{:T(128)}, u32[4096]{0:T(1024)S(1)}, u32[4096]{0:T(1024)S(1)}, s32[4096]{0:T(1024)S(1)}, s32[]{:T(128)}, /*index=5*/s32[]{:T(128)}, s32[]{}) while((s32[]{:T(128)}, u32[4096]{0:T(1024)S(1)}, u32[4096]{0:T(1024)S(1)}, s32[4096]{0:T(1024)S(1)}, s32[]{:T(128)}, /*index=5*/s32[]{:T(128)}, s32[]{}) %tuple.95), condition=%wide.region_6.7_spmd.clone, body=%wide.region_5.6_spmd.clone.sunk | while | flops 77828 | bytes 270437 | solution.py:60
  45.1 23.0 %gather_fusion = s32[4096]{0:T(1024)S(1)} fusion(s32[4096]{0:T(1024)S(1)} %get-tuple-element.310, u32[4096]{0:T(1024)S(1)} %broadcast_clamp_fusion.5), kind=kCustom, calls=%fused_computation.clone.clone.1 | custom fusion | bytes 49152 | tf_op jit(solution)/shard_map/jit(searchsorted)/jit(_searchsorted_scan_impl)/vmap(jit(_searchsorted_scan_impl))/while/body/eval_jaxpr/gather | solution.py:60
  68.2 23.0 %gather_fusion = s32[4096]{0:T(1024)S(1)} fusion(s32[4096]{0:T(1024)S(1)} %get-tuple-element.310, u32[4096]{0:T(1024)S(1)} %broadcast_clamp_fusion.5), kind=kCustom, calls=%fused_computation.clone.clone.1 | custom fusion | bytes 49152 | tf_op jit(solution)/shard_map/jit(searchsorted)/jit(_searchsorted_scan_impl)/vmap(jit(_searchsorted_scan_impl))/while/body/eval_jaxpr/gather | solution.py:60
  91.4 23.0 %gather_fusion = s32[4096]{0:T(1024)S(1)} fusion(s32[4096]{0:T(1024)S(1)} %get-tuple-element.310, u32[4096]{0:T(1024)S(1)} %broadcast_clamp_fusion.5), kind=kCustom, calls=%fused_computation.clone.clone.1 | custom fusion | bytes 49152 | tf_op jit(solution)/shard_map/jit(searchsorted)/jit(_searchsorted_scan_impl)/vmap(jit(_searchsorted_scan_impl))/while/body/eval_jaxpr/gather | solution.py:60
  114.5 23.0 %gather_fusion = s32[4096]{0:T(1024)S(1)} fusion(s32[4096]{0:T(1024)S(1)} %get-tuple-element.310, u32[4096]{0:T(1024)S(1)} %broadcast_clamp_fusion.5), kind=kCustom, calls=%fused_computation.clone.clone.1 | custom fusion | bytes 49152 | tf_op jit(solution)/shard_map/jit(searchsorted)/jit(_searchsorted_scan_impl)/vmap(jit(_searchsorted_scan_impl))/while/body/eval_jaxpr/gather | solution.py:60
  137.6 23.0 %gather_fusion = s32[4096]{0:T(1024)S(1)} fusion(s32[4096]{0:T(1024)S(1)} %get-tuple-element.310, u32[4096]{0:T(1024)S(1)} %broadcast_clamp_fusion.5), kind=kCustom, calls=%fused_computation.clone.clone.1 | custom fusion | bytes 49152 | tf_op jit(solution)/shard_map/jit(searchsorted)/jit(_searchsorted_scan_impl)/vmap(jit(_searchsorted_scan_impl))/while/body/eval_jaxpr/gather | solution.py:60
  160.7 23.0 %gather_fusion = s32[4096]{0:T(1024)S(1)} fusion(s32[4096]{0:T(1024)S(1)} %get-tuple-element.310, u32[4096]{0:T(1024)S(1)} %broadcast_clamp_fusion.5), kind=kCustom, calls=%fused_computation.clone.clone.1 | custom fusion | bytes 49152 | tf_op jit(solution)/shard_map/jit(searchsorted)/jit(_searchsorted_scan_impl)/vmap(jit(_searchsorted_scan_impl))/while/body/eval_jaxpr/gather | solution.py:60
  183.9 23.0 %gather_fusion = s32[4096]{0:T(1024)S(1)} fusion(s32[4096]{0:T(1024)S(1)} %get-tuple-element.310, u32[4096]{0:T(1024)S(1)} %broadcast_clamp_fusion.5), kind=kCustom, calls=%fused_computation.clone.clone.1 | custom fusion | bytes 49152 | tf_op jit(solution)/shard_map/jit(searchsorted)/jit(_searchsorted_scan_impl)/vmap(jit(_searchsorted_scan_impl))/while/body/eval_jaxpr/gather | solution.py:60
  207.0 23.0 %gather_fusion = s32[4096]{0:T(1024)S(1)} fusion(s32[4096]{0:T(1024)S(1)} %get-tuple-element.310, u32[4096]{0:T(1024)S(1)} %broadcast_clamp_fusion.5), kind=kCustom, calls=%fused_computation.clone.clone.1 | custom fusion | bytes 49152 | tf_op jit(solution)/shard_map/jit(searchsorted)/jit(_searchsorted_scan_impl)/vmap(jit(_searchsorted_scan_impl))/while/body/eval_jaxpr/gather | solution.py:60
  230.1 23.0 %gather_fusion = s32[4096]{0:T(1024)S(1)} fusion(s32[4096]{0:T(1024)S(1)} %get-tuple-element.310, u32[4096]{0:T(1024)S(1)} %broadcast_clamp_fusion.5), kind=kCustom, calls=%fused_computation.clone.clone.1 | custom fusion | bytes 49152 | tf_op jit(solution)/shard_map/jit(searchsorted)/jit(_searchsorted_scan_impl)/vmap(jit(_searchsorted_scan_impl))/while/body/eval_jaxpr/gather | solution.py:60
  253.2 23.0 %gather_fusion = s32[4096]{0:T(1024)S(1)} fusion(s32[4096]{0:T(1024)S(1)} %get-tuple-element.310, u32[4096]{0:T(1024)S(1)} %broadcast_clamp_fusion.5), kind=kCustom, calls=%fused_computation.clone.clone.1 | custom fusion | bytes 49152 | tf_op jit(solution)/shard_map/jit(searchsorted)/jit(_searchsorted_scan_impl)/vmap(jit(_searchsorted_scan_impl))/while/body/eval_jaxpr/gather | solution.py:60
  276.4 23.0 %gather_fusion = s32[4096]{0:T(1024)S(1)} fusion(s32[4096]{0:T(1024)S(1)} %get-tuple-element.310, u32[4096]{0:T(1024)S(1)} %broadcast_clamp_fusion.5), kind=kCustom, calls=%fused_computation.clone.clone.1 | custom fusion | bytes 49152 | tf_op jit(solution)/shard_map/jit(searchsorted)/jit(_searchsorted_scan_impl)/vmap(jit(_searchsorted_scan_impl))/while/body/eval_jaxpr/gather | solution.py:60
  299.5 23.0 %gather_fusion = s32[4096]{0:T(1024)S(1)} fusion(s32[4096]{0:T(1024)S(1)} %get-tuple-element.310, u32[4096]{0:T(1024)S(1)} %broadcast_clamp_fusion.5), kind=kCustom, calls=%fused_computation.clone.clone.1 | custom fusion | bytes 49152 | tf_op jit(solution)/shard_map/jit(searchsorted)/jit(_searchsorted_scan_impl)/vmap(jit(_searchsorted_scan_impl))/while/body/eval_jaxpr/gather | solution.py:60
  322.6 23.0 %gather_fusion = s32[4096]{0:T(1024)S(1)} fusion(s32[4096]{0:T(1024)S(1)} %get-tuple-element.310, u32[4096]{0:T(1024)S(1)} %broadcast_clamp_fusion.5), kind=kCustom, calls=%fused_computation.clone.clone.1 | custom fusion | bytes 49152 | tf_op jit(solution)/shard_map/jit(searchsorted)/jit(_searchsorted_scan_impl)/vmap(jit(_searchsorted_scan_impl))/while/body/eval_jaxpr/gather | solution.py:60
  398.1 26.1 %gather_fusion.2 = bf16[6144,768]{1,0:T(8,128)(2,1)} fusion(bf16[2048,768]{1,0:T(8,128)(2,1)S(1)} %copy-done, s32[6144]{0:T(1024)S(1)} %broadcast_clamp_fusion.1), kind=kCustom, calls=%fused_computation.2 | custom fusion | bytes 18898944 | tf_op jit(solution)/shard_map/gather | solution.py:126
  435.3 212.1 %all-reduce = bf16[3072]{0:T(1024)(128)(2,1)S(1)} all-reduce(bf16[3072]{0:T(1024)(128)(2,1)S(1)} %dynamic-update-slice), channel_id=1, replica_groups=mesh['row'=16,'col'=2] {'row'}, use_global_device_ids=true, to_apply=%add | all-reduce | flops 3072 | bytes 12288
  648.0 96.4 %all-gather.1 = bf16[16,48,3]{1,2,0:T(4,128)(2,1)S(1)} all-gather(bf16[1,48,3]{1,2,0:T(4,128)(2,1)S(1)} %bitcast.214), channel_id=1, replica_groups=mesh['row'=16,'col'=2] {'row'}, dimensions={0}, use_global_device_ids=true | all-gather | bytes 4896 | tf_op jit(solution)/shard_map/all_gather | solution.py:108
  744.5 35.5 %all-gather.2 = bf16[16,48,3]{1,2,0:T(4,128)(2,1)S(1)} all-gather(bf16[1,48,3]{1,2,0:T(4,128)(2,1)S(1)} %bitcast.215), channel_id=1, replica_groups=mesh['row'=16,'col'=2] {'row'}, dimensions={0}, use_global_device_ids=true | all-gather | bytes 4896 | tf_op jit(solution)/shard_map/all_gather | solution.py:109
  780.1 38.0 %all-gather = bf16[16,48,7]{1,2,0:T(8,128)(2,1)S(1)} all-gather(bf16[1,48,7]{1,2,0:T(8,128)(2,1)S(1)} %bitcast.213), channel_id=1, replica_groups=mesh['row'=16,'col'=2] {'row'}, dimensions={0}, use_global_device_ids=true | all-gather | bytes 11424 | tf_op jit(solution)/shard_map/all_gather | solution.py:107
  857.9 20.7 all_to_all.32
  886.9 24.9 %gather_fusion.3 = bf16[4096,768]{1,0:T(8,128)(2,1)} fusion(bf16[6144,768]{1,0:T(8,128)(2,1)} %bitcast.158, s32[4096]{0:T(1024)} %get-tuple-element.225), kind=kCustom, calls=%fused_computation.3 | custom fusion | bytes 12599296 | tf_op jit(solution)/shard_map/gather | solution.py:134
  1085.9 26.2 %scatter_custom_fusion.2 = f32[6144,768]{1,0:T(8,128)} fusion(s32[4096]{0:T(1024)} %copy-done.67, f32[4096,768]{1,0:T(8,128)} %bitcast.170, f32[]{:T(128)} %constant.87.clone.1), kind=kCustom, calls=%fused_computation.21 | custom fusion | bytes 18874880 | tf_op jit(solution)/shard_map/scatter | solution.py:251
  1133.9 295.4 %reduce-scatter.32.cloned.1.call-done = bf16[192,768]{1,0:T(8,128)(2,1)} async-done(((bf16[3072,768]{1,0:T(8,128)(2,1)}), bf16[192,768]{1,0:T(8,128)(2,1)}) %reduce-scatter.32.cloned.1.call-update) | async-done | bytes 294928 | tf_op jit(solution)/shard_map/reduce_scatter | solution.py:336
  1431.3 140.0 %reduce-scatter.28.cloned.1.call-done = bf16[48,3072]{1,0:T(8,128)(2,1)} async-done(((bf16[768,3072]{1,0:T(8,128)(2,1)}), bf16[48,3072]{1,0:T(8,128)(2,1)}) %reduce-scatter.28.cloned.1.call-update) | async-done | bytes 294928 | tf_op jit(solution)/shard_map/reduce_scatter | solution.py:333
  1572.1 176.2 %reduce-scatter.24.cloned.1.call-done = bf16[6,48,768]{2,0,1:T(8,128)(2,1)} async-done(((bf16[6,768,768]{2,0,1:T(8,128)(2,1)}), bf16[6,48,768]{2,0,1:T(8,128)(2,1)}) %reduce-scatter.24.cloned.1.call-update) | async-done | bytes 442384 | tf_op jit(solution)/shard_map/reduce_scatter | solution.py:327
  1770.7 40.3 %all-reduce.1 = bf16[3072]{0:T(1024)(128)(2,1)S(1)} all-reduce(bf16[3072]{0:T(1024)(128)(2,1)S(1)} %copy-done.79), channel_id=13, replica_groups=mesh['row'=16,'col'=2] {'row'}, use_global_device_ids=true, to_apply=%region_53.54.clone | all-reduce | flops 3072 | bytes 12288
  1815.2 58.1 %reduce-scatter.44.cloned.1.call-done = bf16[48,3]{1,0:T(8,128)(2,1)} async-done(((bf16[768,3]{1,0:T(8,128)(2,1)}), bf16[48,3]{1,0:T(8,128)(2,1)}) %reduce-scatter.44.cloned.1.call-update) | async-done | bytes 304
  1874.0 124.1 %reduce-scatter.42.cloned.1.call-done = bf16[48,3]{1,0:T(8,128)(2,1)} async-done(((bf16[768,3]{1,0:T(8,128)(2,1)}), bf16[48,3]{1,0:T(8,128)(2,1)}) %reduce-scatter.42.cloned.1.call-update) | async-done | bytes 304
  1998.9 125.1 %reduce-scatter.40.cloned.1.call-done = bf16[48,7]{1,0:T(8,128)(2,1)} async-done(((bf16[768,7]{1,0:T(8,128)(2,1)}), bf16[48,7]{1,0:T(8,128)(2,1)}) %reduce-scatter.40.cloned.1.call-update) | async-done | bytes 688
  2190.0 20.3 all_to_all.33
  2218.6 44.8 %scatter_custom_fusion.3 = f32[2048,768]{1,0:T(8,128)} fusion(s32[6144]{0:T(1024)S(1)} %bitcast.208, bf16[6144,768]{1,0:T(8,128)(2,1)} %bitcast.165, f32[]{:T(128)} %constant.87.clone.1), kind=kCustom, calls=%fused_computation.13 | custom fusion | flops 9437184 | bytes 15728644 | tf_op jit(solution)/shard_map/scatter-add | solution.py:268
  (463 shorter events, 425.8 us)
Async XLA Ops:
  7.2 390.9 %copy-start = (bf16[2048,768]{1,0:T(8,128)(2,1)S(1)}, bf16[2048,768]{1,0:T(8,128)(2,1)}, u32[]{:S(2)}) copy-start(bf16[2048,768]{1,0:T(8,128)(2,1)} %param.20) | copy-start | bytes 9437188
  7.2 814.4 %all-gather.8.cloned.1.call-start = ((), (), s32[]{:S(2)}) async-start(), calls=%async_computation.17 | async-start | bytes 7520256 | tf_op jit(solution)/shard_map/all_gather | solution.py:103
  11.6 826.5 %all-gather.10.cloned.1.call-start = ((), (), s32[]{:S(2)}) async-start(), calls=%async_computation.18 | async-start | bytes 2506752 | tf_op jit(solution)/shard_map/all_gather | solution.py:104
  424.2 223.8 %copy-start.91 = (bf16[3,48]{1,0:T(4,128)(2,1)S(1)}, bf16[3,48]{1,0:T(4,128)(2,1)}, u32[]{:S(2)}) copy-start(bf16[3,48]{1,0:T(4,128)(2,1)} %param.26) | copy-start | bytes 868
  424.2 320.2 %copy-start.92 = (bf16[3,48]{1,0:T(4,128)(2,1)S(1)}, bf16[3,48]{1,0:T(4,128)(2,1)}, u32[]{:S(2)}) copy-start(bf16[3,48]{1,0:T(4,128)(2,1)} %param.27) | copy-start | bytes 868
  424.2 355.8 %copy-start.84 = (bf16[7,48]{1,0:T(8,128)(2,1)S(1)}, bf16[7,48]{1,0:T(8,128)(2,1)}, u32[]{:S(2)}) copy-start(bf16[7,48]{1,0:T(8,128)(2,1)} %param.25) | copy-start | bytes 2020
  424.2 395.9 %copy-start.93 = (s32[1,256]{1,0:T(1,128)S(1)}, s32[1,256]{1,0:T(1,128)}, u32[]{:S(2)}) copy-start(s32[1,256]{1,0:T(1,128)} %param.18) | copy-start | bytes 3076
  424.3 396.6 %copy-start.83 = (s32[1,256]{1,0:T(1,128)S(1)}, s32[1,256]{1,0:T(1,128)}, u32[]{:S(2)}) copy-start(s32[1,256]{1,0:T(1,128)} %param.17) | copy-start | bytes 3076
  424.3 397.3 %copy-start.37 = (bf16[256,768]{1,0:T(8,128)(2,1)S(1)}, bf16[256,768]{1,0:T(8,128)(2,1)}, u32[]{:S(2)}) copy-start(bf16[256,768]{1,0:T(8,128)(2,1)} %param.16) | copy-start | bytes 1179652
  424.3 425.3 %all-to-all-start.2 = ((bf16[16,2,192,768]{3,2,1,0:T(8,128)(2,1)}), bf16[16,2,192,768]{3,2,1,0:T(8,128)(2,1)}, u32[]{:S(2)}, u32[]{:S(2)}) async-start(bf16[16,2,192,768]{3,2,1,0:T(8,128)(2,1)} %bitcast.163), calls=%async_computation.2 | async-start | bytes 18874368 | tf_op jit(solution)/shard_map/all_to_all | solution.py:128
  429.2 506.2 %all-gather.12.cloned.1.call-start = ((), (), s32[]{:S(2)}) async-start(), calls=%async_computation.19 | async-start | bytes 5013504 | tf_op jit(solution)/shard_map/all_gather | solution.py:105
  431.4 510.5 %all-gather.14.cloned.1.call-start = ((), (), s32[]{:S(2)}) async-start(), calls=%async_computation.20 | async-start | bytes 5013504 | tf_op jit(solution)/shard_map/all_gather | solution.py:106
  433.7 698.0 %reduce-scatter.26.cloned.1.call-start = ((), (), s32[]{:S(2)}) async-start(), calls=%async_computation.22 | async-start | bytes 2506752 | tf_op jit(solution)/shard_map/reduce_scatter | solution.py:330
  818.8 14.2 copy-start.51
  840.1 91.9 %copy-start.59 = (f32[256]{0:T(256)}, f32[256]{0:T(256)S(1)}, u32[]{:S(2)}) copy-start(f32[256]{0:T(256)S(1)} %broadcast_multiply_fusion.9) | copy-start | bytes 3076
  997.5 431.8 %reduce-scatter.32.cloned.1.call-start = ((), (), s32[]{:S(2)}) async-start(), calls=%async_computation.25 | async-start | bytes 5013504 | tf_op jit(solution)/shard_map/reduce_scatter | solution.py:336
  1002.8 568.5 %reduce-scatter.28.cloned.1.call-start = ((), (), s32[]{:S(2)}) async-start(), calls=%async_computation.23 | async-start | bytes 5013504 | tf_op jit(solution)/shard_map/reduce_scatter | solution.py:333
  1008.9 739.5 %reduce-scatter.24.cloned.1.call-start = ((), (), s32[]{:S(2)}) async-start(), calls=%async_computation.21 | async-start | bytes 10027008 | tf_op jit(solution)/shard_map/reduce_scatter | solution.py:327
  1123.4 1058.2 %all-to-all-start.4 = ((bf16[16,2,192,768]{3,2,1,0:T(8,128)(2,1)}), bf16[16,2,192,768]{3,2,1,0:T(8,128)(2,1)}, u32[]{:S(2)}, u32[]{:S(2)}) async-start(bf16[16,2,192,768]{3,2,1,0:T(8,128)(2,1)} %bitcast.164), calls=%async_computation.4 | async-start | bytes 18874368 | tf_op jit(solution)/shard_map/all_to_all | solution.py:253
  1128.2 443.7 %copy-start.47 = (s32[16,2,192]{2,0,1:T(8,128)S(1)}, s32[16,2,192]{2,0,1:T(8,128)}, u32[]{:S(2)}) copy-start(s32[16,2,192]{2,0,1:T(8,128)} %copy-done.46) | copy-start | bytes 73732
  1128.3 745.0 %reduce-scatter.44.cloned.1.call-start = ((), (), s32[]{:S(2)}) async-start(), calls=%async_computation.31 | async-start | bytes 208896
  1129.3 868.8 %reduce-scatter.42.cloned.1.call-start = ((), (), s32[]{:S(2)}) async-start(), calls=%async_computation.30 | async-start | bytes 208896
  1130.3 993.7 %reduce-scatter.40.cloned.1.call-start = ((), (), s32[]{:S(2)}) async-start(), calls=%async_computation.29 | async-start | bytes 208896
  1131.6 1001.8 %reduce-scatter.36.cloned.1.call-start = ((), (), s32[]{:S(2)}) async-start(), calls=%async_computation.27 | async-start | bytes 294912
  1133.8 1010.8 %reduce-scatter.38.cloned.1.call-start = ((), (), s32[]{:S(2)}) async-start(), calls=%async_computation.28 | async-start | bytes 589824
  1431.2 724.5 %reduce-scatter.30.cloned.1.call-start = ((), (), s32[]{:S(2)}) async-start(), calls=%async_computation.24 | async-start | bytes 442368 | tf_op jit(solution)/shard_map/reduce_scatter | solution.py:359
  1571.3 596.4 %reduce-scatter.34.cloned.1.call-start = ((), (), s32[]{:S(2)}) async-start(), calls=%async_computation.26 | async-start | bytes 884736
  1759.3 51.8 %copy-start.13 = (f32[256,768]{1,0:T(8,128)S(1)}, f32[256,768]{1,0:T(8,128)}, u32[]{:S(2)}) copy-start(f32[256,768]{1,0:T(8,128)} %copy-done.12) | copy-start | bytes 2359300
  1759.3 51.8 %copy-start.43 = (bf16[1,256,768]{2,1,0:T(8,128)(2,1)S(1)}, bf16[1,256,768]{2,1,0:T(8,128)(2,1)}, u32[]{:S(2)}) copy-start(bf16[1,256,768]{2,1,0:T(8,128)(2,1)} %copy.254) | copy-start | bytes 1179652
  1759.3 51.8 %copy-start.44 = (bf16[1,256,768]{2,1,0:T(8,128)(2,1)S(1)}, bf16[1,256,768]{2,1,0:T(8,128)(2,1)}, u32[]{:S(2)}) copy-start(bf16[1,256,768]{2,1,0:T(8,128)(2,1)} %copy.252) | copy-start | bytes 1179652
  1759.3 51.8 %copy-start.45 = (bf16[1,256,768]{2,1,0:T(8,128)(2,1)S(1)}, bf16[1,256,768]{2,1,0:T(8,128)(2,1)}, u32[]{:S(2)}) copy-start(bf16[1,256,768]{2,1,0:T(8,128)(2,1)} %copy.253) | copy-start | bytes 1179652
  2218.6 44.8 %copy-start.1 = (bf16[2048,768]{1,0:T(8,128)(2,1)S(1)}, bf16[2048,768]{1,0:T(8,128)(2,1)}, u32[]{:S(2)}) copy-start(bf16[2048,768]{1,0:T(8,128)(2,1)} %param.20) | copy-start | bytes 9437188
  (87 other events, 363.2 us)
Sparse Core Ops, SparseCore 0:
  11.7 103.8 all-gather.7
  118.3 60.4 all-gather.9
  432.8 231.4 all-gather.11
  667.0 86.9 all-gather.13
  997.7 124.3 reduce-scatter.25
  1127.9 301.3 reduce-scatter.31
  1435.0 136.1 reduce-scatter.27
  1577.9 170.4 reduce-scatter.23
  1753.0 120.2 reduce-scatter.43
  1877.7 120.3 reduce-scatter.41
  2003.4 120.5 reduce-scatter.39
  2126.7 6.6 reduce-scatter.35
  2135.7 8.9 reduce-scatter.37
  2146.8 8.8 reduce-scatter.29
  2158.5 9.1 reduce-scatter.33
where the time goes:
time: 2280 us; the launch traced here: 2270 us
  waiting for transfers between devices  954 us (42%)
  local copies, waits for them, and re-layouts  558 us (24%)
  blocking collectives  498 us (22%)
  matrix products  140 us (6%)
  other arithmetic  93.1 us (4%)
    unnamed x21, waiting for transfers between devices  333 us
    gather x13, local copies, waits for them, and re-layouts, plan_requests(): first_pos = jnp.searchsorted(sorted_owner, sorted_owner, side='left')  299 us
    reduce_scatter x1, waiting for transfers between devices, on_device(): lax.psum_scatter(grad_w_ff2.astype(jnp.bfloat16), 'row', scatter_dimensio...  295 us
    unnamed x2, blocking collectives  252 us
    reduce_scatter x1, waiting for transfers between devices, on_device(): lax.psum_scatter(grad_in.astype(jnp.bfloat16), 'row', scatter_dimension=1...  176 us
    reduce_scatter x1, waiting for transfers between devices, on_device(): lax.psum_scatter(grad_w_ff1.astype(jnp.bfloat16), 'row', scatter_dimensio...  140 us
    all_gather x1, blocking collectives, on_device(): lax.all_gather(ln_gain, 'row', axis=1, tiled=True)  96.4 us
    unnamed x225, local copies, waits for them, and re-layouts  60.3 us
  transfers between devices with their start and end apart: 17, of which 10 were waited for; matrix products, arithmetic and copies ran while one was open for 29% of the time, Pallas kernels for 0%

commit v1 on v0

v1 whole, which is shorter than its diff:
```python
import functools

import jax
import jax.numpy as jnp
import numpy as np
from jax import lax
from jax.experimental import pallas as pl
from jax.experimental.pallas import tpu as pltpu
from jax.sharding import PartitionSpec as P

H = 12
HD = 64
RANKS = ("row", "col")
BF = jnp.bfloat16
F32 = jnp.float32
VMEM_LIMIT = 60 * 1024 * 1024


def mm(a, b):
    return jnp.dot(a, b, preferred_element_type=F32)


def mm_nt(a, b):
    return lax.dot_general(a, b, (((1,), (1,)), ((), ())), preferred_element_type=F32)


def mm_tn(a, b):
    return lax.dot_general(a, b, (((0,), (0,)), ((), ())), preferred_element_type=F32)


def norm_fwd(resid, gain, shift):
    row_mean = jnp.mean(resid, axis=-1, keepdims=True)
    centered = resid - row_mean
    inv_std = lax.rsqrt(jnp.mean(centered * centered, axis=-1, keepdims=True) + 1e-05)
    normed = centered * inv_std
    return (normed * gain + shift, normed, inv_std)


def norm_back(grad_in, normed, inv_std, gain):
    scaled = grad_in * gain
    return inv_std * (
        scaled
        - jnp.mean(scaled, axis=-1, keepdims=True)
        - normed * jnp.mean(scaled * normed, axis=-1, keepdims=True)
    )


def gelu_parts(pre_act):
    cdf_part = 0.5 * (1.0 + lax.erf(pre_act * 0.7071067811865476))
    density = jnp.exp(-0.5 * pre_act * pre_act) * 0.3989422804014327
    return (pre_act * cdf_part, cdf_part + pre_act * density)


def visible_mask(seg_row, live_row):
    pos = jnp.arange(seg_row.shape[0], dtype=jnp.int32)
    return (
        (pos[None, :] <= pos[:, None])
        & (seg_row[:, None] == seg_row[None, :])
        & ((live_row[None, :] == 1) | (pos[None, :] == pos[:, None]))
    )


def column_sum(array):
    return jnp.sum(array.astype(F32), axis=0)


def bit_orders(n_rows, n_cols):
    row_bits = [("row", 1 << b) for b in reversed(range(n_rows.bit_length() - 1))]
    col_bits = [("col", 1 << b) for b in reversed(range(n_cols.bit_length() - 1))]
    swapped = row_bits[:-2] + row_bits[-1:] + row_bits[-2:-1]
    return row_bits + col_bits, swapped + col_bits


def swap_bit(array, axis, bit):
    pairs = [(i, i ^ bit) for i in range(lax.axis_size(axis))]
    return lax.ppermute(array, axis, pairs)


def gather_bits(blocks, order):
    for axis, bit in order:
        blocks = jnp.concatenate([blocks, swap_bit(blocks, axis, bit)], axis=0)
    return blocks


def scatter_bits(blocks, order):
    for axis, bit in order:
        half = blocks.shape[0] // 2
        blocks = blocks[:half] + swap_bit(blocks[half:], axis, bit)
    return blocks[0]


def offsets(order, first_is_low):
    count = len(order)
    rows = np.zeros(1 << count, np.int32)
    cols = np.zeros(1 << count, np.int32)
    for k, (axis, bit) in enumerate(order):
        place = k if first_is_low else count - 1 - k
        has = (np.arange(1 << count) >> place) & 1
        (rows if axis == "row" else cols)[has == 1] ^= bit
    return rows, cols


def block_of_device(order, n_rows, n_cols):
    rows, cols = offsets(order, True)
    table = np.zeros((n_rows, n_cols), np.int32)
    table[rows, cols] = np.arange(n_rows * n_cols)
    at_row = lax.axis_index("row") ^ jnp.arange(n_rows, dtype=jnp.int32)
    at_col = lax.axis_index("col") ^ jnp.arange(n_cols, dtype=jnp.int32)
    return jnp.asarray(table)[at_row[:, None], at_col[None, :]].reshape(-1)


def device_of_block(order, n_cols):
    rows, cols = offsets(order, False)
    to_row = lax.axis_index("row") ^ jnp.asarray(rows)
    to_col = lax.axis_index("col") ^ jnp.asarray(cols)
    return to_row * n_cols + to_col


def flip_by_position(blocks, stages):
    for k, (axis, bit) in enumerate(stages):
        here = (lax.axis_index(axis) & bit) != 0
        blocks = jnp.where(here, jnp.flip(blocks, axis=k), blocks)
    return blocks


def by_device(blocks, order):
    stages = order[::-1]
    shape = blocks.shape[1:]
    blocks = flip_by_position(blocks.reshape((2,) * len(stages) + shape), stages)
    rank = sorted(range(len(stages)), key=lambda k: (stages[k][0] == "col", -stages[k][1]))
    rest = list(range(len(stages), blocks.ndim))
    return blocks.transpose(rank + rest).reshape((-1,) + shape)


def by_stage(blocks, stages):
    shape = blocks.shape[1:]
    rank = sorted(range(len(stages)), key=lambda k: (stages[k][0] == "col", -stages[k][1]))
    rest = list(range(len(stages), len(stages) + len(shape)))
    back = [rank.index(k) for k in range(len(stages))]
    blocks = blocks.reshape((2,) * len(stages) + shape).transpose(back + rest)
    return flip_by_position(blocks, stages).reshape((-1,) + shape)


def split_cols(array, pieces):
    width = array.shape[1] // pieces
    return jnp.concatenate([array[:, i * width : (i + 1) * width] for i in range(pieces)], axis=0)


def unpack_attn_kernel(perm, blk, w_in, w_out, small, *, rb):
    for k in range(6):
        w_in[k] = blk[0, k * rb : (k + 1) * rb]
    for k in range(2):
        w_out[k] = blk[0, (6 + k) * rb : (7 + k) * rb]
    small[0] = blk[0, 8 * rb :]


def unpack_ff_kernel(perm, blk, ff_in, ff_out, *, rb, cb):
    for k in range(4):
        ff_in[:, k * cb : (k + 1) * cb] = blk[0, k * rb : (k + 1) * rb]
    ff_out[...] = blk[0, 4 * rb :]


def pack_attn_kernel(dest, *refs, rb):
    parts, small, blk = refs[:8], refs[8], refs[9]
    for k in range(8):
        blk[0, k * rb : (k + 1) * rb] = parts[k][...]
    blk[0, 8 * rb :] = small[0]


def pack_ff_kernel(dest, ff_in, ff_out, blk, *, rb, cb):
    for k in range(4):
        blk[0, k * rb : (k + 1) * rb] = ff_in[:, k * cb : (k + 1) * cb]
    blk[0, 4 * rb :] = ff_out[...]


def unpack(attn_blocks, ff_blocks, order_a, order_b, n_rows, n_cols, rb, cb):
    dim, wide = rb * n_rows, 4 * rb * n_rows
    extra = attn_blocks.shape[1] - 8 * rb
    shapes_a = (
        jax.ShapeDtypeStruct((6, dim, dim), BF),
        jax.ShapeDtypeStruct((2, dim, dim), BF),
        jax.ShapeDtypeStruct((n_rows * n_cols, extra, cb), BF),
    )
    shapes_b = (jax.ShapeDtypeStruct((dim, wide), BF), jax.ShapeDtypeStruct((wide, dim), BF))
    if rb % 16 or cb % 128:
        got = by_device(attn_blocks, order_a).reshape(n_rows, n_cols, -1, cb)
        mats = got[:, :, : 8 * rb].reshape(n_rows, n_cols, 8, rb, cb)
        mats = mats.transpose(2, 0, 3, 1, 4).reshape(8, dim, dim)
        small = got[:, :, 8 * rb :].reshape(n_rows * n_cols, extra, cb)
        got = by_device(ff_blocks, order_b).reshape(n_rows, n_cols, 8, rb, cb)
        ff_in = got[:, :, :4].transpose(0, 3, 1, 2, 4).reshape(dim, wide)
        ff_out = got[:, :, 4:].transpose(0, 2, 3, 1, 4).reshape(wide, dim)
        return mats[:6], mats[6:], small, ff_in, ff_out
    at = lambda g, perm: (0, g // n_cols, g % n_cols)
    w_in, w_out, small = pl.pallas_call(
        functools.partial(unpack_attn_kernel, rb=rb),
        grid_spec=pltpu.PrefetchScalarGridSpec(
            num_scalar_prefetch=1,
            grid=(n_rows * n_cols,),
            in_specs=[pl.BlockSpec((1, 8 * rb + extra, cb), lambda g, perm: (perm[g], 0, 0))],
            out_specs=[
                pl.BlockSpec((6, rb, cb), at),
                pl.BlockSpec((2, rb, cb), at),
                pl.BlockSpec((1, extra, cb), lambda g, perm: (g, 0, 0)),
            ],
        ),
        out_shape=shapes_a,
        name="unpack_attn",
    )(block_of_device(order_a, n_rows, n_cols), attn_blocks)
    at = lambda g, perm: (g // n_cols, g % n_cols)
    ff_in, ff_out = pl.pallas_call(
        functools.partial(unpack_ff_kernel, rb=rb, cb=cb),
        grid_spec=pltpu.PrefetchScalarGridSpec(
            num_scalar_prefetch=1,
            grid=(n_rows * n_cols,),
            in_specs=[pl.BlockSpec((1, 8 * rb, cb), lambda g, perm: (perm[g], 0, 0))],
            out_specs=[pl.BlockSpec((rb, 4 * cb), at), pl.BlockSpec((4 * rb, cb), at)],
        ),
        out_shape=shapes_b,
        name="unpack_ff",
    )(block_of_device(order_b, n_rows, n_cols), ff_blocks)
    return w_in, w_out, small, ff_in, ff_out


def pack_attn(mats, small, order, n_rows, n_cols, rb, cb):
    peers, extra = n_rows * n_cols, small.shape[1]
    if rb % 16 or cb % 128:
        got = jnp.stack(mats).reshape(8, n_rows, rb, n_cols, cb).transpose(1, 3, 0, 2, 4)
        got = got.reshape(n_rows, n_cols, 8 * rb, cb)
        low = jnp.broadcast_to(small[:, None], (n_rows, n_cols, extra, cb))
        got = jnp.concatenate([got, low], axis=2).reshape(peers, 8 * rb + extra, cb)
        return by_stage(got, order)
    at = lambda g, dest: (dest[g] // n_cols, dest[g] % n_cols)
    return pl.pallas_call(
        functools.partial(pack_attn_kernel, rb=rb),
        grid_spec=pltpu.PrefetchScalarGridSpec(
            num_scalar_prefetch=1,
            grid=(peers,),
            in_specs=[pl.BlockSpec((rb, cb), at)] * 8
            + [pl.BlockSpec((1, extra, cb), lambda g, dest: (dest[g] // n_cols, 0, 0))],
            out_specs=pl.BlockSpec((1, 8 * rb + extra, cb), lambda g, dest: (g, 0, 0)),
        ),
        out_shape=jax.ShapeDtypeStruct((peers, 8 * rb + extra, cb), BF),
        name="pack_attn",
    )(device_of_block(order, n_cols), *mats, small)


def pack_ff(ff_in, ff_out, order, n_rows, n_cols, rb, cb):
    peers = n_rows * n_cols
    if rb % 16 or cb % 128:
        first = ff_in.reshape(n_rows, rb, n_cols, 4, cb).transpose(0, 2, 3, 1, 4)
        second = ff_out.reshape(n_rows, 4, rb, n_cols, cb).transpose(0, 3, 1, 2, 4)
        got = jnp.concatenate([first, second], axis=2)
        return by_stage(got.reshape(peers, 8 * rb, cb), order)
    at = lambda g, dest: (dest[g] // n_cols, dest[g] % n_cols)
    return pl.pallas_call(
        functools.partial(pack_ff_kernel, rb=rb, cb=cb),
        grid_spec=pltpu.PrefetchScalarGridSpec(
            num_scalar_prefetch=1,
            grid=(peers,),
            in_specs=[pl.BlockSpec((rb, 4 * cb), at), pl.BlockSpec((4 * rb, cb), at)],
            out_specs=pl.BlockSpec((1, 8 * rb, cb), lambda g, dest: (g, 0, 0)),
        ),
        out_shape=jax.ShapeDtypeStruct((peers, 8 * rb, cb), BF),
        name="pack_ff",
    )(device_of_block(order, n_cols), ff_in, ff_out)


def plan_requests(ret_rows, shard_rows, peers, slots):
    flat = ret_rows.reshape(-1)
    count = flat.shape[0]
    owner = flat // shard_rows
    local_row = flat - owner * shard_rows
    mine = owner[:, None] == jnp.arange(peers, dtype=jnp.int32)[None, :]
    run = 256
    runs = count // run
    ones = mine.astype(BF).reshape(runs, run, peers)
    lower = jnp.tril(jnp.ones((run, run), BF))
    within = jnp.einsum("ij,bjo->bio", lower, ones, preferred_element_type=F32)
    totals = within[:, -1, :]
    before = jnp.cumsum(totals, axis=0) - totals
    upto = (within + before[:, None, :]).reshape(count, peers)
    rank = jnp.sum(jnp.where(mine, upto, 0.0), axis=1).astype(jnp.int32) - 1
    place = owner * slots + rank
    row_code = local_row + 1
    entry_code = jnp.arange(count, dtype=jnp.int32)
    digits = jnp.stack([row_code // 64, row_code % 64, entry_code // 64, entry_code % 64])
    left = jnp.where(mine.T[None], digits[:, None, :], 0).astype(BF)
    at_rank = (rank[:, None] == jnp.arange(slots, dtype=jnp.int32)[None, :]).astype(BF)
    codes = mm(left.reshape(4 * peers, count), at_rank).astype(jnp.int32).reshape(4, peers, slots)
    return place, codes[0] * 64 + codes[1], codes[2] * 64 + codes[3]


def own_rows(tokens, ret, heads):
    shape = (heads * tokens, tokens * ret)
    row_tok = lax.broadcasted_iota(jnp.int32, shape, 0) % tokens
    col_tok = lax.broadcasted_iota(jnp.int32, shape, 1) // ret
    return row_tok == col_tok


def cross_fwd_kernel(qk, fetched, mix, probs, *, ret):
    heads, tokens, dim = qk.shape
    own = own_rows(tokens, ret, heads)
    query = qk[...].reshape(heads * tokens, dim)
    rows = fetched[...]
    scores = jnp.where(own, mm_nt(query, rows) * 0.125, -1e30)
    expo = jnp.exp(scores - jnp.max(scores, axis=-1, keepdims=True))
    prob = expo / jnp.sum(expo, axis=-1, keepdims=True)
    probs[0] = prob
    mix[...] = mm(prob.astype(BF), rows).astype(BF).reshape(heads, tokens, dim)


def cross_bwd_kernel(qk, gmix, fetched, probs, grad_rows, grad_s, *, ret):
    heads, tokens, dim = qk.shape
    query = qk[...].reshape(heads * tokens, dim)
    grad_mix = gmix[...].reshape(heads * tokens, dim)
    prob = probs[0]
    grad_p = mm_nt(grad_mix, fetched[...])
    g_s = (prob * (grad_p - jnp.sum(prob * grad_p, axis=-1, keepdims=True))).astype(BF)
    grad_s[0] = g_s
    grad_rows[...] = (
        mm_tn(prob.astype(BF), grad_mix) + mm_tn(g_s, query) * 0.125
    ).astype(BF)


def cross_back_q_kernel(grad_s, fetched, grad_qk):
    heads, tokens, dim = grad_qk.shape
    got = mm(grad_s[0], fetched[...]) * 0.125
    grad_qk[...] = got.astype(BF).reshape(heads, tokens, dim)


def cross_calls(tok_count, ret, dim):
    tb = 16
    blocks = tok_count // tb
    by_head = pl.BlockSpec((H, tb, dim), lambda g: (0, g, 0))
    rows = pl.BlockSpec((tb * ret, dim), lambda g: (g, 0))
    square = pl.BlockSpec((1, H * tb, tb * ret), lambda g: (g, 0, 0))
    heads_shape = jax.ShapeDtypeStruct((H, tok_count, dim), BF)
    square_f32 = jax.ShapeDtypeStruct((blocks, H * tb, tb * ret), F32)
    square_bf = jax.ShapeDtypeStruct((blocks, H * tb, tb * ret), BF)
    params = pltpu.CompilerParams(vmem_limit_bytes=VMEM_LIMIT)
    fwd = pl.pallas_call(
        functools.partial(cross_fwd_kernel, ret=ret),
        grid=(blocks,),
        in_specs=[by_head, rows],
        out_specs=[by_head, square],
        out_shape=(heads_shape, square_f32),
        compiler_params=params,
        name="cross_fwd",
    )
    bwd = pl.pallas_call(
        functools.partial(cross_bwd_kernel, ret=ret),
        grid=(blocks,),
        in_specs=[by_head, by_head, rows, square],
        out_specs=[rows, square],
        out_shape=(jax.ShapeDtypeStruct((tok_count * ret, dim), BF), square_bf),
        compiler_params=params,
        name="cross_bwd",
    )
    back_q = pl.pallas_call(
        cross_back_q_kernel,
        grid=(blocks,),
        in_specs=[square, rows],
        out_specs=by_head,
        out_shape=heads_shape,
        compiler_params=params,
        name="cross_back_q",
    )
    return fwd, bwd, back_q


def store_sum_kernel(asked, returned, total, *, block):
    first = pl.program_id(0) * block + 1
    shape = (block, asked.shape[1])
    hit = lax.broadcasted_iota(jnp.int32, shape, 0) + first == asked[...]
    total[...] = mm(hit.astype(BF), returned[...])


def store_sum(asked, returned, shard_rows):
    count, dim = returned.shape
    block = 256
    return pl.pallas_call(
        functools.partial(store_sum_kernel, block=block),
        grid=(shard_rows // block,),
        in_specs=[
            pl.BlockSpec((1, count), lambda g: (0, 0)),
            pl.BlockSpec((count, dim), lambda g: (0, 0)),
        ],
        out_specs=pl.BlockSpec((block, dim), lambda g: (g, 0)),
        out_shape=jax.ShapeDtypeStruct((shard_rows, dim), F32),
        compiler_params=pltpu.CompilerParams(vmem_limit_bytes=VMEM_LIMIT),
        name="store_sum",
    )(asked.reshape(1, count), returned)


def all_to_all(array):
    return lax.all_to_all(array, RANKS, split_axis=0, concat_axis=0, tiled=True)


def on_device(
    tokens,
    seg_ids,
    live_mask,
    ret_rows,
    enc_store,
    attn_in,
    attn_out,
    ff_in,
    ff_out,
    biases,
    ln_gain,
    ln_shift,
    ff_bias,
    cotangent,
):
    n_rows = lax.axis_size("row")
    n_cols = lax.axis_size("col")
    peers = n_rows * n_cols
    tok_count, dim = tokens.shape
    shard_rows = enc_store.shape[0]
    ret = ret_rows.shape[1]
    slots = 3 * ret_rows.size // (2 * peers)
    rb, cb = attn_in.shape[1], attn_in.shape[2]
    order_a, order_b = bit_orders(n_rows, n_cols)
    far = n_rows.bit_length() - 3

    small_parts = (biases, ln_gain, ln_shift, ff_bias)
    small = jnp.concatenate([part.reshape(-1) for part in small_parts])
    small_rows = -(-small.size // (16 * cb)) * 16
    small = jnp.pad(small, (0, small_rows * cb - small.size)).reshape(small_rows, cb)
    pack_a = jnp.concatenate([attn_in.reshape(-1, cb), attn_out.reshape(-1, cb), small], axis=0)
    pack_b = jnp.concatenate([split_cols(ff_in, 4), ff_out], axis=0)
    part_a = gather_bits(pack_a[None], order_a[:far])
    part_b = gather_bits(pack_b[None], order_b[:far])

    place, wanted, entry = plan_requests(ret_rows, shard_rows, peers, slots)
    asked = all_to_all(wanted)
    answer = enc_store[jnp.maximum(asked - 1, 0)]
    answer, part_a, part_b = lax.optimization_barrier((answer, part_a, part_b))
    arrived = all_to_all(answer)
    part_a = gather_bits(part_a, order_a[far:])
    part_b = gather_bits(part_b, order_b[far:])
    w_in, w_out, small_all, w_ff1, w_ff2 = unpack(
        part_a,
        part_b,
        order_a,
        order_b,
        n_rows,
        n_cols,
        rb,
        cb,
    )
    small_all = small_all.reshape(n_rows, n_cols, -1)[:, 0, : sum(p.size for p in small_parts)]
    small_all = small_all.astype(F32)
    row_block = dim // n_rows
    vectors = small_all[:, : 13 * row_block].reshape(n_rows, 13, row_block)
    vectors = vectors.transpose(1, 0, 2).reshape(13, dim)
    bias_all, gain_all, shift_all = vectors[:7], vectors[7:10], vectors[10:]
    bias_ff = small_all[:, 13 * row_block :].reshape(-1)

    def heads(array):
        return array.reshape(tok_count, H, HD)

    queries = heads((mm(tokens, w_in[0]) + bias_all[0]).astype(BF))
    key_rows = heads(mm(tokens, w_in[1]).astype(BF))
    values = heads((mm(tokens, w_in[2]) + bias_all[1]).astype(BF))
    visible = visible_mask(seg_ids[0], live_mask[0])
    scores = jnp.einsum("qhd,khd->hqk", queries, key_rows, preferred_element_type=F32) * 0.125
    probs = jax.nn.softmax(jnp.where(visible[None], scores, -1e30), axis=-1)
    probs_low = probs.astype(BF)
    mixed = jnp.einsum("hqk,khd->qhd", probs_low, values, preferred_element_type=F32)
    mixed = mixed.reshape(tok_count, dim).astype(BF)
    branch = mm(mixed, w_out[0]) + bias_all[2]
    first, first_norm, first_scale = norm_fwd(
        tokens.astype(F32) + branch, gain_all[0], shift_all[0]
    )
    first_low = first.astype(BF)
    cross_q = (mm(first_low, w_in[3]) + bias_all[3]).astype(BF)

    key_heads = w_in[4].reshape(dim, H, HD)
    val_heads = w_in[5].reshape(dim, H, HD)
    query_keys = jnp.einsum(
        "the,dhe->htd", heads(cross_q), key_heads, preferred_element_type=F32
    ).astype(BF)
    cross_fwd, cross_bwd, cross_back_q = cross_calls(tok_count, ret, dim)
    fetched = arrived.reshape(peers * slots, dim)[place]
    state_mix, cross_p = cross_fwd(query_keys, fetched)
    cross_mix = jnp.einsum("htd,dhe->the", state_mix, val_heads, preferred_element_type=F32)
    cross_low = (cross_mix.reshape(tok_count, dim) + bias_all[4]).astype(BF)
    branch_two = mm(cross_low, w_out[1]) + bias_all[5]
    second, second_norm, second_scale = norm_fwd(first + branch_two, gain_all[1], shift_all[1])
    second_low = second.astype(BF)

    hidden_act, hidden_slope = gelu_parts(mm(second_low, w_ff1) + bias_ff)
    hidden_low = hidden_act.astype(BF)
    branch_ffn = mm(hidden_low, w_ff2) + bias_all[6]
    final, final_norm, final_scale = norm_fwd(second + branch_ffn, gain_all[2], shift_all[2])
    output = final.astype(BF)
    cot = cotangent.astype(F32)
    grad_three = norm_back(cot, final_norm, final_scale, gain_all[2])
    grad_y = grad_three.astype(BF)
    grad_pre = (mm_nt(grad_y, w_ff2) * hidden_slope).astype(BF)
    grad_second = grad_three + mm_nt(grad_pre, w_ff1)
    grad_two = norm_back(grad_second, second_norm, second_scale, gain_all[1])
    grad_o2 = grad_two.astype(BF)
    grad_cmix = mm_nt(grad_o2, w_out[1]).astype(BF)
    grad_smix = jnp.einsum(
        "the,dhe->htd", heads(grad_cmix), val_heads, preferred_element_type=F32
    ).astype(BF)
    grad_rows, grad_cs = cross_bwd(query_keys, grad_smix, fetched, cross_p)
    send_back = grad_rows[entry]
    returned = all_to_all(send_back)

    send_back, hidden_low, grad_cs, second_low, cross_low, state_mix = lax.optimization_barrier(
        (send_back, hidden_low, grad_cs, second_low, cross_low, state_mix)
    )
    grad_w_ff2 = mm_tn(hidden_low, grad_y).astype(BF)
    grad_w_ff1 = mm_tn(second_low, grad_pre).astype(BF)
    blocks_b = pack_ff(
        grad_w_ff1, grad_w_ff2, order_b[::-1], n_rows, n_cols, rb, cb
    )
    sum_b = scatter_bits(blocks_b, order_b[::-1])

    grad_qk = cross_back_q(grad_cs, fetched)
    grad_cq = jnp.einsum("htd,dhe->the", grad_qk, key_heads, preferred_element_type=F32)
    grad_cq = grad_cq.reshape(tok_count, dim).astype(BF)
    grad_first = grad_two + mm_nt(grad_cq, w_in[3])
    grad_one = norm_back(grad_first, first_norm, first_scale, gain_all[0])
    grad_o = grad_one.astype(BF)
    grad_mix = heads(mm_nt(grad_o, w_out[0]).astype(BF))
    grad_probs = jnp.einsum("qhd,khd->hqk", grad_mix, values, preferred_element_type=F32)
    grad_v = jnp.einsum("hqk,qhd->khd", probs_low, grad_mix, preferred_element_type=F32)
    grad_scores = (
        probs * (grad_probs - jnp.sum(probs * grad_probs, axis=-1, keepdims=True))
    ).astype(BF)
    grad_q = jnp.einsum("hqk,khd->qhd", grad_scores, key_rows, preferred_element_type=F32) * 0.125
    grad_k = jnp.einsum("hqk,qhd->khd", grad_scores, queries, preferred_element_type=F32) * 0.125
    grad_q, grad_k, grad_v = (
        part.reshape(tok_count, dim).astype(BF) for part in (grad_q, grad_k, grad_v)
    )
    grad_tokens = (
        grad_one + mm_nt(grad_q, w_in[0]) + mm_nt(grad_k, w_in[1]) + mm_nt(grad_v, w_in[2])
    )

    def by_head(left, right):
        return jnp.einsum("htd,the->dhe", left, heads(right), preferred_element_type=F32)

    mats = (
        mm_tn(tokens, grad_q).astype(BF),
        mm_tn(tokens, grad_k).astype(BF),
        mm_tn(tokens, grad_v).astype(BF),
        mm_tn(first_low, grad_cq).astype(BF),
        by_head(grad_qk, cross_q).reshape(dim, dim).astype(BF),
        by_head(state_mix, grad_cmix).reshape(dim, dim).astype(BF),
        mm_tn(mixed, grad_o).astype(BF),
        mm_tn(cross_low, grad_o2).astype(BF),
    )
    grad_vectors = jnp.stack(
        [
            column_sum(grad_q),
            column_sum(grad_v),
            column_sum(grad_o),
            column_sum(grad_cq),
            column_sum(grad_cmix),
            column_sum(grad_o2),
            column_sum(grad_y),
            jnp.sum(grad_first * first_norm, axis=0),
            jnp.sum(grad_second * second_norm, axis=0),
            jnp.sum(cot * final_norm, axis=0),
            jnp.sum(grad_first, axis=0),
            jnp.sum(grad_second, axis=0),
            jnp.sum(cot, axis=0),
        ]
    )
    grad_small = jnp.concatenate(
        [
            grad_vectors.reshape(13, n_rows, row_block)
            .transpose(1, 0, 2)
            .reshape(n_rows, 13 * row_block),
            column_sum(grad_pre).reshape(n_rows, -1),
        ],
        axis=1,
    ).astype(BF)
    grad_small = jnp.pad(grad_small, ((0, 0), (0, small_rows * cb - grad_small.shape[1])))
    blocks_a = pack_attn(
        mats,
        grad_small.reshape(n_rows, small_rows, cb),
        order_a[::-1],
        n_rows,
        n_cols,
        rb,
        cb,
    )
    sum_a = scatter_bits(blocks_a, order_a[::-1])

    grad_store = store_sum(asked, returned.reshape(peers * slots, dim), shard_rows)

    sum_a = sum_a.astype(F32)
    sum_b = sum_b.astype(F32)
    sum_small = sum_a[8 * rb :].reshape(-1)
    sum_vec = sum_small[: 13 * row_block].reshape(13, row_block)
    return (
        output,
        grad_tokens,
        grad_store,
        sum_a[: 6 * rb].reshape(6, rb, cb),
        sum_a[6 * rb : 8 * rb].reshape(2, rb, cb),
        jnp.concatenate([sum_b[k * rb : (k + 1) * rb] for k in range(4)], axis=1),
        sum_b[4 * rb :],
        sum_vec[:7],
        sum_vec[7:10],
        sum_vec[10:],
        sum_small[13 * row_block : 13 * row_block + ff_bias.size],
    )


def solution(mesh):
    both = ("row", "col")
    return jax.shard_map(
        on_device,
        mesh=mesh,
        in_specs=(
            P(both, None),
            P(both, None),
            P(both, None),
            P(both, None),
            P(both, None),
            P(None, "row", "col"),
            P(None, "row", "col"),
            P("row", "col"),
            P("row", "col"),
            P(None, "row"),
            P(None, "row"),
            P(None, "row"),
            P("row"),
            P(both, None),
        ),
        out_specs=(
            P(both, None),
            P(both, None),
            P(both, None),
            P(None, "row", "col"),
            P(None, "row", "col"),
            P("row", "col"),
            P("row", "col"),
            P(None, "row"),
            P(None, "row"),
            P(None, "row"),
            P("row"),
        ),
        check_vma=False,
    )
```

time: 2280 us -> 869 us (0.38)
  waiting for transfers between devices: 954 us -> 308 us
  blocking collectives: 498 us -> 25.2 us
  local copies, waits for them, and re-layouts: 558 us -> 175 us
  Pallas kernels: 0 us -> 160 us
  matrix products: 140 us -> 86.2 us
  other arithmetic: 93.1 us -> 66 us
  starting transfers between devices: 10.5 us -> 33.9 us
    reduce_scatter x5 -> x0, waiting for transfers between devices: 621 us -> none  [the longest x1 295 us: on_device(): lax.psum_scatter(grad_w_ff2.astype(jnp.bfloat16), 'row', scatter_dimensio...]
    unnamed x21 -> x0, waiting for transfers between devices: 333 us -> none
    ppermute x0 -> x20, waiting for transfers between devices: none -> 308 us  [swap_bit(): return lax.ppermute(array, axis, pairs)]
    gather x16 -> x5, local copies, waits for them, and re-layouts: 374 us -> 84.7 us  [the longest x1 32 us: on_device(): send_back = grad_rows[entry]]
    unnamed x2 -> x0, blocking collectives: 252 us -> none
    all_gather x7 -> x0, blocking collectives: 182 us -> none  [the longest x1 96.4 us: on_device(): lax.all_gather(ln_gain, 'row', axis=1, tiled=True)]
    pallas_call x0 -> x8, Pallas kernels: none -> 160 us  [the longest x1 25.6 us: store_sum(): pl.pallas_call(functools.partial(store_sum_kernel, block=block), grid=(sh...]
    scatter x3 -> x0, local copies, waits for them, and re-layouts: 57.3 us -> none  [the longest x1 26.2 us: on_device(): jnp.zeros((peers * slots, model_dim), f32).at[place].set(grad_fetched)]
  transfers between devices with their start and end apart: 17 -> 22, of which waited for: 10 -> 13; matrix products, arithmetic and copies ran while one was open for 29% -> 27% of each run, Pallas kernels for 0% -> 11%
where the time goes in v1:
time: 869 us; the launch traced here: 858 us
  waiting for transfers between devices  308 us (35%)
  local copies, waits for them, and re-layouts  175 us (20%)
  Pallas kernels  160 us (18%)
  matrix products  86.2 us (10%)
  other arithmetic  66 us (8%)
  starting transfers between devices  33.9 us (4%)
  blocking collectives  25.2 us (3%)
    ppermute x20, waiting for transfers between devices, swap_bit(): return lax.ppermute(array, axis, pairs)  308 us
    gather x1, local copies, waits for them, and re-layouts, on_device(): send_back = grad_rows[entry]  32 us
    concatenate x10, other arithmetic, gather_bits(): blocks = jnp.concatenate([blocks, swap_bit(blocks, axis, bit)], axis=0)  29.7 us
    gather x1, local copies, waits for them, and re-layouts, on_device(): answer = enc_store[jnp.maximum(asked - 1, 0)]  26.2 us
    pallas_call x1, Pallas kernels, store_sum(): pl.pallas_call(functools.partial(store_sum_kernel, block=block), grid=(sh...  25.6 us
    all_to_all x1, blocking collectives, all_to_all(): return lax.all_to_all(array, RANKS, split_axis=0, concat_axis=0, tiled=True)  25.2 us
    ppermute x20, starting transfers between devices, swap_bit(): return lax.ppermute(array, axis, pairs)  24.7 us
    gather x1, local copies, waits for them, and re-layouts, on_device(): fetched = arrived.reshape(peers * slots, dim)[place]  24.1 us
  transfers between devices with their start and end apart: 22, of which 13 were waited for; matrix products, arithmetic and copies ran while one was open for 27% of the time, Pallas kernels for 11%

profile of v1, /device:TPU:0, one launch (start us, length us, event | category | flops | bytes accessed | tf_op | source)
XLA Modules:
  0.0 857.5 jit_solution(12528032919030673249)
XLA Ops:
  41.7 25.2 %all_to_all.16 = s32[32,1,192]{2,1,0:T(1,128)S(1)} all-to-all(s32[32,1,192]{2,1,0:T(1,128)S(1)} %copy.83), channel_id=1, replica_groups=mesh['row'=16,'col'=2] {'row','col'}, dimensions={0} | all-to-all | bytes 49152 | tf_op jit(solution)/shard_map/all_to_all | solution.py:397
  67.7 26.2 %gather_fusion.1 = bf16[6144,768]{1,0:T(8,128)(2,1)} fusion(bf16[2048,768]{1,0:T(8,128)(2,1)S(1)} %copy-done, s32[6144]{0:T(1024)S(1)} %broadcast_clamp_fusion.1), kind=kCustom, calls=%fused_computation.1 | custom fusion | bytes 18898944 | tf_op jit(solution)/shard_map/gather | solution.py:438
  96.8 4.6 all-to-all-start.1
  104.7 116.8 %collective-permute-done.7 = bf16[4,384,384]{2,1,0:T(8,128)(2,1)S(1)} collective-permute-done((bf16[4,384,384]{2,1,0:T(8,128)(2,1)S(1)}, bf16[4,384,384]{2,1,0:T(8,128)(2,1)S(1)}, u32[]{:S(2)}, u32[]{:S(2)}) %collective-permute-start.7) | collective-permute-done | bytes 1179680 | tf_op jit(solution)/shard_map/ppermute | solution.py:76
  223.9 70.7 %collective-permute-done.8 = bf16[8,384,384]{2,1,0:T(8,128)(2,1)S(1)} collective-permute-done((bf16[8,384,384]{2,1,0:T(8,128)(2,1)S(1)}, bf16[8,384,384]{2,1,0:T(8,128)(2,1)S(1)}, u32[]{:S(2)}, u32[]{:S(2)}) %collective-permute-start.8) | collective-permute-done | bytes 2359328 | tf_op jit(solution)/shard_map/ppermute | solution.py:76
  306.0 8.8 %pad_maximum_fusion.1.blk = bf16[32,384,384]{2,1,0:T(8,128)(2,1)} fusion(bf16[16,384,384]{2,1,0:T(8,128)(2,1)} %collective-permute-done.9, bf16[8,384,384]{2,1,0:T(8,128)(2,1)} %copy-done.10, bf16[4,384,384]{2,1,0:T(8,128)(2,1)} %copy-done.6, bf16[4,384,384]{2,1,0:T(8,128)(2,1)S(1)} %pad_maximum_fusion.7), kind=kLoop, calls=%fused_computation.7 | loop fusion | flops 14155776 | bytes 18874368 | tf_op jit(solution)/shard_map/concatenate | solution.py:81
  314.8 20.7 %unpack_ff.1 = (bf16[768,3072]{1,0:T(8,128)(2,1)}, bf16[3072,768]{1,0:T(8,128)(2,1)}) custom-call(s32[32]{0:T(128)} %gather_fusion.3, bf16[32,384,384]{2,1,0:T(8,128)(2,1)} %pad_maximum_fusion.1.blk), custom_call_target="tpu_custom_call" | custom-call | tf_op jit(solution)/shard_map/unpack_ff/pallas_call | solution.py:211
  335.5 8.5 pad_maximum_fusion.blk
  344.0 20.4 %unpack_attn.1 = (bf16[6,768,768]{2,1,0:T(8,128)(2,1)}, bf16[2,768,768]{2,1,0:T(8,128)(2,1)}, bf16[32,16,384]{2,1,0:T(8,128)(2,1)}) custom-call(s32[32]{0:T(128)} %gather_fusion, bf16[32,400,384]{2,1,0:T(8,128)(2,1)} %pad_maximum_fusion.blk), custom_call_target="tpu_custom_call" | custom-call | tf_op jit(solution)/shard_map/unpack_attn/pallas_call | solution.py:195
  386.8 4.4 fusion.112
  403.0 24.1 %gather_fusion.2 = bf16[4096,768]{1,0:T(8,128)(2,1)} fusion(bf16[6144,768]{1,0:T(8,128)(2,1)} %bitcast.28, s32[4096]{0:T(1024)S(1)} %broadcast_clamp_fusion.2), kind=kCustom, calls=%fused_computation.2 | custom fusion | bytes 12599296 | tf_op jit(solution)/shard_map/gather | solution.py:486
  427.1 18.2 %cross_fwd.1 = (bf16[12,256,768]{2,1,0:T(8,128)(2,1)}, f32[16,192,256]{2,1,0:T(8,128)}) custom-call(bf16[12,256,768]{2,1,0:T(8,128)(2,1)} %convolution_convert_fusion.3.qk, bf16[4096,768]{1,0:T(8,128)(2,1)} %gather_fusion.2), custom_call_target="tpu_custom_call" | custom-call | tf_op jit(solution)/shard_map/cross_fwd/pallas_call | solution.py:487
  445.3 4.9 fusion.56
  470.4 20.7 %cross_bwd.1 = (bf16[4096,768]{1,0:T(8,128)(2,1)}, bf16[16,192,256]{2,1,0:T(8,128)(2,1)}) custom-call(bf16[12,256,768]{2,1,0:T(8,128)(2,1)} %convolution_convert_fusion.3.qk, bf16[12,256,768]{2,1,0:T(8,128)(2,1)} %convolution_convert_fusion.2.gmix, bf16[4096,768]{1,0:T(8,128)(2,1)} %gather_fusion.2, f32[16,192,256]{2,1,0:T(8,128)} %get-tuple-element.37.probs), custom_call_target="tpu_custom_call" | custom-call | tf_op jit(solution)/shard_map/cross_bwd/pallas_call | solution.py:510
  491.1 32.0 %gather_fusion.4 = bf16[6144,768]{1,0:T(8,128)(2,1)} fusion(bf16[4096,768]{1,0:T(8,128)(2,1)} %get-tuple-element.38, s32[6144]{0:T(1024)S(1)} %copy-done.51), kind=kCustom, calls=%fused_computation.4 | custom fusion | bytes 18898944 | tf_op jit(solution)/shard_map/gather | solution.py:511
  523.1 4.7 all-to-all-start.2
  528.7 12.8 %cross_back_q.1 = bf16[12,256,768]{2,1,0:T(8,128)(2,1)} custom-call(bf16[16,192,256]{2,1,0:T(8,128)(2,1)} %get-tuple-element.40.grad_s, bf16[4096,768]{1,0:T(8,128)(2,1)} %gather_fusion.2), custom_call_target="tpu_custom_call" | custom-call | tf_op jit(solution)/shard_map/cross_back_q/pallas_call | solution.py:524
  541.5 4.7 bitcast_reduce_fusion.2
  587.5 5.3 convolution_convert_fusion.1.ff_in
  596.4 21.0 %pack_ff.1 = bf16[32,384,384]{2,1,0:T(8,128)(2,1)} custom-call(s32[32]{0:T(128)} %get-tuple-element.94.dest, bf16[768,3072]{1,0:T(8,128)(2,1)} %convolution_convert_fusion.1.ff_in, bf16[3072,768]{1,0:T(8,128)(2,1)} %convolution_convert_fusion.ff_out), custom_call_target="tpu_custom_call" | custom-call | tf_op jit(solution)/shard_map/pack_ff/pallas_call | solution.py:256
  617.5 5.2 slice.388
  640.6 20.6 %pack_attn.1 = bf16[32,400,384]{2,1,0:T(8,128)(2,1)} custom-call(s32[32]{0:T(128)} %get-tuple-element.95.dest, bf16[768,768]{1,0:T(8,128)(2,1)} %fusion.12.refs_0_, bf16[768,768]{1,0:T(8,128)(2,1)} %fusion.13.refs_1_, bf16[768,768]{1,0:T(8,128)(2,1)} %fusion.14.refs_2_, bf16[768,768]{1,0:T(8,128)(2,1)} %convolution_convert_fusion.8.refs_3_, ...), custom_call_target="tpu_custom_call" | custom-call | tf_op jit(solution)/shard_map/pack_attn/pallas_call | solution.py:234
  661.2 5.5 slice.376
  667.1 4.5 slice_add_fusion.1
  675.3 5.2 slice_add_fusion
  684.3 57.4 %collective-permute-done.16 = bf16[8,384,384]{2,1,0:T(8,128)(2,1)} collective-permute-done((bf16[8,384,384]{2,1,0:T(8,128)(2,1)}, bf16[8,384,384]{2,1,0:T(8,128)(2,1)}, u32[]{:S(2)}, u32[]{:S(2)}) %collective-permute-start.16) | collective-permute-done | bytes 2359328 | tf_op jit(solution)/shard_map/ppermute | solution.py:76
  745.5 6.0 collective-permute-done.11
  758.5 17.7 %collective-permute-done.17 = bf16[4,384,384]{2,1,0:T(8,128)(2,1)} collective-permute-done((bf16[4,384,384]{2,1,0:T(8,128)(2,1)}, bf16[4,384,384]{2,1,0:T(8,128)(2,1)}, u32[]{:S(2)}, u32[]{:S(2)}) %collective-permute-start.17) | collective-permute-done | bytes 1179680 | tf_op jit(solution)/shard_map/ppermute | solution.py:76
  786.0 8.4 collective-permute-done.18
  799.3 12.3 %collective-permute-done.19 = bf16[1,384,384]{2,1,0:T(8,128)(2,1)S(1)} collective-permute-done((bf16[1,384,384]{2,1,0:T(8,128)(2,1)S(1)}, bf16[1,384,384]{2,1,0:T(8,128)(2,1)S(1)}, u32[]{:S(2)}, u32[]{:S(2)}) %collective-permute-start.19) | collective-permute-done | bytes 294944 | tf_op jit(solution)/shard_map/ppermute | solution.py:76
  816.8 11.2 %collective-permute-done.14 = bf16[1,400,384]{2,1,0:T(8,128)(2,1)S(1)} collective-permute-done((bf16[1,400,384]{2,1,0:T(8,128)(2,1)S(1)}, bf16[1,400,384]{2,1,0:T(8,128)(2,1)S(1)}, u32[]{:S(2)}, u32[]{:S(2)}) %collective-permute-start.14) | collective-permute-done | bytes 307232 | tf_op jit(solution)/shard_map/ppermute | solution.py:76
  831.4 25.6 %store_sum.1 = f32[2048,768]{1,0:T(8,128)} custom-call(s32[1,6144]{1,0:T(1,128)} %reshape.849.asked, bf16[6144,768]{1,0:T(8,128)(2,1)} %bitcast.49.returned), custom_call_target="tpu_custom_call" | custom-call | tf_op jit(solution)/shard_map/store_sum/pallas_call | solution.py:382
  (443 shorter events, 220.8 us)
Async XLA Ops:
  0.6 67.1 %copy-start = (bf16[2048,768]{1,0:T(8,128)(2,1)S(1)}, bf16[2048,768]{1,0:T(8,128)(2,1)}, u32[]{:S(2)}) copy-start(bf16[2048,768]{1,0:T(8,128)(2,1)} %param.24) | copy-start | bytes 9437188
  7.9 25.1 %collective-permute-start.2 = (bf16[1,384,384]{2,1,0:T(8,128)(2,1)}, bf16[1,384,384]{2,1,0:T(8,128)(2,1)}, u32[]{:S(2)}, u32[]{:S(2)}) collective-permute-start(bf16[1,384,384]{2,1,0:T(8,128)(2,1)} %bitcast.8), channel_id=1, source_target_pairs={{0,16},{2,18},{4,20},{6,22},{8,24},{10,26},{12,28},{14,30},{16,0},... | collective-permute-start | bytes 884744 | tf_op jit(solution)/shard_map/ppermute | solution.py:76
  16.8 22.1 %collective-permute-start = (bf16[1,400,384]{2,1,0:T(8,128)(2,1)}, bf16[1,400,384]{2,1,0:T(8,128)(2,1)}, u32[]{:S(2)}, u32[]{:S(2)}) collective-permute-start(bf16[1,400,384]{2,1,0:T(8,128)(2,1)} %maximum_bitcast_fusion), channel_id=1, source_target_pairs={{0,16},{2,18},{4,20},{6,22},{8,24},{10,26},{12,28},{14,30},{16,0},... | collective-permute-start | bytes 921608 | tf_op jit(solution)/shard_map/ppermute | solution.py:76
  35.0 59.0 %collective-permute-start.3 = (bf16[2,384,384]{2,1,0:T(8,128)(2,1)}, bf16[2,384,384]{2,1,0:T(8,128)(2,1)}, u32[]{:S(2)}, u32[]{:S(2)}) collective-permute-start(bf16[2,384,384]{2,1,0:T(8,128)(2,1)} %pad_maximum_fusion.9), channel_id=1, source_target_pairs={{0,8},{2,10},{4,12},{6,14},{8,0},{10,2},{12,4},{14,6},{16,24},{18,... | collective-permute-start | bytes 1769480 | tf_op jit(solution)/shard_map/ppermute | solution.py:76
  40.8 54.5 %collective-permute-start.1 = (bf16[2,400,384]{2,1,0:T(8,128)(2,1)}, bf16[2,400,384]{2,1,0:T(8,128)(2,1)}, u32[]{:S(2)}, u32[]{:S(2)}) collective-permute-start(bf16[2,400,384]{2,1,0:T(8,128)(2,1)} %pad_maximum_fusion.8), channel_id=1, source_target_pairs={{0,8},{2,10},{4,12},{6,14},{8,0},{10,2},{12,4},{14,6},{16,24},{18,... | collective-permute-start | bytes 1843208 | tf_op jit(solution)/shard_map/ppermute | solution.py:76
  96.8 306.2 %all-to-all-start.1 = ((bf16[32,192,768]{2,1,0:T(8,128)(2,1)}), bf16[32,192,768]{2,1,0:T(8,128)(2,1)}, u32[]{:S(2)}, u32[]{:S(2)}) async-start(bf16[32,192,768]{2,1,0:T(8,128)(2,1)} %bitcast.202), calls=%async_computation.1 | async-start | bytes 18874368 | tf_op jit(solution)/shard_map/all_to_all | solution.py:397
  101.3 120.2 %collective-permute-start.7 = (bf16[4,384,384]{2,1,0:T(8,128)(2,1)S(1)}, bf16[4,384,384]{2,1,0:T(8,128)(2,1)S(1)}, u32[]{:S(2)}, u32[]{:S(2)}) collective-permute-start(bf16[4,384,384]{2,1,0:T(8,128)(2,1)S(1)} %pad_maximum_fusion.7), channel_id=1, source_target_pairs={{0,2},{2,0},{4,6},{6,4},{8,10},{10,8},{12,14},{14,12},{16,18},{18,... | collective-permute-start | bytes 3538952 | tf_op jit(solution)/shard_map/ppermute | solution.py:76
  103.3 118.6 %collective-permute-start.4 = (bf16[4,400,384]{2,1,0:T(8,128)(2,1)S(1)}, bf16[4,400,384]{2,1,0:T(8,128)(2,1)S(1)}, u32[]{:S(2)}, u32[]{:S(2)}) collective-permute-start(bf16[4,400,384]{2,1,0:T(8,128)(2,1)S(1)} %pad_maximum_fusion.6), channel_id=1, source_target_pairs={{0,4},{2,6},{4,0},{6,2},{8,12},{10,14},{12,8},{14,10},{16,20},{18,... | collective-permute-start | bytes 3686408 | tf_op jit(solution)/shard_map/ppermute | solution.py:76
  221.5 73.0 %copy-start.6 = (bf16[4,384,384]{2,1,0:T(8,128)(2,1)}, bf16[4,384,384]{2,1,0:T(8,128)(2,1)S(1)}, u32[]{:S(2)}) copy-start(bf16[4,384,384]{2,1,0:T(8,128)(2,1)S(1)} %collective-permute-done.7) | copy-start | bytes 3538948
  221.8 72.8 %collective-permute-start.8 = (bf16[8,384,384]{2,1,0:T(8,128)(2,1)S(1)}, bf16[8,384,384]{2,1,0:T(8,128)(2,1)S(1)}, u32[]{:S(2)}, u32[]{:S(2)}) collective-permute-start(bf16[8,384,384]{2,1,0:T(8,128)(2,1)S(1)} %pad_maximum_fusion.5), channel_id=1, source_target_pairs={{0,4},{2,6},{4,0},{6,2},{8,12},{10,14},{12,8},{14,10},{16,20},{18,... | collective-permute-start | bytes 7077896 | tf_op jit(solution)/shard_map/ppermute | solution.py:76
  221.9 75.5 %copy-start.4 = (bf16[4,400,384]{2,1,0:T(8,128)(2,1)}, bf16[4,400,384]{2,1,0:T(8,128)(2,1)S(1)}, u32[]{:S(2)}) copy-start(bf16[4,400,384]{2,1,0:T(8,128)(2,1)S(1)} %collective-permute-done.4) | copy-start | bytes 3686404
  222.2 75.2 %collective-permute-start.5 = (bf16[8,400,384]{2,1,0:T(8,128)(2,1)S(1)}, bf16[8,400,384]{2,1,0:T(8,128)(2,1)S(1)}, u32[]{:S(2)}, u32[]{:S(2)}) collective-permute-start(bf16[8,400,384]{2,1,0:T(8,128)(2,1)S(1)} %pad_maximum_fusion.4), channel_id=1, source_target_pairs={{0,2},{2,0},{4,6},{6,4},{8,10},{10,8},{12,14},{14,12},{16,18},{18,... | collective-permute-start | bytes 7372808 | tf_op jit(solution)/shard_map/ppermute | solution.py:76
  297.4 8.6 %collective-permute-start.9 = (bf16[16,384,384]{2,1,0:T(8,128)(2,1)}, bf16[16,384,384]{2,1,0:T(8,128)(2,1)}, u32[]{:S(2)}, u32[]{:S(2)}) collective-permute-start(bf16[16,384,384]{2,1,0:T(8,128)(2,1)} %pad_maximum_fusion.3), channel_id=1, source_target_pairs={{0,1},{1,0},{2,3},{3,2},{4,5},{5,4},{6,7},{7,6},{8,9},{9,8},{10,11... | collective-permute-start | bytes 14155784 | tf_op jit(solution)/shard_map/ppermute | solution.py:76
  300.4 35.1 %collective-permute-start.6 = (bf16[16,400,384]{2,1,0:T(8,128)(2,1)}, bf16[16,400,384]{2,1,0:T(8,128)(2,1)}, u32[]{:S(2)}, u32[]{:S(2)}) collective-permute-start(bf16[16,400,384]{2,1,0:T(8,128)(2,1)} %pad_maximum_fusion.2), channel_id=1, source_target_pairs={{0,1},{1,0},{2,3},{3,2},{4,5},{5,4},{6,7},{7,6},{8,9},{9,8},{10,11... | collective-permute-start | bytes 14745608 | tf_op jit(solution)/shard_map/ppermute | solution.py:76
  314.8 20.7 %copy-start.5 = (bf16[4,400,384]{2,1,0:T(8,128)(2,1)S(1)}, bf16[4,400,384]{2,1,0:T(8,128)(2,1)}, u32[]{:S(2)}) copy-start(bf16[4,400,384]{2,1,0:T(8,128)(2,1)} %copy-done.4) | copy-start | bytes 3686404
  470.4 20.7 %copy-start.51 = (s32[6144]{0:T(1024)S(1)}, s32[6144]{0:T(1024)}, u32[]{:S(2)}) copy-start(s32[6144]{0:T(1024)} %broadcast_clamp_fusion) | copy-start | bytes 73732
  523.1 308.3 %all-to-all-start.2 = ((bf16[32,192,768]{2,1,0:T(8,128)(2,1)}), bf16[32,192,768]{2,1,0:T(8,128)(2,1)}, u32[]{:S(2)}, u32[]{:S(2)}) async-start(bf16[32,192,768]{2,1,0:T(8,128)(2,1)} %bitcast.201), calls=%async_computation.2 | async-start | bytes 18874368 | tf_op jit(solution)/shard_map/all_to_all | solution.py:397
  622.7 44.4 %collective-permute-start.15 = (bf16[16,384,384]{2,1,0:T(8,128)(2,1)}, bf16[16,384,384]{2,1,0:T(8,128)(2,1)}, u32[]{:S(2)}, u32[]{:S(2)}) collective-permute-start(bf16[16,384,384]{2,1,0:T(8,128)(2,1)} %slice.388), channel_id=1, source_target_pairs={{0,1},{1,0},{2,3},{3,2},{4,5},{5,4},{6,7},{7,6},{8,9},{9,8},{10,11... | collective-permute-start | bytes 14155784 | tf_op jit(solution)/shard_map/ppermute | solution.py:76
  666.7 8.5 collective-permute-start.10
  673.3 68.4 %collective-permute-start.16 = (bf16[8,384,384]{2,1,0:T(8,128)(2,1)}, bf16[8,384,384]{2,1,0:T(8,128)(2,1)}, u32[]{:S(2)}, u32[]{:S(2)}) collective-permute-start(bf16[8,384,384]{2,1,0:T(8,128)(2,1)} %slice.390), channel_id=1, source_target_pairs={{0,4},{2,6},{4,0},{6,2},{8,12},{10,14},{12,8},{14,10},{16,20},{18,... | collective-permute-start | bytes 7077896 | tf_op jit(solution)/shard_map/ppermute | solution.py:76
  680.4 71.0 %slice-start.5 = ((s8[4915200]{0:T(1024)(128)(4,1)}), s8[4194304]{0:T(1024)(128)(4,1)S(1)}, s32[]{:S(2)}) async-start(s8[4915200]{0:T(1024)(128)(4,1)} %bitcast.203), calls=%async_computation.8 | async-start | bytes 8388608
  682.5 68.9 %slice-start.6 = ((s8[4915200]{0:T(1024)(128)(4,1)}), s8[720896]{0:T(1024)(128)(4,1)S(1)}, s32[]{:S(2)}) async-start(s8[4915200]{0:T(1024)(128)(4,1)} %bitcast.203), calls=%async_computation.9 | async-start | bytes 1441792
  682.6 68.9 %collective-permute-start.11 = (bf16[8,400,384]{2,1,0:T(8,128)(2,1)S(1)}, bf16[8,400,384]{2,1,0:T(8,128)(2,1)S(1)}, u32[]{:S(2)}, u32[]{:S(2)}) collective-permute-start(bf16[8,400,384]{2,1,0:T(8,128)(2,1)S(1)} %slice.378), channel_id=1, source_target_pairs={{0,2},{2,0},{4,6},{6,4},{8,10},{10,8},{12,14},{14,12},{16,18},{18,... | collective-permute-start | bytes 7372808 | tf_op jit(solution)/shard_map/ppermute | solution.py:76
  744.9 31.4 %collective-permute-start.17 = (bf16[4,384,384]{2,1,0:T(8,128)(2,1)}, bf16[4,384,384]{2,1,0:T(8,128)(2,1)}, u32[]{:S(2)}, u32[]{:S(2)}) collective-permute-start(bf16[4,384,384]{2,1,0:T(8,128)(2,1)} %slice.392), channel_id=1, source_target_pairs={{0,2},{2,0},{4,6},{6,4},{8,10},{10,8},{12,14},{14,12},{16,18},{18,... | collective-permute-start | bytes 3538952 | tf_op jit(solution)/shard_map/ppermute | solution.py:76
  754.3 28.2 %collective-permute-start.12 = (bf16[4,400,384]{2,1,0:T(8,128)(2,1)}, bf16[4,400,384]{2,1,0:T(8,128)(2,1)}, u32[]{:S(2)}, u32[]{:S(2)}) collective-permute-start(bf16[4,400,384]{2,1,0:T(8,128)(2,1)} %slice.380), channel_id=1, source_target_pairs={{0,4},{2,6},{4,0},{6,2},{8,12},{10,14},{12,8},{14,10},{16,20},{18,... | collective-permute-start | bytes 3686408 | tf_op jit(solution)/shard_map/ppermute | solution.py:76
  758.5 21.3 %copy-start.23 = (bf16[12,64,256]{2,1,0:T(8,128)(2,1)S(1)}, bf16[12,64,256]{2,1,0:T(8,128)(2,1)}, u32[]{:S(2)}) copy-start(bf16[12,64,256]{2,1,0:T(8,128)(2,1)} %copy-done.22) | copy-start | bytes 1179652
  758.5 24.0 %copy-start.8 = (bf16[8,400,384]{2,1,0:T(8,128)(2,1)S(1)}, bf16[8,400,384]{2,1,0:T(8,128)(2,1)}, u32[]{:S(2)}) copy-start(bf16[8,400,384]{2,1,0:T(8,128)(2,1)} %copy-done.7) | copy-start | bytes 7372804
  778.1 16.3 %collective-permute-start.18 = (bf16[2,384,384]{2,1,0:T(8,128)(2,1)S(1)}, bf16[2,384,384]{2,1,0:T(8,128)(2,1)S(1)}, u32[]{:S(2)}, u32[]{:S(2)}) collective-permute-start(bf16[2,384,384]{2,1,0:T(8,128)(2,1)S(1)} %slice.394), channel_id=1, source_target_pairs={{0,8},{2,10},{4,12},{6,14},{8,0},{10,2},{12,4},{14,6},{16,24},{18,... | collective-permute-start | bytes 1769480 | tf_op jit(solution)/shard_map/ppermute | solution.py:76
  784.0 28.4 %collective-permute-start.13 = (bf16[2,400,384]{2,1,0:T(8,128)(2,1)S(1)}, bf16[2,400,384]{2,1,0:T(8,128)(2,1)S(1)}, u32[]{:S(2)}, u32[]{:S(2)}) collective-permute-start(bf16[2,400,384]{2,1,0:T(8,128)(2,1)S(1)} %slice.382), channel_id=1, source_target_pairs={{0,8},{2,10},{4,12},{6,14},{8,0},{10,2},{12,4},{14,6},{16,24},{18,... | collective-permute-start | bytes 1843208 | tf_op jit(solution)/shard_map/ppermute | solution.py:76
  794.5 17.1 %collective-permute-start.19 = (bf16[1,384,384]{2,1,0:T(8,128)(2,1)S(1)}, bf16[1,384,384]{2,1,0:T(8,128)(2,1)S(1)}, u32[]{:S(2)}, u32[]{:S(2)}) collective-permute-start(bf16[1,384,384]{2,1,0:T(8,128)(2,1)S(1)} %slice.396), channel_id=1, source_target_pairs={{0,16},{2,18},{4,20},{6,22},{8,24},{10,26},{12,28},{14,30},{16,0},... | collective-permute-start | bytes 884744 | tf_op jit(solution)/shard_map/ppermute | solution.py:76
  812.5 15.4 %collective-permute-start.14 = (bf16[1,400,384]{2,1,0:T(8,128)(2,1)S(1)}, bf16[1,400,384]{2,1,0:T(8,128)(2,1)S(1)}, u32[]{:S(2)}, u32[]{:S(2)}) collective-permute-start(bf16[1,400,384]{2,1,0:T(8,128)(2,1)S(1)} %slice.384), channel_id=1, source_target_pairs={{0,16},{2,18},{4,20},{6,22},{8,24},{10,26},{12,28},{14,30},{16,0},... | collective-permute-start | bytes 921608 | tf_op jit(solution)/shard_map/ppermute | solution.py:76
  831.4 25.6 %copy-start.1 = (bf16[2048,768]{1,0:T(8,128)(2,1)S(1)}, bf16[2048,768]{1,0:T(8,128)(2,1)}, u32[]{:S(2)}) copy-start(bf16[2048,768]{1,0:T(8,128)(2,1)} %param.24) | copy-start | bytes 9437188
  (89 other events, 383.3 us)

commit v2 on v1

v2 whole, which is shorter than its diff:
```python
import functools

import jax
import jax.numpy as jnp
import numpy as np
from jax import lax
from jax.experimental import pallas as pl
from jax.experimental.pallas import tpu as pltpu
from jax.sharding import PartitionSpec as P

H = 12
HD = 64
RANKS = ("row", "col")
BF = jnp.bfloat16
F32 = jnp.float32
VMEM_LIMIT = 60 * 1024 * 1024


def mm(a, b):
    return jnp.dot(a, b, preferred_element_type=F32)


def mm_nt(a, b):
    return lax.dot_general(a, b, (((1,), (1,)), ((), ())), preferred_element_type=F32)


def mm_tn(a, b):
    return lax.dot_general(a, b, (((0,), (0,)), ((), ())), preferred_element_type=F32)


def norm_fwd(resid, gain, shift):
    row_mean = jnp.mean(resid, axis=-1, keepdims=True)
    centered = resid - row_mean
    inv_std = lax.rsqrt(jnp.mean(centered * centered, axis=-1, keepdims=True) + 1e-05)
    normed = centered * inv_std
    return (normed * gain + shift, normed, inv_std)


def norm_back(grad_in, normed, inv_std, gain):
    scaled = grad_in * gain
    return inv_std * (
        scaled
        - jnp.mean(scaled, axis=-1, keepdims=True)
        - normed * jnp.mean(scaled * normed, axis=-1, keepdims=True)
    )


def gelu_parts(pre_act):
    cdf_part = 0.5 * (1.0 + lax.erf(pre_act * 0.7071067811865476))
    density = jnp.exp(-0.5 * pre_act * pre_act) * 0.3989422804014327
    return (pre_act * cdf_part, cdf_part + pre_act * density)


def visible_mask(seg_row, live_row):
    pos = jnp.arange(seg_row.shape[0], dtype=jnp.int32)
    return (
        (pos[None, :] <= pos[:, None])
        & (seg_row[:, None] == seg_row[None, :])
        & ((live_row[None, :] == 1) | (pos[None, :] == pos[:, None]))
    )


def column_sum(array):
    return jnp.sum(array.astype(F32), axis=0)


def bit_orders(n_rows, n_cols):
    row_bits = [("row", 1 << b) for b in reversed(range(n_rows.bit_length() - 1))]
    col_bits = [("col", 1 << b) for b in reversed(range(n_cols.bit_length() - 1))]
    swapped = row_bits[:-2] + row_bits[-1:] + row_bits[-2:-1]
    return row_bits + col_bits, swapped + col_bits


def swap_bit(array, axis, bit):
    pairs = [(i, i ^ bit) for i in range(lax.axis_size(axis))]
    return lax.ppermute(array, axis, pairs)


def gather_bits(blocks, order):
    for axis, bit in order:
        blocks = jnp.concatenate([blocks, swap_bit(blocks, axis, bit)], axis=0)
    return blocks


def scatter_bits(keep, send, order):
    for axis, bit in order:
        got = swap_bit(send, axis, bit)
        half = keep.shape[0] // 2
        keep, send = keep[:half] + got[:half], keep[half:] + got[half:]
    return keep, send


def block_of_row(order, n_rows):
    apart = np.zeros(n_rows, np.int32)
    for k, (_, bit) in enumerate(order[: n_rows.bit_length() - 1]):
        apart[(np.arange(n_rows) >> k) & 1 == 1] ^= bit
    table = np.zeros(n_rows, np.int32)
    table[apart] = np.arange(n_rows)
    return jnp.asarray(table)[lax.axis_index("row") ^ jnp.arange(n_rows, dtype=jnp.int32)]


def flip_by_position(blocks, stages):
    for k, (axis, bit) in enumerate(stages):
        here = (lax.axis_index(axis) & bit) != 0
        blocks = jnp.where(here, jnp.flip(blocks, axis=k), blocks)
    return blocks


def by_device(blocks, order):
    stages = order[::-1]
    shape = blocks.shape[1:]
    blocks = flip_by_position(blocks.reshape((2,) * len(stages) + shape), stages)
    rank = sorted(range(len(stages)), key=lambda k: (stages[k][0] == "col", -stages[k][1]))
    rest = list(range(len(stages), blocks.ndim))
    return blocks.transpose(rank + rest).reshape((-1,) + shape)


def by_stage(blocks, stages):
    shape = blocks.shape[1:]
    rank = sorted(range(len(stages)), key=lambda k: (stages[k][0] == "col", -stages[k][1]))
    rest = list(range(len(stages), len(stages) + len(shape)))
    back = [rank.index(k) for k in range(len(stages))]
    blocks = blocks.reshape((2,) * len(stages) + shape).transpose(back + rest)
    return flip_by_position(blocks, stages).reshape((-1,) + shape)


WAIT = pl.BlockSpec(memory_space=pl.ANY)


def tie_kernel(*refs):
    refs[-1][...] = refs[0][...]


def tie(array, after):
    return pl.pallas_call(
        tie_kernel,
        in_specs=[pl.BlockSpec(memory_space=pltpu.VMEM)] + [WAIT] * len(after),
        out_shape=jax.ShapeDtypeStruct(array.shape, array.dtype),
        name="tie",
    )(array, *after)


def hold_kernel(*refs):
    del refs


def hold(array, after):
    return pl.pallas_call(
        hold_kernel,
        in_specs=[WAIT] * (1 + len(after)),
        out_specs=WAIT,
        out_shape=jax.ShapeDtypeStruct(array.shape, array.dtype),
        input_output_aliases={0: 0},
        name="hold",
    )(array, *after)


def tile_of(buf, k, r, c, shape):
    rows, cols = shape
    return buf.at[
        k, pl.ds(pl.multiple_of(r * rows, rows), rows), pl.ds(pl.multiple_of(c * cols, cols), cols)
    ]


def unpack_kernel(place, own, other, *refs, count, shape, first, beside, extra):
    outs, (buf, *more) = refs[: 1 + bool(extra)], refs[1 + bool(extra) :]
    sems = more[-1]
    n_rows, col, rows = own.shape[0], place[own.shape[0]], shape[0]

    def fill(r, carry):
        j = place[r]
        for src, c, sem in ((own, col, 0), (other, 1 - col, 1)):
            for k in range(count):
                part = src.at[j, pl.ds(first + k * rows, rows)]
                to = (0, r, c * count + k) if beside else (k, r, c)
                pltpu.make_async_copy(part, tile_of(buf, *to, shape), sems.at[sem]).start()
        if extra:
            tail = own.at[j, pl.ds(first + count * rows, extra)]
            pltpu.make_async_copy(tail, more[0].at[r], sems.at[2]).start()
        return carry

    lax.fori_loop(0, n_rows, fill, 0)
    body = own.at[:, pl.ds(first, count * rows)]
    for sem in range(2):
        pltpu.make_async_copy(body, body, sems.at[sem]).wait()
    out = pltpu.make_async_copy(buf, outs[0], sems.at[3])
    out.start()
    if extra:
        pltpu.make_async_copy(more[0], more[0], sems.at[2]).wait()
        tails = pltpu.make_async_copy(more[0], outs[1], sems.at[4])
        tails.start()
        tails.wait()
    out.wait()


def unpack(own, other, place, count, shape, first=0, beside=False, extra=0):
    n_rows = own.shape[0]
    rows, cols = shape
    many, wide = (1, count) if beside else (count, 1)
    whole = jax.ShapeDtypeStruct((many, n_rows * rows, 2 * wide * cols), BF)
    tails = jax.ShapeDtypeStruct((n_rows, extra, cols), BF)
    shapes = [whole] + [tails] * bool(extra)
    got = pl.pallas_call(
        functools.partial(
            unpack_kernel, count=count, shape=shape, first=first, beside=beside, extra=extra
        ),
        in_specs=[pl.BlockSpec(memory_space=pltpu.SMEM)] + [pl.BlockSpec(memory_space=pl.ANY)] * 2,
        out_specs=[pl.BlockSpec(memory_space=pl.ANY)] * len(shapes),
        out_shape=shapes,
        scratch_shapes=[pltpu.VMEM(x.shape, BF) for x in shapes] + [pltpu.SemaphoreType.DMA((5,))],
        compiler_params=pltpu.CompilerParams(vmem_limit_bytes=32 * 1024 * 1024),
        cost_estimate=pl.CostEstimate(
            flops=0, bytes_accessed=4 * whole.size * 2, transcendentals=0
        ),
        name="unpack",
    )(place, own, other)
    return got if extra else got[0]


def split_cols(array, pieces):
    width = array.shape[1] // pieces
    return jnp.concatenate([array[:, i * width : (i + 1) * width] for i in range(pieces)], axis=0)


def join_kernel(attn_in, attn_out, small, ff_in, ff_out, side_a, side_b, *, rb, cb):
    at = 0
    for array in (attn_in, attn_out):
        for k in range(array.shape[0]):
            side_a[0, at : at + rb] = array[k]
            at += rb
    side_a[0, at:] = small[...]
    for k in range(4):
        side_b[0, k * rb : (k + 1) * rb] = ff_in[:, k * cb : (k + 1) * cb]
    side_b[0, 4 * rb :] = ff_out[...]


def join(attn_in, attn_out, small, ff_in, ff_out):
    rb, cb = attn_in.shape[1:]
    if rb % 16 or cb % 128:
        side_a = [attn_in.reshape(-1, cb), attn_out.reshape(-1, cb), small]
        side_b = [split_cols(ff_in, 4), ff_out]
        return tuple(jnp.concatenate(side, axis=0)[None] for side in (side_a, side_b))
    return pl.pallas_call(
        functools.partial(join_kernel, rb=rb, cb=cb),
        out_shape=(
            jax.ShapeDtypeStruct((1, 8 * rb + small.shape[0], cb), BF),
            jax.ShapeDtypeStruct((1, 8 * rb, cb), BF),
        ),
        name="join",
    )(attn_in, attn_out, small, ff_in, ff_out)


def pack_kernel(place, *refs, mats, rows, extra, waits):
    n_ops = 1 + max(max(mat[0]) for mat in mats)
    ops, refs = refs[:n_ops], refs[n_ops:]
    small, refs = refs[: bool(extra)], refs[bool(extra) + waits :]
    keep, send, *bufs, sems = refs
    n_rows, col = keep.shape[0], place[keep.shape[0]]
    loads = {}
    for k, (at, _, _) in enumerate(mats):
        if len(at) == 1:
            loads[k] = pltpu.make_async_copy(ops[at[0]], bufs[k].at[0], sems.at[2 + k])
            loads[k].start()
    for k, (at, _, _) in enumerate(mats):
        if len(at) == 2:
            left, right = ops[at[0]], ops[at[1]]
            _, tall, wide = bufs[k].shape
            tile = min(tall, wide)
            for i in range(0, tall, tile):
                for j in range(0, wide, tile):
                    got = mm_tn(left[:, i : i + tile], right[:, j : j + tile])
                    bufs[k][0, i : i + tile, j : j + tile] = got.astype(BF)
    for load in loads.values():
        load.wait()

    def spread(r, carry):
        j = place[r]
        for dst, c, sem in ((keep, col, 0), (send, 1 - col, 1)):
            first = 0
            for buf, (_, shape, beside) in zip(bufs, mats):
                for k in range(beside):
                    part = dst.at[j, pl.ds(first, shape[0])]
                    tile = tile_of(buf, 0, r, c * beside + k, shape)
                    pltpu.make_async_copy(tile, part, sems.at[sem]).start()
                    first += shape[0]
            if extra:
                tail = dst.at[j, pl.ds(first, extra)]
                pltpu.make_async_copy(small[0].at[r], tail, sems.at[sem]).start()
        return carry

    lax.fori_loop(0, n_rows, spread, 0)
    for dst, sem in ((keep, 0), (send, 1)):
        pltpu.make_async_copy(dst, dst, sems.at[sem]).wait()


def pack(mats, place, small=None, after=()):
    ops, parts, specs, bufs, flops, total = [], [], [], [], 0, 0
    for mat, shape, beside in mats:
        mat = mat if isinstance(mat, tuple) else (mat,)
        parts.append((tuple(range(len(ops), len(ops) + len(mat))), shape, beside))
        ops += mat
        specs += [pl.BlockSpec(memory_space=pltpu.VMEM if len(mat) == 2 else pl.ANY)] * len(mat)
        whole = (mat[0].shape[1], mat[1].shape[1]) if len(mat) == 2 else mat[0].shape
        bufs.append(pltpu.VMEM((1,) + tuple(whole), BF))
        flops += 2 * mat[0].shape[0] * whole[0] * whole[1] if len(mat) == 2 else 0
        total += beside * shape[0]
        n_rows = whole[0] // shape[0]
    extra = 0 if small is None else small.shape[1]
    block = jax.ShapeDtypeStruct((n_rows, total + extra, shape[1]), BF)
    if extra:
        ops.append(small)
        specs.append(pl.BlockSpec(memory_space=pltpu.VMEM))
    return pl.pallas_call(
        functools.partial(
            pack_kernel, mats=tuple(parts), rows=total, extra=extra, waits=len(after)
        ),
        in_specs=[pl.BlockSpec(memory_space=pltpu.SMEM)] + specs + [WAIT] * len(after),
        out_specs=[pl.BlockSpec(memory_space=pl.ANY)] * 2,
        out_shape=[block, block],
        scratch_shapes=bufs + [pltpu.SemaphoreType.DMA((2 + len(mats),))],
        compiler_params=pltpu.CompilerParams(vmem_limit_bytes=48 * 1024 * 1024),
        cost_estimate=pl.CostEstimate(
            flops=flops, bytes_accessed=8 * block.size, transcendentals=0
        ),
        name="pack",
    )(place, *ops, *after)


def unpack_any(blocks, order, n_rows, n_cols, rb):
    cols = blocks.shape[2]
    got = by_device(blocks, order).reshape(n_rows, n_cols, -1, cols)
    return got[:, :, : 8 * rb].reshape(n_rows, n_cols, 8, rb, cols), got[:, 0, 8 * rb :]


def pack_any(mats, order, small, n_rows, n_cols):
    got = []
    for mat, (rows, cols), beside in mats:
        mat = mm_tn(*mat).astype(BF) if isinstance(mat, tuple) else mat
        mat = mat.reshape(n_rows, rows, n_cols, beside, cols).transpose(0, 2, 3, 1, 4)
        got.append(mat.reshape(n_rows, n_cols, beside * rows, cols))
    if small is not None:
        got.append(jnp.broadcast_to(small[:, None], (n_rows, n_cols) + small.shape[1:]))
    got = jnp.concatenate(got, axis=2)
    got = by_stage(got.reshape((-1,) + got.shape[2:]), order)
    half = got.shape[0] // 2
    return got[:half], got[half:]


def plan_requests(ret_rows, shard_rows, peers, slots):
    flat = ret_rows.reshape(-1)
    count = flat.shape[0]
    owner = flat // shard_rows
    local_row = flat - owner * shard_rows
    mine = owner[:, None] == jnp.arange(peers, dtype=jnp.int32)[None, :]
    run = 256
    runs = count // run
    ones = mine.astype(BF).reshape(runs, run, peers)
    lower = jnp.tril(jnp.ones((run, run), BF))
    within = jnp.einsum("ij,bjo->bio", lower, ones, preferred_element_type=F32)
    totals = within[:, -1, :]
    before = jnp.cumsum(totals, axis=0) - totals
    upto = (within + before[:, None, :]).reshape(count, peers)
    rank = jnp.sum(jnp.where(mine, upto, 0.0), axis=1).astype(jnp.int32) - 1
    place = owner * slots + rank
    row_code = local_row + 1
    entry_code = jnp.arange(count, dtype=jnp.int32)
    digits = jnp.stack([row_code // 64, row_code % 64, entry_code // 64, entry_code % 64])
    left = jnp.where(mine.T[None], digits[:, None, :], 0).astype(BF)
    at_rank = (rank[:, None] == jnp.arange(slots, dtype=jnp.int32)[None, :]).astype(BF)
    codes = mm(left.reshape(4 * peers, count), at_rank).astype(jnp.int32).reshape(4, peers, slots)
    return place, codes[0] * 64 + codes[1], codes[2] * 64 + codes[3]


def own_rows(tokens, ret, heads):
    shape = (heads * tokens, tokens * ret)
    row_tok = lax.broadcasted_iota(jnp.int32, shape, 0) % tokens
    col_tok = lax.broadcasted_iota(jnp.int32, shape, 1) // ret
    return row_tok == col_tok


def cross_fwd_kernel(qk, fetched, mix, probs, *, ret):
    heads, tokens, dim = qk.shape
    own = own_rows(tokens, ret, heads)
    query = qk[...].reshape(heads * tokens, dim)
    rows = fetched[...]
    scores = jnp.where(own, mm_nt(query, rows) * 0.125, -1e30)
    expo = jnp.exp(scores - jnp.max(scores, axis=-1, keepdims=True))
    prob = expo / jnp.sum(expo, axis=-1, keepdims=True)
    probs[0] = prob
    mix[...] = mm(prob.astype(BF), rows).astype(BF).reshape(heads, tokens, dim)


def cross_bwd_kernel(qk, gmix, fetched, probs, grad_rows, grad_s, *, ret):
    heads, tokens, dim = qk.shape
    query = qk[...].reshape(heads * tokens, dim)
    grad_mix = gmix[...].reshape(heads * tokens, dim)
    prob = probs[0]
    grad_p = mm_nt(grad_mix, fetched[...])
    g_s = (prob * (grad_p - jnp.sum(prob * grad_p, axis=-1, keepdims=True))).astype(BF)
    grad_s[0] = g_s
    grad_rows[...] = (
        mm_tn(prob.astype(BF), grad_mix) + mm_tn(g_s, query) * 0.125
    ).astype(BF)


def cross_back_q_kernel(grad_s, fetched, grad_qk):
    heads, tokens, dim = grad_qk.shape
    got = mm(grad_s[0], fetched[...]) * 0.125
    grad_qk[...] = got.astype(BF).reshape(heads, tokens, dim)


def cross_calls(tok_count, ret, dim):
    tb = 16
    blocks = tok_count // tb
    by_head = pl.BlockSpec((H, tb, dim), lambda g: (0, g, 0))
    rows = pl.BlockSpec((tb * ret, dim), lambda g: (g, 0))
    square = pl.BlockSpec((1, H * tb, tb * ret), lambda g: (g, 0, 0))
    heads_shape = jax.ShapeDtypeStruct((H, tok_count, dim), BF)
    square_f32 = jax.ShapeDtypeStruct((blocks, H * tb, tb * ret), F32)
    square_bf = jax.ShapeDtypeStruct((blocks, H * tb, tb * ret), BF)
    params = pltpu.CompilerParams(vmem_limit_bytes=VMEM_LIMIT)
    fwd = pl.pallas_call(
        functools.partial(cross_fwd_kernel, ret=ret),
        grid=(blocks,),
        in_specs=[by_head, rows],
        out_specs=[by_head, square],
        out_shape=(heads_shape, square_f32),
        compiler_params=params,
        name="cross_fwd",
    )
    bwd = pl.pallas_call(
        functools.partial(cross_bwd_kernel, ret=ret),
        grid=(blocks,),
        in_specs=[by_head, by_head, rows, square],
        out_specs=[rows, square],
        out_shape=(jax.ShapeDtypeStruct((tok_count * ret, dim), BF), square_bf),
        compiler_params=params,
        name="cross_bwd",
    )
    back_q = pl.pallas_call(
        cross_back_q_kernel,
        grid=(blocks,),
        in_specs=[square, rows],
        out_specs=by_head,
        out_shape=heads_shape,
        compiler_params=params,
        name="cross_back_q",
    )
    return fwd, bwd, back_q


GROUP = 8
LANES = 128
PITCH = LANES // GROUP


def plan_kernel(rows, wanted, token, at_rank, owner, *, shard_rows):
    peers, slots = wanted.shape
    ret, toks = rows.shape
    shape = (toks, toks)
    upper = (
        lax.broadcasted_iota(jnp.int32, shape, 0) <= lax.broadcasted_iota(jnp.int32, shape, 1)
    ).astype(BF)
    peer = lax.broadcasted_iota(jnp.int32, (peers, toks), 0)
    tok_code = (lax.broadcasted_iota(jnp.int32, (peers, toks), 1) + 1).astype(F32)
    k_rows = lax.broadcasted_iota(jnp.int32, (at_rank.shape[0], toks), 0)
    shift = shard_rows.bit_length() - 1
    before = jnp.zeros((peers, 1), F32)
    codes = jnp.zeros((3 * peers, at_rank.shape[0]), F32)
    for r in range(ret):
        row = rows[r : r + 1, :]
        own = lax.shift_right_logical(row, shift)
        code = lax.bitwise_and(row, shard_rows - 1) + 1
        mine = own == peer
        upto = mm(mine.astype(BF), upper) + before
        before = upto[:, toks - 1 :]
        rank = jnp.sum(jnp.where(mine, upto, 0.0), axis=0, keepdims=True).astype(jnp.int32) - 1
        at = (k_rows == rank).astype(BF)
        at_rank[:, r * toks : (r + 1) * toks] = at
        owner[r : r + 1, :] = own
        high = lax.shift_right_logical(code, 6).astype(F32)
        low = lax.bitwise_and(code, 63).astype(F32)
        left = jnp.concatenate(
            [
                jnp.where(mine, high, 0.0).astype(BF),
                jnp.where(mine, low, 0.0).astype(BF),
                jnp.where(mine, tok_code, 0.0).astype(BF),
            ],
            axis=0,
        )
        codes = codes + mm_nt(left, at)
    codes = codes[:, :slots].astype(jnp.int32)
    wanted[...] = codes[:peers] * 64 + codes[peers : 2 * peers]
    token[...] = codes[2 * peers :]


def plan_slots(rows, shard_rows, peers, slots):
    ret, toks = rows.shape
    tall = -(-slots // LANES) * LANES
    return pl.pallas_call(
        functools.partial(plan_kernel, shard_rows=shard_rows),
        out_shape=(
            jax.ShapeDtypeStruct((peers, slots), jnp.int32),
            jax.ShapeDtypeStruct((peers, slots), jnp.int32),
            jax.ShapeDtypeStruct((tall, ret * toks), BF),
            jax.ShapeDtypeStruct((ret, toks), jnp.int32),
        ),
        name="plan",
    )(rows)


def head_sum(dim):
    shape = (dim, LANES)
    head = lax.broadcasted_iota(jnp.int32, shape, 0) // HD
    return (head == lax.broadcasted_iota(jnp.int32, shape, 1)).astype(BF)


def head_spread(dim):
    shape = (LANES, dim)
    head = lax.broadcasted_iota(jnp.int32, shape, 1) // HD
    return (head == lax.broadcasted_iota(jnp.int32, shape, 0)).astype(BF)


def to_lanes(by_peer, k):
    total = by_peer[:k]
    for q in range(1, GROUP):
        total = total + pltpu.roll(by_peer[q * k : (q + 1) * k], PITCH * q, 1)
    return total


def from_lanes(lanes):
    parts = [lanes] + [pltpu.roll(lanes, LANES - PITCH * q, 1) for q in range(1, GROUP)]
    return jnp.concatenate([part.astype(BF) for part in parts], axis=0)


def to_entries(slot_vals, at_rank, owner):
    k, wide = slot_vals.shape
    tall, toks = at_rank.shape[0], owner.shape[1]
    peers = wide // PITCH
    full = jnp.concatenate([slot_vals, jnp.zeros((tall - k, wide), F32)], axis=0).T
    high = full.astype(BF)
    low = (full - high.astype(F32)).astype(BF)
    peer = lax.broadcasted_iota(jnp.int32, (wide, toks), 0) // PITCH
    out = []
    for r in range(owner.shape[0]):
        at = at_rank[:, r * toks : (r + 1) * toks]
        got = mm(high, at) + mm(low, at)
        got = jnp.where(peer == owner[r : r + 1, :], got, 0.0)
        out.append(jnp.sum(got.reshape(peers, PITCH, toks), axis=0))
    return out


def to_slots(entry_vals, at_rank, owner, peers, slots):
    toks = owner.shape[1]
    wide = peers * PITCH
    peer = lax.broadcasted_iota(jnp.int32, (wide, toks), 0) // PITCH
    total = jnp.zeros((at_rank.shape[0], wide), F32)
    for r, vals in enumerate(entry_vals):
        tiled = jnp.concatenate([vals] * peers, axis=0)
        mine = jnp.where(peer == owner[r : r + 1, :], tiled, 0.0).astype(BF)
        total = total + mm_nt(at_rank[:, r * toks : (r + 1) * toks], mine)
    return total[:slots]


def rows_in_kernel(arrived, query, w_k, w_v, keys, vals, scores):
    group, k, dim = arrived.shape
    rows = arrived[...].reshape(group * k, dim)
    key = mm(rows, w_k[...])
    keys[...] = key.astype(BF).reshape(group, k, dim)
    prod = (key * query[...].reshape(group * k, dim).astype(F32)).astype(BF)
    scores[...] = to_lanes(mm(prod, head_sum(dim)), k) * 0.125
    vals[...] = mm(rows, w_v[...]).astype(BF).reshape(group, k, dim)


def attend_kernel(*refs, chunks):
    scores, vals, token_t = refs[:chunks], refs[chunks : 2 * chunks], refs[2 * chunks : 3 * chunks]
    at_rank, owner, bias, prob_tok, prob_slot, mixed, total = refs[3 * chunks :]
    step, steps = pl.program_id(0), pl.num_programs(0)
    k, dim = vals[0].shape[1:]

    @pl.when(step == 0)
    def _():
        entry = to_entries(
            jnp.concatenate([part[...] for part in scores], axis=0), at_rank, owner
        )
        top = functools.reduce(jnp.maximum, entry)
        expo = [jnp.exp(part - top) for part in entry]
        norm = functools.reduce(jnp.add, expo)
        probs = [part / norm for part in expo]
        for r, part in enumerate(probs):
            prob_tok[r * PITCH : (r + 1) * PITCH, :] = part
        peers = scores[0].shape[1] // PITCH
        prob_slot[...] = to_slots(probs, at_rank, owner, peers, chunks * k)
        total[...] = jnp.zeros_like(total)

    spread = head_spread(dim)
    lanes = pl.ds(pl.multiple_of(step * LANES, LANES), LANES)
    acc = total[...]
    for c in range(chunks):
        prob = mm(from_lanes(prob_slot[c * k : (c + 1) * k, lanes]), spread)
        prod = (prob * vals[c][...].reshape(-1, dim).astype(F32)).astype(BF)
        acc = acc + mm(token_t[c][...], prod)
    total[...] = acc

    @pl.when(step == steps - 1)
    def _():
        mixed[...] = (total[...] + bias[...]).astype(BF)


def attend_back_kernel(*refs, chunks):
    vals, token = refs[:chunks], refs[chunks : 2 * chunks]
    grad, prob_tok, at_rank, owner = refs[2 * chunks : 2 * chunks + 4]
    grads, (grad_slot, slot_p) = refs[2 * chunks + 4 : -2], refs[-2:]
    step, steps = pl.program_id(0), pl.num_programs(0)
    k, dim = vals[0].shape[1:]
    lanes = pl.ds(pl.multiple_of(step * LANES, LANES), LANES)
    add_up = head_sum(dim)
    for c in range(chunks):
        wide = mm(token[c][...], grad[...])
        grads[c][...] = wide.astype(BF).reshape(vals[c].shape)
        prod = (wide * vals[c][...].reshape(-1, dim).astype(F32)).astype(BF)
        slot_p[c * k : (c + 1) * k, lanes] = to_lanes(mm(prod, add_up), k)

    @pl.when(step == steps - 1)
    def _():
        entry = to_entries(slot_p[...], at_rank, owner)
        probs = [prob_tok[r * PITCH : (r + 1) * PITCH, :] for r in range(len(entry))]
        dots = functools.reduce(jnp.add, [p * g for p, g in zip(probs, entry)])
        scores = [(p * (g - dots)).astype(BF).astype(F32) for p, g in zip(probs, entry)]
        peers = slot_p.shape[1] // PITCH
        grad_slot[...] = to_slots(scores, at_rank, owner, peers, chunks * k)


def rows_out_kernel(prob_slot, grad_slot, grad, query, w_k, w_v, *refs):
    out, by_prob, by_score = refs[-3:]
    group, k, dim = grad.shape
    spread = head_spread(dim)
    prob = mm(from_lanes(prob_slot[...]), spread)
    mix = (prob * grad[...].reshape(-1, dim).astype(F32)).astype(BF)
    score = mm(from_lanes(grad_slot[...]), spread) * 0.125
    ask = (score * query[...].reshape(-1, dim).astype(F32)).astype(BF)
    out[...] = (mm_nt(mix, w_v[...]) + mm_nt(ask, w_k[...])).astype(BF).reshape(grad.shape)
    by_prob[...] = mix.reshape(grad.shape)
    by_score[...] = ask.reshape(grad.shape)


def query_back_kernel(*refs, chunks):
    keys, token_t = refs[:chunks], refs[chunks : 2 * chunks]
    grad_slot, (out, total) = refs[2 * chunks], refs[-2:]
    step, steps = pl.program_id(0), pl.num_programs(0)
    k, dim = keys[0].shape[1:]

    @pl.when(step == 0)
    def _():
        total[...] = jnp.zeros_like(total)

    spread = head_spread(dim)
    lanes = pl.ds(pl.multiple_of(step * LANES, LANES), LANES)
    acc = total[...]
    for c in range(chunks):
        score = mm(from_lanes(grad_slot[c * k : (c + 1) * k, lanes]), spread) * 0.125
        prod = (score * keys[c][...].reshape(-1, dim).astype(F32)).astype(BF)
        acc = acc + mm(token_t[c][...], prod)
    total[...] = acc

    @pl.when(step == steps - 1)
    def _():
        out[...] = total[...].astype(BF)


def vector_sums_kernel(*refs, plain, pairs):
    ops, (wide, out, out_wide) = refs[: plain + 2 * pairs], refs[plain + 2 * pairs :]
    rows = [ops[i][...].astype(F32) for i in range(plain)]
    lefts = [ops[plain + 2 * i][...].astype(F32) for i in range(pairs)]
    rows += [lefts[i] * ops[plain + 2 * i + 1][...] for i in range(pairs)]
    rows += lefts
    sums = [jnp.sum(row, axis=0, keepdims=True) for row in rows]
    sums.append(jnp.zeros((out.shape[0] - len(sums), out.shape[1]), F32))
    out[...] = jnp.concatenate(sums, axis=0)
    out_wide[...] = jnp.sum(wide[...].astype(F32), axis=0, keepdims=True)


def vector_sums(plain, pairs, wide):
    ops = list(plain) + [x for pair in pairs for x in pair] + [wide]
    dim = plain[0].shape[1]
    return pl.pallas_call(
        functools.partial(vector_sums_kernel, plain=len(plain), pairs=len(pairs)),
        out_shape=(
            jax.ShapeDtypeStruct((16, dim), F32),
            jax.ShapeDtypeStruct((1, wide.shape[1]), F32),
        ),
        compiler_params=pltpu.CompilerParams(vmem_limit_bytes=24 * 1024 * 1024),
        name="vector_sums",
    )(*ops)


class SlotAttention:
    def __init__(self, ret_rows, shard_rows, peers, slots, dim, parts):
        self.toks, self.ret = ret_rows.shape
        chunks = parts
        self.peers, self.slots, self.dim, self.chunks = peers, slots, dim, chunks
        self.k = slots // chunks
        self.sent = []
        self.wanted, token, self.at_rank, self.owner = plan_slots(
            ret_rows.T, shard_rows, peers, slots
        )
        self.codes = [self.part(token, c).reshape(-1) for c in range(chunks)]
        self.heads = jax.ShapeDtypeStruct((slots, peers * PITCH), F32)

    def part(self, array, c):
        return array[:, c * self.k : (c + 1) * self.k]

    def specs(self):
        k, dim, toks = self.k, self.dim, self.toks
        rows = pl.BlockSpec((GROUP, k, dim), lambda g: (g, 0, 0))
        whole = lambda *shape: pl.BlockSpec(shape, lambda g: (0,) * len(shape))
        token = pl.BlockSpec((GROUP * k, toks), lambda g: (g, 0))
        token_t = pl.BlockSpec((toks, GROUP * k), lambda g: (0, g))
        lanes = lambda c: pl.BlockSpec((k, LANES), lambda g: (c, g))
        return rows, whole, token, token_t, lanes

    def call(self, kernel, name, in_specs, out_specs, out_shape, scratch=(), mib=28):
        return pl.pallas_call(
            kernel,
            grid=(self.peers // GROUP,),
            in_specs=in_specs,
            out_specs=out_specs,
            out_shape=out_shape,
            scratch_shapes=list(scratch),
            compiler_params=pltpu.CompilerParams(vmem_limit_bytes=mib * 1024 * 1024),
            name=name,
        )

    def prepare(self, cross_q):
        toks = self.toks
        ids = jnp.arange(1, toks + 1, dtype=jnp.int32)
        self.token = [(code[:, None] == ids[None, :]).astype(BF) for code in self.codes]
        self.token_t = [(ids[:, None] == code[None, :]).astype(BF) for code in self.codes]
        shape = (self.peers, self.k, self.dim)
        self.query = [mm(token, cross_q).astype(BF).reshape(shape) for token in self.token]

    def forward(self, arrived, w_k, w_v, bias):
        rows, whole, token, token_t, lanes = self.specs()
        shape = jax.ShapeDtypeStruct((self.peers, self.k, self.dim), BF)
        dim, toks, chunks = self.dim, self.toks, self.chunks
        self.arrived, self.w_k, self.w_v = arrived, w_k, w_v
        wide = self.peers * PITCH
        first = self.call(
            rows_in_kernel,
            "rows_in",
            [rows, rows, whole(dim, dim), whole(dim, dim)],
            [rows, rows, lanes(0)],
            (shape, shape, jax.ShapeDtypeStruct((self.k, wide), F32)),
        )
        got = [first(part, query, w_k, w_v) for part, query in zip(arrived, self.query)]
        self.keys, self.vals, scores = zip(*got)
        self.prob_tok, self.prob_slot, mixed = self.call(
            functools.partial(attend_kernel, chunks=chunks),
            "attend",
            [whole(self.k, wide)] * chunks
            + [rows] * chunks
            + [token_t] * chunks
            + [whole(*self.at_rank.shape), whole(*self.owner.shape), whole(1, dim)],
            [whole(self.ret * PITCH, toks), whole(self.slots, wide), whole(toks, dim)],
            (
                jax.ShapeDtypeStruct((self.ret * PITCH, toks), F32),
                self.heads,
                jax.ShapeDtypeStruct((toks, dim), BF),
            ),
            [pltpu.VMEM((toks, dim), F32)],
        )(*scores, *self.vals, *self.token_t, self.at_rank, self.owner, bias.reshape(1, dim))
        return mixed

    def backward(self, grad):
        rows, whole, token, token_t, lanes = self.specs()
        shape = jax.ShapeDtypeStruct((self.peers, self.k, self.dim), BF)
        dim, toks, chunks = self.dim, self.toks, self.chunks
        wide = self.peers * PITCH
        *grads, self.grad_slot = self.call(
            functools.partial(attend_back_kernel, chunks=chunks),
            "attend_back",
            [rows] * chunks
            + [token] * chunks
            + [whole(toks, dim), whole(self.ret * PITCH, toks)]
            + [whole(*self.at_rank.shape), whole(*self.owner.shape)],
            [rows] * chunks + [whole(self.slots, wide)],
            [shape] * chunks + [self.heads],
            [pltpu.VMEM((self.slots, wide), F32)],
        )(*self.vals, *self.token, grad, self.prob_tok, self.at_rank, self.owner)
        self.grads = grads

    def send(self, c, after=()):
        rows, whole, _, _, lanes = self.specs()
        shape = jax.ShapeDtypeStruct((self.peers, self.k, self.dim), BF)
        dim = self.dim
        got = self.call(
            rows_out_kernel,
            "rows_out",
            [lanes(c), lanes(c), rows, rows, whole(dim, dim), whole(dim, dim)]
            + [WAIT] * len(after),
            [rows, rows, rows],
            (shape, shape, shape),
        )(
            self.prob_slot,
            self.grad_slot,
            self.grads[c],
            self.query[c],
            self.w_k,
            self.w_v,
            *after,
        )
        self.sent.append(got)
        return got[0]

    def finish(self):
        rows, whole, token, token_t, lanes = self.specs()
        dim, toks, chunks = self.dim, self.toks, self.chunks
        grad_q = self.call(
            functools.partial(query_back_kernel, chunks=chunks),
            "query_back",
            [rows] * chunks
            + [token_t] * chunks
            + [whole(self.slots, self.peers * PITCH), WAIT],
            whole(toks, dim),
            jax.ShapeDtypeStruct((toks, dim), BF),
            [pltpu.VMEM((toks, dim), F32)],
        )(*self.keys, *self.token_t, self.grad_slot, self.sent[0][0])

        def product(parts):
            flat = lambda x: x.reshape(-1, dim)
            both = [mm_tn(flat(a), flat(b)) for a, b in zip(self.arrived, parts)]
            return functools.reduce(jnp.add, both).astype(BF)

        _, by_prob, by_score = zip(*self.sent)
        return grad_q, product(by_score), product(by_prob)


class GatheredAttention:
    def __init__(self, ret_rows, shard_rows, peers, slots, dim, parts):
        self.toks, self.ret = ret_rows.shape
        self.dim, self.slots = dim, slots
        self.place, self.wanted, self.entry = plan_requests(ret_rows, shard_rows, peers, slots)
        self.fwd, self.bwd, self.back_q = cross_calls(self.toks, self.ret, dim)

    def part(self, array, c):
        return array

    def prepare(self, cross_q):
        self.cross_q = cross_q

    def forward(self, arrived, w_k, w_v, bias):
        toks, dim = self.toks, self.dim
        self.key_heads, self.val_heads = w_k.reshape(dim, H, HD), w_v.reshape(dim, H, HD)
        query = self.cross_q.reshape(toks, H, HD)
        self.query_keys = jnp.einsum(
            "the,dhe->htd", query, self.key_heads, preferred_element_type=F32
        ).astype(BF)
        self.fetched = arrived[0].reshape(-1, dim)[self.place]
        self.state_mix, self.cross_p = self.fwd(self.query_keys, self.fetched)
        mixed = jnp.einsum(
            "htd,dhe->the", self.state_mix, self.val_heads, preferred_element_type=F32
        )
        return (mixed.reshape(toks, dim) + bias).astype(BF)

    def backward(self, grad):
        self.grad = grad.reshape(self.toks, H, HD)
        grad_mix = jnp.einsum(
            "the,dhe->htd", self.grad, self.val_heads, preferred_element_type=F32
        ).astype(BF)
        self.rows, self.grad_s = self.bwd(self.query_keys, grad_mix, self.fetched, self.cross_p)

    def send(self, c, after=()):
        return self.rows[self.entry]

    def finish(self):
        toks, dim = self.toks, self.dim
        grad_qk = self.back_q(self.grad_s, self.fetched)
        grad_q = jnp.einsum("htd,dhe->the", grad_qk, self.key_heads, preferred_element_type=F32)

        def product(left, right):
            got = jnp.einsum("htd,the->dhe", left, right, preferred_element_type=F32)
            return got.reshape(dim, dim).astype(BF)

        grad_k = product(grad_qk, self.cross_q.reshape(toks, H, HD))
        return grad_q.reshape(toks, dim).astype(BF), grad_k, product(self.state_mix, self.grad)


def store_sum_kernel(asked, returned, *refs, block, added):
    first = pl.program_id(0) * block + 1
    shape = (block, asked.shape[1])
    hit = lax.broadcasted_iota(jnp.int32, shape, 0) + first == asked[...]
    total = mm(hit.astype(BF), returned[...])
    refs[-1][...] = total + refs[0][...] if added else total


def store_sum(asked, returned, shard_rows, so_far, after=()):
    count, dim = returned.shape
    block = 256
    out = pl.BlockSpec((block, dim), lambda g: (g, 0))
    before = [] if so_far is None else [so_far]
    return pl.pallas_call(
        functools.partial(store_sum_kernel, block=block, added=so_far is not None),
        grid=(shard_rows // block,),
        in_specs=[
            pl.BlockSpec((1, count), lambda g: (0, 0)),
            pl.BlockSpec((count, dim), lambda g: (0, 0)),
        ]
        + [out] * len(before)
        + [WAIT] * len(after),
        out_specs=out,
        out_shape=jax.ShapeDtypeStruct((shard_rows, dim), F32),
        input_output_aliases={2: 0} if before else {},
        compiler_params=pltpu.CompilerParams(vmem_limit_bytes=VMEM_LIMIT),
        name="store_sum",
    )(asked.reshape(1, count), returned, *before, *after)


def all_to_all(array):
    return lax.all_to_all(array, RANKS, split_axis=0, concat_axis=0, tiled=True)


def on_device(
    tokens,
    seg_ids,
    live_mask,
    ret_rows,
    enc_store,
    attn_in,
    attn_out,
    ff_in,
    ff_out,
    biases,
    ln_gain,
    ln_shift,
    ff_bias,
    cotangent,
):
    n_rows = lax.axis_size("row")
    n_cols = lax.axis_size("col")
    peers = n_rows * n_cols
    tok_count, dim = tokens.shape
    shard_rows = enc_store.shape[0]
    ret = ret_rows.shape[1]
    slots = 3 * ret_rows.size // (2 * peers)
    rb, cb = attn_in.shape[1], attn_in.shape[2]
    order_a, order_b = bit_orders(n_rows, n_cols)
    n_row_bits = n_rows.bit_length() - 1
    n_far = n_row_bits - 2
    by_rows = n_cols == 2 and rb % 16 == 0 and cb % 128 == 0
    if by_rows:
        col = lax.axis_index("col").astype(jnp.int32)[None]
        place_a = jnp.concatenate([block_of_row(order_a, n_rows), col])
        place_b = jnp.concatenate([block_of_row(order_b, n_rows), col])

    parts = 2
    in_slots = (
        slots % (16 * parts) == 0
        and peers % GROUP == 0
        and tok_count % LANES == 0
        and tok_count <= 256
        and shard_rows & (shard_rows - 1) == 0
        and H <= PITCH
    )
    parts = parts if in_slots else 1
    attention = (SlotAttention if in_slots else GatheredAttention)(
        ret_rows, shard_rows, peers, slots, dim, parts
    )
    def vector_rows(parts):
        parts = [jnp.pad(part, ((0, 0), (0, cb - part.shape[1]))) for part in parts]
        return jnp.pad(jnp.concatenate(parts, axis=0), ((0, 2), (0, 0)))

    small = vector_rows([biases, ln_gain, ln_shift, ff_bias.reshape(1, -1)])
    cut = 8 * rb + small.shape[0]
    side_a, side_b = join(attn_in, attn_out, small, ff_in, ff_out)
    side_a, side_b = gather_bits(side_a, order_a[:n_far]), gather_bits(side_b, order_b[:n_far])
    asked = all_to_all(attention.wanted)

    answers = [
        enc_store[jnp.maximum(attention.part(asked, c) - 1, 0)] for c in range(parts)
    ]
    if by_rows:
        answers[0] = hold(answers[0], [side_a, side_b])
    side_a = gather_bits(side_a, order_a[n_far : n_far + 1])
    side_b = gather_bits(side_b, order_b[n_far : n_far + 1])
    arrived = [all_to_all(answers[0])]
    for c in range(1, parts):
        if by_rows:
            side_a = hold(side_a, [answers[c]])
            side_b = hold(side_b, [answers[c]])
            answers[c] = hold(answers[c], arrived[-1:])
        arrived.append(all_to_all(answers[c]))
    if by_rows:
        side_a = gather_bits(side_a, order_a[n_far + 1 : n_row_bits])
        side_b = gather_bits(side_b, order_b[n_far + 1 : n_row_bits])
        other_a, other_b = swap_bit(side_a, "col", 1), swap_bit(side_b, "col", 1)
        tile = (rb, cb)
        mats, small_all = unpack(side_a, other_a, place_a, 8, tile, extra=small.shape[0])
        w_ff1 = unpack(side_b, other_b, place_b, 4, tile, beside=True)[0]
        w_ff2 = unpack(side_b, other_b, place_b, 1, (4 * rb, cb), first=4 * rb)[0]
    else:
        side_a = gather_bits(side_a, order_a[n_far + 1 :])
        side_b = gather_bits(side_b, order_b[n_far + 1 :])
        mats, small_all = unpack_any(side_a, order_a, n_rows, n_cols, rb)
        mats = mats.transpose(2, 0, 3, 1, 4).reshape(8, dim, dim)
        ff_blocks, _ = unpack_any(side_b, order_b, n_rows, n_cols, rb)
        w_ff1 = ff_blocks[:, :, :4].transpose(0, 3, 1, 2, 4).reshape(dim, 4 * dim)
        w_ff2 = ff_blocks[:, :, 4:].transpose(0, 2, 3, 1, 4).reshape(4 * dim, dim)
    w_q, w_k, w_v, w_cq, w_ck, w_cv, w_o, w_co = (mats[i] for i in range(8))
    small_all = small_all.astype(F32)
    vectors = small_all[:, :13, :rb].transpose(1, 0, 2).reshape(13, dim)
    bias_all, gain_all, shift_all = vectors[:7], vectors[7:10], vectors[10:]
    bias_ff = small_all[:, 13, : ff_bias.size].reshape(-1)

    def heads(array):
        return array.reshape(tok_count, H, HD)

    queries = heads((mm(tokens, w_q) + bias_all[0]).astype(BF))
    key_rows = heads(mm(tokens, w_k).astype(BF))
    values = heads((mm(tokens, w_v) + bias_all[1]).astype(BF))
    visible = visible_mask(seg_ids[0], live_mask[0])
    scores = jnp.einsum("qhd,khd->hqk", queries, key_rows, preferred_element_type=F32) * 0.125
    probs = jax.nn.softmax(jnp.where(visible[None], scores, -1e30), axis=-1)
    probs_low = probs.astype(BF)
    mixed = jnp.einsum("hqk,khd->qhd", probs_low, values, preferred_element_type=F32)
    mixed = mixed.reshape(tok_count, dim).astype(BF)
    branch = mm(mixed, w_o) + bias_all[2]
    first, first_norm, first_scale = norm_fwd(
        tokens.astype(F32) + branch, gain_all[0], shift_all[0]
    )
    first_low = first.astype(BF)
    cross_q = (mm(first_low, w_cq) + bias_all[3]).astype(BF)

    attention.prepare(cross_q)
    cross_low = attention.forward(arrived, w_ck, w_cv, bias_all[4])
    branch_two = mm(cross_low, w_co) + bias_all[5]
    second, second_norm, second_scale = norm_fwd(first + branch_two, gain_all[1], shift_all[1])
    second_low = second.astype(BF)

    hidden_act, hidden_slope = gelu_parts(mm(second_low, w_ff1) + bias_ff)
    hidden_low = hidden_act.astype(BF)
    branch_ffn = mm(hidden_low, w_ff2) + bias_all[6]
    final, final_norm, final_scale = norm_fwd(second + branch_ffn, gain_all[2], shift_all[2])
    output = final.astype(BF)
    cot = cotangent.astype(F32)
    grad_three = norm_back(cot, final_norm, final_scale, gain_all[2])
    grad_y = grad_three.astype(BF)
    grad_pre = (mm_nt(grad_y, w_ff2) * hidden_slope).astype(BF)
    grad_second = grad_three + mm_nt(grad_pre, w_ff1)
    grad_two = norm_back(grad_second, second_norm, second_scale, gain_all[1])
    grad_o2 = grad_two.astype(BF)
    grad_cmix = mm_nt(grad_o2, w_co).astype(BF)
    attention.backward(grad_cmix)
    send_back = [attention.send(0)]

    def packed(order, place, mats, small=None, after=()):
        if by_rows:
            return pack(mats, place, small, after)
        return pack_any(mats, order[::-1], small, n_rows, n_cols)

    tile = (rb, cb)
    near = len(order_a) - n_far
    back_a, back_b = order_a[::-1], order_b[::-1]
    at_a, at_b = (place_a, place_b) if by_rows else (None, None)
    send_back += [attention.send(c, send_back) for c in range(1, parts)]
    grad_cq, grad_wk, grad_wv = attention.finish()
    ff = [
        (order_a, at_a, [((second_low, grad_pre), tile, 4)]),
        (order_b, at_b, [((hidden_low, grad_y), (4 * rb, cb), 1)]),
    ]
    ff = [packed(*part, None, [grad_cq]) for part in ff]
    grad_first = grad_two + mm_nt(grad_cq, w_cq)
    grad_one = norm_back(grad_first, first_norm, first_scale, gain_all[0])
    grad_o = grad_one.astype(BF)
    grad_mix = heads(mm_nt(grad_o, w_o).astype(BF))
    grad_probs = jnp.einsum("qhd,khd->hqk", grad_mix, values, preferred_element_type=F32)
    grad_v = jnp.einsum("hqk,qhd->khd", probs_low, grad_mix, preferred_element_type=F32)
    grad_scores = (
        probs * (grad_probs - jnp.sum(probs * grad_probs, axis=-1, keepdims=True))
    ).astype(BF)
    grad_q = jnp.einsum("hqk,khd->qhd", grad_scores, key_rows, preferred_element_type=F32) * 0.125
    grad_k = jnp.einsum("hqk,qhd->khd", grad_scores, queries, preferred_element_type=F32) * 0.125
    grad_q, grad_k, grad_v = (
        part.reshape(tok_count, dim).astype(BF) for part in (grad_q, grad_k, grad_v)
    )
    grad_tokens = (
        grad_one + mm_nt(grad_q, w_q) + mm_nt(grad_k, w_k) + mm_nt(grad_v, w_v)
    )

    vectors, wide = vector_sums(
        [grad_q, grad_v, grad_o, grad_cq, grad_cmix, grad_o2, grad_y],
        [(grad_first, first_norm), (grad_second, second_norm), (cotangent, final_norm)],
        grad_pre,
    )
    vectors = vectors[:13].reshape(13, n_rows, rb).transpose(1, 0, 2)
    wide = wide.reshape(n_rows, 1, -1)
    grad_small = [
        jnp.pad(vectors, ((0, 0), (0, 0), (0, cb - rb))),
        jnp.pad(wide, ((0, 0), (0, 2), (0, cb - ff_bias.size))),
    ]
    grad_small = jnp.concatenate(grad_small, axis=1).astype(BF)
    attn_one = packed(
        order_a,
        at_a,
        [
            ((tokens, grad_q), tile, 1),
            ((tokens, grad_k), tile, 1),
            ((tokens, grad_v), tile, 1),
            ((first_low, grad_cq), tile, 1),
        ],
    )
    attn_two = packed(
        order_b,
        at_b,
        [
            (grad_wk, tile, 1),
            (grad_wv, tile, 1),
            ((mixed, grad_o), tile, 1),
            ((cross_low, grad_o2), tile, 1),
        ],
        grad_small,
    )
    if by_rows:
        send_back[1:] = [hold(part, [*attn_one, *attn_two]) for part in send_back[1:]]
    returned = [all_to_all(part) for part in send_back]

    def stored(c, so_far, after):
        rows = returned[c].reshape(-1, dim)
        return store_sum(attention.part(asked, c), rows, shard_rows, so_far, after)

    def join_pairs(one, two):
        return tuple(jnp.concatenate(both, axis=1) for both in zip(one, two))

    ff = [scatter_bits(*part, back[:near]) for part, back in zip(ff, (back_a, back_b))]
    ff = join_pairs(*ff)
    def behind(pair, array):
        return (hold(pair[0], [array]), pair[1]) if by_rows else pair

    attn = [
        scatter_bits(*part, back[: near - 2])
        for part, back in zip((attn_one, attn_two), (back_a, back_b))
    ]
    grad_store = None
    for c in range(parts - 1):
        grad_store = stored(c, grad_store, ())
        attn = [behind(pair, grad_store) for pair in attn]
    attn = [
        scatter_bits(*part, back[near - 2 : near]) for part, back in zip(attn, (back_a, back_b))
    ]
    grad_store = stored(parts - 1, grad_store, ())
    attn = behind(join_pairs(*attn), grad_store)
    total_a, total_b = (
        (keep + swap_bit(send, *order_a[0]))[0].astype(F32)
        for keep, send in (scatter_bits(*pair, back_a[near:-1]) for pair in (attn, ff))
    )

    sum_small = total_a[8 * rb :]
    return (
        output,
        grad_tokens,
        grad_store,
        total_a[: 6 * rb].reshape(6, rb, cb),
        total_a[6 * rb : 8 * rb].reshape(2, rb, cb),
        jnp.concatenate([total_b[k * rb : (k + 1) * rb] for k in range(4)], axis=1),
        total_b[4 * rb :],
        sum_small[:7, :rb],
        sum_small[7:10, :rb],
        sum_small[10:13, :rb],
        sum_small[13, : ff_bias.size],
    )


def solution(mesh):
    both = ("row", "col")
    return jax.shard_map(
        on_device,
        mesh=mesh,
        in_specs=(
            P(both, None),
            P(both, None),
            P(both, None),
            P(both, None),
            P(both, None),
            P(None, "row", "col"),
            P(None, "row", "col"),
            P("row", "col"),
            P("row", "col"),
            P(None, "row"),
            P(None, "row"),
            P(None, "row"),
            P("row"),
            P(both, None),
        ),
        out_specs=(
            P(both, None),
            P(both, None),
            P(both, None),
            P(None, "row", "col"),
            P(None, "row", "col"),
            P("row", "col"),
            P("row", "col"),
            P(None, "row"),
            P(None, "row"),
            P(None, "row"),
            P("row"),
        ),
        check_vma=False,
    )
```

time: 869 us -> 734 us (0.84)
  local copies, waits for them, and re-layouts: 175 us -> 128 us
  waiting for transfers between devices: 308 us -> 269 us
  blocking collectives: 25.2 us -> 0 us
  starting transfers between devices: 33.9 us -> 57.2 us
  Pallas kernels: 160 us -> 137 us
  other arithmetic: 66 us -> 54.2 us
  matrix products: 86.2 us -> 77.4 us
    ppermute x20 -> x26, waiting for transfers between devices: 308 us -> 223 us  [swap_bit(): return lax.ppermute(array, axis, pairs)]
    gather x5 -> x4, local copies, waits for them, and re-layouts: 84.7 us -> 28.5 us  [the longest x2 27.2 us: on_device(): enc_store[jnp.maximum(attention.part(asked, c) - 1, 0)]]
    unnamed x218 -> x317, local copies, waits for them, and re-layouts: 20.9 us -> 73.2 us
    all_to_all x2 -> x5, waiting for transfers between devices: 0.01 us -> 46.6 us  [all_to_all(): return lax.all_to_all(array, RANKS, split_axis=0, concat_axis=0, tiled=True)]
    all_to_all x1 -> x0, blocking collectives: 25.2 us -> none  [all_to_all(): return lax.all_to_all(array, RANKS, split_axis=0, concat_axis=0, tiled=True)]
    pallas_call x8 -> x27, Pallas kernels: 160 us -> 137 us  [the longest x2 29.4 us: store_sum(): pl.pallas_call(functools.partial(store_sum_kernel, block=block, added=so_...]
    slice x27 -> x11, local copies, waits for them, and re-layouts: 27.2 us -> 5.13 us  [the longest x1 1.69 us: on_device(): total_b[4 * rb:]]
    dot_general x7 -> x0, matrix products: 19.9 us -> none  [the longest x1 4.9 us: on_device(): jnp.einsum('htd,dhe->the', state_mix, val_heads, preferred_element_type=F32)]
  transfers between devices with their start and end apart: 22 -> 31, of which waited for: 13 -> 14; matrix products, arithmetic and copies ran while one was open for 27% -> 23% of each run, Pallas kernels for 11% -> 13%
where the time goes in v2:
time: 734 us; the launch traced here: 726 us
  waiting for transfers between devices  269 us (37%)
  Pallas kernels  137 us (19%)
  local copies, waits for them, and re-layouts  128 us (17%)
  matrix products  77.4 us (11%)
  starting transfers between devices  57.2 us (8%)
  other arithmetic  54.2 us (7%)
    ppermute x26, waiting for transfers between devices, swap_bit(): return lax.ppermute(array, axis, pairs)  223 us
    unnamed x317, local copies, waits for them, and re-layouts  73.2 us
    all_to_all x5, waiting for transfers between devices, all_to_all(): return lax.all_to_all(array, RANKS, split_axis=0, concat_axis=0, tiled=True)  46.6 us
    pallas_call x2, Pallas kernels, store_sum(): pl.pallas_call(functools.partial(store_sum_kernel, block=block, added=so_...  29.4 us
    ppermute x26, starting transfers between devices, swap_bit(): return lax.ppermute(array, axis, pairs)  29 us
    all_to_all x5, starting transfers between devices, all_to_all(): return lax.all_to_all(array, RANKS, split_axis=0, concat_axis=0, tiled=True)  28.2 us
    gather x2, local copies, waits for them, and re-layouts, on_device(): enc_store[jnp.maximum(attention.part(asked, c) - 1, 0)]  27.2 us
    dot_general x4, matrix products, mm_tn(): lax.dot_general(a, b, (((0,), (0,)), ((), ())), preferred_element_type=F32)  26.1 us
  transfers between devices with their start and end apart: 31, of which 14 were waited for; matrix products, arithmetic and copies ran while one was open for 23% of the time, Pallas kernels for 13%

profile of v2, /device:TPU:0, one launch (start us, length us, event | category | flops | bytes accessed | tf_op | source)
XLA Modules:
  0.0 725.8 jit_solution(5594768786230740127)
XLA Ops:
  9.0 4.4 plan.1
  14.8 6.1 all-to-all-start
  24.4 13.9 %all-to-all-done = s32[32,1,192]{2,1,0:T(1,128)S(1)} async-done(((s32[32,1,192]{2,1,0:T(1,128)}), s32[32,1,192]{2,1,0:T(1,128)S(1)}, u32[]{:S(2)}, u32[]{:S(2)}) %all-to-all-start) | async-done | bytes 24608 | tf_op jit(solution)/shard_map/all_to_all | solution.py:919
  44.9 13.6 %gather_fusion.2 = bf16[3072,768]{1,0:T(8,128)(2,1)} fusion(bf16[2048,768]{1,0:T(8,128)(2,1)S(1)} %copy-done, s32[3072]{0:T(1024)S(1)} %get-tuple-element.165), kind=kCustom, calls=%fused_computation.2 | custom fusion | bytes 9449472 | tf_op jit(solution)/shard_map/gather | solution.py:979
  63.9 4.7 collective-permute-done.1
  70.6 4.4 all-to-all-start.1
  78.2 13.6 %gather_fusion.1 = bf16[3072,768]{1,0:T(8,128)(2,1)} fusion(bf16[2048,768]{1,0:T(8,128)(2,1)S(1)} %copy-done, s32[3072]{0:T(1024)S(1)} %get-tuple-element.166), kind=kCustom, calls=%fused_computation.1 | custom fusion | bytes 9449472 | tf_op jit(solution)/shard_map/gather | solution.py:979
  91.8 55.0 %collective-permute-done.2 = bf16[4,400,384]{2,1,0:T(8,128)(2,1)} collective-permute-done((bf16[4,400,384]{2,1,0:T(8,128)(2,1)}, bf16[4,400,384]{2,1,0:T(8,128)(2,1)}, u32[]{:S(2)}, u32[]{:S(2)}) %collective-permute-start.2) | collective-permute-done | bytes 1228832 | tf_op jit(solution)/shard_map/ppermute | solution.py:76
  156.8 55.9 %collective-permute-done.3 = bf16[8,400,384]{2,1,0:T(8,128)(2,1)} collective-permute-done((bf16[8,400,384]{2,1,0:T(8,128)(2,1)}, bf16[8,400,384]{2,1,0:T(8,128)(2,1)}, u32[]{:S(2)}, u32[]{:S(2)}) %collective-permute-start.3) | collective-permute-done | bytes 2457632 | tf_op jit(solution)/shard_map/ppermute | solution.py:76
  212.7 4.5 pad_maximum_fusion.own
  220.6 7.3 %all-to-all-start.2 = ((bf16[32,96,768]{2,1,0:T(8,128)(2,1)}), bf16[32,96,768]{2,1,0:T(8,128)(2,1)}, u32[]{:S(2)}, u32[]{:S(2)}) async-start(bf16[32,96,768]{2,1,0:T(8,128)(2,1)} %hold.10), calls=%async_computation.2 | async-start | bytes 9437184 | tf_op jit(solution)/shard_map/all_to_all | solution.py:919
  246.4 5.3 unpack.3
  283.4 10.6 %rows_in.2 = (bf16[32,96,768]{2,1,0:T(8,128)(2,1)S(1)}, bf16[32,96,768]{2,1,0:T(8,128)(2,1)S(1)}, f32[96,512]{1,0:T(8,128)S(1)}) custom-call(bf16[32,96,768]{2,1,0:T(8,128)(2,1)} %all-to-all-done.1.arrived.refs_1_, bf16[32,96,768]{2,1,0:T(8,128)(2,1)S(1)} %bitcast.174, bf16[768,768]{1,0:T(8,128)(2,1)S(1)} %get-tuple-element.108.w_k, ...), custom_call_target="tpu_custom_call" | custom-call | tf_op jit(solution)/shard_map/rows_in/pallas_call | solution.py:755
  300.4 32.7 %all-to-all-done.2.arrived = bf16[32,96,768]{2,1,0:T(8,128)(2,1)} async-done(((bf16[32,96,768]{2,1,0:T(8,128)(2,1)}), bf16[32,96,768]{2,1,0:T(8,128)(2,1)}, u32[]{:S(2)}, u32[]{:S(2)}) %all-to-all-start.2) | async-done | bytes 4718624 | tf_op jit(solution)/shard_map/all_to_all | solution.py:919
  335.5 11.0 %rows_in.3 = (bf16[32,96,768]{2,1,0:T(8,128)(2,1)S(1)}, bf16[32,96,768]{2,1,0:T(8,128)(2,1)S(1)}, f32[96,512]{1,0:T(8,128)S(1)}) custom-call(bf16[32,96,768]{2,1,0:T(8,128)(2,1)} %all-to-all-done.2.arrived, bf16[32,96,768]{2,1,0:T(8,128)(2,1)S(1)} %bitcast.178, bf16[768,768]{1,0:T(8,128)(2,1)S(1)} %get-tuple-element.108.w_k, ...), custom_call_target="tpu_custom_call" | custom-call | tf_op jit(solution)/shard_map/rows_in/pallas_call | solution.py:755
  348.8 9.9 %attend.1 = (f32[256,256]{1,0:T(8,128)S(1)}, f32[192,512]{1,0:T(8,128)S(1)}, bf16[256,768]{1,0:T(8,128)(2,1)S(1)}) custom-call(f32[96,512]{1,0:T(8,128)S(1)} %get-tuple-element.53.refs_0_, f32[96,512]{1,0:T(8,128)S(1)} %get-tuple-element.54.refs_1_, bf16[32,96,768]{2,1,0:T(8,128)(2,1)S(1)} %copy-done.18, ...), custom_call_target="tpu_custom_call" | custom-call | tf_op jit(solution)/shard_map/attend/pallas_call | solution.py:757
  374.4 10.1 %attend_back.1 = (bf16[32,96,768]{2,1,0:T(8,128)(2,1)S(1)}, bf16[32,96,768]{2,1,0:T(8,128)(2,1)S(1)}, f32[192,512]{1,0:T(8,128)S(1)}) custom-call(bf16[32,96,768]{2,1,0:T(8,128)(2,1)S(1)} %copy-done.18, bf16[32,96,768]{2,1,0:T(8,128)(2,1)S(1)} %bitcast.181, bf16[3072,256]{1,0:T(8,128)(2,1)S(1)} %copy-done.40, bf16[3072,256]{1,0:T(8,128)(2,1)S(1)} %copy-done.39, ...), custom_call_target="tpu_custom_call" | custom-call | tf_op jit(solution)/shard_map/attend_back/pallas_call | solution.py:779
  391.3 12.7 %rows_out.2 = (bf16[32,96,768]{2,1,0:T(8,128)(2,1)S(1)}, bf16[32,96,768]{2,1,0:T(8,128)(2,1)S(1)}, bf16[32,96,768]{2,1,0:T(8,128)(2,1)S(1)}) custom-call(f32[192,512]{1,0:T(8,128)S(1)} %get-tuple-element.64.prob_slot, f32[192,512]{1,0:T(8,128)S(1)} %get-tuple-element.63.grad_slot.refs_4_, bf16[32,96,768]{2,1,0:T(8,128)(2,1)S(1)} %copy-done.43, ...), custom_call_target="tpu_custom_call" | custom-call | tf_op jit(solution)/shard_map/rows_out/pallas_call | solution.py:796
  424.1 6.0 query_back.1.refs_7_.refs_3_.refs_2_
  445.5 12.7 %rows_out.3 = (bf16[32,96,768]{2,1,0:T(8,128)(2,1)S(1)}, bf16[32,96,768]{2,1,0:T(8,128)(2,1)S(1)}, bf16[32,96,768]{2,1,0:T(8,128)(2,1)S(1)}) custom-call(f32[192,512]{1,0:T(8,128)S(1)} %copy-done.72, f32[192,512]{1,0:T(8,128)S(1)} %copy-done.63, bf16[32,96,768]{2,1,0:T(8,128)(2,1)S(1)} %copy-done.51, bf16[32,96,768]{2,1,0:T(8,128)(2,1)S(1)} %bitcast.179, ...), custom_call_target="tpu_custom_call" | custom-call | tf_op jit(solution)/shard_map/rows_out/pallas_call | solution.py:796
  485.4 7.3 %fusion.115 = f32[768,768,1]{1,0,2:T(8,128)S(1)} fusion(bf16[32,96,768]{2,1,0:T(8,128)(2,1)} %all-to-all-done.2.arrived, bf16[32,96,768]{2,1,0:T(8,128)(2,1)} %copy-done.90), kind=kOutput, calls=%fused_computation.260 | convolution fusion | flops 3623878656 | bytes 11796480 | tf_op jit(solution)/shard_map/dot_general | solution.py:28
  492.7 6.2 fusion.116
  498.9 6.3 fusion.25.refs_1_
  505.3 6.3 fusion.26.refs_0_
  511.7 4.1 pack.5
  520.8 6.3 all-to-all-start.3
  556.5 41.9 %collective-permute-done.22 = bf16[8,192,384]{2,1,0:T(8,128)(2,1)} collective-permute-done((bf16[8,192,384]{2,1,0:T(8,128)(2,1)}, bf16[8,192,384]{2,1,0:T(8,128)(2,1)}, u32[]{:S(2)}, u32[]{:S(2)}) %collective-permute-start.22) | collective-permute-done | bytes 1179680 | tf_op jit(solution)/shard_map/ppermute | solution.py:76
  607.8 36.2 %collective-permute-done.23 = bf16[4,192,384]{2,1,0:T(8,128)(2,1)S(1)} collective-permute-done((bf16[4,192,384]{2,1,0:T(8,128)(2,1)S(1)}, bf16[4,192,384]{2,1,0:T(8,128)(2,1)S(1)}, u32[]{:S(2)}, u32[]{:S(2)}) %collective-permute-start.23) | collective-permute-done | bytes 589856 | tf_op jit(solution)/shard_map/ppermute | solution.py:76
  649.0 14.4 %store_sum.2.refs_0_.refs_1_ = f32[2048,768]{1,0:T(8,128)} custom-call(s32[1,3072]{1,0:T(1,128)} %reshape.307.asked, bf16[3072,768]{1,0:T(8,128)(2,1)} %bitcast.48.returned), custom_call_target="tpu_custom_call" | custom-call | tf_op jit(solution)/shard_map/store_sum/pallas_call | solution.py:901
  673.9 6.1 collective-permute-done.12
  688.2 14.9 %store_sum.3.refs_1_ = f32[2048,768]{1,0:T(8,128)} custom-call(s32[1,3072]{1,0:T(1,128)} %reshape.303.asked, bf16[3072,768]{1,0:T(8,128)(2,1)} %bitcast.47.returned, f32[2048,768]{1,0:T(8,128)} %store_sum.2.refs_0_.refs_1_), custom_call_target="tpu_custom_call", output_to_operand_aliasing={{}: (2, {})} | custom-call | tf_op jit(solution)/shard_map/store_sum/pallas_call | solution.py:901
  707.9 13.1 %collective-permute-done.17 = bf16[1,400,384]{2,1,0:T(8,128)(2,1)S(1)} collective-permute-done((bf16[1,400,384]{2,1,0:T(8,128)(2,1)S(1)}, bf16[1,400,384]{2,1,0:T(8,128)(2,1)S(1)}, u32[]{:S(2)}, u32[]{:S(2)}) %collective-permute-start.17) | collective-permute-done | bytes 307232 | tf_op jit(solution)/shard_map/ppermute | solution.py:76
  (522 shorter events, 265.2 us)
Async XLA Ops:
  4.9 33.3 %collective-permute-start.5 = (bf16[1,384,384]{2,1,0:T(8,128)(2,1)}, bf16[1,384,384]{2,1,0:T(8,128)(2,1)}, u32[]{:S(2)}, u32[]{:S(2)}) collective-permute-start(bf16[1,384,384]{2,1,0:T(8,128)(2,1)} %get-tuple-element.51), channel_id=1, source_target_pairs={{0,16},{2,18},{4,20},{6,22},{8,24},{10,26},{12,28},{14,30},{16,0},... | collective-permute-start | bytes 884744 | tf_op jit(solution)/shard_map/ppermute | solution.py:76
  9.0 31.8 %collective-permute-start = (bf16[1,400,384]{2,1,0:T(8,128)(2,1)}, bf16[1,400,384]{2,1,0:T(8,128)(2,1)}, u32[]{:S(2)}, u32[]{:S(2)}) collective-permute-start(bf16[1,400,384]{2,1,0:T(8,128)(2,1)} %get-tuple-element.47), channel_id=1, source_target_pairs={{0,16},{2,18},{4,20},{6,22},{8,24},{10,26},{12,28},{14,30},{16,0},... | collective-permute-start | bytes 921608 | tf_op jit(solution)/shard_map/ppermute | solution.py:76
  14.8 23.4 %all-to-all-start = ((s32[32,1,192]{2,1,0:T(1,128)}), s32[32,1,192]{2,1,0:T(1,128)S(1)}, u32[]{:S(2)}, u32[]{:S(2)}) async-start(s32[32,1,192]{2,1,0:T(1,128)} %copy.59), calls=%async_computation | async-start | bytes 65536 | tf_op jit(solution)/shard_map/all_to_all | solution.py:919
  40.2 21.8 %collective-permute-start.6 = (bf16[2,384,384]{2,1,0:T(8,128)(2,1)}, bf16[2,384,384]{2,1,0:T(8,128)(2,1)}, u32[]{:S(2)}, u32[]{:S(2)}) collective-permute-start(bf16[2,384,384]{2,1,0:T(8,128)(2,1)} %pad_maximum_fusion.7), channel_id=1, source_target_pairs={{0,8},{2,10},{4,12},{6,14},{8,0},{10,2},{12,4},{14,6},{16,24},{18,... | collective-permute-start | bytes 1769480 | tf_op jit(solution)/shard_map/ppermute | solution.py:76
  42.7 26.0 %collective-permute-start.1 = (bf16[2,400,384]{2,1,0:T(8,128)(2,1)}, bf16[2,400,384]{2,1,0:T(8,128)(2,1)}, u32[]{:S(2)}, u32[]{:S(2)}) collective-permute-start(bf16[2,400,384]{2,1,0:T(8,128)(2,1)} %pad_maximum_fusion.4), channel_id=1, source_target_pairs={{0,8},{2,10},{4,12},{6,14},{8,0},{10,2},{12,4},{14,6},{16,24},{18,... | collective-permute-start | bytes 1843208 | tf_op jit(solution)/shard_map/ppermute | solution.py:76
  70.6 149.9 %all-to-all-start.1 = ((bf16[32,96,768]{2,1,0:T(8,128)(2,1)}), bf16[32,96,768]{2,1,0:T(8,128)(2,1)}, u32[]{:S(2)}, u32[]{:S(2)}) async-start(bf16[32,96,768]{2,1,0:T(8,128)(2,1)} %hold.9), calls=%async_computation.1 | async-start | bytes 9437184 | tf_op jit(solution)/shard_map/all_to_all | solution.py:919
  75.0 71.8 %collective-permute-start.2 = (bf16[4,400,384]{2,1,0:T(8,128)(2,1)}, bf16[4,400,384]{2,1,0:T(8,128)(2,1)}, u32[]{:S(2)}, u32[]{:S(2)}) collective-permute-start(bf16[4,400,384]{2,1,0:T(8,128)(2,1)} %constant_dynamic-update-slice_fusion.refs_1_), channel_id=1, source_target_pairs={{0,4},{2,6},{4,0},{6,2},{8,12},{10,14},{12,8},{14,10},{16,20},{18,... | collective-permute-start | bytes 3686408 | tf_op jit(solution)/shard_map/ppermute | solution.py:76
  76.7 75.8 %collective-permute-start.7 = (bf16[4,384,384]{2,1,0:T(8,128)(2,1)}, bf16[4,384,384]{2,1,0:T(8,128)(2,1)}, u32[]{:S(2)}, u32[]{:S(2)}) collective-permute-start(bf16[4,384,384]{2,1,0:T(8,128)(2,1)} %constant_dynamic-update-slice_fusion.3.refs_2_), channel_id=1, source_target_pairs={{0,2},{2,0},{4,6},{6,4},{8,10},{10,8},{12,14},{14,12},{16,18},{18,... | collective-permute-start | bytes 3538952 | tf_op jit(solution)/shard_map/ppermute | solution.py:76
  150.1 62.6 %collective-permute-start.3 = (bf16[8,400,384]{2,1,0:T(8,128)(2,1)}, bf16[8,400,384]{2,1,0:T(8,128)(2,1)}, u32[]{:S(2)}, u32[]{:S(2)}) collective-permute-start(bf16[8,400,384]{2,1,0:T(8,128)(2,1)} %hold.8), channel_id=1, source_target_pairs={{0,2},{2,0},{4,6},{6,4},{8,10},{10,8},{12,14},{14,12},{16,18},{18,... | collective-permute-start | bytes 7372808 | tf_op jit(solution)/shard_map/ppermute | solution.py:76
  155.8 61.4 %collective-permute-start.8 = (bf16[8,384,384]{2,1,0:T(8,128)(2,1)}, bf16[8,384,384]{2,1,0:T(8,128)(2,1)S(1)}, u32[]{:S(2)}, u32[]{:S(2)}) collective-permute-start(bf16[8,384,384]{2,1,0:T(8,128)(2,1)} %hold.11), channel_id=1, source_target_pairs={{0,4},{2,6},{4,0},{6,2},{8,12},{10,14},{12,8},{14,10},{16,20},{18,... | collective-permute-start | bytes 7077896 | tf_op jit(solution)/shard_map/ppermute | solution.py:76
  217.2 29.2 %collective-permute-start.4 = (bf16[16,400,384]{2,1,0:T(8,128)(2,1)}, bf16[16,400,384]{2,1,0:T(8,128)(2,1)}, u32[]{:S(2)}, u32[]{:S(2)}) collective-permute-start(bf16[16,400,384]{2,1,0:T(8,128)(2,1)} %pad_maximum_fusion.own), channel_id=1, source_target_pairs={{0,1},{1,0},{2,3},{3,2},{4,5},{5,4},{6,7},{7,6},{8,9},{9,8},{10,11... | collective-permute-start | bytes 14745608 | tf_op jit(solution)/shard_map/ppermute | solution.py:76
  220.0 15.4 %collective-permute-start.9 = (bf16[16,384,384]{2,1,0:T(8,128)(2,1)}, bf16[16,384,384]{2,1,0:T(8,128)(2,1)}, u32[]{:S(2)}, u32[]{:S(2)}) collective-permute-start(bf16[16,384,384]{2,1,0:T(8,128)(2,1)} %pad_maximum_fusion.1.own), channel_id=1, source_target_pairs={{0,1},{1,0},{2,3},{3,2},{4,5},{5,4},{6,7},{7,6},{8,9},{9,8},{10,11... | collective-permute-start | bytes 14155784 | tf_op jit(solution)/shard_map/ppermute | solution.py:76
  220.6 112.6 %all-to-all-start.2 = ((bf16[32,96,768]{2,1,0:T(8,128)(2,1)}), bf16[32,96,768]{2,1,0:T(8,128)(2,1)}, u32[]{:S(2)}, u32[]{:S(2)}) async-start(bf16[32,96,768]{2,1,0:T(8,128)(2,1)} %hold.10), calls=%async_computation.2 | async-start | bytes 9437184 | tf_op jit(solution)/shard_map/all_to_all | solution.py:919
  256.7 104.3 %copy-start.129 = (f32[768]{0:T(1024)}, f32[768]{0:T(1024)S(1)}, u32[]{:S(2)}) copy-start(f32[768]{0:T(1024)S(1)} %add.326) | copy-start | bytes 9220
  410.6 110.1 %all-to-all-start.4 = ((bf16[32,96,768]{2,1,0:T(8,128)(2,1)}), bf16[32,96,768]{2,1,0:T(8,128)(2,1)}, u32[]{:S(2)}, u32[]{:S(2)}) async-start(bf16[32,96,768]{2,1,0:T(8,128)(2,1)} %copy-done.5), calls=%async_computation.4 | async-start | bytes 9437184 | tf_op jit(solution)/shard_map/all_to_all | solution.py:919
  520.8 167.5 %all-to-all-start.3 = ((bf16[32,96,768]{2,1,0:T(8,128)(2,1)}), bf16[32,96,768]{2,1,0:T(8,128)(2,1)}, u32[]{:S(2)}, u32[]{:S(2)}) async-start(bf16[32,96,768]{2,1,0:T(8,128)(2,1)} %hold.12), calls=%async_computation.3 | async-start | bytes 9437184 | tf_op jit(solution)/shard_map/all_to_all | solution.py:919
  531.9 4.8 collective-permute-start.21
  535.9 6.7 collective-permute-start.18
  536.2 11.3 %collective-permute-start.10 = (bf16[16,192,384]{2,1,0:T(8,128)(2,1)}, bf16[16,192,384]{2,1,0:T(8,128)(2,1)}, u32[]{:S(2)}, u32[]{:S(2)}) collective-permute-start(bf16[16,192,384]{2,1,0:T(8,128)(2,1)} %get-tuple-element.70.refs_2_), channel_id=1, source_target_pairs={{0,1},{1,0},{2,3},{3,2},{4,5},{5,4},{6,7},{7,6},{8,9},{9,8},{10,11... | collective-permute-start | bytes 7077896 | tf_op jit(solution)/shard_map/ppermute | solution.py:76
  536.5 14.8 %collective-permute-start.13 = (bf16[16,208,384]{2,1,0:T(8,128)(2,1)}, bf16[16,208,384]{2,1,0:T(8,128)(2,1)}, u32[]{:S(2)}, u32[]{:S(2)}) collective-permute-start(bf16[16,208,384]{2,1,0:T(8,128)(2,1)} %get-tuple-element.78.refs_4_), channel_id=1, source_target_pairs={{0,1},{1,0},{2,3},{3,2},{4,5},{5,4},{6,7},{7,6},{8,9},{9,8},{10,11... | collective-permute-start | bytes 7667720 | tf_op jit(solution)/shard_map/ppermute | solution.py:76
  538.6 59.7 %collective-permute-start.22 = (bf16[8,192,384]{2,1,0:T(8,128)(2,1)}, bf16[8,192,384]{2,1,0:T(8,128)(2,1)}, u32[]{:S(2)}, u32[]{:S(2)}) collective-permute-start(bf16[8,192,384]{2,1,0:T(8,128)(2,1)} %get-tuple-element.114), channel_id=1, source_target_pairs={{0,4},{2,6},{4,0},{6,2},{8,12},{10,14},{12,8},{14,10},{16,20},{18,... | collective-permute-start | bytes 3538952 | tf_op jit(solution)/shard_map/ppermute | solution.py:76
  544.4 57.2 %collective-permute-start.19 = (bf16[8,192,384]{2,1,0:T(8,128)(2,1)}, bf16[8,192,384]{2,1,0:T(8,128)(2,1)}, u32[]{:S(2)}, u32[]{:S(2)}) collective-permute-start(bf16[8,192,384]{2,1,0:T(8,128)(2,1)} %get-tuple-element.112), channel_id=1, source_target_pairs={{0,2},{2,0},{4,6},{6,4},{8,10},{10,8},{12,14},{14,12},{16,18},{18,... | collective-permute-start | bytes 3538952 | tf_op jit(solution)/shard_map/ppermute | solution.py:76
  550.9 112.5 %collective-permute-start.11 = (bf16[8,192,384]{2,1,0:T(8,128)(2,1)}, bf16[8,192,384]{2,1,0:T(8,128)(2,1)}, u32[]{:S(2)}, u32[]{:S(2)}) collective-permute-start(bf16[8,192,384]{2,1,0:T(8,128)(2,1)} %get-tuple-element.116), channel_id=1, source_target_pairs={{0,2},{2,0},{4,6},{6,4},{8,10},{10,8},{12,14},{14,12},{16,18},{18,... | collective-permute-start | bytes 3538952 | tf_op jit(solution)/shard_map/ppermute | solution.py:76
  554.8 112.1 %collective-permute-start.14 = (bf16[8,208,384]{2,1,0:T(8,128)(2,1)}, bf16[8,208,384]{2,1,0:T(8,128)(2,1)}, u32[]{:S(2)}, u32[]{:S(2)}) collective-permute-start(bf16[8,208,384]{2,1,0:T(8,128)(2,1)} %get-tuple-element.110), channel_id=1, source_target_pairs={{0,4},{2,6},{4,0},{6,2},{8,12},{10,14},{12,8},{14,10},{16,20},{18,... | collective-permute-start | bytes 3833864 | tf_op jit(solution)/shard_map/ppermute | solution.py:76
  599.8 44.2 %collective-permute-start.23 = (bf16[4,192,384]{2,1,0:T(8,128)(2,1)S(1)}, bf16[4,192,384]{2,1,0:T(8,128)(2,1)S(1)}, u32[]{:S(2)}, u32[]{:S(2)}) collective-permute-start(bf16[4,192,384]{2,1,0:T(8,128)(2,1)S(1)} %get-tuple-element.122), channel_id=1, source_target_pairs={{0,2},{2,0},{4,6},{6,4},{8,10},{10,8},{12,14},{14,12},{16,18},{18,... | collective-permute-start | bytes 1769480 | tf_op jit(solution)/shard_map/ppermute | solution.py:76
  603.0 42.8 %collective-permute-start.20 = (bf16[4,192,384]{2,1,0:T(8,128)(2,1)S(1)}, bf16[4,192,384]{2,1,0:T(8,128)(2,1)S(1)}, u32[]{:S(2)}, u32[]{:S(2)}) collective-permute-start(bf16[4,192,384]{2,1,0:T(8,128)(2,1)S(1)} %get-tuple-element.120), channel_id=1, source_target_pairs={{0,4},{2,6},{4,0},{6,2},{8,12},{10,14},{12,8},{14,10},{16,20},{18,... | collective-permute-start | bytes 1769480 | tf_op jit(solution)/shard_map/ppermute | solution.py:76
  646.7 24.4 %collective-permute-start.24 = (bf16[2,384,384]{2,1,0:T(8,128)(2,1)}, bf16[2,384,384]{2,1,0:T(8,128)(2,1)}, u32[]{:S(2)}, u32[]{:S(2)}) collective-permute-start(bf16[2,384,384]{2,1,0:T(8,128)(2,1)} %pad_maximum_fusion.8), channel_id=1, source_target_pairs={{0,8},{2,10},{4,12},{6,14},{8,0},{10,2},{12,4},{14,6},{16,24},{18,... | collective-permute-start | bytes 1769480 | tf_op jit(solution)/shard_map/ppermute | solution.py:76
  665.2 14.7 %collective-permute-start.12 = (bf16[4,192,384]{2,1,0:T(8,128)(2,1)S(1)}, bf16[4,192,384]{2,1,0:T(8,128)(2,1)S(1)}, u32[]{:S(2)}, u32[]{:S(2)}) collective-permute-start(bf16[4,192,384]{2,1,0:T(8,128)(2,1)S(1)} %get-tuple-element.124), channel_id=1, source_target_pairs={{0,4},{2,6},{4,0},{6,2},{8,12},{10,14},{12,8},{14,10},{16,20},{18,... | collective-permute-start | bytes 1769480 | tf_op jit(solution)/shard_map/ppermute | solution.py:76
  668.3 15.3 %collective-permute-start.15 = (bf16[4,208,384]{2,1,0:T(8,128)(2,1)S(1)}, bf16[4,208,384]{2,1,0:T(8,128)(2,1)S(1)}, u32[]{:S(2)}, u32[]{:S(2)}) collective-permute-start(bf16[4,208,384]{2,1,0:T(8,128)(2,1)S(1)} %get-tuple-element.118), channel_id=1, source_target_pairs={{0,2},{2,0},{4,6},{6,4},{8,10},{10,8},{12,14},{14,12},{16,18},{18,... | collective-permute-start | bytes 1916936 | tf_op jit(solution)/shard_map/ppermute | solution.py:76
  672.1 15.0 %collective-permute-start.25 = (bf16[1,384,384]{2,1,0:T(8,128)(2,1)S(1)}, bf16[1,384,384]{2,1,0:T(8,128)(2,1)S(1)}, u32[]{:S(2)}, u32[]{:S(2)}) collective-permute-start(bf16[1,384,384]{2,1,0:T(8,128)(2,1)S(1)} %slice_add_fusion.20), channel_id=1, source_target_pairs={{0,16},{2,18},{4,20},{6,22},{8,24},{10,26},{12,28},{14,30},{16,0},... | collective-permute-start | bytes 884744 | tf_op jit(solution)/shard_map/ppermute | solution.py:76
  684.7 19.4 %collective-permute-start.16 = (bf16[2,400,384]{2,1,0:T(8,128)(2,1)}, bf16[2,400,384]{2,1,0:T(8,128)(2,1)}, u32[]{:S(2)}, u32[]{:S(2)}) collective-permute-start(bf16[2,400,384]{2,1,0:T(8,128)(2,1)} %pad_maximum_fusion.6), channel_id=1, source_target_pairs={{0,8},{2,10},{4,12},{6,14},{8,0},{10,2},{12,4},{14,6},{16,24},{18,... | collective-permute-start | bytes 1843208 | tf_op jit(solution)/shard_map/ppermute | solution.py:76
  705.3 15.6 %collective-permute-start.17 = (bf16[1,400,384]{2,1,0:T(8,128)(2,1)S(1)}, bf16[1,400,384]{2,1,0:T(8,128)(2,1)S(1)}, u32[]{:S(2)}, u32[]{:S(2)}) collective-permute-start(bf16[1,400,384]{2,1,0:T(8,128)(2,1)S(1)} %slice_add_fusion.18), channel_id=1, source_target_pairs={{0,16},{2,18},{4,20},{6,22},{8,24},{10,26},{12,28},{14,30},{16,0},... | collective-permute-start | bytes 921608 | tf_op jit(solution)/shard_map/ppermute | solution.py:76
  (155 other events, 1229.8 us)

commit v3 on v2

--- a/solution.py
+++ b/solution.py
@@ -51,15 +51,6 @@
     return (pre_act * cdf_part, cdf_part + pre_act * density)
 
 
-def visible_mask(seg_row, live_row):
-    pos = jnp.arange(seg_row.shape[0], dtype=jnp.int32)
-    return (
-        (pos[None, :] <= pos[:, None])
-        & (seg_row[:, None] == seg_row[None, :])
-        & ((live_row[None, :] == 1) | (pos[None, :] == pos[:, None]))
-    )
-
-
 def column_sum(array):
     return jnp.sum(array.astype(F32), axis=0)
 
@@ -124,7 +115,19 @@
     return flip_by_position(blocks, stages).reshape((-1,) + shape)
 
 
-WAIT = pl.BlockSpec(memory_space=pl.ANY)
+def cost(micros):
+    return pl.CostEstimate(flops=int(micros * 1.1e9), bytes_accessed=0, transcendentals=0)
+
+
+WAIT = pl.BlockSpec(memory_space=pltpu.HBM)
+
+
+def in_hbm(shape, dtype):
+    return pltpu.HBM(shape=shape, dtype=dtype)
+
+
+def from_hbm(array):
+    return pltpu.with_memory_space_constraint(array, pltpu.HBM)
 
 
 def tie_kernel(*refs):
@@ -162,7 +165,7 @@
     ]
 
 
-def unpack_kernel(place, own, other, *refs, count, shape, first, beside, extra):
+def unpack_kernel(place, own, other, *refs, count, shape, extra):
     outs, (buf, *more) = refs[: 1 + bool(extra)], refs[1 + bool(extra) :]
     sems = more[-1]
     n_rows, col, rows = own.shape[0], place[own.shape[0]], shape[0]
@@ -171,16 +174,15 @@
         j = place[r]
         for src, c, sem in ((own, col, 0), (other, 1 - col, 1)):
             for k in range(count):
-                part = src.at[j, pl.ds(first + k * rows, rows)]
-                to = (0, r, c * count + k) if beside else (k, r, c)
-                pltpu.make_async_copy(part, tile_of(buf, *to, shape), sems.at[sem]).start()
+                part = src.at[j, pl.ds(k * rows, rows)]
+                pltpu.make_async_copy(part, tile_of(buf, k, r, c, shape), sems.at[sem]).start()
         if extra:
-            tail = own.at[j, pl.ds(first + count * rows, extra)]
+            tail = own.at[j, pl.ds(count * rows, extra)]
             pltpu.make_async_copy(tail, more[0].at[r], sems.at[2]).start()
         return carry
 
     lax.fori_loop(0, n_rows, fill, 0)
-    body = own.at[:, pl.ds(first, count * rows)]
+    body = own.at[:, pl.ds(0, count * rows)]
     for sem in range(2):
         pltpu.make_async_copy(body, body, sems.at[sem]).wait()
     out = pltpu.make_async_copy(buf, outs[0], sems.at[3])
@@ -193,17 +195,14 @@
     out.wait()
 
 
-def unpack(own, other, place, count, shape, first=0, beside=False, extra=0):
+def unpack(own, other, place, count, shape, extra=0):
     n_rows = own.shape[0]
     rows, cols = shape
-    many, wide = (1, count) if beside else (count, 1)
-    whole = jax.ShapeDtypeStruct((many, n_rows * rows, 2 * wide * cols), BF)
+    whole = jax.ShapeDtypeStruct((count, n_rows * rows, 2 * cols), BF)
     tails = jax.ShapeDtypeStruct((n_rows, extra, cols), BF)
     shapes = [whole] + [tails] * bool(extra)
     got = pl.pallas_call(
-        functools.partial(
-            unpack_kernel, count=count, shape=shape, first=first, beside=beside, extra=extra
-        ),
+        functools.partial(unpack_kernel, count=count, shape=shape, extra=extra),
         in_specs=[pl.BlockSpec(memory_space=pltpu.SMEM)] + [pl.BlockSpec(memory_space=pl.ANY)] * 2,
         out_specs=[pl.BlockSpec(memory_space=pl.ANY)] * len(shapes),
         out_shape=shapes,
@@ -217,37 +216,30 @@
     return got if extra else got[0]
 
 
-def split_cols(array, pieces):
-    width = array.shape[1] // pieces
-    return jnp.concatenate([array[:, i * width : (i + 1) * width] for i in range(pieces)], axis=0)
-
-
-def join_kernel(attn_in, attn_out, small, ff_in, ff_out, side_a, side_b, *, rb, cb):
-    at = 0
-    for array in (attn_in, attn_out):
-        for k in range(array.shape[0]):
-            side_a[0, at : at + rb] = array[k]
-            at += rb
-    side_a[0, at:] = small[...]
+def join_kernel(attn_in, attn_out, small, waited, one, two, *, rb):
+    del waited
     for k in range(4):
-        side_b[0, k * rb : (k + 1) * rb] = ff_in[:, k * cb : (k + 1) * cb]
-    side_b[0, 4 * rb :] = ff_out[...]
-
-
-def join(attn_in, attn_out, small, ff_in, ff_out):
+        one[0, k * rb : (k + 1) * rb] = attn_in[k]
+    for k in range(2):
+        two[0, k * rb : (k + 1) * rb] = attn_in[4 + k]
+        two[0, (2 + k) * rb : (3 + k) * rb] = attn_out[k]
+    two[0, 4 * rb :] = small[...]
+
+
+def join(attn_in, attn_out, small, after):
     rb, cb = attn_in.shape[1:]
     if rb % 16 or cb % 128:
-        side_a = [attn_in.reshape(-1, cb), attn_out.reshape(-1, cb), small]
-        side_b = [split_cols(ff_in, 4), ff_out]
-        return tuple(jnp.concatenate(side, axis=0)[None] for side in (side_a, side_b))
+        two = [attn_in[4:].reshape(-1, cb), attn_out.reshape(-1, cb), small]
+        return attn_in[:4].reshape(1, -1, cb), jnp.concatenate(two, axis=0)[None]
     return pl.pallas_call(
-        functools.partial(join_kernel, rb=rb, cb=cb),
+        functools.partial(join_kernel, rb=rb),
+        in_specs=[pl.BlockSpec(memory_space=pltpu.VMEM)] * 3 + [WAIT],
         out_shape=(
-            jax.ShapeDtypeStruct((1, 8 * rb + small.shape[0], cb), BF),
-            jax.ShapeDtypeStruct((1, 8 * rb, cb), BF),
+            jax.ShapeDtypeStruct((1, 4 * rb, cb), BF),
+            jax.ShapeDtypeStruct((1, 4 * rb + small.shape[0], cb), BF),
         ),
         name="join",
-    )(attn_in, attn_out, small, ff_in, ff_out)
+    )(attn_in, attn_out, small, after)
 
 
 def pack_kernel(place, *refs, mats, rows, extra, waits):
@@ -306,7 +298,7 @@
         total += beside * shape[0]
         n_rows = whole[0] // shape[0]
     extra = 0 if small is None else small.shape[1]
-    block = jax.ShapeDtypeStruct((n_rows, total + extra, shape[1]), BF)
+    block = in_hbm((n_rows, total + extra, shape[1]), BF)
     if extra:
         ops.append(small)
         specs.append(pl.BlockSpec(memory_space=pltpu.VMEM))
@@ -320,16 +312,18 @@
         scratch_shapes=bufs + [pltpu.SemaphoreType.DMA((2 + len(mats),))],
         compiler_params=pltpu.CompilerParams(vmem_limit_bytes=48 * 1024 * 1024),
         cost_estimate=pl.CostEstimate(
-            flops=flops, bytes_accessed=8 * block.size, transcendentals=0
+            flops=flops, bytes_accessed=8 * n_rows * total * shape[1], transcendentals=0
         ),
         name="pack",
     )(place, *ops, *after)
 
 
-def unpack_any(blocks, order, n_rows, n_cols, rb):
-    cols = blocks.shape[2]
+def unpack_any(blocks, order, count, shape, extra, n_rows, n_cols):
+    rows, cols = shape
     got = by_device(blocks, order).reshape(n_rows, n_cols, -1, cols)
-    return got[:, :, : 8 * rb].reshape(n_rows, n_cols, 8, rb, cols), got[:, 0, 8 * rb :]
+    mats = got[:, :, : count * rows].reshape(n_rows, n_cols, count, rows, cols)
+    mats = mats.transpose(2, 0, 3, 1, 4).reshape(count, n_rows * rows, n_cols * cols)
+    return (mats, got[:, 0, count * rows :]) if extra else mats
 
 
 def pack_any(mats, order, small, n_rows, n_cols):
@@ -369,6 +363,116 @@
     at_rank = (rank[:, None] == jnp.arange(slots, dtype=jnp.int32)[None, :]).astype(BF)
     codes = mm(left.reshape(4 * peers, count), at_rank).astype(jnp.int32).reshape(4, peers, slots)
     return place, codes[0] * 64 + codes[1], codes[2] * 64 + codes[3]
+
+
+def row_norm(resid):
+    centered = resid - jnp.mean(resid, axis=-1, keepdims=True)
+    scale = lax.rsqrt(jnp.mean(centered * centered, axis=-1, keepdims=True) + 1e-05)
+    return centered * scale, scale
+
+
+def head_masks():
+    lane = lax.broadcasted_iota(jnp.int32, (1, 2 * HD), 1)
+    return [(lane // HD == i).astype(F32).astype(BF) for i in range(2)]
+
+
+def self_probs(query, key, visible):
+    scores = jnp.where(visible, mm_nt(query, key) * (HD**-0.5), -1e30)
+    expo = jnp.exp(scores - jnp.max(scores, axis=-1, keepdims=True))
+    return expo / jnp.sum(expo, axis=-1, keepdims=True)
+
+
+def visible_pairs(seg_col, seg_row, live_row):
+    shape = (seg_col.shape[0], seg_row.shape[1])
+    at_query = lax.broadcasted_iota(jnp.int32, shape, 0)
+    at_key = lax.broadcasted_iota(jnp.int32, shape, 1)
+    return (
+        (at_key <= at_query)
+        & (seg_col[...] == seg_row[...])
+        & ((live_row[...] == 1) | (at_key == at_query))
+    )
+
+
+def self_fwd_kernel(*refs):
+    tokens, seg_col, seg_row, live_row, w_qkvc, w_o, bias, gain, shift = refs[:9]
+    queries, keys, values, mixed, first, normed, scale, cross_q = refs[9:]
+    x = tokens[...]
+    queries[...] = (mm(x, w_qkvc[0]) + bias[0:1]).astype(BF)
+    keys[...] = mm(x, w_qkvc[1]).astype(BF)
+    values[...] = (mm(x, w_qkvc[2]) + bias[1:2]).astype(BF)
+    visible = visible_pairs(seg_col, seg_row, live_row)
+    for pair in range(H // 2):
+        lanes = slice(2 * HD * pair, 2 * HD * (pair + 1))
+        total = 0.0
+        for mask in head_masks():
+            prob = self_probs(queries[:, lanes], keys[:, lanes] * mask, visible)
+            total = total + mm(prob.astype(BF), values[:, lanes] * mask)
+        mixed[:, lanes] = total.astype(BF)
+    resid = x.astype(F32) + mm(mixed[...], w_o[...]) + bias[2:3]
+    norm, inv = row_norm(resid)
+    normed[...] = norm
+    scale[...] = jnp.broadcast_to(inv, scale.shape)
+    out = norm * gain[0:1] + shift[0:1]
+    first[...] = out
+    cross_q[...] = (mm(out.astype(BF), w_qkvc[3]) + bias[3:4]).astype(BF)
+
+
+def self_fwd(tokens, seg, live, w_qkvc, w_o, bias, gain, shift):
+    toks, dim = tokens.shape
+    low = jax.ShapeDtypeStruct((toks, dim), BF)
+    full = jax.ShapeDtypeStruct((toks, dim), F32)
+    column = jax.ShapeDtypeStruct((toks, 128), F32)
+    return pl.pallas_call(
+        self_fwd_kernel,
+        out_shape=(low, low, low, low, full, full, column, low),
+        compiler_params=pltpu.CompilerParams(vmem_limit_bytes=28 * 1024 * 1024),
+        cost_estimate=cost(5),
+        name="self_fwd",
+    )(tokens, seg.reshape(toks, 1), seg, live, w_qkvc, w_o, bias, gain, shift)
+
+
+def self_bwd_kernel(*refs):
+    grad_cq, grad_two, normed, scale, gain, queries, keys, values = refs[:8]
+    seg_col, seg_row, live_row, w_qkvc, w_o = refs[8:13]
+    grad_first, grad_one, grad_o, grad_q, grad_k, grad_v, grad_mix = refs[13:]
+    incoming = grad_two[...] + mm_nt(grad_cq[...], w_qkvc[3])
+    grad_first[...] = incoming
+    one = norm_back(incoming, normed[...], scale[:, 0:1], gain[0:1])
+    grad_one[...] = one
+    low = one.astype(BF)
+    grad_o[...] = low
+    grad_mix[...] = mm_nt(low, w_o[...]).astype(BF)
+    visible = visible_pairs(seg_col, seg_row, live_row)
+    for pair in range(H // 2):
+        lanes = slice(2 * HD * pair, 2 * HD * (pair + 1))
+        by_query, by_key, by_value = 0.0, 0.0, 0.0
+        for mask in head_masks():
+            query, key = queries[:, lanes] * mask, keys[:, lanes] * mask
+            grad = grad_mix[:, lanes] * mask
+            prob = self_probs(query, key, visible)
+            grad_p = mm_nt(grad, values[:, lanes])
+            dot = jnp.sum(prob * grad_p, axis=-1, keepdims=True)
+            grad_s = (prob * (grad_p - dot)).astype(BF)
+            by_query = by_query + mm(grad_s, key)
+            by_key = by_key + mm_tn(grad_s, query)
+            by_value = by_value + mm_tn(prob.astype(BF), grad)
+        grad_q[:, lanes] = (by_query * (HD**-0.5)).astype(BF)
+        grad_k[:, lanes] = (by_key * (HD**-0.5)).astype(BF)
+        grad_v[:, lanes] = by_value.astype(BF)
+
+
+def self_bwd(grad_cq, grad_two, normed, scale, gain, qkv, seg, live, w_qkvc, w_o):
+    toks, dim = grad_two.shape
+    low = jax.ShapeDtypeStruct((toks, dim), BF)
+    full = jax.ShapeDtypeStruct((toks, dim), F32)
+    return pl.pallas_call(
+        self_bwd_kernel,
+        out_shape=(full, full, low, low, low, low),
+        scratch_shapes=[pltpu.VMEM((toks, dim), BF)],
+        compiler_params=pltpu.CompilerParams(vmem_limit_bytes=28 * 1024 * 1024),
+        cost_estimate=cost(6),
+        name="self_bwd",
+    )(grad_cq, grad_two, normed, scale, gain, *qkv, seg.reshape(toks, 1), seg, live, w_qkvc, w_o)
 
 
 def own_rows(tokens, ret, heads):
@@ -505,6 +609,7 @@
             jax.ShapeDtypeStruct((tall, ret * toks), BF),
             jax.ShapeDtypeStruct((ret, toks), jnp.int32),
         ),
+        cost_estimate=cost(4),
         name="plan",
     )(rows)
 
@@ -562,6 +667,17 @@
     return total[:slots]
 
 
+def token_marks_kernel(column, row, marks, marks_t):
+    marks[...] = (
+        column[...] == lax.broadcasted_iota(jnp.int32, marks.shape, 1) + 1
+    ).astype(BF)
+    marks_t[...] = (row[...] == lax.broadcasted_iota(jnp.int32, marks_t.shape, 0) + 1).astype(BF)
+
+
+def query_rows_kernel(token, query, out):
+    out[...] = mm(token[...], query[...]).astype(BF).reshape(out.shape)
+
+
 def rows_in_kernel(arrived, query, w_k, w_v, keys, vals, scores):
     group, k, dim = arrived.shape
     rows = arrived[...].reshape(group * k, dim)
@@ -572,98 +688,108 @@
     vals[...] = mm(rows, w_v[...]).astype(BF).reshape(group, k, dim)
 
 
-def attend_kernel(*refs, chunks):
-    scores, vals, token_t = refs[:chunks], refs[chunks : 2 * chunks], refs[2 * chunks : 3 * chunks]
-    at_rank, owner, bias, prob_tok, prob_slot, mixed, total = refs[3 * chunks :]
-    step, steps = pl.program_id(0), pl.num_programs(0)
-    k, dim = vals[0].shape[1:]
-
-    @pl.when(step == 0)
+def attend_kernel(
+    scores, vals, token_t, at_rank, owner, bias, prob_tok, prob_slot, mixed, total
+):
+    step, part = pl.program_id(0), pl.program_id(1)
+    k, dim = vals.shape[1:]
+    slots, wide = scores.shape
+
+    @pl.when((step == 0) & (part == 0))
     def _():
-        entry = to_entries(
-            jnp.concatenate([part[...] for part in scores], axis=0), at_rank, owner
-        )
+        entry = to_entries(scores[...], at_rank, owner)
         top = functools.reduce(jnp.maximum, entry)
         expo = [jnp.exp(part - top) for part in entry]
         norm = functools.reduce(jnp.add, expo)
         probs = [part / norm for part in expo]
         for r, part in enumerate(probs):
             prob_tok[r * PITCH : (r + 1) * PITCH, :] = part
-        peers = scores[0].shape[1] // PITCH
-        prob_slot[...] = to_slots(probs, at_rank, owner, peers, chunks * k)
+        prob_slot[...] = to_slots(probs, at_rank, owner, wide // PITCH, slots)
         total[...] = jnp.zeros_like(total)
 
-    spread = head_spread(dim)
     lanes = pl.ds(pl.multiple_of(step * LANES, LANES), LANES)
-    acc = total[...]
-    for c in range(chunks):
-        prob = mm(from_lanes(prob_slot[c * k : (c + 1) * k, lanes]), spread)
-        prod = (prob * vals[c][...].reshape(-1, dim).astype(F32)).astype(BF)
-        acc = acc + mm(token_t[c][...], prod)
-    total[...] = acc
-
-    @pl.when(step == steps - 1)
+    here = pl.ds(pl.multiple_of(part * k, 16), k)
+    prob = mm(from_lanes(prob_slot[here, lanes]), head_spread(dim))
+    prod = (prob * vals[...].reshape(-1, dim).astype(F32)).astype(BF)
+    total[...] += mm(token_t[...], prod)
+
+    @pl.when((step == pl.num_programs(0) - 1) & (part == pl.num_programs(1) - 1))
     def _():
         mixed[...] = (total[...] + bias[...]).astype(BF)
 
 
-def attend_back_kernel(*refs, chunks):
-    vals, token = refs[:chunks], refs[chunks : 2 * chunks]
-    grad, prob_tok, at_rank, owner = refs[2 * chunks : 2 * chunks + 4]
-    grads, (grad_slot, slot_p) = refs[2 * chunks + 4 : -2], refs[-2:]
-    step, steps = pl.program_id(0), pl.num_programs(0)
-    k, dim = vals[0].shape[1:]
+def attend_back_kernel(
+    vals, token, grad, prob_tok, at_rank, owner, grads, grad_slot, slot_p
+):
+    step, part = pl.program_id(0), pl.program_id(1)
+    k, dim = vals.shape[1:]
+    slots, wide = slot_p.shape
     lanes = pl.ds(pl.multiple_of(step * LANES, LANES), LANES)
-    add_up = head_sum(dim)
-    for c in range(chunks):
-        wide = mm(token[c][...], grad[...])
-        grads[c][...] = wide.astype(BF).reshape(vals[c].shape)
-        prod = (wide * vals[c][...].reshape(-1, dim).astype(F32)).astype(BF)
-        slot_p[c * k : (c + 1) * k, lanes] = to_lanes(mm(prod, add_up), k)
-
-    @pl.when(step == steps - 1)
+    here = pl.ds(pl.multiple_of(part * k, 16), k)
+    rows = mm(token[...], grad[...])
+    grads[...] = rows.astype(BF).reshape(vals.shape)
+    prod = (rows * vals[...].reshape(-1, dim).astype(F32)).astype(BF)
+    slot_p[here, lanes] = to_lanes(mm(prod, head_sum(dim)), k)
+
+    @pl.when((step == pl.num_programs(0) - 1) & (part == pl.num_programs(1) - 1))
     def _():
         entry = to_entries(slot_p[...], at_rank, owner)
         probs = [prob_tok[r * PITCH : (r + 1) * PITCH, :] for r in range(len(entry))]
         dots = functools.reduce(jnp.add, [p * g for p, g in zip(probs, entry)])
         scores = [(p * (g - dots)).astype(BF).astype(F32) for p, g in zip(probs, entry)]
-        peers = slot_p.shape[1] // PITCH
-        grad_slot[...] = to_slots(scores, at_rank, owner, peers, chunks * k)
-
-
-def rows_out_kernel(prob_slot, grad_slot, grad, query, w_k, w_v, *refs):
-    out, by_prob, by_score = refs[-3:]
-    group, k, dim = grad.shape
+        grad_slot[...] = to_slots(scores, at_rank, owner, wide // PITCH, slots)
+
+
+def weigh(prob_slot, grad_slot, grad, query):
+    dim = grad.shape[2]
     spread = head_spread(dim)
     prob = mm(from_lanes(prob_slot[...]), spread)
     mix = (prob * grad[...].reshape(-1, dim).astype(F32)).astype(BF)
     score = mm(from_lanes(grad_slot[...]), spread) * 0.125
-    ask = (score * query[...].reshape(-1, dim).astype(F32)).astype(BF)
+    return mix, (score * query[...].reshape(-1, dim).astype(F32)).astype(BF)
+
+
+def rows_out_kernel(prob_slot, grad_slot, grad, query, w_k, w_v, out, flag):
+    mix, ask = weigh(prob_slot, grad_slot, grad, query)
     out[...] = (mm_nt(mix, w_v[...]) + mm_nt(ask, w_k[...])).astype(BF).reshape(grad.shape)
-    by_prob[...] = mix.reshape(grad.shape)
-    by_score[...] = ask.reshape(grad.shape)
-
-
-def query_back_kernel(*refs, chunks):
-    keys, token_t = refs[:chunks], refs[chunks : 2 * chunks]
-    grad_slot, (out, total) = refs[2 * chunks], refs[-2:]
-    step, steps = pl.program_id(0), pl.num_programs(0)
-    k, dim = keys[0].shape[1:]
-
-    @pl.when(step == 0)
+    flag[...] = jnp.zeros_like(flag)
+
+
+def rows_weights_kernel(*refs):
+    prob_slot, grad_slot, grad, query, rows = refs[:5]
+    by_key, by_value, key_sum, value_sum = refs[-4:]
+    step, part = pl.program_id(0), pl.program_id(1)
+
+    @pl.when((step == 0) & (part == 0))
+    def _():
+        key_sum[...] = jnp.zeros_like(key_sum)
+        value_sum[...] = jnp.zeros_like(value_sum)
+
+    mix, ask = weigh(prob_slot, grad_slot, grad, query)
+    left = rows[...].reshape(mix.shape)
+    key_sum[...] += mm_tn(left, ask)
+    value_sum[...] += mm_tn(left, mix)
+
+    @pl.when((step == pl.num_programs(0) - 1) & (part == pl.num_programs(1) - 1))
+    def _():
+        by_key[...] = key_sum[...].astype(BF)
+        by_value[...] = value_sum[...].astype(BF)
+
+
+def query_back_kernel(keys, token_t, grad_slot, waited, out, total):
+    del waited
+    step, part = pl.program_id(0), pl.program_id(1)
+    k, dim = keys.shape[1:]
+
+    @pl.when((step == 0) & (part == 0))
     def _():
         total[...] = jnp.zeros_like(total)
 
-    spread = head_spread(dim)
-    lanes = pl.ds(pl.multiple_of(step * LANES, LANES), LANES)
-    acc = total[...]
-    for c in range(chunks):
-        score = mm(from_lanes(grad_slot[c * k : (c + 1) * k, lanes]), spread) * 0.125
-        prod = (score * keys[c][...].reshape(-1, dim).astype(F32)).astype(BF)
-        acc = acc + mm(token_t[c][...], prod)
-    total[...] = acc
-
-    @pl.when(step == steps - 1)
+    score = mm(from_lanes(grad_slot[...]), head_spread(dim)) * 0.125
+    prod = (score * keys[...].reshape(-1, dim).astype(F32)).astype(BF)
+    total[...] += mm(token_t[...], prod)
+
+    @pl.when((step == pl.num_programs(0) - 1) & (part == pl.num_programs(1) - 1))
     def _():
         out[...] = total[...].astype(BF)
 
@@ -690,160 +816,155 @@
             jax.ShapeDtypeStruct((1, wide.shape[1]), F32),
         ),
         compiler_params=pltpu.CompilerParams(vmem_limit_bytes=24 * 1024 * 1024),
+        cost_estimate=cost(2),
         name="vector_sums",
     )(*ops)
 
 
 class SlotAttention:
-    def __init__(self, ret_rows, shard_rows, peers, slots, dim, parts):
+    split = 2
+
+    def __init__(self, ret_rows, shard_rows, peers, slots, dim):
         self.toks, self.ret = ret_rows.shape
-        chunks = parts
-        self.peers, self.slots, self.dim, self.chunks = peers, slots, dim, chunks
-        self.k = slots // chunks
-        self.sent = []
+        self.peers, self.slots, self.dim = peers, slots, dim
+        self.k = slots // self.split
         self.wanted, token, self.at_rank, self.owner = plan_slots(
             ret_rows.T, shard_rows, peers, slots
         )
-        self.codes = [self.part(token, c).reshape(-1) for c in range(chunks)]
-        self.heads = jax.ShapeDtypeStruct((slots, peers * PITCH), F32)
-
-    def part(self, array, c):
-        return array[:, c * self.k : (c + 1) * self.k]
-
-    def specs(self):
         k, dim, toks = self.k, self.dim, self.toks
-        rows = pl.BlockSpec((GROUP, k, dim), lambda g: (g, 0, 0))
-        whole = lambda *shape: pl.BlockSpec(shape, lambda g: (0,) * len(shape))
-        token = pl.BlockSpec((GROUP * k, toks), lambda g: (g, 0))
-        token_t = pl.BlockSpec((toks, GROUP * k), lambda g: (0, g))
-        lanes = lambda c: pl.BlockSpec((k, LANES), lambda g: (c, g))
-        return rows, whole, token, token_t, lanes
-
-    def call(self, kernel, name, in_specs, out_specs, out_shape, scratch=(), mib=28):
+        groups, wide = peers // GROUP, peers * PITCH
+        self.grid = (groups, self.split)
+        self.rows = pl.BlockSpec((GROUP, k, dim), lambda g, c: (g, c, 0))
+        self.lanes = pl.BlockSpec((k, LANES), lambda g, c: (c, g))
+        self.mark = pl.BlockSpec((GROUP * k, toks), lambda g, c: (c * groups + g, 0))
+        self.mark_t = pl.BlockSpec((toks, GROUP * k), lambda g, c: (0, c * groups + g))
+        self.square = self.whole(dim, dim)
+        self.heads = self.whole(slots, wide)
+        self.slot_rows = in_hbm((peers, slots, dim), BF)
+        self.slot_heads = jax.ShapeDtypeStruct((slots, wide), F32)
+        token = token.reshape(peers, self.split, k).transpose(1, 0, 2)
+        self.token, self.token_t = self.call(
+            token_marks_kernel,
+            "token_marks",
+            5,
+            [
+                pl.BlockSpec((GROUP * k, 1), lambda g, c: (c * groups + g, 0)),
+                pl.BlockSpec((1, GROUP * k), lambda g, c: (0, c * groups + g)),
+            ],
+            [self.mark, self.mark_t],
+            (in_hbm((peers * slots, toks), BF), in_hbm((toks, peers * slots), BF)),
+        )(token.reshape(-1, 1), token.reshape(1, -1))
+
+    @staticmethod
+    def whole(*shape):
+        return pl.BlockSpec(shape, lambda g, c: (0,) * len(shape))
+
+    def call(self, kernel, name, micros, in_specs, out_specs, out_shape, scratch=(), mib=28):
         return pl.pallas_call(
             kernel,
-            grid=(self.peers // GROUP,),
+            grid=self.grid,
             in_specs=in_specs,
             out_specs=out_specs,
             out_shape=out_shape,
             scratch_shapes=list(scratch),
             compiler_params=pltpu.CompilerParams(vmem_limit_bytes=mib * 1024 * 1024),
+            cost_estimate=cost(micros),
             name=name,
         )
 
     def prepare(self, cross_q):
-        toks = self.toks
-        ids = jnp.arange(1, toks + 1, dtype=jnp.int32)
-        self.token = [(code[:, None] == ids[None, :]).astype(BF) for code in self.codes]
-        self.token_t = [(ids[:, None] == code[None, :]).astype(BF) for code in self.codes]
-        shape = (self.peers, self.k, self.dim)
-        self.query = [mm(token, cross_q).astype(BF).reshape(shape) for token in self.token]
+        self.query = self.call(
+            query_rows_kernel,
+            "query_rows",
+            7,
+            [self.mark, self.whole(self.toks, self.dim)],
+            self.rows,
+            self.slot_rows,
+        )(self.token, cross_q)
 
     def forward(self, arrived, w_k, w_v, bias):
-        rows, whole, token, token_t, lanes = self.specs()
-        shape = jax.ShapeDtypeStruct((self.peers, self.k, self.dim), BF)
-        dim, toks, chunks = self.dim, self.toks, self.chunks
+        dim, toks = self.dim, self.toks
         self.arrived, self.w_k, self.w_v = arrived, w_k, w_v
-        wide = self.peers * PITCH
-        first = self.call(
+        self.keys, self.vals, scores = self.call(
             rows_in_kernel,
             "rows_in",
-            [rows, rows, whole(dim, dim), whole(dim, dim)],
-            [rows, rows, lanes(0)],
-            (shape, shape, jax.ShapeDtypeStruct((self.k, wide), F32)),
-        )
-        got = [first(part, query, w_k, w_v) for part, query in zip(arrived, self.query)]
-        self.keys, self.vals, scores = zip(*got)
+            22,
+            [self.rows, self.rows, self.square, self.square],
+            [self.rows, self.rows, self.lanes],
+            (self.slot_rows, self.slot_rows, self.slot_heads),
+        )(from_hbm(arrived), from_hbm(self.query), w_k, w_v)
+        entries = (self.ret * PITCH, toks)
         self.prob_tok, self.prob_slot, mixed = self.call(
-            functools.partial(attend_kernel, chunks=chunks),
+            attend_kernel,
             "attend",
-            [whole(self.k, wide)] * chunks
-            + [rows] * chunks
-            + [token_t] * chunks
-            + [whole(*self.at_rank.shape), whole(*self.owner.shape), whole(1, dim)],
-            [whole(self.ret * PITCH, toks), whole(self.slots, wide), whole(toks, dim)],
+            11,
+            [self.heads, self.rows, self.mark_t]
+            + [self.whole(*self.at_rank.shape), self.whole(*self.owner.shape), self.whole(1, dim)],
+            [self.whole(*entries), self.heads, self.whole(toks, dim)],
             (
-                jax.ShapeDtypeStruct((self.ret * PITCH, toks), F32),
-                self.heads,
+                jax.ShapeDtypeStruct(entries, F32),
+                self.slot_heads,
                 jax.ShapeDtypeStruct((toks, dim), BF),
             ),
             [pltpu.VMEM((toks, dim), F32)],
-        )(*scores, *self.vals, *self.token_t, self.at_rank, self.owner, bias.reshape(1, dim))
+        )(scores, from_hbm(self.vals), self.token_t, self.at_rank, self.owner, bias.reshape(1, dim))
         return mixed
 
     def backward(self, grad):
-        rows, whole, token, token_t, lanes = self.specs()
-        shape = jax.ShapeDtypeStruct((self.peers, self.k, self.dim), BF)
-        dim, toks, chunks = self.dim, self.toks, self.chunks
-        wide = self.peers * PITCH
-        *grads, self.grad_slot = self.call(
-            functools.partial(attend_back_kernel, chunks=chunks),
+        dim, toks = self.dim, self.toks
+        grads, self.grad_slot = self.call(
+            attend_back_kernel,
             "attend_back",
-            [rows] * chunks
-            + [token] * chunks
-            + [whole(toks, dim), whole(self.ret * PITCH, toks)]
-            + [whole(*self.at_rank.shape), whole(*self.owner.shape)],
-            [rows] * chunks + [whole(self.slots, wide)],
-            [shape] * chunks + [self.heads],
-            [pltpu.VMEM((self.slots, wide), F32)],
-        )(*self.vals, *self.token, grad, self.prob_tok, self.at_rank, self.owner)
-        self.grads = grads
-
-    def send(self, c, after=()):
-        rows, whole, _, _, lanes = self.specs()
-        shape = jax.ShapeDtypeStruct((self.peers, self.k, self.dim), BF)
-        dim = self.dim
-        got = self.call(
+            13,
+            [self.rows, self.mark, self.whole(toks, dim), self.whole(self.ret * PITCH, toks)]
+            + [self.whole(*self.at_rank.shape), self.whole(*self.owner.shape)],
+            [self.rows, self.heads],
+            (self.slot_rows, self.slot_heads),
+            [pltpu.VMEM(self.slot_heads.shape, F32)],
+        )(from_hbm(self.vals), self.token, grad, self.prob_tok, self.at_rank, self.owner)
+        self.factors = (self.prob_slot, self.grad_slot, from_hbm(grads), from_hbm(self.query))
+        self.factor_specs = [self.lanes, self.lanes, self.rows, self.rows]
+        sent, self.flag = self.call(
             rows_out_kernel,
             "rows_out",
-            [lanes(c), lanes(c), rows, rows, whole(dim, dim), whole(dim, dim)]
-            + [WAIT] * len(after),
-            [rows, rows, rows],
-            (shape, shape, shape),
-        )(
-            self.prob_slot,
-            self.grad_slot,
-            self.grads[c],
-            self.query[c],
-            self.w_k,
-            self.w_v,
-            *after,
-        )
-        self.sent.append(got)
-        return got[0]
-
-    def finish(self):
-        rows, whole, token, token_t, lanes = self.specs()
-        dim, toks, chunks = self.dim, self.toks, self.chunks
-        grad_q = self.call(
-            functools.partial(query_back_kernel, chunks=chunks),
+            28,
+            self.factor_specs + [self.square, self.square],
+            [self.rows, self.whole(8, LANES)],
+            (self.slot_rows, jax.ShapeDtypeStruct((8, LANES), F32)),
+        )(*self.factors, self.w_k, self.w_v)
+        return sent
+
+    def query_grad(self):
+        dim, toks = self.dim, self.toks
+        return self.call(
+            query_back_kernel,
             "query_back",
-            [rows] * chunks
-            + [token_t] * chunks
-            + [whole(self.slots, self.peers * PITCH), WAIT],
-            whole(toks, dim),
+            7,
+            [self.rows, self.mark_t, self.lanes, self.whole(8, LANES)],
+            self.whole(toks, dim),
             jax.ShapeDtypeStruct((toks, dim), BF),
             [pltpu.VMEM((toks, dim), F32)],
-        )(*self.keys, *self.token_t, self.grad_slot, self.sent[0][0])
-
-        def product(parts):
-            flat = lambda x: x.reshape(-1, dim)
-            both = [mm_tn(flat(a), flat(b)) for a, b in zip(self.arrived, parts)]
-            return functools.reduce(jnp.add, both).astype(BF)
-
-        _, by_prob, by_score = zip(*self.sent)
-        return grad_q, product(by_score), product(by_prob)
+        )(from_hbm(self.keys), self.token_t, self.grad_slot, self.flag)
+
+    def weights(self, after):
+        square = (self.dim, self.dim)
+        return self.call(
+            rows_weights_kernel,
+            "rows_weights",
+            24,
+            self.factor_specs + [self.rows] + [WAIT] * len(after),
+            [self.square, self.square],
+            (jax.ShapeDtypeStruct(square, BF), jax.ShapeDtypeStruct(square, BF)),
+            [pltpu.VMEM(square, F32), pltpu.VMEM(square, F32)],
+        )(*self.factors, from_hbm(self.arrived), *after)
 
 
 class GatheredAttention:
-    def __init__(self, ret_rows, shard_rows, peers, slots, dim, parts):
+    def __init__(self, ret_rows, shard_rows, peers, slots, dim):
         self.toks, self.ret = ret_rows.shape
         self.dim, self.slots = dim, slots
         self.place, self.wanted, self.entry = plan_requests(ret_rows, shard_rows, peers, slots)
         self.fwd, self.bwd, self.back_q = cross_calls(self.toks, self.ret, dim)
-
-    def part(self, array, c):
-        return array
 
     def prepare(self, cross_q):
         self.cross_q = cross_q
@@ -855,7 +976,7 @@
         self.query_keys = jnp.einsum(
             "the,dhe->htd", query, self.key_heads, preferred_element_type=F32
         ).astype(BF)
-        self.fetched = arrived[0].reshape(-1, dim)[self.place]
+        self.fetched = arrived.reshape(-1, dim)[self.place]
         self.state_mix, self.cross_p = self.fwd(self.query_keys, self.fetched)
         mixed = jnp.einsum(
             "htd,dhe->the", self.state_mix, self.val_heads, preferred_element_type=F32
@@ -867,22 +988,23 @@
         grad_mix = jnp.einsum(
             "the,dhe->htd", self.grad, self.val_heads, preferred_element_type=F32
         ).astype(BF)
-        self.rows, self.grad_s = self.bwd(self.query_keys, grad_mix, self.fetched, self.cross_p)
-
-    def send(self, c, after=()):
-        return self.rows[self.entry]
-
-    def finish(self):
-        toks, dim = self.toks, self.dim
-        grad_qk = self.back_q(self.grad_s, self.fetched)
-        grad_q = jnp.einsum("htd,dhe->the", grad_qk, self.key_heads, preferred_element_type=F32)
-
+        rows, self.grad_s = self.bwd(self.query_keys, grad_mix, self.fetched, self.cross_p)
+        return rows[self.entry]
+
+    def query_grad(self):
+        self.grad_qk = self.back_q(self.grad_s, self.fetched)
+        grad_q = jnp.einsum(
+            "htd,dhe->the", self.grad_qk, self.key_heads, preferred_element_type=F32
+        )
+        return grad_q.reshape(self.toks, self.dim).astype(BF)
+
+    def weights(self, after):
         def product(left, right):
             got = jnp.einsum("htd,the->dhe", left, right, preferred_element_type=F32)
-            return got.reshape(dim, dim).astype(BF)
-
-        grad_k = product(grad_qk, self.cross_q.reshape(toks, H, HD))
-        return grad_q.reshape(toks, dim).astype(BF), grad_k, product(self.state_mix, self.grad)
+            return got.reshape(self.dim, self.dim).astype(BF)
+
+        grad_k = product(self.grad_qk, self.cross_q.reshape(self.toks, H, HD))
+        return grad_k, product(self.state_mix, self.grad)
 
 
 def store_sum_kernel(asked, returned, *refs, block, added):
@@ -911,6 +1033,7 @@
         out_shape=jax.ShapeDtypeStruct((shard_rows, dim), F32),
         input_output_aliases={2: 0} if before else {},
         compiler_params=pltpu.CompilerParams(vmem_limit_bytes=VMEM_LIMIT),
+        cost_estimate=cost(25),
         name="store_sum",
     )(asked.reshape(1, count), returned, *before, *after)
 
@@ -947,95 +1070,85 @@
     n_row_bits = n_rows.bit_length() - 1
     n_far = n_row_bits - 2
     by_rows = n_cols == 2 and rb % 16 == 0 and cb % 128 == 0
+    orders = (order_a, order_b, order_a, order_b)
+    shapes = ((rb, cb), (rb, cb), (rb, 4 * cb), (4 * rb, cb))
+    counts = (4, 4, 1, 1)
     if by_rows:
         col = lax.axis_index("col").astype(jnp.int32)[None]
         place_a = jnp.concatenate([block_of_row(order_a, n_rows), col])
         place_b = jnp.concatenate([block_of_row(order_b, n_rows), col])
-
-    parts = 2
+        places = (place_a, place_b, place_a, place_b)
+
     in_slots = (
-        slots % (16 * parts) == 0
+        by_rows
+        and slots % (16 * SlotAttention.split) == 0
         and peers % GROUP == 0
         and tok_count % LANES == 0
         and tok_count <= 256
         and shard_rows & (shard_rows - 1) == 0
         and H <= PITCH
     )
-    parts = parts if in_slots else 1
     attention = (SlotAttention if in_slots else GatheredAttention)(
-        ret_rows, shard_rows, peers, slots, dim, parts
-    )
+        ret_rows, shard_rows, peers, slots, dim
+    )
+
     def vector_rows(parts):
         parts = [jnp.pad(part, ((0, 0), (0, cb - part.shape[1]))) for part in parts]
         return jnp.pad(jnp.concatenate(parts, axis=0), ((0, 2), (0, 0)))
 
     small = vector_rows([biases, ln_gain, ln_shift, ff_bias.reshape(1, -1)])
-    cut = 8 * rb + small.shape[0]
-    side_a, side_b = join(attn_in, attn_out, small, ff_in, ff_out)
-    side_a, side_b = gather_bits(side_a, order_a[:n_far]), gather_bits(side_b, order_b[:n_far])
+    packs = [*join(attn_in, attn_out, small, attention.wanted), ff_in[None], ff_out[None]]
+    packs = [gather_bits(p, order[:1]) for p, order in zip(packs, orders)]
     asked = all_to_all(attention.wanted)
-
-    answers = [
-        enc_store[jnp.maximum(attention.part(asked, c) - 1, 0)] for c in range(parts)
-    ]
-    if by_rows:
-        answers[0] = hold(answers[0], [side_a, side_b])
-    side_a = gather_bits(side_a, order_a[n_far : n_far + 1])
-    side_b = gather_bits(side_b, order_b[n_far : n_far + 1])
-    arrived = [all_to_all(answers[0])]
-    for c in range(1, parts):
+    asked = tie(asked, packs) if by_rows else asked
+    packs = [gather_bits(p, order[1:n_far]) for p, order in zip(packs, orders)]
+
+    answer = enc_store[jnp.maximum(asked - 1, 0)]
+    for i in range(2):
+        packs[i] = gather_bits(packs[i], orders[i][n_far : n_far + 1])
+    arrived = all_to_all(hold(answer, packs) if by_rows else answer)
+    if in_slots:
+        packs[0] = hold(packs[0], [attention.token, attention.token_t])
+    extras = (0, small.shape[0], 0, 0)
+
+    def whole(i, after=()):
+        done = n_far + 1
         if by_rows:
-            side_a = hold(side_a, [answers[c]])
-            side_b = hold(side_b, [answers[c]])
-            answers[c] = hold(answers[c], arrived[-1:])
-        arrived.append(all_to_all(answers[c]))
-    if by_rows:
-        side_a = gather_bits(side_a, order_a[n_far + 1 : n_row_bits])
-        side_b = gather_bits(side_b, order_b[n_far + 1 : n_row_bits])
-        other_a, other_b = swap_bit(side_a, "col", 1), swap_bit(side_b, "col", 1)
-        tile = (rb, cb)
-        mats, small_all = unpack(side_a, other_a, place_a, 8, tile, extra=small.shape[0])
-        w_ff1 = unpack(side_b, other_b, place_b, 4, tile, beside=True)[0]
-        w_ff2 = unpack(side_b, other_b, place_b, 1, (4 * rb, cb), first=4 * rb)[0]
-    else:
-        side_a = gather_bits(side_a, order_a[n_far + 1 :])
-        side_b = gather_bits(side_b, order_b[n_far + 1 :])
-        mats, small_all = unpack_any(side_a, order_a, n_rows, n_cols, rb)
-        mats = mats.transpose(2, 0, 3, 1, 4).reshape(8, dim, dim)
-        ff_blocks, _ = unpack_any(side_b, order_b, n_rows, n_cols, rb)
-        w_ff1 = ff_blocks[:, :, :4].transpose(0, 3, 1, 2, 4).reshape(dim, 4 * dim)
-        w_ff2 = ff_blocks[:, :, 4:].transpose(0, 2, 3, 1, 4).reshape(4 * dim, dim)
-    w_q, w_k, w_v, w_cq, w_ck, w_cv, w_o, w_co = (mats[i] for i in range(8))
+            own = gather_bits(packs[i], orders[i][done:n_row_bits])
+            other = swap_bit(own, "col", 1)
+            other = hold(other, after) if after else other
+            return unpack(own, other, places[i], counts[i], shapes[i], extras[i])
+        blocks = gather_bits(packs[i], orders[i][done:])
+        return unpack_any(blocks, orders[i], counts[i], shapes[i], extras[i], n_rows, n_cols)
+
+    mats = [whole(0), whole(1)]
+    w_q, w_k, w_v = (mats[0][i] for i in range(3))
+    w_ck, w_cv, w_o, w_co = (mats[1][0][i] for i in range(4))
+    small_all = mats[1][1]
     small_all = small_all.astype(F32)
     vectors = small_all[:, :13, :rb].transpose(1, 0, 2).reshape(13, dim)
     bias_all, gain_all, shift_all = vectors[:7], vectors[7:10], vectors[10:]
     bias_ff = small_all[:, 13, : ff_bias.size].reshape(-1)
 
-    def heads(array):
-        return array.reshape(tok_count, H, HD)
-
-    queries = heads((mm(tokens, w_q) + bias_all[0]).astype(BF))
-    key_rows = heads(mm(tokens, w_k).astype(BF))
-    values = heads((mm(tokens, w_v) + bias_all[1]).astype(BF))
-    visible = visible_mask(seg_ids[0], live_mask[0])
-    scores = jnp.einsum("qhd,khd->hqk", queries, key_rows, preferred_element_type=F32) * 0.125
-    probs = jax.nn.softmax(jnp.where(visible[None], scores, -1e30), axis=-1)
-    probs_low = probs.astype(BF)
-    mixed = jnp.einsum("hqk,khd->qhd", probs_low, values, preferred_element_type=F32)
-    mixed = mixed.reshape(tok_count, dim).astype(BF)
-    branch = mm(mixed, w_o) + bias_all[2]
-    first, first_norm, first_scale = norm_fwd(
-        tokens.astype(F32) + branch, gain_all[0], shift_all[0]
+    *qkv, mixed, first, first_norm, first_scale, cross_q = self_fwd(
+        tokens, seg_ids, live_mask, mats[0], w_o, bias_all, gain_all, shift_all
     )
     first_low = first.astype(BF)
-    cross_q = (mm(first_low, w_cq) + bias_all[3]).astype(BF)
 
     attention.prepare(cross_q)
+    if in_slots:
+        for i in (2, 3):
+            packs[i] = gather_bits(packs[i], orders[i][n_far : n_far + 1])
+    else:
+        for i in (2, 3):
+            packs[i] = gather_bits(packs[i], orders[i][n_far : n_far + 1])
     cross_low = attention.forward(arrived, w_ck, w_cv, bias_all[4])
     branch_two = mm(cross_low, w_co) + bias_all[5]
     second, second_norm, second_scale = norm_fwd(first + branch_two, gain_all[1], shift_all[1])
     second_low = second.astype(BF)
 
+    after = [attention.query] if in_slots else []
+    w_ff1, w_ff2 = whole(2, after)[0], whole(3, after)[0]
     hidden_act, hidden_slope = gelu_parts(mm(second_low, w_ff1) + bias_ff)
     hidden_low = hidden_act.astype(BF)
     branch_ffn = mm(hidden_low, w_ff2) + bias_all[6]
@@ -1049,38 +1162,42 @@
     grad_two = norm_back(grad_second, second_norm, second_scale, gain_all[1])
     grad_o2 = grad_two.astype(BF)
     grad_cmix = mm_nt(grad_o2, w_co).astype(BF)
-    attention.backward(grad_cmix)
-    send_back = [attention.send(0)]
+    send_back = attention.backward(grad_cmix)
+    returned = all_to_all(send_back)
 
     def packed(order, place, mats, small=None, after=()):
         if by_rows:
             return pack(mats, place, small, after)
         return pack_any(mats, order[::-1], small, n_rows, n_cols)
 
+    def on_both(pairs, start, stop):
+        return [
+            scatter_bits(*pair, back[start:stop]) for pair, back in zip(pairs, (back_a, back_b))
+        ]
+
     tile = (rb, cb)
     near = len(order_a) - n_far
     back_a, back_b = order_a[::-1], order_b[::-1]
     at_a, at_b = (place_a, place_b) if by_rows else (None, None)
-    send_back += [attention.send(c, send_back) for c in range(1, parts)]
-    grad_cq, grad_wk, grad_wv = attention.finish()
+    grad_cq = attention.query_grad()
     ff = [
         (order_a, at_a, [((second_low, grad_pre), tile, 4)]),
         (order_b, at_b, [((hidden_low, grad_y), (4 * rb, cb), 1)]),
     ]
     ff = [packed(*part, None, [grad_cq]) for part in ff]
-    grad_first = grad_two + mm_nt(grad_cq, w_cq)
-    grad_one = norm_back(grad_first, first_norm, first_scale, gain_all[0])
-    grad_o = grad_one.astype(BF)
-    grad_mix = heads(mm_nt(grad_o, w_o).astype(BF))
-    grad_probs = jnp.einsum("qhd,khd->hqk", grad_mix, values, preferred_element_type=F32)
-    grad_v = jnp.einsum("hqk,qhd->khd", probs_low, grad_mix, preferred_element_type=F32)
-    grad_scores = (
-        probs * (grad_probs - jnp.sum(probs * grad_probs, axis=-1, keepdims=True))
-    ).astype(BF)
-    grad_q = jnp.einsum("hqk,khd->qhd", grad_scores, key_rows, preferred_element_type=F32) * 0.125
-    grad_k = jnp.einsum("hqk,qhd->khd", grad_scores, queries, preferred_element_type=F32) * 0.125
-    grad_q, grad_k, grad_v = (
-        part.reshape(tok_count, dim).astype(BF) for part in (grad_q, grad_k, grad_v)
+    if by_rows:
+        grad_cq = hold(grad_cq, [x for pair in ff for x in pair])
+    grad_first, grad_one, grad_o, grad_q, grad_k, grad_v = self_bwd(
+        grad_cq,
+        grad_two,
+        first_norm,
+        first_scale,
+        gain_all,
+        qkv,
+        seg_ids,
+        live_mask,
+        mats[0],
+        w_o,
     )
     grad_tokens = (
         grad_one + mm_nt(grad_q, w_q) + mm_nt(grad_k, w_k) + mm_nt(grad_v, w_v)
@@ -1108,6 +1225,9 @@
             ((first_low, grad_cq), tile, 1),
         ],
     )
+    ff = on_both(ff, 0, near - 2)
+    before = [*attn_one, ff[0][1], ff[1][1]] if in_slots else []
+    grad_wk, grad_wv = attention.weights(before)
     attn_two = packed(
         order_b,
         at_b,
@@ -1119,38 +1239,17 @@
         ],
         grad_small,
     )
+    def join_pairs(pairs):
+        return tuple(jnp.concatenate(both, axis=1) for both in zip(*pairs))
+
+    ff = join_pairs(on_both(ff, near - 2, near))
+    attn = join_pairs(on_both([attn_one, attn_two], 0, near))
+    grad_store = store_sum(asked, returned.reshape(-1, dim), shard_rows, None)
     if by_rows:
-        send_back[1:] = [hold(part, [*attn_one, *attn_two]) for part in send_back[1:]]
-    returned = [all_to_all(part) for part in send_back]
-
-    def stored(c, so_far, after):
-        rows = returned[c].reshape(-1, dim)
-        return store_sum(attention.part(asked, c), rows, shard_rows, so_far, after)
-
-    def join_pairs(one, two):
-        return tuple(jnp.concatenate(both, axis=1) for both in zip(one, two))
-
-    ff = [scatter_bits(*part, back[:near]) for part, back in zip(ff, (back_a, back_b))]
-    ff = join_pairs(*ff)
-    def behind(pair, array):
-        return (hold(pair[0], [array]), pair[1]) if by_rows else pair
-
-    attn = [
-        scatter_bits(*part, back[: near - 2])
-        for part, back in zip((attn_one, attn_two), (back_a, back_b))
-    ]
-    grad_store = None
-    for c in range(parts - 1):
-        grad_store = stored(c, grad_store, ())
-        attn = [behind(pair, grad_store) for pair in attn]
-    attn = [
-        scatter_bits(*part, back[near - 2 : near]) for part, back in zip(attn, (back_a, back_b))
-    ]
-    grad_store = stored(parts - 1, grad_store, ())
-    attn = behind(join_pairs(*attn), grad_store)
+        ff, attn = ((hold(keep, [grad_store]), send) for keep, send in (ff, attn))
+    ff, attn = (scatter_bits(*pair, back_a[near:-1]) for pair in (ff, attn))
     total_a, total_b = (
-        (keep + swap_bit(send, *order_a[0]))[0].astype(F32)
-        for keep, send in (scatter_bits(*pair, back_a[near:-1]) for pair in (attn, ff))
+        (keep + swap_bit(send, *order_a[0]))[0].astype(F32) for keep, send in (attn, ff)
     )
 
     sum_small = total_a[8 * rb :]

time: 734 us -> 699 us (0.952)
  Pallas kernels: 137 us -> 200 us
  matrix products: 77.4 us -> 17.8 us
  local copies, waits for them, and re-layouts: 128 us -> 104 us
  other arithmetic: 54.2 us -> 34 us
  starting transfers between devices: 57.2 us -> 67.8 us
    pallas_call x8 -> x12, Pallas kernels: 75 us -> 140 us  [the longest x1 28.4 us: backward(): self.call(rows_out_kernel, 'rows_out', 28, self.factor_specs + [self.squa...]
    all_to_all x5 -> x3, waiting for transfers between devices: 46.6 us -> 0.01 us  [all_to_all(): return lax.all_to_all(array, RANKS, split_axis=0, concat_axis=0, tiled=True)]
    ppermute x26 -> x36, waiting for transfers between devices: 223 us -> 266 us  [swap_bit(): return lax.ppermute(array, axis, pairs)]
    dot_general x9 -> x0, matrix products: 36.5 us -> none  [the longest x4 26.1 us: mm_tn(): lax.dot_general(a, b, (((0,), (0,)), ((), ())), preferred_element_type=F32)]
    unnamed x317 -> x296, local copies, waits for them, and re-layouts: 73.2 us -> 49.8 us
    ppermute x26 -> x36, starting transfers between devices: 29 us -> 46 us  [swap_bit(): return lax.ppermute(array, axis, pairs)]
    dot_general x10 -> x3, matrix products: 21.5 us -> 5.74 us  [mm(): return jnp.dot(a, b, preferred_element_type=F32)]
    convert_element_type x5 -> x0, local copies, waits for them, and re-layouts: 7.76 us -> none  [the longest x3 5.91 us: on_device(): part.reshape(tok_count, dim).astype(BF)]
  transfers between devices with their start and end apart: 31 -> 39, of which waited for: 14 -> 16; matrix products, arithmetic and copies ran while one was open for 23% -> 15% of each run, Pallas kernels for 13% -> 17%
where the time goes in v3:
time: 699 us; the launch traced here: 692 us
  waiting for transfers between devices  266 us (38%)
  Pallas kernels  200 us (29%)
  local copies, waits for them, and re-layouts  104 us (15%)
  starting transfers between devices  67.8 us (10%)
  other arithmetic  34 us (5%)
  matrix products  17.8 us (3%)
    ppermute x36, waiting for transfers between devices, swap_bit(): return lax.ppermute(array, axis, pairs)  266 us
    unnamed x296, local copies, waits for them, and re-layouts  49.8 us
    ppermute x36, starting transfers between devices, swap_bit(): return lax.ppermute(array, axis, pairs)  46 us
    pallas_call x1, Pallas kernels, backward(): self.call(rows_out_kernel, 'rows_out', 28, self.factor_specs + [self.squa...  28.4 us
    gather x1, local copies, waits for them, and re-layouts, on_device(): answer = enc_store[jnp.maximum(asked - 1, 0)]  26.3 us
    pallas_call x1, Pallas kernels, store_sum(): pl.pallas_call(functools.partial(store_sum_kernel, block=block, added=so_...  25.4 us
    pallas_call x1, Pallas kernels, weights(): self.call(rows_weights_kernel, 'rows_weights', 24, self.factor_specs + [s...  24.2 us
    pallas_call x1, Pallas kernels, forward(): self.call(rows_in_kernel, 'rows_in', 22, [self.rows, self.rows, self.squa...  22.6 us
  transfers between devices with their start and end apart: 39, of which 16 were waited for; matrix products, arithmetic and copies ran while one was open for 15% of the time, Pallas kernels for 17%

profile of v3, /device:TPU:0, one launch (start us, length us, event | category | flops | bytes accessed | tf_op | source)
XLA Modules:
  0.0 692.2 jit_solution(18158423663298977285)
XLA Ops:
  4.9 4.4 plan.1
  10.7 6.1 all-to-all-start
  41.4 26.3 %gather_fusion.2 = bf16[6144,768]{1,0:T(8,128)(2,1)} fusion(bf16[2048,768]{1,0:T(8,128)(2,1)S(1)} %copy-done, s32[6144]{0:T(1024)S(1)} %broadcast_clamp_fusion), kind=kCustom, calls=%fused_computation.2 | custom fusion | bytes 18898944 | tf_op jit(solution)/shard_map/gather | solution.py:1106
  79.2 4.5 collective-permute-done.2
  89.3 5.0 all-to-all-start.1
  99.5 4.7 token_marks.1
  109.2 91.9 %collective-permute-done.8 = bf16[8,208,384]{2,1,0:T(8,128)(2,1)} collective-permute-done((bf16[8,208,384]{2,1,0:T(8,128)(2,1)}, bf16[8,208,384]{2,1,0:T(8,128)(2,1)}, u32[]{:S(2)}, u32[]{:S(2)}) %collective-permute-start.8) | collective-permute-done | bytes 1277984 | tf_op jit(solution)/shard_map/ppermute | solution.py:67
  203.6 11.6 %collective-permute-done.3 = bf16[8,192,384]{2,1,0:T(8,128)(2,1)} collective-permute-done((bf16[8,192,384]{2,1,0:T(8,128)(2,1)}, bf16[8,192,384]{2,1,0:T(8,128)(2,1)}, u32[]{:S(2)}, u32[]{:S(2)}) %collective-permute-start.3) | collective-permute-done | bytes 1179680 | tf_op jit(solution)/shard_map/ppermute | solution.py:67
  217.5 9.6 %collective-permute-done.17 = bf16[4,192,384]{2,1,0:T(8,128)(2,1)S(1)} collective-permute-done((bf16[4,192,384]{2,1,0:T(8,128)(2,1)}, bf16[4,192,384]{2,1,0:T(8,128)(2,1)S(1)}, u32[]{:S(2)}, u32[]{:S(2)}) %collective-permute-start.17) | collective-permute-done | bytes 589856 | tf_op jit(solution)/shard_map/ppermute | solution.py:67
  236.6 25.7 %collective-permute-done.18 = bf16[8,192,384]{2,1,0:T(8,128)(2,1)S(1)} collective-permute-done((bf16[8,192,384]{2,1,0:T(8,128)(2,1)S(1)}, bf16[8,192,384]{2,1,0:T(8,128)(2,1)S(1)}, u32[]{:S(2)}, u32[]{:S(2)}) %collective-permute-start.18) | collective-permute-done | bytes 1179680 | tf_op jit(solution)/shard_map/ppermute | solution.py:67
  283.7 4.7 self_fwd.1
  288.5 7.0 %query_rows.1.query.refs_1_.refs_3_ = bf16[32,192,768]{2,1,0:T(8,128)(2,1)} custom-call(bf16[6144,256]{1,0:T(8,128)(2,1)S(1)} %copy-done.16, bf16[256,768]{1,0:T(8,128)(2,1)S(1)} %get-tuple-element.66.query), custom_call_target="tpu_custom_call" | custom-call | flops 7699999744 | tf_op jit(solution)/shard_map/query_rows/pallas_call | solution.py:876
  309.1 22.6 %rows_in.1 = (bf16[32,192,768]{2,1,0:T(8,128)(2,1)}, bf16[32,192,768]{2,1,0:T(8,128)(2,1)}, f32[192,512]{1,0:T(8,128)S(1)}) custom-call(bf16[32,192,768]{2,1,0:T(8,128)(2,1)} %all-to-all-done.1.arrived.refs_4_, bf16[32,192,768]{2,1,0:T(8,128)(2,1)} %query_rows.1.query.refs_1_.refs_3_, bf16[768,768]{1,0:T(8,128)(2,1)S(1)} %copy-done.48, ...), custom_call_target="tpu_custom_call" | custom-call | flops 24199999488 | tf_op jit(solution)/shard_map/rows_in/pallas_call | solution.py:888
  331.7 13.5 %attend.1 = (f32[256,256]{1,0:T(8,128)S(1)}, f32[192,512]{1,0:T(8,128)S(1)}, bf16[256,768]{1,0:T(8,128)(2,1)S(1)}) custom-call(f32[192,512]{1,0:T(8,128)S(1)} %get-tuple-element.67.scores, bf16[32,192,768]{2,1,0:T(8,128)(2,1)} %get-tuple-element.68.vals, bf16[256,6144]{1,0:T(8,128)(2,1)S(1)} %copy-done.14, bf16[256,4096]{1,0:T(8,128)(2,1)S(1)} %copy-done.82, ...), custom_call_target="tpu_custom_call" | custom-call | flops 12099999744 | tf_op jit(solution)/shard_map/attend/pallas_call | solution.py:897
  361.3 17.0 %attend_back.1 = (bf16[32,192,768]{2,1,0:T(8,128)(2,1)}, f32[192,512]{1,0:T(8,128)S(1)}) custom-call(bf16[32,192,768]{2,1,0:T(8,128)(2,1)} %get-tuple-element.68.vals, bf16[6144,256]{1,0:T(8,128)(2,1)S(1)} %copy-done.17, bf16[256,768]{1,0:T(8,128)(2,1)S(1)} %convolution_convert_fusion.grad.refs_4_, f32[256,256]{1,0:T(8,128)S(1)} %get-tuple-element.73.prob_tok, ...), custom_call_target="tpu_custom_call" | custom-call | flops 14300000256 | tf_op jit(solution)/shard_map/attend_back/pallas_call | solution.py:915
  378.3 28.4 %rows_out.1 = (bf16[32,192,768]{2,1,0:T(8,128)(2,1)}, f32[8,128]{1,0:T(8,128)S(1)}) custom-call(f32[192,512]{1,0:T(8,128)S(1)} %get-tuple-element.75.prob_slot.refs_0_, f32[192,512]{1,0:T(8,128)S(1)} %get-tuple-element.74.grad_slot.refs_1_, bf16[32,192,768]{2,1,0:T(8,128)(2,1)} %get-tuple-element.76.grad.refs_2_, ...), custom_call_target="tpu_custom_call" | custom-call | flops 30799998976 | tf_op jit(solution)/shard_map/rows_out/pallas_call | solution.py:927
  407.3 10.7 %all-to-all-start.2 = ((bf16[32,192,768]{2,1,0:T(8,128)(2,1)}), bf16[32,192,768]{2,1,0:T(8,128)(2,1)}, u32[]{:S(2)}, u32[]{:S(2)}) async-start(bf16[32,192,768]{2,1,0:T(8,128)(2,1)} %get-tuple-element.91), calls=%async_computation.2 | async-start | bytes 18874368 | tf_op jit(solution)/shard_map/all_to_all | solution.py:1042
  419.7 9.7 %query_back.1.refs_2_.refs_0_ = bf16[256,768]{1,0:T(8,128)(2,1)S(1)} custom-call(bf16[32,192,768]{2,1,0:T(8,128)(2,1)} %get-tuple-element.72.keys, bf16[256,6144]{1,0:T(8,128)(2,1)S(1)} %copy-done.15, f32[192,512]{1,0:T(8,128)S(1)} %copy-done.90, f32[8,128]{1,0:T(8,128)S(1)} %copy-done.98), custom_call_target="tpu_custom_call" | custom-call | flops 7699999744 | tf_op jit(solution)/shard_map/query_back/pallas_call | solution.py:939
  429.4 4.2 pack.5
  433.9 4.2 pack.4
  451.5 5.6 self_bwd.1
  463.1 4.2 pack.6
  474.8 24.2 %rows_weights.1 = (bf16[768,768]{1,0:T(8,128)(2,1)S(1)}, bf16[768,768]{1,0:T(8,128)(2,1)S(1)}) custom-call(f32[192,512]{1,0:T(8,128)S(1)} %copy-done.95, f32[192,512]{1,0:T(8,128)S(1)} %copy-done.91, bf16[32,192,768]{2,1,0:T(8,128)(2,1)} %get-tuple-element.76.grad.refs_2_, bf16[32,192,768]{2,1,0:T(8,128)(2,1)} %query_rows.1.query.refs_1_.refs_3_, ...), custom_call_target="tpu_custom_call" | custom-call | flops 26400000000 | tf_op jit(solution)/shard_map/rows_weights/pallas_call | solution.py:951
  499.1 4.1 pack.7
  516.6 40.2 %collective-permute-done.32 = bf16[8,192,384]{2,1,0:T(8,128)(2,1)S(1)} collective-permute-done((bf16[8,192,384]{2,1,0:T(8,128)(2,1)}, bf16[8,192,384]{2,1,0:T(8,128)(2,1)S(1)}, u32[]{:S(2)}, u32[]{:S(2)}) %collective-permute-start.32) | collective-permute-done | bytes 1179680 | tf_op jit(solution)/shard_map/ppermute | solution.py:67
  560.0 23.7 %collective-permute-done.21 = bf16[8,192,384]{2,1,0:T(8,128)(2,1)S(1)} collective-permute-done((bf16[8,192,384]{2,1,0:T(8,128)(2,1)S(1)}, bf16[8,192,384]{2,1,0:T(8,128)(2,1)S(1)}, u32[]{:S(2)}, u32[]{:S(2)}) %collective-permute-start.21) | collective-permute-done | bytes 1179680 | tf_op jit(solution)/shard_map/ppermute | solution.py:67
  584.0 23.8 %collective-permute-done.33 = bf16[4,192,384]{2,1,0:T(8,128)(2,1)S(1)} collective-permute-done((bf16[4,192,384]{2,1,0:T(8,128)(2,1)S(1)}, bf16[4,192,384]{2,1,0:T(8,128)(2,1)S(1)}, u32[]{:S(2)}, u32[]{:S(2)}) %collective-permute-start.33) | collective-permute-done | bytes 589856 | tf_op jit(solution)/shard_map/ppermute | solution.py:67
  608.1 4.5 collective-permute-done.31
  613.5 7.1 %collective-permute-start.34 = (bf16[2,384,384]{2,1,0:T(8,128)(2,1)}, bf16[2,384,384]{2,1,0:T(8,128)(2,1)}, u32[]{:S(2)}, u32[]{:S(2)}) collective-permute-start(bf16[2,384,384]{2,1,0:T(8,128)(2,1)} %pad_maximum_fusion.10), channel_id=1, source_target_pairs={{0,8},{2,10},{4,12},{6,14},{8,0},{10,2},{12,4},{14,6},{16,24},{18,... | collective-permute-start | bytes 1769480 | tf_op jit(solution)/shard_map/ppermute | solution.py:67
  625.5 9.3 %collective-permute-start.28 = (bf16[2,400,384]{2,1,0:T(8,128)(2,1)S(1)}, bf16[2,400,384]{2,1,0:T(8,128)(2,1)S(1)}, u32[]{:S(2)}, u32[]{:S(2)}) collective-permute-start(bf16[2,400,384]{2,1,0:T(8,128)(2,1)S(1)} %pad_maximum_fusion.5), channel_id=1, source_target_pairs={{0,8},{2,10},{4,12},{6,14},{8,0},{10,2},{12,4},{14,6},{16,24},{18,... | collective-permute-start | bytes 1843208 | tf_op jit(solution)/shard_map/ppermute | solution.py:67
  634.8 25.4 %store_sum.1.refs_1_ = f32[2048,768]{1,0:T(8,128)} custom-call(s32[1,6144]{1,0:T(1,128)} %reshape.150.asked, bf16[6144,768]{1,0:T(8,128)(2,1)} %bitcast.19.returned), custom_call_target="tpu_custom_call" | custom-call | flops 27499999232 | tf_op jit(solution)/shard_map/store_sum/pallas_call | solution.py:1023
  666.5 15.6 %collective-permute-done.35 = bf16[1,384,384]{2,1,0:T(8,128)(2,1)S(1)} collective-permute-done((bf16[1,384,384]{2,1,0:T(8,128)(2,1)S(1)}, bf16[1,384,384]{2,1,0:T(8,128)(2,1)S(1)}, u32[]{:S(2)}, u32[]{:S(2)}) %collective-permute-start.35) | collective-permute-done | bytes 294944 | tf_op jit(solution)/shard_map/ppermute | solution.py:67
  (487 shorter events, 190.0 us)
Async XLA Ops:
  0.7 25.5 %collective-permute-start.10 = (bf16[1,48,1536]{2,1,0:T(8,128)(2,1)}, bf16[1,48,1536]{2,1,0:T(8,128)(2,1)S(1)}, u32[]{:S(2)}, u32[]{:S(2)}) collective-permute-start(bf16[1,48,1536]{2,1,0:T(8,128)(2,1)} %bitcast.111), channel_id=1, source_target_pairs={{0,16},{2,18},{4,20},{6,22},{8,24},{10,26},{12,28},{14,30},{16,0},... | collective-permute-start | bytes 442376 | tf_op jit(solution)/shard_map/ppermute | solution.py:67
  4.8 24.6 %collective-permute-start.11 = (bf16[1,192,384]{2,1,0:T(8,128)(2,1)}, bf16[1,192,384]{2,1,0:T(8,128)(2,1)}, u32[]{:S(2)}, u32[]{:S(2)}) collective-permute-start(bf16[1,192,384]{2,1,0:T(8,128)(2,1)} %bitcast.107), channel_id=1, source_target_pairs={{0,16},{2,18},{4,20},{6,22},{8,24},{10,26},{12,28},{14,30},{16,0},... | collective-permute-start | bytes 442376 | tf_op jit(solution)/shard_map/ppermute | solution.py:67
  27.5 49.0 %collective-permute-start.12 = (bf16[2,48,1536]{2,1,0:T(8,128)(2,1)}, bf16[2,48,1536]{2,1,0:T(8,128)(2,1)S(1)}, u32[]{:S(2)}, u32[]{:S(2)}) collective-permute-start(bf16[2,48,1536]{2,1,0:T(8,128)(2,1)} %pad_maximum_fusion.11.refs_3_), channel_id=1, source_target_pairs={{0,8},{2,10},{4,12},{6,14},{8,0},{10,2},{12,4},{14,6},{16,24},{18,... | collective-permute-start | bytes 884744 | tf_op jit(solution)/shard_map/ppermute | solution.py:67
  31.1 43.5 %collective-permute-start.13 = (bf16[2,192,384]{2,1,0:T(8,128)(2,1)}, bf16[2,192,384]{2,1,0:T(8,128)(2,1)}, u32[]{:S(2)}, u32[]{:S(2)}) collective-permute-start(bf16[2,192,384]{2,1,0:T(8,128)(2,1)} %pad_maximum_fusion.12.refs_4_), channel_id=1, source_target_pairs={{0,8},{2,10},{4,12},{6,14},{8,0},{10,2},{12,4},{14,6},{16,24},{18,... | collective-permute-start | bytes 884744 | tf_op jit(solution)/shard_map/ppermute | solution.py:67
  35.4 32.3 %collective-permute-start.1 = (bf16[2,192,384]{2,1,0:T(8,128)(2,1)}, bf16[2,192,384]{2,1,0:T(8,128)(2,1)}, u32[]{:S(2)}, u32[]{:S(2)}) collective-permute-start(bf16[2,192,384]{2,1,0:T(8,128)(2,1)} %get-tuple-element.164.refs_1_), channel_id=1, source_target_pairs={{0,8},{2,10},{4,12},{6,14},{8,0},{10,2},{12,4},{14,6},{16,24},{18,... | collective-permute-start | bytes 884744 | tf_op jit(solution)/shard_map/ppermute | solution.py:67
  38.3 32.6 %collective-permute-start.6 = (bf16[2,208,384]{2,1,0:T(8,128)(2,1)}, bf16[2,208,384]{2,1,0:T(8,128)(2,1)}, u32[]{:S(2)}, u32[]{:S(2)}) collective-permute-start(bf16[2,208,384]{2,1,0:T(8,128)(2,1)} %get-tuple-element.160.refs_2_), channel_id=1, source_target_pairs={{0,8},{2,10},{4,12},{6,14},{8,0},{10,2},{12,4},{14,6},{16,24},{18,... | collective-permute-start | bytes 958472 | tf_op jit(solution)/shard_map/ppermute | solution.py:67
  89.3 217.3 %all-to-all-start.1 = ((bf16[32,192,768]{2,1,0:T(8,128)(2,1)}), bf16[32,192,768]{2,1,0:T(8,128)(2,1)}, u32[]{:S(2)}, u32[]{:S(2)}) async-start(bf16[32,192,768]{2,1,0:T(8,128)(2,1)} %hold.8), calls=%async_computation.1 | async-start | bytes 18874368 | tf_op jit(solution)/shard_map/all_to_all | solution.py:1042
  97.6 103.5 %collective-permute-start.8 = (bf16[8,208,384]{2,1,0:T(8,128)(2,1)}, bf16[8,208,384]{2,1,0:T(8,128)(2,1)}, u32[]{:S(2)}, u32[]{:S(2)}) collective-permute-start(bf16[8,208,384]{2,1,0:T(8,128)(2,1)} %copy-done.121), channel_id=1, source_target_pairs={{0,4},{2,6},{4,0},{6,2},{8,12},{10,14},{12,8},{14,10},{16,20},{18,... | collective-permute-start | bytes 3833864 | tf_op jit(solution)/shard_map/ppermute | solution.py:67
  104.3 110.9 %collective-permute-start.3 = (bf16[8,192,384]{2,1,0:T(8,128)(2,1)}, bf16[8,192,384]{2,1,0:T(8,128)(2,1)}, u32[]{:S(2)}, u32[]{:S(2)}) collective-permute-start(bf16[8,192,384]{2,1,0:T(8,128)(2,1)} %hold.7), channel_id=1, source_target_pairs={{0,2},{2,0},{4,6},{6,4},{8,10},{10,8},{12,14},{14,12},{16,18},{18,... | collective-permute-start | bytes 3538952 | tf_op jit(solution)/shard_map/ppermute | solution.py:67
  108.1 120.2 %collective-permute-start.14 = (bf16[4,48,1536]{2,1,0:T(8,128)(2,1)}, bf16[4,48,1536]{2,1,0:T(8,128)(2,1)S(1)}, u32[]{:S(2)}, u32[]{:S(2)}) collective-permute-start(bf16[4,48,1536]{2,1,0:T(8,128)(2,1)} %pad_maximum_fusion.7.refs_3_), channel_id=1, source_target_pairs={{0,4},{2,6},{4,0},{6,2},{8,12},{10,14},{12,8},{14,10},{16,20},{18,... | collective-permute-start | bytes 1769480 | tf_op jit(solution)/shard_map/ppermute | solution.py:67
  108.6 118.4 %collective-permute-start.17 = (bf16[4,192,384]{2,1,0:T(8,128)(2,1)}, bf16[4,192,384]{2,1,0:T(8,128)(2,1)S(1)}, u32[]{:S(2)}, u32[]{:S(2)}) collective-permute-start(bf16[4,192,384]{2,1,0:T(8,128)(2,1)} %pad_maximum_fusion.8.refs_4_), channel_id=1, source_target_pairs={{0,2},{2,0},{4,6},{6,4},{8,10},{10,8},{12,14},{14,12},{16,18},{18,... | collective-permute-start | bytes 1769480 | tf_op jit(solution)/shard_map/ppermute | solution.py:67
  203.6 65.8 %collective-permute-start.9 = (bf16[16,208,384]{2,1,0:T(8,128)(2,1)}, bf16[16,208,384]{2,1,0:T(8,128)(2,1)S(1)}, u32[]{:S(2)}, u32[]{:S(2)}) collective-permute-start(bf16[16,208,384]{2,1,0:T(8,128)(2,1)} %constant_dynamic-update-slice_fusion.12.own), channel_id=1, source_target_pairs={{0,1},{1,0},{2,3},{3,2},{4,5},{5,4},{6,7},{7,6},{8,9},{9,8},{10,11... | collective-permute-start | bytes 7667720 | tf_op jit(solution)/shard_map/ppermute | solution.py:67
  216.7 48.5 %collective-permute-start.4 = (bf16[16,192,384]{2,1,0:T(8,128)(2,1)S(1)}, bf16[16,192,384]{2,1,0:T(8,128)(2,1)S(1)}, u32[]{:S(2)}, u32[]{:S(2)}) collective-permute-start(bf16[16,192,384]{2,1,0:T(8,128)(2,1)S(1)} %pad_maximum_fusion.own), channel_id=1, source_target_pairs={{0,1},{1,0},{2,3},{3,2},{4,5},{5,4},{6,7},{7,6},{8,9},{9,8},{10,11... | collective-permute-start | bytes 7077896 | tf_op jit(solution)/shard_map/ppermute | solution.py:67
  228.2 34.1 %collective-permute-start.18 = (bf16[8,192,384]{2,1,0:T(8,128)(2,1)S(1)}, bf16[8,192,384]{2,1,0:T(8,128)(2,1)S(1)}, u32[]{:S(2)}, u32[]{:S(2)}) collective-permute-start(bf16[8,192,384]{2,1,0:T(8,128)(2,1)S(1)} %pad_maximum_fusion.2), channel_id=1, source_target_pairs={{0,4},{2,6},{4,0},{6,2},{8,12},{10,14},{12,8},{14,10},{16,20},{18,... | collective-permute-start | bytes 3538952 | tf_op jit(solution)/shard_map/ppermute | solution.py:67
  228.5 35.0 %collective-permute-start.15 = (bf16[8,48,1536]{2,1,0:T(8,128)(2,1)S(1)}, bf16[8,48,1536]{2,1,0:T(8,128)(2,1)S(1)}, u32[]{:S(2)}, u32[]{:S(2)}) collective-permute-start(bf16[8,48,1536]{2,1,0:T(8,128)(2,1)S(1)} %pad_maximum_fusion.1), channel_id=1, source_target_pairs={{0,2},{2,0},{4,6},{6,4},{8,10},{10,8},{12,14},{14,12},{16,18},{18,... | collective-permute-start | bytes 3538952 | tf_op jit(solution)/shard_map/ppermute | solution.py:67
  263.5 32.0 %collective-permute-start.19 = (bf16[16,192,384]{2,1,0:T(8,128)(2,1)}, bf16[16,192,384]{2,1,0:T(8,128)(2,1)}, u32[]{:S(2)}, u32[]{:S(2)}) collective-permute-start(bf16[16,192,384]{2,1,0:T(8,128)(2,1)} %constant_dynamic-update-slice_fusion.22.own), channel_id=1, source_target_pairs={{0,1},{1,0},{2,3},{3,2},{4,5},{5,4},{6,7},{7,6},{8,9},{9,8},{10,11... | collective-permute-start | bytes 7077896 | tf_op jit(solution)/shard_map/ppermute | solution.py:67
  264.6 36.4 %collective-permute-start.16 = (bf16[16,48,1536]{2,1,0:T(8,128)(2,1)}, bf16[16,48,1536]{2,1,0:T(8,128)(2,1)}, u32[]{:S(2)}, u32[]{:S(2)}) collective-permute-start(bf16[16,48,1536]{2,1,0:T(8,128)(2,1)} %constant_dynamic-update-slice_fusion.17.own), channel_id=1, source_target_pairs={{0,1},{1,0},{2,3},{3,2},{4,5},{5,4},{6,7},{7,6},{8,9},{9,8},{10,11... | collective-permute-start | bytes 7077896 | tf_op jit(solution)/shard_map/ppermute | solution.py:67
  407.3 227.5 %all-to-all-start.2 = ((bf16[32,192,768]{2,1,0:T(8,128)(2,1)}), bf16[32,192,768]{2,1,0:T(8,128)(2,1)}, u32[]{:S(2)}, u32[]{:S(2)}) async-start(bf16[32,192,768]{2,1,0:T(8,128)(2,1)} %get-tuple-element.91), calls=%async_computation.2 | async-start | bytes 18874368 | tf_op jit(solution)/shard_map/all_to_all | solution.py:1042
  433.7 33.9 %collective-permute-start.24 = (bf16[16,192,384]{2,1,0:T(8,128)(2,1)}, bf16[16,192,384]{2,1,0:T(8,128)(2,1)}, u32[]{:S(2)}, u32[]{:S(2)}) collective-permute-start(bf16[16,192,384]{2,1,0:T(8,128)(2,1)} %get-tuple-element.81.refs_4_), channel_id=1, source_target_pairs={{0,1},{1,0},{2,3},{3,2},{4,5},{5,4},{6,7},{7,6},{8,9},{9,8},{10,11... | collective-permute-start | bytes 7077896 | tf_op jit(solution)/shard_map/ppermute | solution.py:67
  438.1 32.6 %collective-permute-start.23 = (bf16[16,192,384]{2,1,0:T(8,128)(2,1)}, bf16[16,192,384]{2,1,0:T(8,128)(2,1)}, u32[]{:S(2)}, u32[]{:S(2)}) collective-permute-start(bf16[16,192,384]{2,1,0:T(8,128)(2,1)} %get-tuple-element.79.refs_2_), channel_id=1, source_target_pairs={{0,1},{1,0},{2,3},{3,2},{4,5},{5,4},{6,7},{7,6},{8,9},{9,8},{10,11... | collective-permute-start | bytes 7077896 | tf_op jit(solution)/shard_map/ppermute | solution.py:67
  467.3 43.9 %collective-permute-start.20 = (bf16[16,192,384]{2,1,0:T(8,128)(2,1)}, bf16[16,192,384]{2,1,0:T(8,128)(2,1)}, u32[]{:S(2)}, u32[]{:S(2)}) collective-permute-start(bf16[16,192,384]{2,1,0:T(8,128)(2,1)} %get-tuple-element.93.refs_6_), channel_id=1, source_target_pairs={{0,1},{1,0},{2,3},{3,2},{4,5},{5,4},{6,7},{7,6},{8,9},{9,8},{10,11... | collective-permute-start | bytes 7077896 | tf_op jit(solution)/shard_map/ppermute | solution.py:67
  504.4 52.4 %collective-permute-start.32 = (bf16[8,192,384]{2,1,0:T(8,128)(2,1)}, bf16[8,192,384]{2,1,0:T(8,128)(2,1)S(1)}, u32[]{:S(2)}, u32[]{:S(2)}) collective-permute-start(bf16[8,192,384]{2,1,0:T(8,128)(2,1)} %copy-done.52), channel_id=1, source_target_pairs={{0,4},{2,6},{4,0},{6,2},{8,12},{10,14},{12,8},{14,10},{16,20},{18,... | collective-permute-start | bytes 3538952 | tf_op jit(solution)/shard_map/ppermute | solution.py:67
  509.6 50.1 %collective-permute-start.30 = (bf16[8,192,384]{2,1,0:T(8,128)(2,1)S(1)}, bf16[8,192,384]{2,1,0:T(8,128)(2,1)S(1)}, u32[]{:S(2)}, u32[]{:S(2)}) collective-permute-start(bf16[8,192,384]{2,1,0:T(8,128)(2,1)S(1)} %copy-done.51), channel_id=1, source_target_pairs={{0,2},{2,0},{4,6},{6,4},{8,10},{10,8},{12,14},{14,12},{16,18},{18,... | collective-permute-start | bytes 3538952 | tf_op jit(solution)/shard_map/ppermute | solution.py:67
  513.0 70.7 %collective-permute-start.21 = (bf16[8,192,384]{2,1,0:T(8,128)(2,1)S(1)}, bf16[8,192,384]{2,1,0:T(8,128)(2,1)S(1)}, u32[]{:S(2)}, u32[]{:S(2)}) collective-permute-start(bf16[8,192,384]{2,1,0:T(8,128)(2,1)S(1)} %get-tuple-element.126), channel_id=1, source_target_pairs={{0,2},{2,0},{4,6},{6,4},{8,10},{10,8},{12,14},{14,12},{16,18},{18,... | collective-permute-start | bytes 3538952 | tf_op jit(solution)/shard_map/ppermute | solution.py:67
  515.9 91.9 %collective-permute-start.26 = (bf16[8,208,384]{2,1,0:T(8,128)(2,1)S(1)}, bf16[8,208,384]{2,1,0:T(8,128)(2,1)S(1)}, u32[]{:S(2)}, u32[]{:S(2)}) collective-permute-start(bf16[8,208,384]{2,1,0:T(8,128)(2,1)S(1)} %get-tuple-element.120), channel_id=1, source_target_pairs={{0,4},{2,6},{4,0},{6,2},{8,12},{10,14},{12,8},{14,10},{16,20},{18,... | collective-permute-start | bytes 3833864 | tf_op jit(solution)/shard_map/ppermute | solution.py:67
  556.9 50.9 %collective-permute-start.33 = (bf16[4,192,384]{2,1,0:T(8,128)(2,1)S(1)}, bf16[4,192,384]{2,1,0:T(8,128)(2,1)S(1)}, u32[]{:S(2)}, u32[]{:S(2)}) collective-permute-start(bf16[4,192,384]{2,1,0:T(8,128)(2,1)S(1)} %get-tuple-element.135), channel_id=1, source_target_pairs={{0,2},{2,0},{4,6},{6,4},{8,10},{10,8},{12,14},{14,12},{16,18},{18,... | collective-permute-start | bytes 1769480 | tf_op jit(solution)/shard_map/ppermute | solution.py:67
  560.0 52.6 %collective-permute-start.31 = (bf16[4,192,384]{2,1,0:T(8,128)(2,1)S(1)}, bf16[4,192,384]{2,1,0:T(8,128)(2,1)S(1)}, u32[]{:S(2)}, u32[]{:S(2)}) collective-permute-start(bf16[4,192,384]{2,1,0:T(8,128)(2,1)S(1)} %get-tuple-element.133), channel_id=1, source_target_pairs={{0,4},{2,6},{4,0},{6,2},{8,12},{10,14},{12,8},{14,10},{16,20},{18,... | collective-permute-start | bytes 1769480 | tf_op jit(solution)/shard_map/ppermute | solution.py:67
  583.9 41.2 %collective-permute-start.22 = (bf16[4,192,384]{2,1,0:T(8,128)(2,1)S(1)}, bf16[4,192,384]{2,1,0:T(8,128)(2,1)S(1)}, u32[]{:S(2)}, u32[]{:S(2)}) collective-permute-start(bf16[4,192,384]{2,1,0:T(8,128)(2,1)S(1)} %get-tuple-element.137), channel_id=1, source_target_pairs={{0,4},{2,6},{4,0},{6,2},{8,12},{10,14},{12,8},{14,10},{16,20},{18,... | collective-permute-start | bytes 1769480 | tf_op jit(solution)/shard_map/ppermute | solution.py:67
  613.5 46.7 %collective-permute-start.34 = (bf16[2,384,384]{2,1,0:T(8,128)(2,1)}, bf16[2,384,384]{2,1,0:T(8,128)(2,1)}, u32[]{:S(2)}, u32[]{:S(2)}) collective-permute-start(bf16[2,384,384]{2,1,0:T(8,128)(2,1)} %pad_maximum_fusion.10), channel_id=1, source_target_pairs={{0,8},{2,10},{4,12},{6,14},{8,0},{10,2},{12,4},{14,6},{16,24},{18,... | collective-permute-start | bytes 1769480 | tf_op jit(solution)/shard_map/ppermute | solution.py:67
  625.5 36.8 %collective-permute-start.28 = (bf16[2,400,384]{2,1,0:T(8,128)(2,1)S(1)}, bf16[2,400,384]{2,1,0:T(8,128)(2,1)S(1)}, u32[]{:S(2)}, u32[]{:S(2)}) collective-permute-start(bf16[2,400,384]{2,1,0:T(8,128)(2,1)S(1)} %pad_maximum_fusion.5), channel_id=1, source_target_pairs={{0,8},{2,10},{4,12},{6,14},{8,0},{10,2},{12,4},{14,6},{16,24},{18,... | collective-permute-start | bytes 1843208 | tf_op jit(solution)/shard_map/ppermute | solution.py:67
  661.3 20.8 %collective-permute-start.35 = (bf16[1,384,384]{2,1,0:T(8,128)(2,1)S(1)}, bf16[1,384,384]{2,1,0:T(8,128)(2,1)S(1)}, u32[]{:S(2)}, u32[]{:S(2)}) collective-permute-start(bf16[1,384,384]{2,1,0:T(8,128)(2,1)S(1)} %slice_add_fusion.20), channel_id=1, source_target_pairs={{0,16},{2,18},{4,20},{6,22},{8,24},{10,26},{12,28},{14,30},{16,0},... | collective-permute-start | bytes 884744 | tf_op jit(solution)/shard_map/ppermute | solution.py:67
  663.5 25.1 %collective-permute-start.29 = (bf16[1,400,384]{2,1,0:T(8,128)(2,1)S(1)}, bf16[1,400,384]{2,1,0:T(8,128)(2,1)S(1)}, u32[]{:S(2)}, u32[]{:S(2)}) collective-permute-start(bf16[1,400,384]{2,1,0:T(8,128)(2,1)S(1)} %slice_add_fusion.18), channel_id=1, source_target_pairs={{0,16},{2,18},{4,20},{6,22},{8,24},{10,26},{12,28},{14,30},{16,0},... | collective-permute-start | bytes 921608 | tf_op jit(solution)/shard_map/ppermute | solution.py:67
  (148 other events, 1655.0 us)

commit v4 on v3

--- a/solution.py
+++ b/solution.py
@@ -417,18 +417,32 @@
     cross_q[...] = (mm(out.astype(BF), w_qkvc[3]) + bias[3:4]).astype(BF)
 
 
-def self_fwd(tokens, seg, live, w_qkvc, w_o, bias, gain, shift):
+def one_step(ops, picks):
+    specs = []
+    for i, op in enumerate(ops):
+        block, at = op.shape, (0,) * op.ndim
+        if i in picks:
+            block, at = (None,) + op.shape[1:], (picks[i],) + at[1:]
+        specs.append(pl.BlockSpec(block, lambda g, at=at: at))
+    return specs
+
+
+def self_fwd(tokens, seg, live, w_qkvc, mats, bias, gain, shift):
     toks, dim = tokens.shape
+    ops = (tokens, seg.reshape(toks, 1), seg, live, w_qkvc, mats, bias, gain, shift)
     low = jax.ShapeDtypeStruct((toks, dim), BF)
     full = jax.ShapeDtypeStruct((toks, dim), F32)
     column = jax.ShapeDtypeStruct((toks, 128), F32)
     return pl.pallas_call(
         self_fwd_kernel,
+        grid=(1,),
+        in_specs=one_step(ops, {5: 2}),
+        out_specs=one_step((low, low, low, low, full, full, column, low), {}),
         out_shape=(low, low, low, low, full, full, column, low),
         compiler_params=pltpu.CompilerParams(vmem_limit_bytes=28 * 1024 * 1024),
         cost_estimate=cost(5),
         name="self_fwd",
-    )(tokens, seg.reshape(toks, 1), seg, live, w_qkvc, w_o, bias, gain, shift)
+    )(*ops)
 
 
 def self_bwd_kernel(*refs):
@@ -461,18 +475,23 @@
         grad_v[:, lanes] = by_value.astype(BF)
 
 
-def self_bwd(grad_cq, grad_two, normed, scale, gain, qkv, seg, live, w_qkvc, w_o):
+def self_bwd(grad_cq, grad_two, normed, scale, gain, qkv, seg, live, w_qkvc, mats):
     toks, dim = grad_two.shape
+    ops = (grad_cq, grad_two, normed, scale, gain, *qkv)
+    ops += (seg.reshape(toks, 1), seg, live, w_qkvc, mats)
     low = jax.ShapeDtypeStruct((toks, dim), BF)
     full = jax.ShapeDtypeStruct((toks, dim), F32)
     return pl.pallas_call(
         self_bwd_kernel,
+        grid=(1,),
+        in_specs=one_step(ops, {12: 2}),
+        out_specs=one_step((full, full, low, low, low, low), {}),
         out_shape=(full, full, low, low, low, low),
         scratch_shapes=[pltpu.VMEM((toks, dim), BF)],
         compiler_params=pltpu.CompilerParams(vmem_limit_bytes=28 * 1024 * 1024),
         cost_estimate=cost(6),
         name="self_bwd",
-    )(grad_cq, grad_two, normed, scale, gain, *qkv, seg.reshape(toks, 1), seg, live, w_qkvc, w_o)
+    )(*ops)
 
 
 def own_rows(tokens, ret, heads):
@@ -556,6 +575,7 @@
 GROUP = 8
 LANES = 128
 PITCH = LANES // GROUP
+TILE = 256
 
 
 def plan_kernel(rows, wanted, token, at_rank, owner, *, shard_rows):
@@ -681,11 +701,15 @@
 def rows_in_kernel(arrived, query, w_k, w_v, keys, vals, scores):
     group, k, dim = arrived.shape
     rows = arrived[...].reshape(group * k, dim)
-    key = mm(rows, w_k[...])
-    keys[...] = key.astype(BF).reshape(group, k, dim)
-    prod = (key * query[...].reshape(group * k, dim).astype(F32)).astype(BF)
-    scores[...] = to_lanes(mm(prod, head_sum(dim)), k) * 0.125
-    vals[...] = mm(rows, w_v[...]).astype(BF).reshape(group, k, dim)
+    total = jnp.zeros((group * k, LANES), F32)
+    for at in range(0, dim, TILE):
+        tile = slice(at, at + TILE)
+        key = mm(rows, w_k[:, tile])
+        keys[:, :, tile] = key.astype(BF).reshape(group, k, TILE)
+        prod = (key * query[:, :, tile].reshape(group * k, TILE).astype(F32)).astype(BF)
+        total = total + mm(prod, head_sum(dim)[tile])
+        vals[:, :, tile] = mm(rows, w_v[:, tile]).astype(BF).reshape(group, k, TILE)
+    scores[...] = to_lanes(total, k) * 0.125
 
 
 def attend_kernel(
@@ -750,8 +774,12 @@
 
 
 def rows_out_kernel(prob_slot, grad_slot, grad, query, w_k, w_v, out, flag):
+    group, k, dim = grad.shape
     mix, ask = weigh(prob_slot, grad_slot, grad, query)
-    out[...] = (mm_nt(mix, w_v[...]) + mm_nt(ask, w_k[...])).astype(BF).reshape(grad.shape)
+    for at in range(0, dim, TILE):
+        tile = slice(at, at + TILE)
+        got = mm_nt(mix, w_v[tile]) + mm_nt(ask, w_k[tile])
+        out[:, :, tile] = got.astype(BF).reshape(group, k, TILE)
     flag[...] = jnp.zeros_like(flag)
 
 
@@ -822,7 +850,7 @@
 
 
 class SlotAttention:
-    split = 2
+    split = 1
 
     def __init__(self, ret_rows, shard_rows, peers, slots, dim):
         self.toks, self.ret = ret_rows.shape
@@ -839,6 +867,7 @@
         self.mark = pl.BlockSpec((GROUP * k, toks), lambda g, c: (c * groups + g, 0))
         self.mark_t = pl.BlockSpec((toks, GROUP * k), lambda g, c: (0, c * groups + g))
         self.square = self.whole(dim, dim)
+        self.w_specs = [pl.BlockSpec((None, dim, dim), lambda g, c, i=i: (i, 0, 0)) for i in range(2)]
         self.heads = self.whole(slots, wide)
         self.slot_rows = in_hbm((peers, slots, dim), BF)
         self.slot_heads = jax.ShapeDtypeStruct((slots, wide), F32)
@@ -859,7 +888,7 @@
     def whole(*shape):
         return pl.BlockSpec(shape, lambda g, c: (0,) * len(shape))
 
-    def call(self, kernel, name, micros, in_specs, out_specs, out_shape, scratch=(), mib=28):
+    def call(self, kernel, name, micros, in_specs, out_specs, out_shape, scratch=(), mib=44):
         return pl.pallas_call(
             kernel,
             grid=self.grid,
@@ -882,17 +911,17 @@
             self.slot_rows,
         )(self.token, cross_q)
 
-    def forward(self, arrived, w_k, w_v, bias):
+    def forward(self, arrived, mats, bias):
         dim, toks = self.dim, self.toks
-        self.arrived, self.w_k, self.w_v = arrived, w_k, w_v
+        self.arrived, self.mats = arrived, mats
         self.keys, self.vals, scores = self.call(
             rows_in_kernel,
             "rows_in",
             22,
-            [self.rows, self.rows, self.square, self.square],
+            [self.rows, self.rows, *self.w_specs],
             [self.rows, self.rows, self.lanes],
             (self.slot_rows, self.slot_rows, self.slot_heads),
-        )(from_hbm(arrived), from_hbm(self.query), w_k, w_v)
+        )(from_hbm(arrived), from_hbm(self.query), mats, mats)
         entries = (self.ret * PITCH, toks)
         self.prob_tok, self.prob_slot, mixed = self.call(
             attend_kernel,
@@ -928,10 +957,10 @@
             rows_out_kernel,
             "rows_out",
             28,
-            self.factor_specs + [self.square, self.square],
+            self.factor_specs + self.w_specs,
             [self.rows, self.whole(8, LANES)],
             (self.slot_rows, jax.ShapeDtypeStruct((8, LANES), F32)),
-        )(*self.factors, self.w_k, self.w_v)
+        )(*self.factors, self.mats, self.mats)
         return sent
 
     def query_grad(self):
@@ -969,8 +998,9 @@
     def prepare(self, cross_q):
         self.cross_q = cross_q
 
-    def forward(self, arrived, w_k, w_v, bias):
+    def forward(self, arrived, mats, bias):
         toks, dim = self.toks, self.dim
+        w_k, w_v = mats[0], mats[1]
         self.key_heads, self.val_heads = w_k.reshape(dim, H, HD), w_v.reshape(dim, H, HD)
         query = self.cross_q.reshape(toks, H, HD)
         self.query_keys = jnp.einsum(
@@ -1007,35 +1037,33 @@
         return grad_k, product(self.state_mix, self.grad)
 
 
-def store_sum_kernel(asked, returned, *refs, block, added):
-    first = pl.program_id(0) * block + 1
+def store_sum_kernel(asked, returned, *refs, block, skip):
+    first = (pl.program_id(0) + skip) * block + 1
     shape = (block, asked.shape[1])
     hit = lax.broadcasted_iota(jnp.int32, shape, 0) + first == asked[...]
-    total = mm(hit.astype(BF), returned[...])
-    refs[-1][...] = total + refs[0][...] if added else total
-
-
-def store_sum(asked, returned, shard_rows, so_far, after=()):
+    refs[-1][...] = mm(hit.astype(BF), returned[...])
+
+
+def store_sum(asked, returned, shard_rows, part, so_far=(), after=()):
     count, dim = returned.shape
     block = 256
-    out = pl.BlockSpec((block, dim), lambda g: (g, 0))
-    before = [] if so_far is None else [so_far]
+    steps = shard_rows // block // 2
+    skip = part * steps
     return pl.pallas_call(
-        functools.partial(store_sum_kernel, block=block, added=so_far is not None),
-        grid=(shard_rows // block,),
+        functools.partial(store_sum_kernel, block=block, skip=skip),
+        grid=(steps,),
         in_specs=[
             pl.BlockSpec((1, count), lambda g: (0, 0)),
             pl.BlockSpec((count, dim), lambda g: (0, 0)),
         ]
-        + [out] * len(before)
-        + [WAIT] * len(after),
-        out_specs=out,
-        out_shape=jax.ShapeDtypeStruct((shard_rows, dim), F32),
-        input_output_aliases={2: 0} if before else {},
+        + [WAIT] * (len(so_far) + len(after)),
+        out_specs=pl.BlockSpec((block, dim), lambda g: (g + skip, 0)),
+        out_shape=in_hbm((shard_rows, dim), F32),
+        input_output_aliases={2: 0} if so_far else {},
         compiler_params=pltpu.CompilerParams(vmem_limit_bytes=VMEM_LIMIT),
-        cost_estimate=cost(25),
+        cost_estimate=cost(13),
         name="store_sum",
-    )(asked.reshape(1, count), returned, *before, *after)
+    )(asked.reshape(1, count), returned, *so_far, *after)
 
 
 def all_to_all(array):
@@ -1100,7 +1128,7 @@
     packs = [*join(attn_in, attn_out, small, attention.wanted), ff_in[None], ff_out[None]]
     packs = [gather_bits(p, order[:1]) for p, order in zip(packs, orders)]
     asked = all_to_all(attention.wanted)
-    asked = tie(asked, packs) if by_rows else asked
+    asked = tie(asked, packs[:2]) if by_rows else asked
     packs = [gather_bits(p, order[1:n_far]) for p, order in zip(packs, orders)]
 
     answer = enc_store[jnp.maximum(asked - 1, 0)]
@@ -1114,16 +1142,17 @@
     def whole(i, after=()):
         done = n_far + 1
         if by_rows:
-            own = gather_bits(packs[i], orders[i][done:n_row_bits])
+            got = swap_bit(packs[i], *orders[i][done])
+            own = hold(packs[i], after) if after else packs[i]
+            own = jnp.concatenate([own, got], axis=0)
             other = swap_bit(own, "col", 1)
-            other = hold(other, after) if after else other
             return unpack(own, other, places[i], counts[i], shapes[i], extras[i])
         blocks = gather_bits(packs[i], orders[i][done:])
         return unpack_any(blocks, orders[i], counts[i], shapes[i], extras[i], n_rows, n_cols)
 
     mats = [whole(0), whole(1)]
     w_q, w_k, w_v = (mats[0][i] for i in range(3))
-    w_ck, w_cv, w_o, w_co = (mats[1][0][i] for i in range(4))
+    w_co = mats[1][0][3]
     small_all = mats[1][1]
     small_all = small_all.astype(F32)
     vectors = small_all[:, :13, :rb].transpose(1, 0, 2).reshape(13, dim)
@@ -1131,7 +1160,7 @@
     bias_ff = small_all[:, 13, : ff_bias.size].reshape(-1)
 
     *qkv, mixed, first, first_norm, first_scale, cross_q = self_fwd(
-        tokens, seg_ids, live_mask, mats[0], w_o, bias_all, gain_all, shift_all
+        tokens, seg_ids, live_mask, mats[0], mats[1][0], bias_all, gain_all, shift_all
     )
     first_low = first.astype(BF)
 
@@ -1142,7 +1171,7 @@
     else:
         for i in (2, 3):
             packs[i] = gather_bits(packs[i], orders[i][n_far : n_far + 1])
-    cross_low = attention.forward(arrived, w_ck, w_cv, bias_all[4])
+    cross_low = attention.forward(arrived, mats[1][0], bias_all[4])
     branch_two = mm(cross_low, w_co) + bias_all[5]
     second, second_norm, second_scale = norm_fwd(first + branch_two, gain_all[1], shift_all[1])
     second_low = second.astype(BF)
@@ -1197,7 +1226,7 @@
         seg_ids,
         live_mask,
         mats[0],
-        w_o,
+        mats[1][0],
     )
     grad_tokens = (
         grad_one + mm_nt(grad_q, w_q) + mm_nt(grad_k, w_k) + mm_nt(grad_v, w_v)
@@ -1244,13 +1273,17 @@
 
     ff = join_pairs(on_both(ff, near - 2, near))
     attn = join_pairs(on_both([attn_one, attn_two], 0, near))
-    grad_store = store_sum(asked, returned.reshape(-1, dim), shard_rows, None)
-    if by_rows:
-        ff, attn = ((hold(keep, [grad_store]), send) for keep, send in (ff, attn))
-    ff, attn = (scatter_bits(*pair, back_a[near:-1]) for pair in (ff, attn))
-    total_a, total_b = (
-        (keep + swap_bit(send, *order_a[0]))[0].astype(F32) for keep, send in (attn, ff)
-    )
+    def behind(pair, array):
+        return (hold(pair[0], [array]), pair[1]) if by_rows else pair
+
+    rows = returned.reshape(-1, dim)
+    grad_store = store_sum(asked, rows, shard_rows, 0)
+    ff, attn = (scatter_bits(*behind(x, grad_store), back_a[near:-1]) for x in (ff, attn))
+    last = join_pairs([attn, ff])
+    grad_store = store_sum(asked, rows, shard_rows, 1, (grad_store,), (last[1],))
+    keep, send = behind(last, grad_store)
+    total = (keep + swap_bit(send, *order_a[0]))[0].astype(F32)
+    total_a, total_b = total[: attn[0].shape[1]], total[attn[0].shape[1] :]
 
     sum_small = total_a[8 * rb :]
     return (

time: 699 us -> 678 us (0.970)
  waiting for transfers between devices: 266 us -> 251 us
  other arithmetic: 34 us -> 43.2 us
    ppermute x36 -> x35, waiting for transfers between devices: 266 us -> 241 us  [swap_bit(): return lax.ppermute(array, axis, pairs)]
    all_to_all x3, waiting for transfers between devices: 0.01 us -> 9.8 us  [all_to_all(): return lax.all_to_all(array, RANKS, split_axis=0, concat_axis=0, tiled=True)]
    pallas_call x5 -> x6, Pallas kernels: 86.7 us -> 91.8 us  [the longest x2 30.3 us: store_sum(): pl.pallas_call(functools.partial(store_sum_kernel, block=block, skip=skip...]
    unnamed x296 -> x262, local copies, waits for them, and re-layouts: 49.8 us -> 53.6 us
    concatenate x9 -> x8, other arithmetic: 10.5 us -> 14.1 us  [gather_bits(): blocks = jnp.concatenate([blocks, swap_bit(blocks, axis, bit)], axis=0)]
    ppermute x36 -> x35, starting transfers between devices: 46 us -> 48.6 us  [swap_bit(): return lax.ppermute(array, axis, pairs)]
  transfers between devices with their start and end apart: 39 -> 38, of which waited for: 16 -> 16; matrix products, arithmetic and copies ran while one was open for 15% -> 14% of each run, Pallas kernels for 17% -> 18%
where the time goes in v4:
time: 678 us; the launch traced here: 672 us
  waiting for transfers between devices  251 us (37%)
  Pallas kernels  196 us (29%)
  local copies, waits for them, and re-layouts  100 us (15%)
  starting transfers between devices  63.7 us (9%)
  other arithmetic  43.2 us (6%)
  matrix products  15.4 us (2%)
    ppermute x35, waiting for transfers between devices, swap_bit(): return lax.ppermute(array, axis, pairs)  241 us
    unnamed x262, local copies, waits for them, and re-layouts  53.6 us
    ppermute x35, starting transfers between devices, swap_bit(): return lax.ppermute(array, axis, pairs)  48.6 us
    pallas_call x2, Pallas kernels, store_sum(): pl.pallas_call(functools.partial(store_sum_kernel, block=block, skip=skip...  30.3 us
    pallas_call x1, Pallas kernels, backward(): self.call(rows_out_kernel, 'rows_out', 28, self.factor_specs + self.w_spe...  28.2 us
    gather x1, local copies, waits for them, and re-layouts, on_device(): answer = enc_store[jnp.maximum(asked - 1, 0)]  26.3 us
    pallas_call x1, Pallas kernels, weights(): self.call(rows_weights_kernel, 'rows_weights', 24, self.factor_specs + [s...  24.2 us
    pallas_call x1, Pallas kernels, forward(): self.call(rows_in_kernel, 'rows_in', 22, [self.rows, self.rows, *self.w_s...  22.9 us
  transfers between devices with their start and end apart: 38, of which 16 were waited for; matrix products, arithmetic and copies ran while one was open for 14% of the time, Pallas kernels for 18%

profile of v4, /device:TPU:0, one launch (start us, length us, event | category | flops | bytes accessed | tf_op | source)
XLA Modules:
  0.0 672.1 jit_solution(4210843825488635324)
XLA Ops:
  4.9 4.4 plan.1
  10.8 6.1 all-to-all-start
  41.5 26.3 %gather_fusion.2 = bf16[6144,768]{1,0:T(8,128)(2,1)} fusion(bf16[2048,768]{1,0:T(8,128)(2,1)S(1)} %copy-done, s32[6144]{0:T(1024)S(1)} %broadcast_clamp_fusion), kind=kCustom, calls=%fused_computation.2 | custom fusion | bytes 18898944 | tf_op jit(solution)/shard_map/gather | solution.py:1134
  88.4 5.0 all-to-all-start.1
  103.4 96.2 %collective-permute-done.8 = bf16[8,208,384]{2,1,0:T(8,128)(2,1)} collective-permute-done((bf16[8,208,384]{2,1,0:T(8,128)(2,1)}, bf16[8,208,384]{2,1,0:T(8,128)(2,1)}, u32[]{:S(2)}, u32[]{:S(2)}) %collective-permute-start.8) | collective-permute-done | bytes 1277984 | tf_op jit(solution)/shard_map/ppermute | solution.py:67
  202.2 11.4 %collective-permute-done.3 = bf16[8,192,384]{2,1,0:T(8,128)(2,1)S(1)} collective-permute-done((bf16[8,192,384]{2,1,0:T(8,128)(2,1)}, bf16[8,192,384]{2,1,0:T(8,128)(2,1)S(1)}, u32[]{:S(2)}, u32[]{:S(2)}) %collective-permute-start.3) | collective-permute-done | bytes 1179680 | tf_op jit(solution)/shard_map/ppermute | solution.py:67
  217.4 13.6 %collective-permute-done.17 = bf16[4,192,384]{2,1,0:T(8,128)(2,1)} collective-permute-done((bf16[4,192,384]{2,1,0:T(8,128)(2,1)}, bf16[4,192,384]{2,1,0:T(8,128)(2,1)}, u32[]{:S(2)}, u32[]{:S(2)}) %collective-permute-start.17) | collective-permute-done | bytes 589856 | tf_op jit(solution)/shard_map/ppermute | solution.py:67
  236.9 4.4 collective-permute-start.15
  258.4 4.7 self_fwd.1
  263.9 5.3 query_rows.1.query.refs_1_.refs_3_
  269.3 4.7 collective-permute-done.18
  293.0 9.8 %all-to-all-done.1.arrived.refs_4_ = bf16[32,192,768]{2,1,0:T(8,128)(2,1)} async-done(((bf16[32,192,768]{2,1,0:T(8,128)(2,1)}), bf16[32,192,768]{2,1,0:T(8,128)(2,1)}, u32[]{:S(2)}, u32[]{:S(2)}) %all-to-all-start.1) | async-done | bytes 9437216 | tf_op jit(solution)/shard_map/all_to_all | solution.py:1070
  305.1 22.9 %rows_in.1 = (bf16[32,192,768]{2,1,0:T(8,128)(2,1)}, bf16[32,192,768]{2,1,0:T(8,128)(2,1)}, f32[192,512]{1,0:T(8,128)S(1)}) custom-call(bf16[32,192,768]{2,1,0:T(8,128)(2,1)} %all-to-all-done.1.arrived.refs_4_, bf16[32,192,768]{2,1,0:T(8,128)(2,1)} %query_rows.1.query.refs_1_.refs_3_, bf16[4,768,768]{2,1,0:T(8,128)(2,1)S(1)} %copy-done.63, ...), custom_call_target="tpu_custom_call" | custom-call | flops 24199999488 | tf_op jit(solution)/shard_map/rows_in/pallas_call | solution.py:917
  328.1 11.6 %attend.1 = (f32[256,256]{1,0:T(8,128)S(1)}, f32[192,512]{1,0:T(8,128)S(1)}, bf16[256,768]{1,0:T(8,128)(2,1)S(1)}) custom-call(f32[192,512]{1,0:T(8,128)S(1)} %get-tuple-element.67.scores, bf16[32,192,768]{2,1,0:T(8,128)(2,1)} %get-tuple-element.68.vals, bf16[256,6144]{1,0:T(8,128)(2,1)S(1)} %copy-done.13, bf16[256,4096]{1,0:T(8,128)(2,1)S(1)} %copy-done.80, ...), custom_call_target="tpu_custom_call" | custom-call | flops 12099999744 | tf_op jit(solution)/shard_map/attend/pallas_call | solution.py:926
  354.0 14.2 %attend_back.1 = (bf16[32,192,768]{2,1,0:T(8,128)(2,1)}, f32[192,512]{1,0:T(8,128)S(1)}) custom-call(bf16[32,192,768]{2,1,0:T(8,128)(2,1)} %get-tuple-element.68.vals, bf16[6144,256]{1,0:T(8,128)(2,1)S(1)} %copy-done.16, bf16[256,768]{1,0:T(8,128)(2,1)S(1)} %convolution_convert_fusion.grad.refs_4_, f32[256,256]{1,0:T(8,128)S(1)} %get-tuple-element.73.prob_tok, ...), custom_call_target="tpu_custom_call" | custom-call | flops 14300000256 | tf_op jit(solution)/shard_map/attend_back/pallas_call | solution.py:944
  368.3 28.2 %rows_out.1 = (bf16[32,192,768]{2,1,0:T(8,128)(2,1)}, f32[8,128]{1,0:T(8,128)S(1)}) custom-call(f32[192,512]{1,0:T(8,128)S(1)} %get-tuple-element.75.prob_slot.refs_0_, f32[192,512]{1,0:T(8,128)S(1)} %get-tuple-element.74.grad_slot.refs_1_, bf16[32,192,768]{2,1,0:T(8,128)(2,1)} %get-tuple-element.76.grad.refs_2_, ...), custom_call_target="tpu_custom_call" | custom-call | flops 30799998976 | tf_op jit(solution)/shard_map/rows_out/pallas_call | solution.py:956
  402.8 7.8 %query_back.1.refs_2_.refs_0_ = bf16[256,768]{1,0:T(8,128)(2,1)S(1)} custom-call(bf16[32,192,768]{2,1,0:T(8,128)(2,1)} %get-tuple-element.72.keys, bf16[256,6144]{1,0:T(8,128)(2,1)S(1)} %copy-done.14, f32[192,512]{1,0:T(8,128)S(1)} %copy-done.89, f32[8,128]{1,0:T(8,128)S(1)} %copy-done.98), custom_call_target="tpu_custom_call" | custom-call | flops 7699999744 | tf_op jit(solution)/shard_map/query_back/pallas_call | solution.py:968
  410.7 4.2 pack.5
  415.0 4.2 pack.4
  433.8 5.6 self_bwd.1
  447.3 4.1 pack.6
  458.8 24.2 %rows_weights.1 = (bf16[768,768]{1,0:T(8,128)(2,1)S(1)}, bf16[768,768]{1,0:T(8,128)(2,1)S(1)}) custom-call(f32[192,512]{1,0:T(8,128)S(1)} %copy-done.94, f32[192,512]{1,0:T(8,128)S(1)} %copy-done.90, bf16[32,192,768]{2,1,0:T(8,128)(2,1)} %get-tuple-element.76.grad.refs_2_, bf16[32,192,768]{2,1,0:T(8,128)(2,1)} %query_rows.1.query.refs_1_.refs_3_, ...), custom_call_target="tpu_custom_call" | custom-call | flops 26400000000 | tf_op jit(solution)/shard_map/rows_weights/pallas_call | solution.py:980
  483.1 4.2 pack.7
  500.7 39.1 %collective-permute-done.31 = bf16[8,192,384]{2,1,0:T(8,128)(2,1)S(1)} collective-permute-done((bf16[8,192,384]{2,1,0:T(8,128)(2,1)}, bf16[8,192,384]{2,1,0:T(8,128)(2,1)S(1)}, u32[]{:S(2)}, u32[]{:S(2)}) %collective-permute-start.31) | collective-permute-done | bytes 1179680 | tf_op jit(solution)/shard_map/ppermute | solution.py:67
  544.1 22.3 %collective-permute-done.21 = bf16[8,192,384]{2,1,0:T(8,128)(2,1)S(1)} collective-permute-done((bf16[8,192,384]{2,1,0:T(8,128)(2,1)S(1)}, bf16[8,192,384]{2,1,0:T(8,128)(2,1)S(1)}, u32[]{:S(2)}, u32[]{:S(2)}) %collective-permute-start.21) | collective-permute-done | bytes 1179680 | tf_op jit(solution)/shard_map/ppermute | solution.py:67
  566.6 24.1 %collective-permute-done.32 = bf16[4,192,384]{2,1,0:T(8,128)(2,1)S(1)} collective-permute-done((bf16[4,192,384]{2,1,0:T(8,128)(2,1)S(1)}, bf16[4,192,384]{2,1,0:T(8,128)(2,1)S(1)}, u32[]{:S(2)}, u32[]{:S(2)}) %collective-permute-start.32) | collective-permute-done | bytes 589856 | tf_op jit(solution)/shard_map/ppermute | solution.py:67
  591.1 4.6 collective-permute-done.30
  596.6 8.5 %collective-permute-start.33 = (bf16[2,384,384]{2,1,0:T(8,128)(2,1)}, bf16[2,384,384]{2,1,0:T(8,128)(2,1)}, u32[]{:S(2)}, u32[]{:S(2)}) collective-permute-start(bf16[2,384,384]{2,1,0:T(8,128)(2,1)} %pad_maximum_fusion.14), channel_id=1, source_target_pairs={{0,8},{2,10},{4,12},{6,14},{8,0},{10,2},{12,4},{14,6},{16,24},{18,... | collective-permute-start | bytes 1769480 | tf_op jit(solution)/shard_map/ppermute | solution.py:67
  608.5 10.6 %collective-permute-start.28 = (bf16[2,400,384]{2,1,0:T(8,128)(2,1)S(1)}, bf16[2,400,384]{2,1,0:T(8,128)(2,1)S(1)}, u32[]{:S(2)}, u32[]{:S(2)}) collective-permute-start(bf16[2,400,384]{2,1,0:T(8,128)(2,1)S(1)} %pad_maximum_fusion.7), channel_id=1, source_target_pairs={{0,8},{2,10},{4,12},{6,14},{8,0},{10,2},{12,4},{14,6},{16,24},{18,... | collective-permute-start | bytes 1843208 | tf_op jit(solution)/shard_map/ppermute | solution.py:67
  620.0 15.0 %store_sum.2.refs_1_.refs_0_ = f32[2048,768]{1,0:T(8,128)} custom-call(s32[1,6144]{1,0:T(1,128)} %reshape.138.asked, bf16[6144,768]{1,0:T(8,128)(2,1)} %bitcast.15.returned), custom_call_target="tpu_custom_call" | custom-call | flops 14300000256 | tf_op jit(solution)/shard_map/store_sum/pallas_call | solution.py:1052
  638.2 15.3 %store_sum.3.refs_1_ = f32[2048,768]{1,0:T(8,128)} custom-call(s32[1,6144]{1,0:T(1,128)} %reshape.138.asked, bf16[6144,768]{1,0:T(8,128)(2,1)} %bitcast.15.returned, f32[2048,768]{1,0:T(8,128)} %store_sum.2.refs_1_.refs_0_, bf16[1,784,384]{2,1,0:T(8,128)(2,1)} %copy-done.117), custom_call_target="tpu_custom_call", output_to_operand_aliasing={{}: (2, {})} | custom-call | flops 14300000256 | tf_op jit(solution)/shard_map/store_sum/pallas_call | solution.py:1052
  654.4 11.0 %collective-permute-done.34 = bf16[1,784,384]{2,1,0:T(8,128)(2,1)} collective-permute-done((bf16[1,784,384]{2,1,0:T(8,128)(2,1)S(1)}, bf16[1,784,384]{2,1,0:T(8,128)(2,1)}, u32[]{:S(2)}, u32[]{:S(2)}) %collective-permute-start.34) | collective-permute-done | bytes 602144 | tf_op jit(solution)/shard_map/ppermute | solution.py:67
  (451 shorter events, 195.7 us)
Async XLA Ops:
  0.7 25.5 %collective-permute-start.10 = (bf16[1,48,1536]{2,1,0:T(8,128)(2,1)}, bf16[1,48,1536]{2,1,0:T(8,128)(2,1)}, u32[]{:S(2)}, u32[]{:S(2)}) collective-permute-start(bf16[1,48,1536]{2,1,0:T(8,128)(2,1)} %bitcast.98), channel_id=1, source_target_pairs={{0,16},{2,18},{4,20},{6,22},{8,24},{10,26},{12,28},{14,30},{16,0},... | collective-permute-start | bytes 442376 | tf_op jit(solution)/shard_map/ppermute | solution.py:67
  4.8 24.9 %collective-permute-start.12 = (bf16[1,192,384]{2,1,0:T(8,128)(2,1)}, bf16[1,192,384]{2,1,0:T(8,128)(2,1)}, u32[]{:S(2)}, u32[]{:S(2)}) collective-permute-start(bf16[1,192,384]{2,1,0:T(8,128)(2,1)} %bitcast.94), channel_id=1, source_target_pairs={{0,16},{2,18},{4,20},{6,22},{8,24},{10,26},{12,28},{14,30},{16,0},... | collective-permute-start | bytes 442376 | tf_op jit(solution)/shard_map/ppermute | solution.py:67
  10.8 14.8 %all-to-all-start = ((s32[32,1,192]{2,1,0:T(1,128)}), s32[32,1,192]{2,1,0:T(1,128)S(1)}, u32[]{:S(2)}, u32[]{:S(2)}) async-start(s32[32,1,192]{2,1,0:T(1,128)} %copy.52), calls=%async_computation | async-start | bytes 65536 | tf_op jit(solution)/shard_map/all_to_all | solution.py:1070
  27.9 48.6 %collective-permute-start.11 = (bf16[2,48,1536]{2,1,0:T(8,128)(2,1)}, bf16[2,48,1536]{2,1,0:T(8,128)(2,1)}, u32[]{:S(2)}, u32[]{:S(2)}) collective-permute-start(bf16[2,48,1536]{2,1,0:T(8,128)(2,1)} %pad_maximum_fusion.15), channel_id=1, source_target_pairs={{0,8},{2,10},{4,12},{6,14},{8,0},{10,2},{12,4},{14,6},{16,24},{18,... | collective-permute-start | bytes 884744 | tf_op jit(solution)/shard_map/ppermute | solution.py:67
  31.3 43.3 %collective-permute-start.13 = (bf16[2,192,384]{2,1,0:T(8,128)(2,1)}, bf16[2,192,384]{2,1,0:T(8,128)(2,1)}, u32[]{:S(2)}, u32[]{:S(2)}) collective-permute-start(bf16[2,192,384]{2,1,0:T(8,128)(2,1)} %pad_maximum_fusion.16), channel_id=1, source_target_pairs={{0,8},{2,10},{4,12},{6,14},{8,0},{10,2},{12,4},{14,6},{16,24},{18,... | collective-permute-start | bytes 884744 | tf_op jit(solution)/shard_map/ppermute | solution.py:67
  35.5 32.3 %collective-permute-start.1 = (bf16[2,192,384]{2,1,0:T(8,128)(2,1)}, bf16[2,192,384]{2,1,0:T(8,128)(2,1)}, u32[]{:S(2)}, u32[]{:S(2)}) collective-permute-start(bf16[2,192,384]{2,1,0:T(8,128)(2,1)} %get-tuple-element.167.refs_1_), channel_id=1, source_target_pairs={{0,8},{2,10},{4,12},{6,14},{8,0},{10,2},{12,4},{14,6},{16,24},{18,... | collective-permute-start | bytes 884744 | tf_op jit(solution)/shard_map/ppermute | solution.py:67
  38.3 32.6 %collective-permute-start.6 = (bf16[2,208,384]{2,1,0:T(8,128)(2,1)}, bf16[2,208,384]{2,1,0:T(8,128)(2,1)}, u32[]{:S(2)}, u32[]{:S(2)}) collective-permute-start(bf16[2,208,384]{2,1,0:T(8,128)(2,1)} %get-tuple-element.163.refs_2_), channel_id=1, source_target_pairs={{0,8},{2,10},{4,12},{6,14},{8,0},{10,2},{12,4},{14,6},{16,24},{18,... | collective-permute-start | bytes 958472 | tf_op jit(solution)/shard_map/ppermute | solution.py:67
  72.0 15.2 %collective-permute-start.7 = (bf16[4,208,384]{2,1,0:T(8,128)(2,1)S(1)}, bf16[4,208,384]{2,1,0:T(8,128)(2,1)S(1)}, u32[]{:S(2)}, u32[]{:S(2)}) collective-permute-start(bf16[4,208,384]{2,1,0:T(8,128)(2,1)S(1)} %pad_maximum_fusion.5), channel_id=1, source_target_pairs={{0,2},{2,0},{4,6},{6,4},{8,10},{10,8},{12,14},{14,12},{16,18},{18,... | collective-permute-start | bytes 1916936 | tf_op jit(solution)/shard_map/ppermute | solution.py:67
  88.4 214.3 %all-to-all-start.1 = ((bf16[32,192,768]{2,1,0:T(8,128)(2,1)}), bf16[32,192,768]{2,1,0:T(8,128)(2,1)}, u32[]{:S(2)}, u32[]{:S(2)}) async-start(bf16[32,192,768]{2,1,0:T(8,128)(2,1)} %hold.9), calls=%async_computation.1 | async-start | bytes 18874368 | tf_op jit(solution)/shard_map/all_to_all | solution.py:1070
  96.5 103.1 %collective-permute-start.8 = (bf16[8,208,384]{2,1,0:T(8,128)(2,1)}, bf16[8,208,384]{2,1,0:T(8,128)(2,1)}, u32[]{:S(2)}, u32[]{:S(2)}) collective-permute-start(bf16[8,208,384]{2,1,0:T(8,128)(2,1)} %get-tuple-element.157.refs_2_), channel_id=1, source_target_pairs={{0,4},{2,6},{4,0},{6,2},{8,12},{10,14},{12,8},{14,10},{16,20},{18,... | collective-permute-start | bytes 3833864 | tf_op jit(solution)/shard_map/ppermute | solution.py:67
  102.0 111.6 %collective-permute-start.3 = (bf16[8,192,384]{2,1,0:T(8,128)(2,1)}, bf16[8,192,384]{2,1,0:T(8,128)(2,1)S(1)}, u32[]{:S(2)}, u32[]{:S(2)}) collective-permute-start(bf16[8,192,384]{2,1,0:T(8,128)(2,1)} %hold.8), channel_id=1, source_target_pairs={{0,2},{2,0},{4,6},{6,4},{8,10},{10,8},{12,14},{14,12},{16,18},{18,... | collective-permute-start | bytes 3538952 | tf_op jit(solution)/shard_map/ppermute | solution.py:67
  202.1 44.0 %collective-permute-start.9 = (bf16[16,208,384]{2,1,0:T(8,128)(2,1)}, bf16[16,208,384]{2,1,0:T(8,128)(2,1)}, u32[]{:S(2)}, u32[]{:S(2)}) collective-permute-start(bf16[16,208,384]{2,1,0:T(8,128)(2,1)} %constant_dynamic-update-slice_fusion.12.own), channel_id=1, source_target_pairs={{0,1},{1,0},{2,3},{3,2},{4,5},{5,4},{6,7},{7,6},{8,9},{9,8},{10,11... | collective-permute-start | bytes 7667720 | tf_op jit(solution)/shard_map/ppermute | solution.py:67
  213.9 27.4 %collective-permute-start.4 = (bf16[16,192,384]{2,1,0:T(8,128)(2,1)S(1)}, bf16[16,192,384]{2,1,0:T(8,128)(2,1)}, u32[]{:S(2)}, u32[]{:S(2)}) collective-permute-start(bf16[16,192,384]{2,1,0:T(8,128)(2,1)S(1)} %pad_maximum_fusion.own), channel_id=1, source_target_pairs={{0,1},{1,0},{2,3},{3,2},{4,5},{5,4},{6,7},{7,6},{8,9},{9,8},{10,11... | collective-permute-start | bytes 7077896 | tf_op jit(solution)/shard_map/ppermute | solution.py:67
  214.0 17.0 %collective-permute-start.17 = (bf16[4,192,384]{2,1,0:T(8,128)(2,1)}, bf16[4,192,384]{2,1,0:T(8,128)(2,1)}, u32[]{:S(2)}, u32[]{:S(2)}) collective-permute-start(bf16[4,192,384]{2,1,0:T(8,128)(2,1)} %pad_maximum_fusion.12.refs_4_), channel_id=1, source_target_pairs={{0,2},{2,0},{4,6},{6,4},{8,10},{10,8},{12,14},{14,12},{16,18},{18,... | collective-permute-start | bytes 1769480 | tf_op jit(solution)/shard_map/ppermute | solution.py:67
  214.1 20.5 %collective-permute-start.14 = (bf16[4,48,1536]{2,1,0:T(8,128)(2,1)S(1)}, bf16[4,48,1536]{2,1,0:T(8,128)(2,1)}, u32[]{:S(2)}, u32[]{:S(2)}) collective-permute-start(bf16[4,48,1536]{2,1,0:T(8,128)(2,1)S(1)} %copy-done.111), channel_id=1, source_target_pairs={{0,4},{2,6},{4,0},{6,2},{8,12},{10,14},{12,8},{14,10},{16,20},{18,... | collective-permute-start | bytes 1769480 | tf_op jit(solution)/shard_map/ppermute | solution.py:67
  233.3 40.7 %collective-permute-start.18 = (bf16[8,192,384]{2,1,0:T(8,128)(2,1)}, bf16[8,192,384]{2,1,0:T(8,128)(2,1)}, u32[]{:S(2)}, u32[]{:S(2)}) collective-permute-start(bf16[8,192,384]{2,1,0:T(8,128)(2,1)} %pad_maximum_fusion.4.refs_0_), channel_id=1, source_target_pairs={{0,4},{2,6},{4,0},{6,2},{8,12},{10,14},{12,8},{14,10},{16,20},{18,... | collective-permute-start | bytes 3538952 | tf_op jit(solution)/shard_map/ppermute | solution.py:67
  236.9 37.1 %collective-permute-start.15 = (bf16[8,48,1536]{2,1,0:T(8,128)(2,1)}, bf16[8,48,1536]{2,1,0:T(8,128)(2,1)}, u32[]{:S(2)}, u32[]{:S(2)}) collective-permute-start(bf16[8,48,1536]{2,1,0:T(8,128)(2,1)} %pad_maximum_fusion.3.refs_0_), channel_id=1, source_target_pairs={{0,2},{2,0},{4,6},{6,4},{8,10},{10,8},{12,14},{14,12},{16,18},{18,... | collective-permute-start | bytes 3538952 | tf_op jit(solution)/shard_map/ppermute | solution.py:67
  397.1 222.9 %all-to-all-start.2 = ((bf16[32,192,768]{2,1,0:T(8,128)(2,1)}), bf16[32,192,768]{2,1,0:T(8,128)(2,1)}, u32[]{:S(2)}, u32[]{:S(2)}) async-start(bf16[32,192,768]{2,1,0:T(8,128)(2,1)} %get-tuple-element.91), calls=%async_computation.2 | async-start | bytes 18874368 | tf_op jit(solution)/shard_map/all_to_all | solution.py:1070
  414.9 36.7 %collective-permute-start.24 = (bf16[16,192,384]{2,1,0:T(8,128)(2,1)}, bf16[16,192,384]{2,1,0:T(8,128)(2,1)}, u32[]{:S(2)}, u32[]{:S(2)}) collective-permute-start(bf16[16,192,384]{2,1,0:T(8,128)(2,1)} %get-tuple-element.81.refs_4_), channel_id=1, source_target_pairs={{0,1},{1,0},{2,3},{3,2},{4,5},{5,4},{6,7},{7,6},{8,9},{9,8},{10,11... | collective-permute-start | bytes 7077896 | tf_op jit(solution)/shard_map/ppermute | solution.py:67
  419.2 35.5 %collective-permute-start.23 = (bf16[16,192,384]{2,1,0:T(8,128)(2,1)}, bf16[16,192,384]{2,1,0:T(8,128)(2,1)}, u32[]{:S(2)}, u32[]{:S(2)}) collective-permute-start(bf16[16,192,384]{2,1,0:T(8,128)(2,1)} %get-tuple-element.79.refs_2_), channel_id=1, source_target_pairs={{0,1},{1,0},{2,3},{3,2},{4,5},{5,4},{6,7},{7,6},{8,9},{9,8},{10,11... | collective-permute-start | bytes 7077896 | tf_op jit(solution)/shard_map/ppermute | solution.py:67
  451.4 44.1 %collective-permute-start.20 = (bf16[16,192,384]{2,1,0:T(8,128)(2,1)}, bf16[16,192,384]{2,1,0:T(8,128)(2,1)}, u32[]{:S(2)}, u32[]{:S(2)}) collective-permute-start(bf16[16,192,384]{2,1,0:T(8,128)(2,1)} %get-tuple-element.93.refs_6_), channel_id=1, source_target_pairs={{0,1},{1,0},{2,3},{3,2},{4,5},{5,4},{6,7},{7,6},{8,9},{9,8},{10,11... | collective-permute-start | bytes 7077896 | tf_op jit(solution)/shard_map/ppermute | solution.py:67
  488.5 51.3 %collective-permute-start.31 = (bf16[8,192,384]{2,1,0:T(8,128)(2,1)}, bf16[8,192,384]{2,1,0:T(8,128)(2,1)S(1)}, u32[]{:S(2)}, u32[]{:S(2)}) collective-permute-start(bf16[8,192,384]{2,1,0:T(8,128)(2,1)} %copy-done.45), channel_id=1, source_target_pairs={{0,4},{2,6},{4,0},{6,2},{8,12},{10,14},{12,8},{14,10},{16,20},{18,... | collective-permute-start | bytes 3538952 | tf_op jit(solution)/shard_map/ppermute | solution.py:67
  494.0 49.8 %collective-permute-start.29 = (bf16[8,192,384]{2,1,0:T(8,128)(2,1)S(1)}, bf16[8,192,384]{2,1,0:T(8,128)(2,1)S(1)}, u32[]{:S(2)}, u32[]{:S(2)}) collective-permute-start(bf16[8,192,384]{2,1,0:T(8,128)(2,1)S(1)} %copy-done.44), channel_id=1, source_target_pairs={{0,2},{2,0},{4,6},{6,4},{8,10},{10,8},{12,14},{14,12},{16,18},{18,... | collective-permute-start | bytes 3538952 | tf_op jit(solution)/shard_map/ppermute | solution.py:67
  497.5 68.8 %collective-permute-start.21 = (bf16[8,192,384]{2,1,0:T(8,128)(2,1)S(1)}, bf16[8,192,384]{2,1,0:T(8,128)(2,1)S(1)}, u32[]{:S(2)}, u32[]{:S(2)}) collective-permute-start(bf16[8,192,384]{2,1,0:T(8,128)(2,1)S(1)} %get-tuple-element.122), channel_id=1, source_target_pairs={{0,2},{2,0},{4,6},{6,4},{8,10},{10,8},{12,14},{14,12},{16,18},{18,... | collective-permute-start | bytes 3538952 | tf_op jit(solution)/shard_map/ppermute | solution.py:67
  500.3 90.5 %collective-permute-start.26 = (bf16[8,208,384]{2,1,0:T(8,128)(2,1)S(1)}, bf16[8,208,384]{2,1,0:T(8,128)(2,1)S(1)}, u32[]{:S(2)}, u32[]{:S(2)}) collective-permute-start(bf16[8,208,384]{2,1,0:T(8,128)(2,1)S(1)} %get-tuple-element.120), channel_id=1, source_target_pairs={{0,4},{2,6},{4,0},{6,2},{8,12},{10,14},{12,8},{14,10},{16,20},{18,... | collective-permute-start | bytes 3833864 | tf_op jit(solution)/shard_map/ppermute | solution.py:67
  539.9 50.8 %collective-permute-start.32 = (bf16[4,192,384]{2,1,0:T(8,128)(2,1)S(1)}, bf16[4,192,384]{2,1,0:T(8,128)(2,1)S(1)}, u32[]{:S(2)}, u32[]{:S(2)}) collective-permute-start(bf16[4,192,384]{2,1,0:T(8,128)(2,1)S(1)} %get-tuple-element.134), channel_id=1, source_target_pairs={{0,2},{2,0},{4,6},{6,4},{8,10},{10,8},{12,14},{14,12},{16,18},{18,... | collective-permute-start | bytes 1769480 | tf_op jit(solution)/shard_map/ppermute | solution.py:67
  544.0 51.6 %collective-permute-start.30 = (bf16[4,192,384]{2,1,0:T(8,128)(2,1)S(1)}, bf16[4,192,384]{2,1,0:T(8,128)(2,1)S(1)}, u32[]{:S(2)}, u32[]{:S(2)}) collective-permute-start(bf16[4,192,384]{2,1,0:T(8,128)(2,1)S(1)} %get-tuple-element.132), channel_id=1, source_target_pairs={{0,4},{2,6},{4,0},{6,2},{8,12},{10,14},{12,8},{14,10},{16,20},{18,... | collective-permute-start | bytes 1769480 | tf_op jit(solution)/shard_map/ppermute | solution.py:67
  566.5 41.7 %collective-permute-start.22 = (bf16[4,192,384]{2,1,0:T(8,128)(2,1)S(1)}, bf16[4,192,384]{2,1,0:T(8,128)(2,1)S(1)}, u32[]{:S(2)}, u32[]{:S(2)}) collective-permute-start(bf16[4,192,384]{2,1,0:T(8,128)(2,1)S(1)} %get-tuple-element.130), channel_id=1, source_target_pairs={{0,4},{2,6},{4,0},{6,2},{8,12},{10,14},{12,8},{14,10},{16,20},{18,... | collective-permute-start | bytes 1769480 | tf_op jit(solution)/shard_map/ppermute | solution.py:67
  591.0 17.3 %collective-permute-start.27 = (bf16[4,208,384]{2,1,0:T(8,128)(2,1)S(1)}, bf16[4,208,384]{2,1,0:T(8,128)(2,1)S(1)}, u32[]{:S(2)}, u32[]{:S(2)}) collective-permute-start(bf16[4,208,384]{2,1,0:T(8,128)(2,1)S(1)} %get-tuple-element.128), channel_id=1, source_target_pairs={{0,2},{2,0},{4,6},{6,4},{8,10},{10,8},{12,14},{14,12},{16,18},{18,... | collective-permute-start | bytes 1916936 | tf_op jit(solution)/shard_map/ppermute | solution.py:67
  596.6 38.4 %collective-permute-start.33 = (bf16[2,384,384]{2,1,0:T(8,128)(2,1)}, bf16[2,384,384]{2,1,0:T(8,128)(2,1)}, u32[]{:S(2)}, u32[]{:S(2)}) collective-permute-start(bf16[2,384,384]{2,1,0:T(8,128)(2,1)} %pad_maximum_fusion.14), channel_id=1, source_target_pairs={{0,8},{2,10},{4,12},{6,14},{8,0},{10,2},{12,4},{14,6},{16,24},{18,... | collective-permute-start | bytes 1769480 | tf_op jit(solution)/shard_map/ppermute | solution.py:67
  608.5 28.7 %collective-permute-start.28 = (bf16[2,400,384]{2,1,0:T(8,128)(2,1)S(1)}, bf16[2,400,384]{2,1,0:T(8,128)(2,1)S(1)}, u32[]{:S(2)}, u32[]{:S(2)}) collective-permute-start(bf16[2,400,384]{2,1,0:T(8,128)(2,1)S(1)} %pad_maximum_fusion.7), channel_id=1, source_target_pairs={{0,8},{2,10},{4,12},{6,14},{8,0},{10,2},{12,4},{14,6},{16,24},{18,... | collective-permute-start | bytes 1843208 | tf_op jit(solution)/shard_map/ppermute | solution.py:67
  637.4 28.0 %collective-permute-start.34 = (bf16[1,784,384]{2,1,0:T(8,128)(2,1)S(1)}, bf16[1,784,384]{2,1,0:T(8,128)(2,1)}, u32[]{:S(2)}, u32[]{:S(2)}) collective-permute-start(bf16[1,784,384]{2,1,0:T(8,128)(2,1)S(1)} %pad_maximum_fusion.8.refs_1_), channel_id=1, source_target_pairs={{0,16},{2,18},{4,20},{6,22},{8,24},{10,26},{12,28},{14,30},{16,0},... | collective-permute-start | bytes 1806344 | tf_op jit(solution)/shard_map/ppermute | solution.py:67
  (134 other events, 1140.4 us)

commit v5 on v4

--- a/solution.py
+++ b/solution.py
@@ -773,13 +773,10 @@
     return mix, (score * query[...].reshape(-1, dim).astype(F32)).astype(BF)
 
 
-def rows_out_kernel(prob_slot, grad_slot, grad, query, w_k, w_v, out, flag):
-    group, k, dim = grad.shape
+def rows_out_kernel(prob_slot, grad_slot, grad, query, w_k, w_v, *refs):
+    out, flag = refs[-2:]
     mix, ask = weigh(prob_slot, grad_slot, grad, query)
-    for at in range(0, dim, TILE):
-        tile = slice(at, at + TILE)
-        got = mm_nt(mix, w_v[tile]) + mm_nt(ask, w_k[tile])
-        out[:, :, tile] = got.astype(BF).reshape(group, k, TILE)
+    out[...] = (mm_nt(mix, w_v[...]) + mm_nt(ask, w_k[...])).astype(BF).reshape(grad.shape)
     flag[...] = jnp.zeros_like(flag)
 
 
@@ -953,14 +950,24 @@
         )(from_hbm(self.vals), self.token, grad, self.prob_tok, self.at_rank, self.owner)
         self.factors = (self.prob_slot, self.grad_slot, from_hbm(grads), from_hbm(self.query))
         self.factor_specs = [self.lanes, self.lanes, self.rows, self.rows]
+        return [self.send(0), self.send(1)]
+
+    def send(self, part):
+        k = self.slots // 2
+        some = pl.BlockSpec((GROUP, k, self.dim), lambda g, c: (g, part, 0))
+        lanes = pl.BlockSpec((k, LANES), lambda g, c: (part, g))
+        before = [self.flag] if part else []
         sent, self.flag = self.call(
             rows_out_kernel,
             "rows_out",
-            28,
-            self.factor_specs + self.w_specs,
-            [self.rows, self.whole(8, LANES)],
-            (self.slot_rows, jax.ShapeDtypeStruct((8, LANES), F32)),
-        )(*self.factors, self.mats, self.mats)
+            14,
+            [lanes, lanes, some, some] + self.w_specs + [self.whole(8, LANES)] * part,
+            [pl.BlockSpec((GROUP, k, self.dim), lambda g, c: (g, 0, 0)), self.whole(8, LANES)],
+            (
+                in_hbm((self.peers, k, self.dim), BF),
+                jax.ShapeDtypeStruct((8, LANES), F32),
+            ),
+        )(*self.factors, self.mats, self.mats, *before)
         return sent
 
     def query_grad(self):
@@ -1019,7 +1026,7 @@
             "the,dhe->htd", self.grad, self.val_heads, preferred_element_type=F32
         ).astype(BF)
         rows, self.grad_s = self.bwd(self.query_keys, grad_mix, self.fetched, self.cross_p)
-        return rows[self.entry]
+        return [rows[self.entry]]
 
     def query_grad(self):
         self.grad_qk = self.back_q(self.grad_s, self.fetched)
@@ -1037,31 +1044,35 @@
         return grad_k, product(self.state_mix, self.grad)
 
 
-def store_sum_kernel(asked, returned, *refs, block, skip):
+def store_sum_kernel(asked, returned, *refs, block, skip, added):
     first = (pl.program_id(0) + skip) * block + 1
     shape = (block, asked.shape[1])
     hit = lax.broadcasted_iota(jnp.int32, shape, 0) + first == asked[...]
-    refs[-1][...] = mm(hit.astype(BF), returned[...])
-
-
-def store_sum(asked, returned, shard_rows, part, so_far=(), after=()):
+    total = mm(hit.astype(BF), returned[...])
+    refs[-1][...] = total + refs[0][...] if added else total
+
+
+def store_sum(asked, returned, shard_rows, so_far=(), rows=(0, 1), after=()):
     count, dim = returned.shape
     block = 256
-    steps = shard_rows // block // 2
+    part, parts = rows
+    steps = shard_rows // block // parts
     skip = part * steps
+    here = pl.BlockSpec((block, dim), lambda g: (g + skip, 0))
     return pl.pallas_call(
-        functools.partial(store_sum_kernel, block=block, skip=skip),
+        functools.partial(store_sum_kernel, block=block, skip=skip, added=bool(so_far)),
         grid=(steps,),
         in_specs=[
             pl.BlockSpec((1, count), lambda g: (0, 0)),
             pl.BlockSpec((count, dim), lambda g: (0, 0)),
         ]
-        + [WAIT] * (len(so_far) + len(after)),
-        out_specs=pl.BlockSpec((block, dim), lambda g: (g + skip, 0)),
+        + [here] * len(so_far)
+        + [WAIT] * len(after),
+        out_specs=here,
         out_shape=in_hbm((shard_rows, dim), F32),
         input_output_aliases={2: 0} if so_far else {},
         compiler_params=pltpu.CompilerParams(vmem_limit_bytes=VMEM_LIMIT),
-        cost_estimate=cost(13),
+        cost_estimate=cost(13 if parts == 1 else 8),
         name="store_sum",
     )(asked.reshape(1, count), returned, *so_far, *after)
 
@@ -1192,7 +1203,7 @@
     grad_o2 = grad_two.astype(BF)
     grad_cmix = mm_nt(grad_o2, w_co).astype(BF)
     send_back = attention.backward(grad_cmix)
-    returned = all_to_all(send_back)
+    returned = [all_to_all(send_back[0])]
 
     def packed(order, place, mats, small=None, after=()):
         if by_rows:
@@ -1268,20 +1279,45 @@
         ],
         grad_small,
     )
+    ff = on_both(ff, near - 2, near - 1)
+    if len(send_back) > 1:
+        attn_one = scatter_bits(*attn_one, back_a[: near - 2])
+    for part in send_back[1:]:
+        before = [*returned, *attn_two, *attn_one, *ff[0], *ff[1]]
+        returned.append(all_to_all(hold(part, before)))
+
     def join_pairs(pairs):
         return tuple(jnp.concatenate(both, axis=1) for both in zip(*pairs))
 
-    ff = join_pairs(on_both(ff, near - 2, near))
-    attn = join_pairs(on_both([attn_one, attn_two], 0, near))
+    if len(send_back) > 1:
+        attn_two = scatter_bits(*attn_two, back_b[: near - 2])
+        attn = join_pairs(on_both([attn_one, attn_two], near - 2, near))
+    else:
+        attn = join_pairs(on_both([attn_one, attn_two], 0, near))
     def behind(pair, array):
         return (hold(pair[0], [array]), pair[1]) if by_rows else pair
 
-    rows = returned.reshape(-1, dim)
-    grad_store = store_sum(asked, rows, shard_rows, 0)
-    ff, attn = (scatter_bits(*behind(x, grad_store), back_a[near:-1]) for x in (ff, attn))
+    size = asked.shape[1] // len(returned)
+    lists = [
+        (asked[:, i * size : (i + 1) * size], rows.reshape(-1, dim), shard_rows)
+        for i, rows in enumerate(returned)
+    ]
+    so_far = ()
+    for args in lists[:-1]:
+        so_far = (store_sum(*args),)
+        ff = [behind(pair, so_far[0]) for pair in ff]
+    ff = join_pairs(on_both(ff, near - 1, near))
+    grad_store = store_sum(*lists[-1], so_far, (0, 2)) if so_far else None
+    if so_far:
+        ff, attn = behind(ff, grad_store), behind(attn, grad_store)
+    ff, attn = (scatter_bits(*x, back_a[near:-1]) for x in (ff, attn))
     last = join_pairs([attn, ff])
-    grad_store = store_sum(asked, rows, shard_rows, 1, (grad_store,), (last[1],))
-    keep, send = behind(last, grad_store)
+    if so_far:
+        grad_store = store_sum(*lists[-1], (grad_store,), (1, 2), (last[1],))
+        keep, send = behind(last, grad_store)
+    else:
+        grad_store = store_sum(*lists[-1])
+        keep, send = last
     total = (keep + swap_bit(send, *order_a[0]))[0].astype(F32)
     total_a, total_b = total[: attn[0].shape[1]], total[attn[0].shape[1] :]
 

time: 678 us -> 676 us (level)
  waiting for transfers between devices: 251 us -> 240 us
    ppermute x35, waiting for transfers between devices: 241 us -> 230 us  [swap_bit(): return lax.ppermute(array, axis, pairs)]
    all_to_all x3 -> x4, starting transfers between devices: 15.1 us -> 20.1 us  [all_to_all(): return lax.all_to_all(array, RANKS, split_axis=0, concat_axis=0, tiled=True)]
    pallas_call x1 -> x2, Pallas kernels: 28.2 us -> 31.1 us  [send(): self.call(rows_out_kernel, 'rows_out', 14, [lanes, lanes, some, some] + s...]
    pallas_call x2 -> x3, Pallas kernels: 30.3 us -> 32.7 us  [store_sum(): pl.pallas_call(functools.partial(store_sum_kernel, block=block, skip=skip...]
    unnamed x262 -> x258, local copies, waits for them, and re-layouts: 53.6 us -> 52.4 us
  transfers between devices with their start and end apart: 38 -> 39, of which waited for: 16 -> 15; matrix products, arithmetic and copies ran while one was open for 14% -> 15% of each run, Pallas kernels for 18% -> 21%
where the time goes in v5:
time: 676 us; the launch traced here: 670 us
  waiting for transfers between devices  240 us (36%)
  Pallas kernels  202 us (30%)
  local copies, waits for them, and re-layouts  99.6 us (15%)
  starting transfers between devices  62 us (9%)
  other arithmetic  48.5 us (7%)
  matrix products  14.8 us (2%)
    ppermute x35, waiting for transfers between devices, swap_bit(): return lax.ppermute(array, axis, pairs)  230 us
    unnamed x258, local copies, waits for them, and re-layouts  52.4 us
    ppermute x35, starting transfers between devices, swap_bit(): return lax.ppermute(array, axis, pairs)  41.9 us
    pallas_call x3, Pallas kernels, store_sum(): pl.pallas_call(functools.partial(store_sum_kernel, block=block, skip=skip...  32.7 us
    pallas_call x2, Pallas kernels, send(): self.call(rows_out_kernel, 'rows_out', 14, [lanes, lanes, some, some] + s...  31.1 us
    gather x1, local copies, waits for them, and re-layouts, on_device(): answer = enc_store[jnp.maximum(asked - 1, 0)]  26.3 us
    pallas_call x1, Pallas kernels, weights(): self.call(rows_weights_kernel, 'rows_weights', 24, self.factor_specs + [s...  24.4 us
    pallas_call x1, Pallas kernels, forward(): self.call(rows_in_kernel, 'rows_in', 22, [self.rows, self.rows, *self.w_s...  23.2 us
  transfers between devices with their start and end apart: 39, of which 15 were waited for; matrix products, arithmetic and copies ran while one was open for 15% of the time, Pallas kernels for 21%

profile of v5, /device:TPU:0, one launch (start us, length us, event | category | flops | bytes accessed | tf_op | source)
XLA Modules:
  0.0 669.5 jit_solution(5270319404957632678)
XLA Ops:
  0.7 4.1 collective-permute-start.10
  4.9 4.5 plan.1
  10.8 6.1 all-to-all-start
  41.5 26.3 %gather_fusion.2 = bf16[6144,768]{1,0:T(8,128)(2,1)} fusion(bf16[2048,768]{1,0:T(8,128)(2,1)S(1)} %copy-done, s32[6144]{0:T(1024)S(1)} %broadcast_clamp_fusion), kind=kCustom, calls=%fused_computation.2 | custom fusion | bytes 18898944 | tf_op jit(solution)/shard_map/gather | solution.py:1145
  88.4 5.1 all-to-all-start.1
  103.5 96.2 %collective-permute-done.8 = bf16[8,208,384]{2,1,0:T(8,128)(2,1)} collective-permute-done((bf16[8,208,384]{2,1,0:T(8,128)(2,1)}, bf16[8,208,384]{2,1,0:T(8,128)(2,1)}, u32[]{:S(2)}, u32[]{:S(2)}) %collective-permute-start.8) | collective-permute-done | bytes 1277984 | tf_op jit(solution)/shard_map/ppermute | solution.py:67
  202.3 11.4 %collective-permute-done.3 = bf16[8,192,384]{2,1,0:T(8,128)(2,1)S(1)} collective-permute-done((bf16[8,192,384]{2,1,0:T(8,128)(2,1)}, bf16[8,192,384]{2,1,0:T(8,128)(2,1)S(1)}, u32[]{:S(2)}, u32[]{:S(2)}) %collective-permute-start.3) | collective-permute-done | bytes 1179680 | tf_op jit(solution)/shard_map/ppermute | solution.py:67
  217.5 13.6 %collective-permute-done.17 = bf16[4,192,384]{2,1,0:T(8,128)(2,1)} collective-permute-done((bf16[4,192,384]{2,1,0:T(8,128)(2,1)}, bf16[4,192,384]{2,1,0:T(8,128)(2,1)}, u32[]{:S(2)}, u32[]{:S(2)}) %collective-permute-start.17) | collective-permute-done | bytes 589856 | tf_op jit(solution)/shard_map/ppermute | solution.py:67
  237.0 4.4 collective-permute-start.15
  258.4 4.7 self_fwd.1
  263.9 5.3 query_rows.1.query.refs_1_.refs_3_
  269.3 4.8 collective-permute-done.18
  293.3 9.6 %all-to-all-done.1.arrived.refs_4_ = bf16[32,192,768]{2,1,0:T(8,128)(2,1)} async-done(((bf16[32,192,768]{2,1,0:T(8,128)(2,1)}), bf16[32,192,768]{2,1,0:T(8,128)(2,1)}, u32[]{:S(2)}, u32[]{:S(2)}) %all-to-all-start.1) | async-done | bytes 9437216 | tf_op jit(solution)/shard_map/all_to_all | solution.py:1081
  305.2 23.2 %rows_in.1 = (bf16[32,192,768]{2,1,0:T(8,128)(2,1)}, bf16[32,192,768]{2,1,0:T(8,128)(2,1)}, f32[192,512]{1,0:T(8,128)S(1)}) custom-call(bf16[32,192,768]{2,1,0:T(8,128)(2,1)} %all-to-all-done.1.arrived.refs_4_, bf16[32,192,768]{2,1,0:T(8,128)(2,1)} %query_rows.1.query.refs_1_.refs_3_, bf16[4,768,768]{2,1,0:T(8,128)(2,1)S(1)} %copy-done.59, ...), custom_call_target="tpu_custom_call" | custom-call | flops 24199999488 | tf_op jit(solution)/shard_map/rows_in/pallas_call | solution.py:914
  328.4 11.6 %attend.1 = (f32[256,256]{1,0:T(8,128)S(1)}, f32[192,512]{1,0:T(8,128)S(1)}, bf16[256,768]{1,0:T(8,128)(2,1)S(1)}) custom-call(f32[192,512]{1,0:T(8,128)S(1)} %get-tuple-element.69.scores, bf16[32,192,768]{2,1,0:T(8,128)(2,1)} %get-tuple-element.70.vals, bf16[256,6144]{1,0:T(8,128)(2,1)S(1)} %copy-done.13, bf16[256,4096]{1,0:T(8,128)(2,1)S(1)} %copy-done.77, ...), custom_call_target="tpu_custom_call" | custom-call | flops 12099999744 | tf_op jit(solution)/shard_map/attend/pallas_call | solution.py:923
  354.1 14.3 %attend_back.1 = (bf16[32,192,768]{2,1,0:T(8,128)(2,1)}, f32[192,512]{1,0:T(8,128)S(1)}) custom-call(bf16[32,192,768]{2,1,0:T(8,128)(2,1)} %get-tuple-element.70.vals, bf16[6144,256]{1,0:T(8,128)(2,1)S(1)} %copy-done.16, bf16[256,768]{1,0:T(8,128)(2,1)S(1)} %convolution_convert_fusion.grad.refs_4_, f32[256,256]{1,0:T(8,128)S(1)} %get-tuple-element.75.prob_tok, ...), custom_call_target="tpu_custom_call" | custom-call | flops 14300000256 | tf_op jit(solution)/shard_map/attend_back/pallas_call | solution.py:941
  368.4 15.6 %rows_out.2 = (bf16[32,96,768]{2,1,0:T(8,128)(2,1)}, f32[8,128]{1,0:T(8,128)S(1)}) custom-call(f32[192,512]{1,0:T(8,128)S(1)} %get-tuple-element.77.prob_slot.refs_0_, f32[192,512]{1,0:T(8,128)S(1)} %get-tuple-element.76.grad_slot.refs_1_, bf16[32,192,768]{2,1,0:T(8,128)(2,1)} %get-tuple-element.78.grad.refs_2_, ...), custom_call_target="tpu_custom_call" | custom-call | flops 15399999488 | tf_op jit(solution)/shard_map/rows_out/pallas_call | solution.py:960
  390.2 15.6 %rows_out.3 = (bf16[32,96,768]{2,1,0:T(8,128)(2,1)}, f32[8,128]{1,0:T(8,128)S(1)}) custom-call(f32[192,512]{1,0:T(8,128)S(1)} %copy-done.90, f32[192,512]{1,0:T(8,128)S(1)} %get-tuple-element.76.grad_slot.refs_1_, bf16[32,192,768]{2,1,0:T(8,128)(2,1)} %get-tuple-element.78.grad.refs_2_, bf16[32,192,768]{2,1,0:T(8,128)(2,1)} %query_rows.1.query.refs_1_.refs_3_, ...), custom_call_target="tpu_custom_call" | custom-call | flops 15399999488 | tf_op jit(solution)/shard_map/rows_out/pallas_call | solution.py:960
  405.8 7.9 %query_back.1.refs_2_.refs_0_ = bf16[256,768]{1,0:T(8,128)(2,1)S(1)} custom-call(bf16[32,192,768]{2,1,0:T(8,128)(2,1)} %get-tuple-element.74.keys, bf16[256,6144]{1,0:T(8,128)(2,1)S(1)} %copy-done.14, f32[192,512]{1,0:T(8,128)S(1)} %get-tuple-element.76.grad_slot.refs_1_, f32[8,128]{1,0:T(8,128)S(1)} %get-tuple-element.80.waited), custom_call_target="tpu_custom_call" | custom-call | flops 7699999744 | tf_op jit(solution)/shard_map/query_back/pallas_call | solution.py:975
  413.7 4.2 pack.5
  418.2 4.2 pack.4
  436.8 5.6 self_bwd.1
  450.3 4.1 pack.6
  462.1 24.4 %rows_weights.1 = (bf16[768,768]{1,0:T(8,128)(2,1)S(1)}, bf16[768,768]{1,0:T(8,128)(2,1)S(1)}) custom-call(f32[192,512]{1,0:T(8,128)S(1)} %copy-done.91, f32[192,512]{1,0:T(8,128)S(1)} %copy-done.86, bf16[32,192,768]{2,1,0:T(8,128)(2,1)} %get-tuple-element.78.grad.refs_2_, bf16[32,192,768]{2,1,0:T(8,128)(2,1)} %query_rows.1.query.refs_1_.refs_3_, ...), custom_call_target="tpu_custom_call" | custom-call | flops 26400000000 | tf_op jit(solution)/shard_map/rows_weights/pallas_call | solution.py:987
  486.6 4.2 pack.7
  497.7 5.0 all-to-all-start.3
  514.7 61.1 %collective-permute-done.25 = bf16[8,192,384]{2,1,0:T(8,128)(2,1)} collective-permute-done((bf16[8,192,384]{2,1,0:T(8,128)(2,1)}, bf16[8,192,384]{2,1,0:T(8,128)(2,1)}, u32[]{:S(2)}, u32[]{:S(2)}) %collective-permute-start.25) | collective-permute-done | bytes 1179680 | tf_op jit(solution)/shard_map/ppermute | solution.py:67
  587.5 11.9 %collective-permute-done.26 = bf16[4,192,384]{2,1,0:T(8,128)(2,1)S(1)} collective-permute-done((bf16[4,192,384]{2,1,0:T(8,128)(2,1)S(1)}, bf16[4,192,384]{2,1,0:T(8,128)(2,1)S(1)}, u32[]{:S(2)}, u32[]{:S(2)}) %collective-permute-start.26) | collective-permute-done | bytes 589856 | tf_op jit(solution)/shard_map/ppermute | solution.py:67
  608.0 14.4 %store_sum.3.refs_0_.refs_1_ = f32[2048,768]{1,0:T(8,128)} custom-call(s32[1,3072]{1,0:T(1,128)} %reshape.148.asked, bf16[3072,768]{1,0:T(8,128)(2,1)} %bitcast.17.returned), custom_call_target="tpu_custom_call" | custom-call | flops 14300000256 | tf_op jit(solution)/shard_map/store_sum/pallas_call | solution.py:1062
  625.7 9.1 %store_sum.4.refs_1_.refs_0_ = f32[2048,768]{1,0:T(8,128)} custom-call(s32[1,3072]{1,0:T(1,128)} %reshape.144.asked, bf16[3072,768]{1,0:T(8,128)(2,1)} %bitcast.16.returned, f32[2048,768]{1,0:T(8,128)} %store_sum.3.refs_0_.refs_1_), custom_call_target="tpu_custom_call", output_to_operand_aliasing={{}: (2, {})} | custom-call | flops 8800000000 | tf_op jit(solution)/shard_map/store_sum/pallas_call | solution.py:1062
  640.3 9.1 %store_sum.5.refs_1_ = f32[2048,768]{1,0:T(8,128)} custom-call(s32[1,3072]{1,0:T(1,128)} %reshape.144.asked, bf16[3072,768]{1,0:T(8,128)(2,1)} %bitcast.16.returned, f32[2048,768]{1,0:T(8,128)} %store_sum.4.refs_1_.refs_0_, bf16[1,784,384]{2,1,0:T(8,128)(2,1)} %copy-done.115), custom_call_target="tpu_custom_call", output_to_operand_aliasing={{}: (2, {})} | custom-call | flops 8800000000 | tf_op jit(solution)/shard_map/store_sum/pallas_call | solution.py:1062
  649.4 13.7 %collective-permute-done.34 = bf16[1,784,384]{2,1,0:T(8,128)(2,1)} collective-permute-done((bf16[1,784,384]{2,1,0:T(8,128)(2,1)S(1)}, bf16[1,784,384]{2,1,0:T(8,128)(2,1)}, u32[]{:S(2)}, u32[]{:S(2)}) %collective-permute-start.34) | collective-permute-done | bytes 602144 | tf_op jit(solution)/shard_map/ppermute | solution.py:67
  (456 shorter events, 212.0 us)
Async XLA Ops:
  0.7 25.5 %collective-permute-start.10 = (bf16[1,48,1536]{2,1,0:T(8,128)(2,1)}, bf16[1,48,1536]{2,1,0:T(8,128)(2,1)}, u32[]{:S(2)}, u32[]{:S(2)}) collective-permute-start(bf16[1,48,1536]{2,1,0:T(8,128)(2,1)} %bitcast.99), channel_id=1, source_target_pairs={{0,16},{2,18},{4,20},{6,22},{8,24},{10,26},{12,28},{14,30},{16,0},... | collective-permute-start | bytes 442376 | tf_op jit(solution)/shard_map/ppermute | solution.py:67
  4.8 24.9 %collective-permute-start.12 = (bf16[1,192,384]{2,1,0:T(8,128)(2,1)}, bf16[1,192,384]{2,1,0:T(8,128)(2,1)}, u32[]{:S(2)}, u32[]{:S(2)}) collective-permute-start(bf16[1,192,384]{2,1,0:T(8,128)(2,1)} %bitcast.95), channel_id=1, source_target_pairs={{0,16},{2,18},{4,20},{6,22},{8,24},{10,26},{12,28},{14,30},{16,0},... | collective-permute-start | bytes 442376 | tf_op jit(solution)/shard_map/ppermute | solution.py:67
  10.8 14.8 %all-to-all-start = ((s32[32,1,192]{2,1,0:T(1,128)}), s32[32,1,192]{2,1,0:T(1,128)S(1)}, u32[]{:S(2)}, u32[]{:S(2)}) async-start(s32[32,1,192]{2,1,0:T(1,128)} %copy.56), calls=%async_computation | async-start | bytes 65536 | tf_op jit(solution)/shard_map/all_to_all | solution.py:1081
  27.8 48.7 %collective-permute-start.11 = (bf16[2,48,1536]{2,1,0:T(8,128)(2,1)}, bf16[2,48,1536]{2,1,0:T(8,128)(2,1)}, u32[]{:S(2)}, u32[]{:S(2)}) collective-permute-start(bf16[2,48,1536]{2,1,0:T(8,128)(2,1)} %pad_maximum_fusion.15), channel_id=1, source_target_pairs={{0,8},{2,10},{4,12},{6,14},{8,0},{10,2},{12,4},{14,6},{16,24},{18,... | collective-permute-start | bytes 884744 | tf_op jit(solution)/shard_map/ppermute | solution.py:67
  31.3 43.3 %collective-permute-start.13 = (bf16[2,192,384]{2,1,0:T(8,128)(2,1)}, bf16[2,192,384]{2,1,0:T(8,128)(2,1)}, u32[]{:S(2)}, u32[]{:S(2)}) collective-permute-start(bf16[2,192,384]{2,1,0:T(8,128)(2,1)} %pad_maximum_fusion.16), channel_id=1, source_target_pairs={{0,8},{2,10},{4,12},{6,14},{8,0},{10,2},{12,4},{14,6},{16,24},{18,... | collective-permute-start | bytes 884744 | tf_op jit(solution)/shard_map/ppermute | solution.py:67
  35.5 32.3 %collective-permute-start.1 = (bf16[2,192,384]{2,1,0:T(8,128)(2,1)}, bf16[2,192,384]{2,1,0:T(8,128)(2,1)}, u32[]{:S(2)}, u32[]{:S(2)}) collective-permute-start(bf16[2,192,384]{2,1,0:T(8,128)(2,1)} %get-tuple-element.171.refs_1_), channel_id=1, source_target_pairs={{0,8},{2,10},{4,12},{6,14},{8,0},{10,2},{12,4},{14,6},{16,24},{18,... | collective-permute-start | bytes 884744 | tf_op jit(solution)/shard_map/ppermute | solution.py:67
  38.3 32.6 %collective-permute-start.6 = (bf16[2,208,384]{2,1,0:T(8,128)(2,1)}, bf16[2,208,384]{2,1,0:T(8,128)(2,1)}, u32[]{:S(2)}, u32[]{:S(2)}) collective-permute-start(bf16[2,208,384]{2,1,0:T(8,128)(2,1)} %get-tuple-element.167.refs_2_), channel_id=1, source_target_pairs={{0,8},{2,10},{4,12},{6,14},{8,0},{10,2},{12,4},{14,6},{16,24},{18,... | collective-permute-start | bytes 958472 | tf_op jit(solution)/shard_map/ppermute | solution.py:67
  72.1 15.2 %collective-permute-start.7 = (bf16[4,208,384]{2,1,0:T(8,128)(2,1)S(1)}, bf16[4,208,384]{2,1,0:T(8,128)(2,1)S(1)}, u32[]{:S(2)}, u32[]{:S(2)}) collective-permute-start(bf16[4,208,384]{2,1,0:T(8,128)(2,1)S(1)} %pad_maximum_fusion.5), channel_id=1, source_target_pairs={{0,2},{2,0},{4,6},{6,4},{8,10},{10,8},{12,14},{14,12},{16,18},{18,... | collective-permute-start | bytes 1916936 | tf_op jit(solution)/shard_map/ppermute | solution.py:67
  88.4 214.4 %all-to-all-start.1 = ((bf16[32,192,768]{2,1,0:T(8,128)(2,1)}), bf16[32,192,768]{2,1,0:T(8,128)(2,1)}, u32[]{:S(2)}, u32[]{:S(2)}) async-start(bf16[32,192,768]{2,1,0:T(8,128)(2,1)} %hold.12), calls=%async_computation.1 | async-start | bytes 18874368 | tf_op jit(solution)/shard_map/all_to_all | solution.py:1081
  96.6 103.1 %collective-permute-start.8 = (bf16[8,208,384]{2,1,0:T(8,128)(2,1)}, bf16[8,208,384]{2,1,0:T(8,128)(2,1)}, u32[]{:S(2)}, u32[]{:S(2)}) collective-permute-start(bf16[8,208,384]{2,1,0:T(8,128)(2,1)} %get-tuple-element.161.refs_2_), channel_id=1, source_target_pairs={{0,4},{2,6},{4,0},{6,2},{8,12},{10,14},{12,8},{14,10},{16,20},{18,... | collective-permute-start | bytes 3833864 | tf_op jit(solution)/shard_map/ppermute | solution.py:67
  102.0 111.7 %collective-permute-start.3 = (bf16[8,192,384]{2,1,0:T(8,128)(2,1)}, bf16[8,192,384]{2,1,0:T(8,128)(2,1)S(1)}, u32[]{:S(2)}, u32[]{:S(2)}) collective-permute-start(bf16[8,192,384]{2,1,0:T(8,128)(2,1)} %hold.11), channel_id=1, source_target_pairs={{0,2},{2,0},{4,6},{6,4},{8,10},{10,8},{12,14},{14,12},{16,18},{18,... | collective-permute-start | bytes 3538952 | tf_op jit(solution)/shard_map/ppermute | solution.py:67
  202.2 44.0 %collective-permute-start.9 = (bf16[16,208,384]{2,1,0:T(8,128)(2,1)}, bf16[16,208,384]{2,1,0:T(8,128)(2,1)}, u32[]{:S(2)}, u32[]{:S(2)}) collective-permute-start(bf16[16,208,384]{2,1,0:T(8,128)(2,1)} %constant_dynamic-update-slice_fusion.12.own), channel_id=1, source_target_pairs={{0,1},{1,0},{2,3},{3,2},{4,5},{5,4},{6,7},{7,6},{8,9},{9,8},{10,11... | collective-permute-start | bytes 7667720 | tf_op jit(solution)/shard_map/ppermute | solution.py:67
  214.0 27.4 %collective-permute-start.4 = (bf16[16,192,384]{2,1,0:T(8,128)(2,1)S(1)}, bf16[16,192,384]{2,1,0:T(8,128)(2,1)}, u32[]{:S(2)}, u32[]{:S(2)}) collective-permute-start(bf16[16,192,384]{2,1,0:T(8,128)(2,1)S(1)} %pad_maximum_fusion.own), channel_id=1, source_target_pairs={{0,1},{1,0},{2,3},{3,2},{4,5},{5,4},{6,7},{7,6},{8,9},{9,8},{10,11... | collective-permute-start | bytes 7077896 | tf_op jit(solution)/shard_map/ppermute | solution.py:67
  214.0 17.0 %collective-permute-start.17 = (bf16[4,192,384]{2,1,0:T(8,128)(2,1)}, bf16[4,192,384]{2,1,0:T(8,128)(2,1)}, u32[]{:S(2)}, u32[]{:S(2)}) collective-permute-start(bf16[4,192,384]{2,1,0:T(8,128)(2,1)} %pad_maximum_fusion.12.refs_4_), channel_id=1, source_target_pairs={{0,2},{2,0},{4,6},{6,4},{8,10},{10,8},{12,14},{14,12},{16,18},{18,... | collective-permute-start | bytes 1769480 | tf_op jit(solution)/shard_map/ppermute | solution.py:67
  214.1 20.5 %collective-permute-start.14 = (bf16[4,48,1536]{2,1,0:T(8,128)(2,1)S(1)}, bf16[4,48,1536]{2,1,0:T(8,128)(2,1)}, u32[]{:S(2)}, u32[]{:S(2)}) collective-permute-start(bf16[4,48,1536]{2,1,0:T(8,128)(2,1)S(1)} %copy-done.109), channel_id=1, source_target_pairs={{0,4},{2,6},{4,0},{6,2},{8,12},{10,14},{12,8},{14,10},{16,20},{18,... | collective-permute-start | bytes 1769480 | tf_op jit(solution)/shard_map/ppermute | solution.py:67
  233.4 40.7 %collective-permute-start.18 = (bf16[8,192,384]{2,1,0:T(8,128)(2,1)}, bf16[8,192,384]{2,1,0:T(8,128)(2,1)}, u32[]{:S(2)}, u32[]{:S(2)}) collective-permute-start(bf16[8,192,384]{2,1,0:T(8,128)(2,1)} %pad_maximum_fusion.4.refs_0_), channel_id=1, source_target_pairs={{0,4},{2,6},{4,0},{6,2},{8,12},{10,14},{12,8},{14,10},{16,20},{18,... | collective-permute-start | bytes 3538952 | tf_op jit(solution)/shard_map/ppermute | solution.py:67
  237.0 37.1 %collective-permute-start.15 = (bf16[8,48,1536]{2,1,0:T(8,128)(2,1)}, bf16[8,48,1536]{2,1,0:T(8,128)(2,1)}, u32[]{:S(2)}, u32[]{:S(2)}) collective-permute-start(bf16[8,48,1536]{2,1,0:T(8,128)(2,1)} %pad_maximum_fusion.3.refs_0_), channel_id=1, source_target_pairs={{0,2},{2,0},{4,6},{6,4},{8,10},{10,8},{12,14},{14,12},{16,18},{18,... | collective-permute-start | bytes 3538952 | tf_op jit(solution)/shard_map/ppermute | solution.py:67
  383.9 113.7 %all-to-all-start.2 = ((bf16[32,96,768]{2,1,0:T(8,128)(2,1)}), bf16[32,96,768]{2,1,0:T(8,128)(2,1)}, u32[]{:S(2)}, u32[]{:S(2)}) async-start(bf16[32,96,768]{2,1,0:T(8,128)(2,1)} %get-tuple-element.95), calls=%async_computation.2 | async-start | bytes 9437184 | tf_op jit(solution)/shard_map/all_to_all | solution.py:1081
  417.9 36.8 %collective-permute-start.21 = (bf16[16,192,384]{2,1,0:T(8,128)(2,1)}, bf16[16,192,384]{2,1,0:T(8,128)(2,1)}, u32[]{:S(2)}, u32[]{:S(2)}) collective-permute-start(bf16[16,192,384]{2,1,0:T(8,128)(2,1)} %get-tuple-element.84.refs_4_), channel_id=1, source_target_pairs={{0,1},{1,0},{2,3},{3,2},{4,5},{5,4},{6,7},{7,6},{8,9},{9,8},{10,11... | collective-permute-start | bytes 7077896 | tf_op jit(solution)/shard_map/ppermute | solution.py:67
  422.4 36.2 %collective-permute-start.20 = (bf16[16,192,384]{2,1,0:T(8,128)(2,1)}, bf16[16,192,384]{2,1,0:T(8,128)(2,1)}, u32[]{:S(2)}, u32[]{:S(2)}) collective-permute-start(bf16[16,192,384]{2,1,0:T(8,128)(2,1)} %get-tuple-element.82.refs_2_), channel_id=1, source_target_pairs={{0,1},{1,0},{2,3},{3,2},{4,5},{5,4},{6,7},{7,6},{8,9},{9,8},{10,11... | collective-permute-start | bytes 7077896 | tf_op jit(solution)/shard_map/ppermute | solution.py:67
  454.4 36.3 %collective-permute-start.22 = (bf16[16,192,384]{2,1,0:T(8,128)(2,1)}, bf16[16,192,384]{2,1,0:T(8,128)(2,1)}, u32[]{:S(2)}, u32[]{:S(2)}) collective-permute-start(bf16[16,192,384]{2,1,0:T(8,128)(2,1)} %get-tuple-element.97.refs_6_), channel_id=1, source_target_pairs={{0,1},{1,0},{2,3},{3,2},{4,5},{5,4},{6,7},{7,6},{8,9},{9,8},{10,11... | collective-permute-start | bytes 7077896 | tf_op jit(solution)/shard_map/ppermute | solution.py:67
  456.8 37.3 %collective-permute-start.24 = (bf16[8,192,384]{2,1,0:T(8,128)(2,1)S(1)}, bf16[8,192,384]{2,1,0:T(8,128)(2,1)S(1)}, u32[]{:S(2)}, u32[]{:S(2)}) collective-permute-start(bf16[8,192,384]{2,1,0:T(8,128)(2,1)S(1)} %get-tuple-element.126.refs_8_), channel_id=1, source_target_pairs={{0,4},{2,6},{4,0},{6,2},{8,12},{10,14},{12,8},{14,10},{16,20},{18,... | collective-permute-start | bytes 3538952 | tf_op jit(solution)/shard_map/ppermute | solution.py:67
  460.5 34.8 %collective-permute-start.23 = (bf16[8,192,384]{2,1,0:T(8,128)(2,1)S(1)}, bf16[8,192,384]{2,1,0:T(8,128)(2,1)}, u32[]{:S(2)}, u32[]{:S(2)}) collective-permute-start(bf16[8,192,384]{2,1,0:T(8,128)(2,1)S(1)} %get-tuple-element.128.refs_7_), channel_id=1, source_target_pairs={{0,2},{2,0},{4,6},{6,4},{8,10},{10,8},{12,14},{14,12},{16,18},{18,... | collective-permute-start | bytes 3538952 | tf_op jit(solution)/shard_map/ppermute | solution.py:67
  497.7 128.0 %all-to-all-start.3 = ((bf16[32,96,768]{2,1,0:T(8,128)(2,1)}), bf16[32,96,768]{2,1,0:T(8,128)(2,1)}, u32[]{:S(2)}, u32[]{:S(2)}) async-start(bf16[32,96,768]{2,1,0:T(8,128)(2,1)} %hold.16), calls=%async_computation.3 | async-start | bytes 9437184 | tf_op jit(solution)/shard_map/all_to_all | solution.py:1081
  503.2 72.7 %collective-permute-start.25 = (bf16[8,192,384]{2,1,0:T(8,128)(2,1)}, bf16[8,192,384]{2,1,0:T(8,128)(2,1)}, u32[]{:S(2)}, u32[]{:S(2)}) collective-permute-start(bf16[8,192,384]{2,1,0:T(8,128)(2,1)} %get-tuple-element.129.refs_5_), channel_id=1, source_target_pairs={{0,2},{2,0},{4,6},{6,4},{8,10},{10,8},{12,14},{14,12},{16,18},{18,... | collective-permute-start | bytes 3538952 | tf_op jit(solution)/shard_map/ppermute | solution.py:67
  509.6 67.7 %collective-permute-start.28 = (bf16[8,208,384]{2,1,0:T(8,128)(2,1)}, bf16[8,208,384]{2,1,0:T(8,128)(2,1)}, u32[]{:S(2)}, u32[]{:S(2)}) collective-permute-start(bf16[8,208,384]{2,1,0:T(8,128)(2,1)} %get-tuple-element.124), channel_id=1, source_target_pairs={{0,4},{2,6},{4,0},{6,2},{8,12},{10,14},{12,8},{14,10},{16,20},{18,... | collective-permute-start | bytes 3833864 | tf_op jit(solution)/shard_map/ppermute | solution.py:67
  577.2 22.1 %collective-permute-start.26 = (bf16[4,192,384]{2,1,0:T(8,128)(2,1)S(1)}, bf16[4,192,384]{2,1,0:T(8,128)(2,1)S(1)}, u32[]{:S(2)}, u32[]{:S(2)}) collective-permute-start(bf16[4,192,384]{2,1,0:T(8,128)(2,1)S(1)} %get-tuple-element.134), channel_id=1, source_target_pairs={{0,4},{2,6},{4,0},{6,2},{8,12},{10,14},{12,8},{14,10},{16,20},{18,... | collective-permute-start | bytes 1769480 | tf_op jit(solution)/shard_map/ppermute | solution.py:67
  578.8 23.7 %collective-permute-start.29 = (bf16[4,208,384]{2,1,0:T(8,128)(2,1)S(1)}, bf16[4,208,384]{2,1,0:T(8,128)(2,1)S(1)}, u32[]{:S(2)}, u32[]{:S(2)}) collective-permute-start(bf16[4,208,384]{2,1,0:T(8,128)(2,1)S(1)} %get-tuple-element.132), channel_id=1, source_target_pairs={{0,2},{2,0},{4,6},{6,4},{8,10},{10,8},{12,14},{14,12},{16,18},{18,... | collective-permute-start | bytes 1916936 | tf_op jit(solution)/shard_map/ppermute | solution.py:67
  585.5 36.9 %collective-permute-start.32 = (bf16[4,192,384]{2,1,0:T(8,128)(2,1)S(1)}, bf16[4,192,384]{2,1,0:T(8,128)(2,1)}, u32[]{:S(2)}, u32[]{:S(2)}) collective-permute-start(bf16[4,192,384]{2,1,0:T(8,128)(2,1)S(1)} %copy-done.108), channel_id=1, source_target_pairs={{0,2},{2,0},{4,6},{6,4},{8,10},{10,8},{12,14},{14,12},{16,18},{18,... | collective-permute-start | bytes 1769480 | tf_op jit(solution)/shard_map/ppermute | solution.py:67
  585.6 39.0 %collective-permute-start.31 = (bf16[4,192,384]{2,1,0:T(8,128)(2,1)}, bf16[4,192,384]{2,1,0:T(8,128)(2,1)S(1)}, u32[]{:S(2)}, u32[]{:S(2)}) collective-permute-start(bf16[4,192,384]{2,1,0:T(8,128)(2,1)} %get-tuple-element.137.refs_7_), channel_id=1, source_target_pairs={{0,4},{2,6},{4,0},{6,2},{8,12},{10,14},{12,8},{14,10},{16,20},{18,... | collective-permute-start | bytes 1769480 | tf_op jit(solution)/shard_map/ppermute | solution.py:67
  603.5 31.3 %collective-permute-start.30 = (bf16[2,400,384]{2,1,0:T(8,128)(2,1)}, bf16[2,400,384]{2,1,0:T(8,128)(2,1)}, u32[]{:S(2)}, u32[]{:S(2)}) collective-permute-start(bf16[2,400,384]{2,1,0:T(8,128)(2,1)} %pad_maximum_fusion.7), channel_id=1, source_target_pairs={{0,8},{2,10},{4,12},{6,14},{8,0},{10,2},{12,4},{14,6},{16,24},{18,... | collective-permute-start | bytes 1843208 | tf_op jit(solution)/shard_map/ppermute | solution.py:67
  637.2 25.9 %collective-permute-start.34 = (bf16[1,784,384]{2,1,0:T(8,128)(2,1)S(1)}, bf16[1,784,384]{2,1,0:T(8,128)(2,1)}, u32[]{:S(2)}, u32[]{:S(2)}) collective-permute-start(bf16[1,784,384]{2,1,0:T(8,128)(2,1)S(1)} %pad_maximum_fusion.8.refs_1_), channel_id=1, source_target_pairs={{0,16},{2,18},{4,20},{6,22},{8,24},{10,26},{12,28},{14,30},{16,0},... | collective-permute-start | bytes 1806344 | tf_op jit(solution)/shard_map/ppermute | solution.py:67
  (133 other events, 1231.1 us)

commit v6 on v5

--- a/solution.py
+++ b/solution.py
@@ -1291,9 +1291,10 @@
 
     if len(send_back) > 1:
         attn_two = scatter_bits(*attn_two, back_b[: near - 2])
-        attn = join_pairs(on_both([attn_one, attn_two], near - 2, near))
+        attn = on_both([attn_one, attn_two], near - 2, near - 1)
     else:
-        attn = join_pairs(on_both([attn_one, attn_two], 0, near))
+        attn = on_both([attn_one, attn_two], 0, near - 1)
+
     def behind(pair, array):
         return (hold(pair[0], [array]), pair[1]) if by_rows else pair
 
@@ -1306,7 +1307,9 @@
     for args in lists[:-1]:
         so_far = (store_sum(*args),)
         ff = [behind(pair, so_far[0]) for pair in ff]
+        attn = [behind(pair, so_far[0]) for pair in attn]
     ff = join_pairs(on_both(ff, near - 1, near))
+    attn = join_pairs(on_both(attn, near - 1, near))
     grad_store = store_sum(*lists[-1], so_far, (0, 2)) if so_far else None
     if so_far:
         ff, attn = behind(ff, grad_store), behind(attn, grad_store)

time: 676 us -> 676 us (level)
  transfers between devices with their start and end apart: 39 -> 39, of which waited for: 15 -> 15; matrix products, arithmetic and copies ran while one was open for 15% -> 16% of each run, Pallas kernels for 21% -> 21%
where the time goes in v6:
time: 676 us; the launch traced here: 669 us
  waiting for transfers between devices  237 us (35%)
  Pallas kernels  202 us (30%)
  local copies, waits for them, and re-layouts  99.6 us (15%)
  starting transfers between devices  59.2 us (9%)
  other arithmetic  53.7 us (8%)
  matrix products  15 us (2%)
    ppermute x35, waiting for transfers between devices, swap_bit(): return lax.ppermute(array, axis, pairs)  227 us
    unnamed x258, local copies, waits for them, and re-layouts  52.4 us
    ppermute x35, starting transfers between devices, swap_bit(): return lax.ppermute(array, axis, pairs)  39.1 us
    pallas_call x3, Pallas kernels, store_sum(): pl.pallas_call(functools.partial(store_sum_kernel, block=block, skip=skip...  32.7 us
    pallas_call x2, Pallas kernels, send(): self.call(rows_out_kernel, 'rows_out', 14, [lanes, lanes, some, some] + s...  31.1 us
    gather x1, local copies, waits for them, and re-layouts, on_device(): answer = enc_store[jnp.maximum(asked - 1, 0)]  26.3 us
    pallas_call x1, Pallas kernels, weights(): self.call(rows_weights_kernel, 'rows_weights', 24, self.factor_specs + [s...  24.4 us
    pallas_call x1, Pallas kernels, forward(): self.call(rows_in_kernel, 'rows_in', 22, [self.rows, self.rows, *self.w_s...  23.2 us
  transfers between devices with their start and end apart: 39, of which 15 were waited for; matrix products, arithmetic and copies ran while one was open for 16% of the time, Pallas kernels for 21%

profile of v6, /device:TPU:0, one launch (start us, length us, event | category | flops | bytes accessed | tf_op | source)
XLA Modules:
  0.0 669.1 jit_solution(7051433223170355147)
XLA Ops:
  4.9 4.5 plan.1
  10.8 6.1 all-to-all-start
  41.5 26.3 %gather_fusion.2 = bf16[6144,768]{1,0:T(8,128)(2,1)} fusion(bf16[2048,768]{1,0:T(8,128)(2,1)S(1)} %copy-done, s32[6144]{0:T(1024)S(1)} %broadcast_clamp_fusion), kind=kCustom, calls=%fused_computation.2 | custom fusion | bytes 18898944 | tf_op jit(solution)/shard_map/gather | solution.py:1145
  88.4 5.1 all-to-all-start.1
  103.5 96.2 %collective-permute-done.8 = bf16[8,208,384]{2,1,0:T(8,128)(2,1)} collective-permute-done((bf16[8,208,384]{2,1,0:T(8,128)(2,1)}, bf16[8,208,384]{2,1,0:T(8,128)(2,1)}, u32[]{:S(2)}, u32[]{:S(2)}) %collective-permute-start.8) | collective-permute-done | bytes 1277984 | tf_op jit(solution)/shard_map/ppermute | solution.py:67
  202.3 11.4 %collective-permute-done.3 = bf16[8,192,384]{2,1,0:T(8,128)(2,1)S(1)} collective-permute-done((bf16[8,192,384]{2,1,0:T(8,128)(2,1)}, bf16[8,192,384]{2,1,0:T(8,128)(2,1)S(1)}, u32[]{:S(2)}, u32[]{:S(2)}) %collective-permute-start.3) | collective-permute-done | bytes 1179680 | tf_op jit(solution)/shard_map/ppermute | solution.py:67
  217.5 13.6 %collective-permute-done.17 = bf16[4,192,384]{2,1,0:T(8,128)(2,1)} collective-permute-done((bf16[4,192,384]{2,1,0:T(8,128)(2,1)}, bf16[4,192,384]{2,1,0:T(8,128)(2,1)}, u32[]{:S(2)}, u32[]{:S(2)}) %collective-permute-start.17) | collective-permute-done | bytes 589856 | tf_op jit(solution)/shard_map/ppermute | solution.py:67
  237.0 4.4 collective-permute-start.15
  258.4 4.7 self_fwd.1
  263.9 5.3 query_rows.1.query.refs_1_.refs_3_
  269.3 4.8 collective-permute-done.18
  293.3 9.6 %all-to-all-done.1.arrived.refs_4_ = bf16[32,192,768]{2,1,0:T(8,128)(2,1)} async-done(((bf16[32,192,768]{2,1,0:T(8,128)(2,1)}), bf16[32,192,768]{2,1,0:T(8,128)(2,1)}, u32[]{:S(2)}, u32[]{:S(2)}) %all-to-all-start.1) | async-done | bytes 9437216 | tf_op jit(solution)/shard_map/all_to_all | solution.py:1081
  305.2 23.2 %rows_in.1 = (bf16[32,192,768]{2,1,0:T(8,128)(2,1)}, bf16[32,192,768]{2,1,0:T(8,128)(2,1)}, f32[192,512]{1,0:T(8,128)S(1)}) custom-call(bf16[32,192,768]{2,1,0:T(8,128)(2,1)} %all-to-all-done.1.arrived.refs_4_, bf16[32,192,768]{2,1,0:T(8,128)(2,1)} %query_rows.1.query.refs_1_.refs_3_, bf16[4,768,768]{2,1,0:T(8,128)(2,1)S(1)} %copy-done.59, ...), custom_call_target="tpu_custom_call" | custom-call | flops 24199999488 | tf_op jit(solution)/shard_map/rows_in/pallas_call | solution.py:914
  328.4 11.6 %attend.1 = (f32[256,256]{1,0:T(8,128)S(1)}, f32[192,512]{1,0:T(8,128)S(1)}, bf16[256,768]{1,0:T(8,128)(2,1)S(1)}) custom-call(f32[192,512]{1,0:T(8,128)S(1)} %get-tuple-element.69.scores, bf16[32,192,768]{2,1,0:T(8,128)(2,1)} %get-tuple-element.70.vals, bf16[256,6144]{1,0:T(8,128)(2,1)S(1)} %copy-done.13, bf16[256,4096]{1,0:T(8,128)(2,1)S(1)} %copy-done.77, ...), custom_call_target="tpu_custom_call" | custom-call | flops 12099999744 | tf_op jit(solution)/shard_map/attend/pallas_call | solution.py:923
  354.1 14.3 %attend_back.1 = (bf16[32,192,768]{2,1,0:T(8,128)(2,1)}, f32[192,512]{1,0:T(8,128)S(1)}) custom-call(bf16[32,192,768]{2,1,0:T(8,128)(2,1)} %get-tuple-element.70.vals, bf16[6144,256]{1,0:T(8,128)(2,1)S(1)} %copy-done.16, bf16[256,768]{1,0:T(8,128)(2,1)S(1)} %convolution_convert_fusion.grad.refs_4_, f32[256,256]{1,0:T(8,128)S(1)} %get-tuple-element.75.prob_tok, ...), custom_call_target="tpu_custom_call" | custom-call | flops 14300000256 | tf_op jit(solution)/shard_map/attend_back/pallas_call | solution.py:941
  368.4 15.6 %rows_out.2 = (bf16[32,96,768]{2,1,0:T(8,128)(2,1)}, f32[8,128]{1,0:T(8,128)S(1)}) custom-call(f32[192,512]{1,0:T(8,128)S(1)} %get-tuple-element.77.prob_slot.refs_0_, f32[192,512]{1,0:T(8,128)S(1)} %get-tuple-element.76.grad_slot.refs_1_, bf16[32,192,768]{2,1,0:T(8,128)(2,1)} %get-tuple-element.78.grad.refs_2_, ...), custom_call_target="tpu_custom_call" | custom-call | flops 15399999488 | tf_op jit(solution)/shard_map/rows_out/pallas_call | solution.py:960
  390.2 15.6 %rows_out.3 = (bf16[32,96,768]{2,1,0:T(8,128)(2,1)}, f32[8,128]{1,0:T(8,128)S(1)}) custom-call(f32[192,512]{1,0:T(8,128)S(1)} %copy-done.90, f32[192,512]{1,0:T(8,128)S(1)} %get-tuple-element.76.grad_slot.refs_1_, bf16[32,192,768]{2,1,0:T(8,128)(2,1)} %get-tuple-element.78.grad.refs_2_, bf16[32,192,768]{2,1,0:T(8,128)(2,1)} %query_rows.1.query.refs_1_.refs_3_, ...), custom_call_target="tpu_custom_call" | custom-call | flops 15399999488 | tf_op jit(solution)/shard_map/rows_out/pallas_call | solution.py:960
  405.8 7.9 %query_back.1.refs_2_.refs_0_ = bf16[256,768]{1,0:T(8,128)(2,1)S(1)} custom-call(bf16[32,192,768]{2,1,0:T(8,128)(2,1)} %get-tuple-element.74.keys, bf16[256,6144]{1,0:T(8,128)(2,1)S(1)} %copy-done.14, f32[192,512]{1,0:T(8,128)S(1)} %get-tuple-element.76.grad_slot.refs_1_, f32[8,128]{1,0:T(8,128)S(1)} %get-tuple-element.80.waited), custom_call_target="tpu_custom_call" | custom-call | flops 7699999744 | tf_op jit(solution)/shard_map/query_back/pallas_call | solution.py:975
  413.7 4.2 pack.5
  418.2 4.2 pack.4
  436.8 5.6 self_bwd.1
  450.3 4.1 pack.6
  462.1 24.4 %rows_weights.1 = (bf16[768,768]{1,0:T(8,128)(2,1)S(1)}, bf16[768,768]{1,0:T(8,128)(2,1)S(1)}) custom-call(f32[192,512]{1,0:T(8,128)S(1)} %copy-done.91, f32[192,512]{1,0:T(8,128)S(1)} %copy-done.86, bf16[32,192,768]{2,1,0:T(8,128)(2,1)} %get-tuple-element.78.grad.refs_2_, bf16[32,192,768]{2,1,0:T(8,128)(2,1)} %query_rows.1.query.refs_1_.refs_3_, ...), custom_call_target="tpu_custom_call" | custom-call | flops 26400000000 | tf_op jit(solution)/shard_map/rows_weights/pallas_call | solution.py:987
  486.6 4.2 pack.7
  497.7 5.1 all-to-all-start.3
  521.5 55.0 %collective-permute-done.25 = bf16[8,192,384]{2,1,0:T(8,128)(2,1)} collective-permute-done((bf16[8,192,384]{2,1,0:T(8,128)(2,1)}, bf16[8,192,384]{2,1,0:T(8,128)(2,1)}, u32[]{:S(2)}, u32[]{:S(2)}) %collective-permute-start.25) | collective-permute-done | bytes 1179680 | tf_op jit(solution)/shard_map/ppermute | solution.py:67
  583.4 14.4 %store_sum.3.refs_0_.refs_1_ = f32[2048,768]{1,0:T(8,128)} custom-call(s32[1,3072]{1,0:T(1,128)} %reshape.148.asked, bf16[3072,768]{1,0:T(8,128)(2,1)} %bitcast.17.returned), custom_call_target="tpu_custom_call" | custom-call | flops 14300000256 | tf_op jit(solution)/shard_map/store_sum/pallas_call | solution.py:1062
  603.7 5.1 collective-permute-done.26
  614.2 9.1 %store_sum.4.refs_1_.refs_0_ = f32[2048,768]{1,0:T(8,128)} custom-call(s32[1,3072]{1,0:T(1,128)} %reshape.144.asked, bf16[3072,768]{1,0:T(8,128)(2,1)} %bitcast.16.returned, f32[2048,768]{1,0:T(8,128)} %store_sum.3.refs_0_.refs_1_), custom_call_target="tpu_custom_call", output_to_operand_aliasing={{}: (2, {})} | custom-call | flops 8800000000 | tf_op jit(solution)/shard_map/store_sum/pallas_call | solution.py:1062
  625.6 8.4 %collective-permute-done.30 = bf16[2,400,384]{2,1,0:T(8,128)(2,1)S(1)} collective-permute-done((bf16[2,400,384]{2,1,0:T(8,128)(2,1)}, bf16[2,400,384]{2,1,0:T(8,128)(2,1)S(1)}, u32[]{:S(2)}, u32[]{:S(2)}) %collective-permute-start.30) | collective-permute-done | bytes 614432 | tf_op jit(solution)/shard_map/ppermute | solution.py:67
  635.1 9.1 %store_sum.5.refs_1_ = f32[2048,768]{1,0:T(8,128)} custom-call(s32[1,3072]{1,0:T(1,128)} %reshape.144.asked, bf16[3072,768]{1,0:T(8,128)(2,1)} %bitcast.16.returned, f32[2048,768]{1,0:T(8,128)} %store_sum.4.refs_1_.refs_0_, bf16[1,784,384]{2,1,0:T(8,128)(2,1)} %copy-done.115), custom_call_target="tpu_custom_call", output_to_operand_aliasing={{}: (2, {})} | custom-call | flops 8800000000 | tf_op jit(solution)/shard_map/store_sum/pallas_call | solution.py:1062
  644.2 18.4 %collective-permute-done.34 = bf16[1,784,384]{2,1,0:T(8,128)(2,1)} collective-permute-done((bf16[1,784,384]{2,1,0:T(8,128)(2,1)S(1)}, bf16[1,784,384]{2,1,0:T(8,128)(2,1)}, u32[]{:S(2)}, u32[]{:S(2)}) %collective-permute-start.34) | collective-permute-done | bytes 602144 | tf_op jit(solution)/shard_map/ppermute | solution.py:67
  (458 shorter events, 215.4 us)
Async XLA Ops:
  0.7 25.5 %collective-permute-start.10 = (bf16[1,48,1536]{2,1,0:T(8,128)(2,1)}, bf16[1,48,1536]{2,1,0:T(8,128)(2,1)}, u32[]{:S(2)}, u32[]{:S(2)}) collective-permute-start(bf16[1,48,1536]{2,1,0:T(8,128)(2,1)} %bitcast.99), channel_id=1, source_target_pairs={{0,16},{2,18},{4,20},{6,22},{8,24},{10,26},{12,28},{14,30},{16,0},... | collective-permute-start | bytes 442376 | tf_op jit(solution)/shard_map/ppermute | solution.py:67
  4.8 24.9 %collective-permute-start.12 = (bf16[1,192,384]{2,1,0:T(8,128)(2,1)}, bf16[1,192,384]{2,1,0:T(8,128)(2,1)}, u32[]{:S(2)}, u32[]{:S(2)}) collective-permute-start(bf16[1,192,384]{2,1,0:T(8,128)(2,1)} %bitcast.95), channel_id=1, source_target_pairs={{0,16},{2,18},{4,20},{6,22},{8,24},{10,26},{12,28},{14,30},{16,0},... | collective-permute-start | bytes 442376 | tf_op jit(solution)/shard_map/ppermute | solution.py:67
  27.8 48.7 %collective-permute-start.11 = (bf16[2,48,1536]{2,1,0:T(8,128)(2,1)}, bf16[2,48,1536]{2,1,0:T(8,128)(2,1)}, u32[]{:S(2)}, u32[]{:S(2)}) collective-permute-start(bf16[2,48,1536]{2,1,0:T(8,128)(2,1)} %pad_maximum_fusion.15), channel_id=1, source_target_pairs={{0,8},{2,10},{4,12},{6,14},{8,0},{10,2},{12,4},{14,6},{16,24},{18,... | collective-permute-start | bytes 884744 | tf_op jit(solution)/shard_map/ppermute | solution.py:67
  31.3 43.3 %collective-permute-start.13 = (bf16[2,192,384]{2,1,0:T(8,128)(2,1)}, bf16[2,192,384]{2,1,0:T(8,128)(2,1)}, u32[]{:S(2)}, u32[]{:S(2)}) collective-permute-start(bf16[2,192,384]{2,1,0:T(8,128)(2,1)} %pad_maximum_fusion.16), channel_id=1, source_target_pairs={{0,8},{2,10},{4,12},{6,14},{8,0},{10,2},{12,4},{14,6},{16,24},{18,... | collective-permute-start | bytes 884744 | tf_op jit(solution)/shard_map/ppermute | solution.py:67
  35.5 32.3 %collective-permute-start.1 = (bf16[2,192,384]{2,1,0:T(8,128)(2,1)}, bf16[2,192,384]{2,1,0:T(8,128)(2,1)}, u32[]{:S(2)}, u32[]{:S(2)}) collective-permute-start(bf16[2,192,384]{2,1,0:T(8,128)(2,1)} %get-tuple-element.171.refs_1_), channel_id=1, source_target_pairs={{0,8},{2,10},{4,12},{6,14},{8,0},{10,2},{12,4},{14,6},{16,24},{18,... | collective-permute-start | bytes 884744 | tf_op jit(solution)/shard_map/ppermute | solution.py:67
  38.3 32.6 %collective-permute-start.6 = (bf16[2,208,384]{2,1,0:T(8,128)(2,1)}, bf16[2,208,384]{2,1,0:T(8,128)(2,1)}, u32[]{:S(2)}, u32[]{:S(2)}) collective-permute-start(bf16[2,208,384]{2,1,0:T(8,128)(2,1)} %get-tuple-element.167.refs_2_), channel_id=1, source_target_pairs={{0,8},{2,10},{4,12},{6,14},{8,0},{10,2},{12,4},{14,6},{16,24},{18,... | collective-permute-start | bytes 958472 | tf_op jit(solution)/shard_map/ppermute | solution.py:67
  72.1 15.2 %collective-permute-start.7 = (bf16[4,208,384]{2,1,0:T(8,128)(2,1)S(1)}, bf16[4,208,384]{2,1,0:T(8,128)(2,1)S(1)}, u32[]{:S(2)}, u32[]{:S(2)}) collective-permute-start(bf16[4,208,384]{2,1,0:T(8,128)(2,1)S(1)} %pad_maximum_fusion.5), channel_id=1, source_target_pairs={{0,2},{2,0},{4,6},{6,4},{8,10},{10,8},{12,14},{14,12},{16,18},{18,... | collective-permute-start | bytes 1916936 | tf_op jit(solution)/shard_map/ppermute | solution.py:67
  88.4 214.4 %all-to-all-start.1 = ((bf16[32,192,768]{2,1,0:T(8,128)(2,1)}), bf16[32,192,768]{2,1,0:T(8,128)(2,1)}, u32[]{:S(2)}, u32[]{:S(2)}) async-start(bf16[32,192,768]{2,1,0:T(8,128)(2,1)} %hold.14), calls=%async_computation.1 | async-start | bytes 18874368 | tf_op jit(solution)/shard_map/all_to_all | solution.py:1081
  96.6 103.1 %collective-permute-start.8 = (bf16[8,208,384]{2,1,0:T(8,128)(2,1)}, bf16[8,208,384]{2,1,0:T(8,128)(2,1)}, u32[]{:S(2)}, u32[]{:S(2)}) collective-permute-start(bf16[8,208,384]{2,1,0:T(8,128)(2,1)} %get-tuple-element.161.refs_2_), channel_id=1, source_target_pairs={{0,4},{2,6},{4,0},{6,2},{8,12},{10,14},{12,8},{14,10},{16,20},{18,... | collective-permute-start | bytes 3833864 | tf_op jit(solution)/shard_map/ppermute | solution.py:67
  102.0 111.7 %collective-permute-start.3 = (bf16[8,192,384]{2,1,0:T(8,128)(2,1)}, bf16[8,192,384]{2,1,0:T(8,128)(2,1)S(1)}, u32[]{:S(2)}, u32[]{:S(2)}) collective-permute-start(bf16[8,192,384]{2,1,0:T(8,128)(2,1)} %hold.13), channel_id=1, source_target_pairs={{0,2},{2,0},{4,6},{6,4},{8,10},{10,8},{12,14},{14,12},{16,18},{18,... | collective-permute-start | bytes 3538952 | tf_op jit(solution)/shard_map/ppermute | solution.py:67
  202.2 44.0 %collective-permute-start.9 = (bf16[16,208,384]{2,1,0:T(8,128)(2,1)}, bf16[16,208,384]{2,1,0:T(8,128)(2,1)}, u32[]{:S(2)}, u32[]{:S(2)}) collective-permute-start(bf16[16,208,384]{2,1,0:T(8,128)(2,1)} %constant_dynamic-update-slice_fusion.12.own), channel_id=1, source_target_pairs={{0,1},{1,0},{2,3},{3,2},{4,5},{5,4},{6,7},{7,6},{8,9},{9,8},{10,11... | collective-permute-start | bytes 7667720 | tf_op jit(solution)/shard_map/ppermute | solution.py:67
  214.0 27.4 %collective-permute-start.4 = (bf16[16,192,384]{2,1,0:T(8,128)(2,1)S(1)}, bf16[16,192,384]{2,1,0:T(8,128)(2,1)}, u32[]{:S(2)}, u32[]{:S(2)}) collective-permute-start(bf16[16,192,384]{2,1,0:T(8,128)(2,1)S(1)} %pad_maximum_fusion.own), channel_id=1, source_target_pairs={{0,1},{1,0},{2,3},{3,2},{4,5},{5,4},{6,7},{7,6},{8,9},{9,8},{10,11... | collective-permute-start | bytes 7077896 | tf_op jit(solution)/shard_map/ppermute | solution.py:67
  214.0 17.0 %collective-permute-start.17 = (bf16[4,192,384]{2,1,0:T(8,128)(2,1)}, bf16[4,192,384]{2,1,0:T(8,128)(2,1)}, u32[]{:S(2)}, u32[]{:S(2)}) collective-permute-start(bf16[4,192,384]{2,1,0:T(8,128)(2,1)} %pad_maximum_fusion.12.refs_4_), channel_id=1, source_target_pairs={{0,2},{2,0},{4,6},{6,4},{8,10},{10,8},{12,14},{14,12},{16,18},{18,... | collective-permute-start | bytes 1769480 | tf_op jit(solution)/shard_map/ppermute | solution.py:67
  214.1 20.5 %collective-permute-start.14 = (bf16[4,48,1536]{2,1,0:T(8,128)(2,1)S(1)}, bf16[4,48,1536]{2,1,0:T(8,128)(2,1)}, u32[]{:S(2)}, u32[]{:S(2)}) collective-permute-start(bf16[4,48,1536]{2,1,0:T(8,128)(2,1)S(1)} %copy-done.109), channel_id=1, source_target_pairs={{0,4},{2,6},{4,0},{6,2},{8,12},{10,14},{12,8},{14,10},{16,20},{18,... | collective-permute-start | bytes 1769480 | tf_op jit(solution)/shard_map/ppermute | solution.py:67
  233.4 40.7 %collective-permute-start.18 = (bf16[8,192,384]{2,1,0:T(8,128)(2,1)}, bf16[8,192,384]{2,1,0:T(8,128)(2,1)}, u32[]{:S(2)}, u32[]{:S(2)}) collective-permute-start(bf16[8,192,384]{2,1,0:T(8,128)(2,1)} %pad_maximum_fusion.4.refs_0_), channel_id=1, source_target_pairs={{0,4},{2,6},{4,0},{6,2},{8,12},{10,14},{12,8},{14,10},{16,20},{18,... | collective-permute-start | bytes 3538952 | tf_op jit(solution)/shard_map/ppermute | solution.py:67
  237.0 37.1 %collective-permute-start.15 = (bf16[8,48,1536]{2,1,0:T(8,128)(2,1)}, bf16[8,48,1536]{2,1,0:T(8,128)(2,1)}, u32[]{:S(2)}, u32[]{:S(2)}) collective-permute-start(bf16[8,48,1536]{2,1,0:T(8,128)(2,1)} %pad_maximum_fusion.3.refs_0_), channel_id=1, source_target_pairs={{0,2},{2,0},{4,6},{6,4},{8,10},{10,8},{12,14},{14,12},{16,18},{18,... | collective-permute-start | bytes 3538952 | tf_op jit(solution)/shard_map/ppermute | solution.py:67
  383.9 113.7 %all-to-all-start.2 = ((bf16[32,96,768]{2,1,0:T(8,128)(2,1)}), bf16[32,96,768]{2,1,0:T(8,128)(2,1)}, u32[]{:S(2)}, u32[]{:S(2)}) async-start(bf16[32,96,768]{2,1,0:T(8,128)(2,1)} %get-tuple-element.95), calls=%async_computation.2 | async-start | bytes 9437184 | tf_op jit(solution)/shard_map/all_to_all | solution.py:1081
  417.9 36.8 %collective-permute-start.21 = (bf16[16,192,384]{2,1,0:T(8,128)(2,1)}, bf16[16,192,384]{2,1,0:T(8,128)(2,1)}, u32[]{:S(2)}, u32[]{:S(2)}) collective-permute-start(bf16[16,192,384]{2,1,0:T(8,128)(2,1)} %get-tuple-element.84.refs_4_), channel_id=1, source_target_pairs={{0,1},{1,0},{2,3},{3,2},{4,5},{5,4},{6,7},{7,6},{8,9},{9,8},{10,11... | collective-permute-start | bytes 7077896 | tf_op jit(solution)/shard_map/ppermute | solution.py:67
  422.4 36.2 %collective-permute-start.20 = (bf16[16,192,384]{2,1,0:T(8,128)(2,1)}, bf16[16,192,384]{2,1,0:T(8,128)(2,1)}, u32[]{:S(2)}, u32[]{:S(2)}) collective-permute-start(bf16[16,192,384]{2,1,0:T(8,128)(2,1)} %get-tuple-element.82.refs_2_), channel_id=1, source_target_pairs={{0,1},{1,0},{2,3},{3,2},{4,5},{5,4},{6,7},{7,6},{8,9},{9,8},{10,11... | collective-permute-start | bytes 7077896 | tf_op jit(solution)/shard_map/ppermute | solution.py:67
  454.4 36.3 %collective-permute-start.22 = (bf16[16,192,384]{2,1,0:T(8,128)(2,1)}, bf16[16,192,384]{2,1,0:T(8,128)(2,1)}, u32[]{:S(2)}, u32[]{:S(2)}) collective-permute-start(bf16[16,192,384]{2,1,0:T(8,128)(2,1)} %get-tuple-element.97.refs_6_), channel_id=1, source_target_pairs={{0,1},{1,0},{2,3},{3,2},{4,5},{5,4},{6,7},{7,6},{8,9},{9,8},{10,11... | collective-permute-start | bytes 7077896 | tf_op jit(solution)/shard_map/ppermute | solution.py:67
  456.8 37.3 %collective-permute-start.24 = (bf16[8,192,384]{2,1,0:T(8,128)(2,1)S(1)}, bf16[8,192,384]{2,1,0:T(8,128)(2,1)S(1)}, u32[]{:S(2)}, u32[]{:S(2)}) collective-permute-start(bf16[8,192,384]{2,1,0:T(8,128)(2,1)S(1)} %get-tuple-element.126.refs_8_), channel_id=1, source_target_pairs={{0,4},{2,6},{4,0},{6,2},{8,12},{10,14},{12,8},{14,10},{16,20},{18,... | collective-permute-start | bytes 3538952 | tf_op jit(solution)/shard_map/ppermute | solution.py:67
  460.5 34.8 %collective-permute-start.23 = (bf16[8,192,384]{2,1,0:T(8,128)(2,1)S(1)}, bf16[8,192,384]{2,1,0:T(8,128)(2,1)}, u32[]{:S(2)}, u32[]{:S(2)}) collective-permute-start(bf16[8,192,384]{2,1,0:T(8,128)(2,1)S(1)} %get-tuple-element.128.refs_7_), channel_id=1, source_target_pairs={{0,2},{2,0},{4,6},{6,4},{8,10},{10,8},{12,14},{14,12},{16,18},{18,... | collective-permute-start | bytes 3538952 | tf_op jit(solution)/shard_map/ppermute | solution.py:67
  497.7 116.6 %all-to-all-start.3 = ((bf16[32,96,768]{2,1,0:T(8,128)(2,1)}), bf16[32,96,768]{2,1,0:T(8,128)(2,1)}, u32[]{:S(2)}, u32[]{:S(2)}) async-start(bf16[32,96,768]{2,1,0:T(8,128)(2,1)} %hold.18), calls=%async_computation.3 | async-start | bytes 9437184 | tf_op jit(solution)/shard_map/all_to_all | solution.py:1081
  503.2 73.3 %collective-permute-start.25 = (bf16[8,192,384]{2,1,0:T(8,128)(2,1)}, bf16[8,192,384]{2,1,0:T(8,128)(2,1)}, u32[]{:S(2)}, u32[]{:S(2)}) collective-permute-start(bf16[8,192,384]{2,1,0:T(8,128)(2,1)} %get-tuple-element.129.refs_5_), channel_id=1, source_target_pairs={{0,2},{2,0},{4,6},{6,4},{8,10},{10,8},{12,14},{14,12},{16,18},{18,... | collective-permute-start | bytes 3538952 | tf_op jit(solution)/shard_map/ppermute | solution.py:67
  509.6 69.3 %collective-permute-start.28 = (bf16[8,208,384]{2,1,0:T(8,128)(2,1)}, bf16[8,208,384]{2,1,0:T(8,128)(2,1)}, u32[]{:S(2)}, u32[]{:S(2)}) collective-permute-start(bf16[8,208,384]{2,1,0:T(8,128)(2,1)} %get-tuple-element.124), channel_id=1, source_target_pairs={{0,4},{2,6},{4,0},{6,2},{8,12},{10,14},{12,8},{14,10},{16,20},{18,... | collective-permute-start | bytes 3833864 | tf_op jit(solution)/shard_map/ppermute | solution.py:67
  519.4 78.4 %collective-permute-start.32 = (bf16[4,192,384]{2,1,0:T(8,128)(2,1)}, bf16[4,192,384]{2,1,0:T(8,128)(2,1)}, u32[]{:S(2)}, u32[]{:S(2)}) collective-permute-start(bf16[4,192,384]{2,1,0:T(8,128)(2,1)} %get-tuple-element.135.refs_9_), channel_id=1, source_target_pairs={{0,2},{2,0},{4,6},{6,4},{8,10},{10,8},{12,14},{14,12},{16,18},{18,... | collective-permute-start | bytes 1769480 | tf_op jit(solution)/shard_map/ppermute | solution.py:67
  520.9 78.3 %collective-permute-start.31 = (bf16[4,192,384]{2,1,0:T(8,128)(2,1)}, bf16[4,192,384]{2,1,0:T(8,128)(2,1)}, u32[]{:S(2)}, u32[]{:S(2)}) collective-permute-start(bf16[4,192,384]{2,1,0:T(8,128)(2,1)} %get-tuple-element.137.refs_7_), channel_id=1, source_target_pairs={{0,4},{2,6},{4,0},{6,2},{8,12},{10,14},{12,8},{14,10},{16,20},{18,... | collective-permute-start | bytes 1769480 | tf_op jit(solution)/shard_map/ppermute | solution.py:67
  578.9 30.0 %collective-permute-start.26 = (bf16[4,192,384]{2,1,0:T(8,128)(2,1)}, bf16[4,192,384]{2,1,0:T(8,128)(2,1)}, u32[]{:S(2)}, u32[]{:S(2)}) collective-permute-start(bf16[4,192,384]{2,1,0:T(8,128)(2,1)} %get-tuple-element.134), channel_id=1, source_target_pairs={{0,4},{2,6},{4,0},{6,2},{8,12},{10,14},{12,8},{14,10},{16,20},{18,... | collective-permute-start | bytes 1769480 | tf_op jit(solution)/shard_map/ppermute | solution.py:67
  581.3 28.7 %collective-permute-start.29 = (bf16[4,208,384]{2,1,0:T(8,128)(2,1)}, bf16[4,208,384]{2,1,0:T(8,128)(2,1)S(1)}, u32[]{:S(2)}, u32[]{:S(2)}) collective-permute-start(bf16[4,208,384]{2,1,0:T(8,128)(2,1)} %get-tuple-element.132), channel_id=1, source_target_pairs={{0,2},{2,0},{4,6},{6,4},{8,10},{10,8},{12,14},{14,12},{16,18},{18,... | collective-permute-start | bytes 1916936 | tf_op jit(solution)/shard_map/ppermute | solution.py:67
  602.3 21.1 %collective-permute-start.33 = (bf16[2,384,384]{2,1,0:T(8,128)(2,1)}, bf16[2,384,384]{2,1,0:T(8,128)(2,1)}, u32[]{:S(2)}, u32[]{:S(2)}) collective-permute-start(bf16[2,384,384]{2,1,0:T(8,128)(2,1)} %pad_maximum_fusion.14), channel_id=1, source_target_pairs={{0,8},{2,10},{4,12},{6,14},{8,0},{10,2},{12,4},{14,6},{16,24},{18,... | collective-permute-start | bytes 1769480 | tf_op jit(solution)/shard_map/ppermute | solution.py:67
  611.0 22.9 %collective-permute-start.30 = (bf16[2,400,384]{2,1,0:T(8,128)(2,1)}, bf16[2,400,384]{2,1,0:T(8,128)(2,1)S(1)}, u32[]{:S(2)}, u32[]{:S(2)}) collective-permute-start(bf16[2,400,384]{2,1,0:T(8,128)(2,1)} %pad_maximum_fusion.7), channel_id=1, source_target_pairs={{0,8},{2,10},{4,12},{6,14},{8,0},{10,2},{12,4},{14,6},{16,24},{18,... | collective-permute-start | bytes 1843208 | tf_op jit(solution)/shard_map/ppermute | solution.py:67
  634.1 28.6 %collective-permute-start.34 = (bf16[1,784,384]{2,1,0:T(8,128)(2,1)S(1)}, bf16[1,784,384]{2,1,0:T(8,128)(2,1)}, u32[]{:S(2)}, u32[]{:S(2)}) collective-permute-start(bf16[1,784,384]{2,1,0:T(8,128)(2,1)S(1)} %pad_maximum_fusion.8.refs_1_), channel_id=1, source_target_pairs={{0,16},{2,18},{4,20},{6,22},{8,24},{10,26},{12,28},{14,30},{16,0},... | collective-permute-start | bytes 1806344 | tf_op jit(solution)/shard_map/ppermute | solution.py:67
  (133 other events, 1241.0 us)
